TPU v7x, 256 devices: a whole 4x4x8 slice. The times are simulated.
256 devices in a mesh: leaf: 16 (over z, core), front: 16 (over x, y).
Axes of the slice: x: 4, y: 4, z: 8, core: 2. Of those that a mesh axis runs over, the one named last changes fastest.
Arguments:
- rhs_leaf: float32 [16, 1024, 256], P('leaf', 'front'), may hold values from -6 to 6
- rhs_top: float32 [15, 1024, 256], P(None, 'front'), may hold values from -6 to 6
- inv_leaf: bfloat16 [16, 1024, 1024], P('leaf', 'front'), as said below
- inv_top: bfloat16 [15, 1024, 1024], P(None, 'front'), as said below
- off_leaf: bfloat16 [16, 1024, 1024], P('leaf', None, 'front'), may hold values from -0.09375 to 0.09375
- off_top: bfloat16 [14, 1024, 1024], P(None, None, 'front'), may hold values from -0.09375 to 0.09375
- idx_leaf: int32 [16, 1024], P('leaf'), may hold values from 0 to 4095, as said below
- idx_top: int32 [14, 1024], replicated, may hold values from 0 to 3071, as said below
Outputs:
- leaf_solution: float32 [16, 1024, 256], P('leaf', 'front')
- ancestor_solution: float32 [16, 4, 1024, 256], P('leaf', None, 'front')
Inputs may be any that keep to these rules, and one draw needn't show every extreme that they name: `idx_leaf`: entry r of row g is a * 1024 + q with a < 4: update row r of split-level front g lands on row q of its depth-a ancestor. `idx_top`: row j belongs to the upper front with heap number h = j + 2; its entries are a * 1024 + q with a < floor(log2 h): update row r lands on row q of h's depth-a ancestor. `inv_leaf`: every block is lower triangular with a positive diagonal. `inv_top`: every block is lower triangular with a positive diagonal.
All inputs are finite; a program needn't handle non-finite values.
Results may differ from a plain program's by a relative error of at most 0.0055.
Values may be sent and summed in bfloat16 or wider, within the bound.
No kernel may reach another device: no remote copies, remote signals or barrier semaphores. Data moves between devices by JAX's collectives and lax.ppermute only.
A program may use at most 64 MiB of HBM per device.

v0:
```python
import jax
import jax.numpy as jnp
from jax import lax
from jax.sharding import PartitionSpec as P


def partner(block, axis, stride):
    count = lax.axis_size(axis)
    route = []
    for low in range(count):
        high = low | 1 << stride
        if high != low and high < count:
            route += [(low, high), (high, low)]
    return lax.ppermute(block, axis, route)


def local(rhs_leaf, rhs_top, inv_leaf, inv_top, off_leaf, off_top, idx_leaf, idx_top):
    front_width = inv_leaf.shape[2]
    rhs_count = rhs_leaf.shape[2]
    leaves = lax.axis_size("leaf")
    depth_count = leaves.bit_length() - 1
    leaf_pos = lax.axis_index("leaf")

    def apply_inverse(inverse, right_side):
        rounded = right_side.astype(jnp.bfloat16)
        return jnp.dot(
            inverse,
            lax.all_gather(rounded, "front", axis=0, tiled=True),
            preferred_element_type=jnp.float32,
        )

    def spread(off_block, solution, row_list, count):
        partial_value = jnp.dot(
            off_block, solution.astype(jnp.bfloat16), preferred_element_type=jnp.float32
        )
        dense_rows = jax.ops.segment_sum(partial_value, row_list, num_segments=count * front_width)
        dense_rows = dense_rows.reshape(count, front_width, rhs_count)
        return lax.psum_scatter(dense_rows, "front", scatter_dimension=1, tiled=True)

    leaf_solution = apply_inverse(inv_leaf[0], rhs_leaf[0])
    pending = spread(off_leaf[0], leaf_solution, idx_leaf[0], depth_count)
    solved = []
    for section_num in range(depth_count):
        pending = pending + partner(pending, "leaf", section_num)
        heap_node = jnp.right_shift(leaves + leaf_pos, section_num + 1)
        right_side = (
            lax.dynamic_index_in_dim(rhs_top, heap_node - 1, 0, keepdims=False) - pending[0]
        )
        inverse = lax.dynamic_index_in_dim(inv_top, heap_node - 1, 0, keepdims=False)
        solution = apply_inverse(inverse, right_side)
        solved.append(solution)
        if section_num + 1 < depth_count:
            off_block = lax.dynamic_index_in_dim(off_top, heap_node - 2, 0, keepdims=False)
            row_list = lax.dynamic_index_in_dim(idx_top, heap_node - 2, 0, keepdims=False)
            pending = pending[1:] + spread(
                off_block, solution, row_list, depth_count - section_num - 1
            )
    return (leaf_solution[None], jnp.stack(solved)[None])


def solution(mesh):
    placed = (
        P("leaf", "front", None),
        P(None, "front", None),
        P("leaf", "front", None),
        P(None, "front", None),
        P("leaf", None, "front"),
        P(None, None, "front"),
        P("leaf", None),
        P(),
    )
    return jax.shard_map(
        local,
        mesh=mesh,
        in_specs=placed,
        out_specs=(P("leaf", "front", None), P("leaf", None, "front", None)),
        check_vma=False,
    )
```

profile of v0, /device:TPU:32, one launch (start us, length us, event | category | flops | bytes accessed | tf_op | source)
XLA Modules:
  0.0 521.0 jit_solution(1386196292948095497)
XLA Ops:
  7.2 1.0 convert_element_type.42
  8.2 24.3 %all-gather = bf16[1,1024,256]{2,1,0:T(8,128)(2,1)S(1)} all-gather(bf16[1,64,256]{2,1,0:T(8,128)(2,1)S(1)} %convert_element_type.42), channel_id=2, replica_groups=mesh['leaf'=16,'front'=16] {'front'}, dimensions={1}, use_global_device_ids=true | all-gather | bytes 557056 | tf_op jit(solution)/shard_map/all_gather | solution.py:28
  32.5 1.1 fusion.13
  33.6 1.2 convolution_bitcast_fusion
  34.8 1.3 copy.10
  36.1 8.7 %scatter_custom_fusion = f32[4096,256]{1,0:T(8,128)} fusion(s32[1024]{0:T(1024)} %bitcast.71, f32[1024,256]{1,0:T(8,128)} %copy.10, f32[]{:T(128)} %constant.69.clone.1), kind=kCustom, calls=%fused_computation.4 | custom fusion | flops 262144 | bytes 4194816 | tf_op jit(solution)/shard_map/scatter-add | solution.py:36
  44.9 83.3 %reduce-scatter.5.cloned.1.call-done = f32[4,64,256]{2,1,0:T(8,128)} async-done(((f32[4,1024,256]{2,1,0:T(8,128)}), f32[4,64,256]{2,1,0:T(8,128)}) %reduce-scatter.5.cloned.1.call-update) | async-done | bytes 262160 | tf_op jit(solution)/shard_map/reduce_scatter | solution.py:38
  128.2 0.9 constant_dynamic-slice_fusion.2
  129.1 0.9 collective-permute-done
  129.9 1.0 add.98
  130.9 0.9 fusion.38
  131.8 23.3 %all-gather.1 = bf16[1,1024,256]{2,1,0:T(8,128)(2,1)S(1)} all-gather(bf16[1,64,256]{2,1,0:T(8,128)(2,1)S(1)} %fusion.38), channel_id=3, replica_groups=mesh['leaf'=16,'front'=16] {'front'}, dimensions={1}, use_global_device_ids=true | all-gather | bytes 557056 | tf_op jit(solution)/shard_map/all_gather | solution.py:28
  155.2 1.2 fusion.23
  156.5 7.9 %scatter_custom_fusion.1 = f32[3072,256]{1,0:T(8,128)} fusion(s32[1024]{0:T(1024)S(1)} %bitcast.70, f32[1024,256]{1,0:T(8,128)S(1)} %fusion.23, f32[]{:T(128)} %constant.69.clone.1), kind=kCustom, calls=%fused_computation.6 | custom fusion | flops 262144 | bytes 3145732 | tf_op jit(solution)/shard_map/scatter-add | solution.py:36
  164.4 79.7 %reduce-scatter.7.cloned.1.call-done = f32[3,64,256]{2,1,0:T(8,128)} async-done(((f32[3,1024,256]{2,1,0:T(8,128)}), f32[3,64,256]{2,1,0:T(8,128)}) %reduce-scatter.7.cloned.1.call-update) | async-done | bytes 196624 | tf_op jit(solution)/shard_map/reduce_scatter | solution.py:38
  244.1 0.9 slice_add_fusion
  245.6 5.2 collective-permute-done.1
  251.7 23.5 %all-gather.2 = bf16[1,1024,256]{2,1,0:T(8,128)(2,1)S(1)} all-gather(bf16[1,64,256]{2,1,0:T(8,128)(2,1)S(1)} %fusion.37), channel_id=4, replica_groups=mesh['leaf'=16,'front'=16] {'front'}, dimensions={1}, use_global_device_ids=true | all-gather | bytes 557056 | tf_op jit(solution)/shard_map/all_gather | solution.py:28
  275.4 1.2 fusion.20
  276.7 7.5 %scatter_custom_fusion.2 = f32[2048,256]{1,0:T(8,128)} fusion(s32[1024]{0:T(1024)S(1)} %bitcast.69, f32[1024,256]{1,0:T(8,128)S(1)} %fusion.20, f32[]{:T(128)} %constant.69.clone.1), kind=kCustom, calls=%fused_computation.10 | custom fusion | flops 262144 | bytes 2097156 | tf_op jit(solution)/shard_map/scatter-add | solution.py:36
  284.2 78.2 %reduce-scatter.9.cloned.1.call-done = f32[2,64,256]{2,1,0:T(8,128)} async-done(((f32[2,1024,256]{2,1,0:T(8,128)}), f32[2,64,256]{2,1,0:T(8,128)}) %reduce-scatter.9.cloned.1.call-update) | async-done | bytes 131088 | tf_op jit(solution)/shard_map/reduce_scatter | solution.py:38
  362.4 0.9 slice_add_fusion.1
  363.3 2.6 collective-permute-start.2
  365.9 3.8 collective-permute-done.2
  369.8 0.9 fusion.36
  370.6 23.2 %all-gather.3 = bf16[1,1024,256]{2,1,0:T(8,128)(2,1)S(1)} all-gather(bf16[1,64,256]{2,1,0:T(8,128)(2,1)S(1)} %fusion.36), channel_id=5, replica_groups=mesh['leaf'=16,'front'=16] {'front'}, dimensions={1}, use_global_device_ids=true | all-gather | bytes 557056 | tf_op jit(solution)/shard_map/all_gather | solution.py:28
  394.1 1.2 fusion.17
  395.3 7.1 %scatter_custom_fusion.3 = f32[1024,256]{1,0:T(8,128)} fusion(s32[1024]{0:T(1024)S(1)} %bitcast.68, f32[1024,256]{1,0:T(8,128)S(1)} %fusion.17, f32[]{:T(128)} %constant.69.clone.1), kind=kCustom, calls=%fused_computation.21 | custom fusion | flops 262144 | bytes 1048580 | tf_op jit(solution)/shard_map/scatter-add | solution.py:36
  402.4 77.7 %reduce-scatter.11.cloned.1.call-done = f32[1,64,256]{2,1,0:T(8,128)} async-done(((f32[1,1024,256]{2,1,0:T(8,128)}), f32[1,64,256]{2,1,0:T(8,128)}) %reduce-scatter.11.cloned.1.call-update) | async-done | bytes 65552 | tf_op jit(solution)/shard_map/reduce_scatter | solution.py:38
  480.9 5.0 collective-permute-start.3
  485.9 3.4 collective-permute-done.3
  490.2 23.3 %all-gather.4 = bf16[1,1024,256]{2,1,0:T(8,128)(2,1)S(1)} all-gather(bf16[1,64,256]{2,1,0:T(8,128)(2,1)S(1)} %subtract_convert_fusion), channel_id=6, replica_groups=mesh['leaf'=16,'front'=16] {'front'}, dimensions={1}, use_global_device_ids=true | all-gather | bytes 557056 | tf_op jit(solution)/shard_map/all_gather | solution.py:28
  (24 shorter events, 5.0 us)
Async XLA Ops:
  7.2 147.9 %copy-start = (bf16[15,64,1024]{2,1,0:T(8,128)(2,1)S(1)}, bf16[15,64,1024]{2,1,0:T(8,128)(2,1)}, u32[]{:S(2)}) copy-start(bf16[15,64,1024]{2,1,0:T(8,128)(2,1)} %param.11) | copy-start | bytes 5898244
  7.2 121.0 %reduce-scatter.5.cloned.1.call-start = ((), (), s32[]{:S(2)}) async-start(), calls=%async_computation.4 | async-start | bytes 4456448 | tf_op jit(solution)/shard_map/reduce_scatter | solution.py:38
  33.6 11.2 %copy-start.1 = (f32[64,256]{1,0:T(8,128)}, f32[64,256]{1,0:T(8,128)S(1)}, u32[]{:S(2)}) copy-start(f32[64,256]{1,0:T(8,128)S(1)} %fusion.13) | copy-start | bytes 196612
  44.8 199.3 %reduce-scatter.7.cloned.1.call-start = ((), (), s32[]{:S(2)}) async-start(), calls=%async_computation.5 | async-start | bytes 3342336 | tf_op jit(solution)/shard_map/reduce_scatter | solution.py:38
  128.2 1.7 collective-permute-start
  164.4 198.0 %reduce-scatter.9.cloned.1.call-start = ((), (), s32[]{:S(2)}) async-start(), calls=%async_computation.6 | async-start | bytes 2228224 | tf_op jit(solution)/shard_map/reduce_scatter | solution.py:38
  245.1 5.8 %collective-permute-start.1 = (f32[3,64,256]{2,1,0:T(8,128)S(1)}, f32[3,64,256]{2,1,0:T(8,128)S(1)}, u32[]{:S(2)}, u32[]{:S(2)}) collective-permute-start(f32[3,64,256]{2,1,0:T(8,128)S(1)} %slice_add_fusion), channel_id=1, source_target_pairs={{0,32},{32,0},{16,48},{48,16},{64,96},{96,64},{80,112},{112,80},{1... | collective-permute-start | bytes 589832 | tf_op jit(solution)/shard_map/ppermute | solution.py:14
  284.2 195.9 %reduce-scatter.11.cloned.1.call-start = ((), (), s32[]{:S(2)}) async-start(), calls=%async_computation.7 | async-start | bytes 1114112 | tf_op jit(solution)/shard_map/reduce_scatter | solution.py:38
  363.3 6.5 %collective-permute-start.2 = (f32[2,64,256]{2,1,0:T(8,128)S(1)}, f32[2,64,256]{2,1,0:T(8,128)S(1)}, u32[]{:S(2)}, u32[]{:S(2)}) collective-permute-start(f32[2,64,256]{2,1,0:T(8,128)S(1)} %slice_add_fusion.1), channel_id=1, source_target_pairs={{0,64},{64,0},{16,80},{80,16},{32,96},{96,32},{48,112},{112,48},{1... | collective-permute-start | bytes 393224 | tf_op jit(solution)/shard_map/ppermute | solution.py:14
  480.9 8.4 %collective-permute-start.3 = (f32[1,64,256]{2,1,0:T(8,128)S(1)}, f32[1,64,256]{2,1,0:T(8,128)S(1)}, u32[]{:S(2)}, u32[]{:S(2)}) collective-permute-start(f32[1,64,256]{2,1,0:T(8,128)S(1)} %slice_add_fusion.2), channel_id=1, source_target_pairs={{0,128},{128,0},{16,144},{144,16},{32,160},{160,32},{48,176},{176,... | collective-permute-start | bytes 196616 | tf_op jit(solution)/shard_map/ppermute | solution.py:14
Sparse Core Ops, SparseCore 0:
  45.0 83.1 reduce-scatter.4
  164.5 79.5 reduce-scatter.6
  284.3 78.0 reduce-scatter.8
  402.5 77.5 reduce-scatter.10
where the time goes:
time: 522 us; the launch traced here: 521 us
  waiting for transfers between devices  332 us (64%)
  blocking collectives  118 us (23%)
  other arithmetic  39.9 us (8%)
  between operations  13.9 us (3%)
  starting transfers between devices  8.32 us (2%)
  matrix products  6.91 us (1%)
    reduce_scatter x4, waiting for transfers between devices, spread(): lax.psum_scatter(dense_rows, 'front', scatter_dimension=1, tiled=True)  319 us
    all_gather x5, blocking collectives, apply_inverse(): lax.all_gather(rounded, 'front', axis=0, tiled=True)  118 us
    scatter-add x4, other arithmetic, spread(): jax.ops.segment_sum(partial_value, row_list, num_segments=count * front_w...  31.1 us
    ppermute x4, waiting for transfers between devices, partner(): return lax.ppermute(block, axis, route)  13.3 us
  transfers between devices with their start and end apart: 8, of which 8 were waited for; matrix products, arithmetic and copies ran while one was open for 0% of the time, Pallas kernels for 0%

commit v1 on v0

v1 whole, which is shorter than its diff:
```python
import functools

import jax
import jax.numpy as jnp
from jax import lax
from jax.experimental import pallas as pl
from jax.experimental.pallas import tpu as pltpu
from jax.sharding import PartitionSpec as P

BF = jnp.bfloat16
F32 = jnp.float32
FRONTS = 16
COLS = 16
WIDTHS = (8, 4, 2, 1)
STARTS = (0, 8, 12, 14)

VMEM = pl.BlockSpec(memory_space=pltpu.VMEM)
SMEM = pl.BlockSpec(memory_space=pltpu.SMEM)


def nt(a, b):
    return lax.dot_general(a, b, (((1,), (1,)), ((), ())), preferred_element_type=F32)


def nn(a, b):
    return jnp.dot(a, b, preferred_element_type=F32)


def halves(value):
    high = value.astype(BF)
    low = (value - high.astype(F32)).astype(BF)
    return high, low


def iota(shape, dim):
    return lax.broadcasted_iota(jnp.int32, shape, dim)


def params():
    return pltpu.CompilerParams(vmem_limit_bytes=40 * 2**20)


def call(kernel, outs, specs, args, flops=10**8, bytes_accessed=10**6):
    many = isinstance(outs, (tuple, list))
    return pl.pallas_call(
        kernel,
        out_shape=outs,
        in_specs=specs,
        out_specs=tuple(VMEM for _ in outs) if many else VMEM,
        compiler_params=params(),
        cost_estimate=pl.CostEstimate(
            flops=flops, bytes_accessed=bytes_accessed, transcendentals=0
        ),
    )(*args)


def weights_kernel(place, inv_ref, off_ref, out_ref):
    core = place[8]
    rows = inv_ref.shape[1]
    out_ref[:rows, :] = inv_ref[0]
    pick = (iota((rows, 2 * rows), 1) == iota((rows, 2 * rows), 0) + core * rows).astype(BF)
    out_ref[rows:, :] = nt(pick, off_ref[0]).astype(BF)


def path_weights(place, inv_top, off_top, levels):
    width = inv_top.shape[2]
    rows = inv_top.shape[1] // 2
    return pl.pallas_call(
        weights_kernel,
        grid_spec=pltpu.PrefetchScalarGridSpec(
            num_scalar_prefetch=1,
            grid=(levels,),
            in_specs=[
                pl.BlockSpec((1, rows, width), lambda a, s: (s[a] - 1, s[8], 0)),
                pl.BlockSpec((1, width, 2 * rows), lambda a, s: (s[a] - 2, 0, 0)),
            ],
            out_specs=pl.BlockSpec((2 * rows, width), lambda a, s: (a, 0)),
        ),
        out_shape=jax.ShapeDtypeStruct((levels * 2 * rows, width), BF),
        compiler_params=params(),
    )(place, inv_top, off_top)


def shares_kernel(place, *refs):
    rhs_refs, out_ref = refs[:4], refs[4]
    parity = place[9]
    total = jnp.zeros(out_ref.shape, F32)
    to = iota((256, 256), 0)
    come = iota((256, 256), 1)
    slot = to % 16
    for a in range(4):
        sub = place[4 + a]
        width, start = WIDTHS[a], STARTS[a]
        from_col = (to - slot) + sub * width + (slot - start)
        chosen = (slot >= start) & (slot < start + width) & (come == from_col)
        high, low = halves(rhs_refs[a][0])
        high = high.astype(F32)
        low = low.astype(F32)
        even = (parity == 0).astype(F32)
        odd = 1.0 - even
        stacked = jnp.concatenate([high * even, high * odd, low * even, low * odd], axis=0)
        total = total + nt(chosen.astype(BF), stacked.astype(BF))
    out_ref[...] = total.astype(BF)


def rhs_shares(place, rhs_top):
    rows, cols = rhs_top.shape[1:]
    return pl.pallas_call(
        shares_kernel,
        grid_spec=pltpu.PrefetchScalarGridSpec(
            num_scalar_prefetch=1,
            grid=(1,),
            in_specs=[
                pl.BlockSpec((1, rows, cols), lambda i, s, a=a: (s[a] - 1, 0, 0)) for a in range(4)
            ],
            out_specs=pl.BlockSpec((256, 256), lambda i, s: (0, 0)),
        ),
        out_shape=jax.ShapeDtypeStruct((256, 256), BF),
        compiler_params=params(),
    )(place, rhs_top, rhs_top, rhs_top, rhs_top)


def leaf_solve_kernel(inv_ref, rhs_ref, off_ref, shares_ref, x_ref, out_ref):
    right = rhs_ref[...].reshape(1024, 256)
    x = nn(inv_ref[0], right)
    x_ref[...] = x
    xt = x.T.astype(BF)
    update = nt(xt, off_ref[0])
    out_ref[:, :, :1024] = update.astype(BF).reshape(16, 16, 1024)
    out_ref[:, :, 1024:] = shares_ref[...].reshape(16, 16, 256)


def push(update, idx, count):
    high, low = halves(update)
    both = jnp.concatenate([high, low], axis=0)
    blocks = []
    step = 512
    for a in range(count):
        parts = []
        for t in range(1024 // step):
            hit = iota((step, 1024), 0) + (a * 1024 + t * step) == idx
            got = nt(both, jnp.where(hit, 1.0, 0.0).astype(BF))
            parts.append(got[:16] + got[16:])
        blocks.append(jnp.concatenate(parts, axis=1))
    return blocks


def leaf_update_kernel(place, got_ref, idx_ref, out_ref):
    update = jnp.zeros((16, 1024), F32)
    for s in range(FRONTS):
        update = update + got_ref[s, :, :1024].astype(F32)
    pending = push(update, idx_ref[...], 4)
    high, low = [], []
    for g in range(FRONTS // 2):
        pair = got_ref[2 * g, :, 1024:].astype(F32) + got_ref[2 * g + 1, :, 1024:].astype(F32)
        high.append(pair[:, :128])
        low.append(pair[:, 128:])
    high = jnp.concatenate(high, axis=1).astype(BF)
    low = jnp.concatenate(low, axis=1).astype(BF)
    row = iota((16, 16), 0)
    slot = iota((16, 16), 1)
    for a in range(4):
        width, start = WIDTHS[a], STARTS[a]
        put = (slot >= start) & (slot < start + width)
        put = put & (row == place[4 + a] * width + slot - start)
        put = jnp.where(put, 1.0, 0.0).astype(BF)
        out_ref[a * 16 : (a + 1) * 16, :] = nn(put, high) + nn(put, low) - pending[a]


def solve_kernel(left, own_ref, other_ref, weights_ref, ux_ref, *rest):
    total = own_ref[...] + other_ref[...]
    right = total[:16].astype(BF)
    inverse = weights_ref[:, :32, :].reshape(512, 1024)
    off = weights_ref[:, 32:, :].reshape(512, 1024)
    x = nt(right, inverse)
    ux_ref[:, :1024] = nn(x.astype(BF), off)
    ux_ref[:, 1024:] = x
    rest[0][...] = total[16:]


def top_solve(own, other, weights, level):
    left = own.shape[0] // 16 - 1
    return pl.pallas_call(
        functools.partial(solve_kernel, left),
        grid=(1,),
        in_specs=[
            pl.BlockSpec(own.shape, lambda i: (0, 0)),
            pl.BlockSpec(own.shape, lambda i: (0, 0)),
            pl.BlockSpec((16, 64, 1024), lambda i: (0, level, 0)),
        ],
        out_specs=(
            pl.BlockSpec((16, 1536), lambda i: (0, 0)),
            pl.BlockSpec((left * 16, 1024), lambda i: (0, 0)),
        ),
        out_shape=(
            jax.ShapeDtypeStruct((16, 1536), F32),
            jax.ShapeDtypeStruct((left * 16, 1024), F32),
        ),
        compiler_params=params(),
    )(own, other, weights)


def update_kernel(own_ref, other_ref, rest_ref, idx_ref, out_ref):
    update = own_ref[:, :1024] + other_ref[:, :1024]
    count = out_ref.shape[0] // 16
    for a, block in enumerate(push(update, idx_ref[...], count)):
        out_ref[a * 16 : (a + 1) * 16, :] = rest_ref[a * 16 : (a + 1) * 16, :] - block


def ship_kernel(place, own_ref, other_ref, out_ref):
    first = place[8] == 0
    own = own_ref[:, 1024:]
    other = other_ref[:, 1024:]
    low_core = jnp.where(first, own, other)
    high_core = jnp.where(first, other, own)
    for f in range(FRONTS):
        at = slice(f * 32, (f + 1) * 32)
        value = jnp.concatenate([low_core[:, at], high_core[:, at]], axis=1)
        high = value.astype(BF).astype(F32)
        low = value - high
        out_ref[f] = jnp.concatenate([high, low], axis=1).astype(BF)


def root_right_kernel(own_ref, other_ref, s3_ref, s2_ref, s1_ref, out_ref):
    right = (own_ref[...] + other_ref[...]).astype(BF)
    for f in range(FRONTS):
        out_ref[f, :, :1024] = right
    out_ref[:, :, 1024:1152] = s3_ref[...]
    out_ref[:, :, 1152:1280] = s2_ref[...]
    out_ref[:, :, 1280:] = s1_ref[...]


def root_kernel(got_ref, inv_ref, out_ref):
    right = got_ref[:, :, :1024].reshape(256, 1024)
    out_ref[3] = nt(inv_ref[0], right)
    for a in range(3):
        at = 1024 + a * 128
        both = got_ref[:, :, at : at + 128].reshape(256, 128).astype(F32).T
        out_ref[a] = both[:64] + both[64:]


def swap(block, pairs):
    return lax.ppermute(block, "leaf", pairs)


def core_pairs():
    return [(i, i ^ 1) for i in range(16)]


def chip_pairs(level):
    pairs = []
    for i in range(16):
        z, core = i // 2, i % 2
        if level == 0:
            to = z ^ 1
        elif level == 1:
            to = z ^ 2
        else:
            to = (6, 7, 4, 5, 2, 3, 0, 1)[z]
        pairs.append((i, 2 * to + core))
    return pairs


def local(rhs_leaf, rhs_top, inv_leaf, inv_top, off_leaf, off_top, idx_leaf, idx_top):
    leaf = lax.axis_index("leaf")
    front = lax.axis_index("front")
    nodes = [jnp.right_shift(16 + leaf, a + 1) for a in range(4)]
    subs = [leaf & (2 ** (a + 1) - 1) for a in range(4)]
    place = jnp.stack(nodes + subs + [leaf & 1, front & 1]).astype(jnp.int32)

    rounded = rhs_leaf[0].astype(BF)
    sent = jnp.broadcast_to(rounded[None], (FRONTS, *rounded.shape))
    right = lax.all_to_all(sent, "front", 0, 0)

    path = path_weights(place, inv_top, off_top, 3)
    weights = lax.all_gather(path, "front", axis=0, tiled=False)
    shares = rhs_shares(place, rhs_top)

    leaf_x, sent = call(
        leaf_solve_kernel,
        (jax.ShapeDtypeStruct((64, 256), F32), jax.ShapeDtypeStruct((16, 16, 1280), BF)),
        [VMEM] * 4,
        (inv_leaf, right, off_leaf, shares),
    )
    got = lax.all_to_all(sent, "front", 0, 0)
    state = call(
        leaf_update_kernel,
        jax.ShapeDtypeStruct((64, 1024), F32),
        [SMEM, VMEM, VMEM],
        (place, got, idx_leaf),
    )
    other = swap(state, core_pairs())
    ships = []
    for level in range(3):
        ux, rest = top_solve(state, other, weights, level)
        ux_other = swap(ux, core_pairs())
        rows = lax.dynamic_slice_in_dim(idx_top, nodes[level] - 2, 1, 0)
        state = call(
            update_kernel,
            jax.ShapeDtypeStruct(rest.shape, F32),
            [VMEM] * 4,
            (ux, ux_other, rest, rows),
        )
        other = swap(state, chip_pairs(level))
        ships.append(
            call(
                ship_kernel,
                jax.ShapeDtypeStruct((16, 16, 128), BF),
                [SMEM, VMEM, VMEM],
                (place, ux, ux_other),
            )
        )
    sent = call(
        root_right_kernel,
        jax.ShapeDtypeStruct((16, 16, 1408), BF),
        [VMEM] * 5,
        (state, other, *ships),
    )
    got = lax.all_to_all(sent, "front", 0, 0)
    ancestors = call(
        root_kernel,
        jax.ShapeDtypeStruct((4, 64, 256), F32),
        [VMEM] * 2,
        (got, inv_top[:1]),
    )
    return (leaf_x[None], ancestors[None])


def solution(mesh):
    placed = (
        P("leaf", "front", None),
        P(None, "front", None),
        P("leaf", "front", None),
        P(None, "front", None),
        P("leaf", None, "front"),
        P(None, None, "front"),
        P("leaf", None),
        P(),
    )
    return jax.shard_map(
        local,
        mesh=mesh,
        in_specs=placed,
        out_specs=(P("leaf", "front", None), P("leaf", None, "front", None)),
        check_vma=False,
    )
```

time: 522 us -> 150 us (0.29)
  waiting for transfers between devices: 332 us -> 66.3 us
  blocking collectives: 118 us -> 14.9 us
  other arithmetic: 39.9 us -> 0.01 us
  Pallas kernels: 0 us -> 17.3 us
  local copies, waits for them, and re-layouts: 2.21 us -> 16.7 us
  starting transfers between devices: 8.32 us -> 19.6 us
  matrix products: 6.91 us -> 0 us
    reduce_scatter x4 -> x0, waiting for transfers between devices: 319 us -> none  [spread(): lax.psum_scatter(dense_rows, 'front', scatter_dimension=1, tiled=True)]
    all_gather x5 -> x0, blocking collectives: 118 us -> none  [apply_inverse(): lax.all_gather(rounded, 'front', axis=0, tiled=True)]
    scatter-add x4 -> x0, other arithmetic: 31.1 us -> none  [spread(): jax.ops.segment_sum(partial_value, row_list, num_segments=count * front_w...]
    all_gather x0 -> x1, waiting for transfers between devices: none -> 26.1 us  [local(): weights = lax.all_gather(path, 'front', axis=0, tiled=False)]
    all_to_all x0 -> x2, waiting for transfers between devices: none -> 21.5 us  [the longest x1 13.4 us: local(): got = lax.all_to_all(sent, 'front', 0, 0)]
    pallas_call x0 -> x15, Pallas kernels: none -> 17.3 us  [the longest x10 12.3 us: call(): pl.pallas_call(kernel, out_shape=outs, in_specs=specs, out_specs=tuple((V...]
    all_to_all x0 -> x1, blocking collectives: none -> 14.9 us  [local(): got = lax.all_to_all(sent, 'front', 0, 0)]
    unnamed x4 -> x24, local copies, waits for them, and re-layouts: 0.02 us -> 14.7 us
  transfers between devices with their start and end apart: 8 -> 10, of which waited for: 8 -> 10; matrix products, arithmetic and copies ran while one was open for 0% -> 2% of each run, Pallas kernels for 0% -> 5%
where the time goes in v1:
time: 150 us; the launch traced here: 149 us
  waiting for transfers between devices  66.3 us (44%)
  starting transfers between devices  19.6 us (13%)
  Pallas kernels  17.3 us (12%)
  local copies, waits for them, and re-layouts  16.7 us (11%)
  blocking collectives  14.9 us (10%)
  between operations  14.2 us (9%)
    all_gather x1, waiting for transfers between devices, local(): weights = lax.all_gather(path, 'front', axis=0, tiled=False)  26.1 us
    ppermute x7, waiting for transfers between devices, swap(): return lax.ppermute(block, 'leaf', pairs)  18.6 us
    all_to_all x1, blocking collectives, local(): got = lax.all_to_all(sent, 'front', 0, 0)  14.9 us
    unnamed x24, local copies, waits for them, and re-layouts  14.7 us
    all_to_all x1, waiting for transfers between devices, local(): got = lax.all_to_all(sent, 'front', 0, 0)  13.4 us
    pallas_call x10, Pallas kernels, call(): pl.pallas_call(kernel, out_shape=outs, in_specs=specs, out_specs=tuple((V...  12.3 us
    all_to_all x1, waiting for transfers between devices, local(): right = lax.all_to_all(sent, 'front', 0, 0)  8.17 us
    ppermute x7, starting transfers between devices, swap(): return lax.ppermute(block, 'leaf', pairs)  7.33 us
  transfers between devices with their start and end apart: 10, of which 10 were waited for; matrix products, arithmetic and copies ran while one was open for 2% of the time, Pallas kernels for 5%

profile of v1, /device:TPU:32, one launch (start us, length us, event | category | flops | bytes accessed | tf_op | source)
XLA Modules:
  0.0 149.0 jit_solution(185165720163578860)
XLA Ops:
  7.2 4.7 %copy.11.off_ref = bf16[14,1024,64]{2,1,0:T(8,128)(2,1)} copy(bf16[14,1024,64]{1,2,0:T(8,128)(2,1)} %param.13) | data formatting | bytes 3670016 | tf_op args[5]
  12.0 2.0 %copy-done.3 = bf16[14,1024,64]{2,1,0:T(8,128)(2,1)S(1)} copy-done((bf16[14,1024,64]{2,1,0:T(8,128)(2,1)S(1)}, bf16[14,1024,64]{2,1,0:T(8,128)(2,1)}, u32[]{:S(2)}) %copy-start.3) | copy-done | bytes 1835032
  14.1 2.3 %shard_map.98 = bf16[192,1024]{1,0:T(8,128)(2,1)} custom-call(s32[10]{0:T(128)S(1)} %stack.40.place, bf16[15,64,1024]{2,1,0:T(8,128)(2,1)S(1)} %copy-done.4, bf16[14,1024,64]{2,1,0:T(8,128)(2,1)S(1)} %copy-done.3), custom_call_target="tpu_custom_call" | custom-call | tf_op jit(solution)/shard_map/pallas_call | solution.py:68
  16.4 0.9 broadcast_in_dim.15
  17.2 7.0 %all-to-all-start = ((bf16[16,64,256]{2,1,0:T(8,128)(2,1)}), bf16[16,64,256]{2,1,0:T(8,128)(2,1)S(1)}, u32[]{:S(2)}, u32[]{:S(2)}) async-start(bf16[16,64,256]{2,1,0:T(8,128)(2,1)} %broadcast_in_dim.15), calls=%async_computation | async-start | bytes 1048576 | tf_op jit(solution)/shard_map/all_to_all | solution.py:273
  24.3 1.8 %copy.10.off_ref = bf16[1,1024,64]{2,1,0:T(8,128)(2,1)} copy(bf16[1,1024,64]{1,2,0:T(8,128)(2,1)} %param.12) | data formatting | bytes 262144 | tf_op args[4]
  26.1 0.9 shard_map.95.shares_ref
  27.6 8.2 %all-to-all-done.rhs_ref = bf16[16,64,256]{2,1,0:T(8,128)(2,1)S(1)} async-done(((bf16[16,64,256]{2,1,0:T(8,128)(2,1)}), bf16[16,64,256]{2,1,0:T(8,128)(2,1)S(1)}, u32[]{:S(2)}, u32[]{:S(2)}) %all-to-all-start) | async-done | bytes 524320 | tf_op jit(solution)/shard_map/all_to_all | solution.py:273
  35.8 0.9 copy-done.5
  36.7 0.9 copy-done.7
  37.6 0.9 copy-done.8
  38.5 1.2 shard_map.96
  39.8 14.9 %all_to_all.15.got_ref = bf16[16,16,1280]{2,1,0:T(8,128)(2,1)S(1)} all-to-all(bf16[16,16,1280]{2,1,0:T(8,128)(2,1)S(1)} %get-tuple-element.11), channel_id=1, replica_groups=mesh['leaf'=16,'front'=16] {'front'}, dimensions={0} | all-to-all | bytes 1310720 | tf_op jit(solution)/shard_map/all_to_all | solution.py:285
  54.6 3.1 %shard_map.97.own_ref = f32[64,1024]{1,0:T(8,128)S(1)} custom-call(s32[10]{0:T(128)S(1)} %stack.40.place, bf16[16,16,1280]{2,1,0:T(8,128)(2,1)S(1)} %all_to_all.15.got_ref, s32[1,1024]{1,0:T(1,128)S(1)} %copy-done.9), custom_call_target="tpu_custom_call" | custom-call | flops 100000000 | bytes 1000000 | tf_op jit(solution)/shard_map/pallas_call | solution.py:45
  57.8 1.5 %collective-permute-done.other_ref = f32[64,1024]{1,0:T(8,128)S(1)} collective-permute-done((f32[64,1024]{1,0:T(8,128)S(1)}, f32[64,1024]{1,0:T(8,128)S(1)}, u32[]{:S(2)}, u32[]{:S(2)}) %collective-permute-start) | collective-permute-done | bytes 262176 | tf_op jit(solution)/shard_map/ppermute | solution.py:243
  59.4 26.1 %all-gather.3.cloned.1.call-done = bf16[3072,1024]{1,0:T(8,128)(2,1)} async-done(((bf16[192,1024]{1,0:T(8,128)(2,1)}), bf16[3072,1024]{1,0:T(8,128)(2,1)}) %all-gather.3.cloned.1.call-update) | async-done | bytes 6291472 | tf_op jit(solution)/shard_map/all_gather | solution.py:276
  85.5 2.8 %copy-done = bf16[3072,1024]{1,0:T(8,128)(2,1)S(1)} copy-done((bf16[3072,1024]{1,0:T(8,128)(2,1)S(1)}, bf16[3072,1024]{1,0:T(8,128)(2,1)}, u32[]{:S(2)}) %copy-start) | copy-done | bytes 6291480
  88.9 1.1 constant_dynamic-slice_fusion
  90.2 1.9 %shard_map.100.own_ref = f32[48,1024]{1,0:T(8,128)S(1)} custom-call(f32[16,1536]{1,0:T(8,128)S(1)} %get-tuple-element.12.own_ref, f32[16,1536]{1,0:T(8,128)S(1)} %collective-permute-done.1.other_ref, f32[48,1024]{1,0:T(8,128)S(1)} %get-tuple-element.13.rest_ref, s32[1,1024]{1,0:T(1,128)S(1)} %get-tuple-element.19.idx_ref), custom_call_target="tpu_custom_call" | custom-call | flops 100000000 | bytes 1000000 | tf_op jit(solution)/shard_map/pallas_call | solution.py:45
  92.6 6.9 %collective-permute-done.2.other_ref = f32[48,1024]{1,0:T(8,128)S(1)} collective-permute-done((f32[48,1024]{1,0:T(8,128)S(1)}, f32[48,1024]{1,0:T(8,128)S(1)}, u32[]{:S(2)}, u32[]{:S(2)}) %collective-permute-start.2) | collective-permute-done | bytes 196640 | tf_op jit(solution)/shard_map/ppermute | solution.py:243
  100.0 1.3 collective-permute-done.3.other_ref
  101.4 1.3 shard_map.102.own_ref
  102.6 2.5 %collective-permute-start.4 = (f32[32,1024]{1,0:T(8,128)S(1)}, f32[32,1024]{1,0:T(8,128)S(1)}, u32[]{:S(2)}, u32[]{:S(2)}) collective-permute-start(f32[32,1024]{1,0:T(8,128)S(1)} %shard_map.102.own_ref), channel_id=1, source_target_pairs={{0,64},{16,80},{32,96},{48,112},{64,0},{80,16},{96,32},{112,48},{1... | collective-permute-start | bytes 393224 | tf_op jit(solution)/shard_map/ppermute | solution.py:243
  105.2 5.8 %collective-permute-done.4.other_ref = f32[32,1024]{1,0:T(8,128)S(1)} collective-permute-done((f32[32,1024]{1,0:T(8,128)S(1)}, f32[32,1024]{1,0:T(8,128)S(1)}, u32[]{:S(2)}, u32[]{:S(2)}) %collective-permute-start.4) | collective-permute-done | bytes 131104 | tf_op jit(solution)/shard_map/ppermute | solution.py:243
  111.6 1.3 collective-permute-done.5.other_ref
  113.6 4.2 %collective-permute-start.6 = (f32[16,1024]{1,0:T(8,128)S(1)}, f32[16,1024]{1,0:T(8,128)S(1)}, u32[]{:S(2)}, u32[]{:S(2)}) collective-permute-start(f32[16,1024]{1,0:T(8,128)S(1)} %shard_map.104.own_ref), channel_id=1, source_target_pairs={{0,192},{16,208},{32,224},{48,240},{64,128},{80,144},{96,160},{112... | collective-permute-start | bytes 196616 | tf_op jit(solution)/shard_map/ppermute | solution.py:243
  118.5 0.7 shard_map.106.s2_ref
  120.0 1.6 %collective-permute-done.6.other_ref = f32[16,1024]{1,0:T(8,128)S(1)} collective-permute-done((f32[16,1024]{1,0:T(8,128)S(1)}, f32[16,1024]{1,0:T(8,128)S(1)}, u32[]{:S(2)}, u32[]{:S(2)}) %collective-permute-start.6) | collective-permute-done | bytes 65568 | tf_op jit(solution)/shard_map/ppermute | solution.py:243
  121.6 0.9 shard_map.108
  122.5 5.2 %all-to-all-start.2 = ((bf16[16,16,1408]{2,1,0:T(8,128)(2,1)}), bf16[16,16,1408]{2,1,0:T(8,128)(2,1)S(1)}, u32[]{:S(2)}, u32[]{:S(2)}) async-start(bf16[16,16,1408]{2,1,0:T(8,128)(2,1)} %shard_map.108), calls=%async_computation.2 | async-start | bytes 1441792 | tf_op jit(solution)/shard_map/all_to_all | solution.py:319
  127.8 13.4 %all-to-all-done.2.got_ref = bf16[16,16,1408]{2,1,0:T(8,128)(2,1)S(1)} async-done(((bf16[16,16,1408]{2,1,0:T(8,128)(2,1)}), bf16[16,16,1408]{2,1,0:T(8,128)(2,1)S(1)}, u32[]{:S(2)}, u32[]{:S(2)}) %all-to-all-start.2) | async-done | bytes 720928 | tf_op jit(solution)/shard_map/all_to_all | solution.py:319
  141.1 1.0 shard_map.109
  (34 shorter events, 5.7 us)
Async XLA Ops:
  7.2 4.9 %copy-start.4 = (bf16[15,64,1024]{2,1,0:T(8,128)(2,1)S(1)}, bf16[15,64,1024]{2,1,0:T(8,128)(2,1)}, u32[]{:S(2)}) copy-start(bf16[15,64,1024]{2,1,0:T(8,128)(2,1)} %inv_ref.3) | copy-start | bytes 5898244
  7.2 78.3 %all-gather.3.cloned.1.call-start = ((), (), s32[]{:S(2)}) async-start(), calls=%async_computation.3 | async-start | bytes 6684672 | tf_op jit(solution)/shard_map/all_gather | solution.py:276
  7.2 9.1 %copy-start.10 = (f32[1,64,256]{2,1,0:T(8,128)S(1)}, f32[1,64,256]{2,1,0:T(8,128)}, u32[]{:S(2)}) copy-start(f32[1,64,256]{2,1,0:T(8,128)} %param.8) | copy-start | bytes 196612
  12.0 2.0 %copy-start.3 = (bf16[14,1024,64]{2,1,0:T(8,128)(2,1)S(1)}, bf16[14,1024,64]{2,1,0:T(8,128)(2,1)}, u32[]{:S(2)}) copy-start(bf16[14,1024,64]{2,1,0:T(8,128)(2,1)} %copy.11.off_ref) | copy-start | bytes 5505028
  14.1 12.0 %copy-start.2 = (f32[15,64,256]{2,1,0:T(8,128)S(1)}, f32[15,64,256]{2,1,0:T(8,128)}, u32[]{:S(2)}) copy-start(f32[15,64,256]{2,1,0:T(8,128)} %refs_3_.1) | copy-start | bytes 2949124
  17.2 18.5 %all-to-all-start = ((bf16[16,64,256]{2,1,0:T(8,128)(2,1)}), bf16[16,64,256]{2,1,0:T(8,128)(2,1)S(1)}, u32[]{:S(2)}, u32[]{:S(2)}) async-start(bf16[16,64,256]{2,1,0:T(8,128)(2,1)} %broadcast_in_dim.15), calls=%async_computation | async-start | bytes 1048576 | tf_op jit(solution)/shard_map/all_to_all | solution.py:273
  24.3 30.3 %copy-start.9 = (s32[1,1024]{1,0:T(1,128)S(1)}, s32[1,1024]{1,0:T(1,128)}, u32[]{:S(2)}) copy-start(s32[1,1024]{1,0:T(1,128)} %idx_ref.1) | copy-start | bytes 12292
  27.0 0.6 copy-start.6
  35.8 1.0 copy-start.5
  36.7 0.9 copy-start.7
  37.6 0.9 copy-start.8
  57.7 1.6 %collective-permute-start = (f32[64,1024]{1,0:T(8,128)S(1)}, f32[64,1024]{1,0:T(8,128)S(1)}, u32[]{:S(2)}, u32[]{:S(2)}) collective-permute-start(f32[64,1024]{1,0:T(8,128)S(1)} %shard_map.97.own_ref), channel_id=1, source_target_pairs={{0,16},{16,0},{32,48},{48,32},{64,80},{80,64},{96,112},{112,96},{1... | collective-permute-start | bytes 786440 | tf_op jit(solution)/shard_map/ppermute | solution.py:243
  85.5 2.8 %copy-start = (bf16[3072,1024]{1,0:T(8,128)(2,1)S(1)}, bf16[3072,1024]{1,0:T(8,128)(2,1)}, u32[]{:S(2)}) copy-start(bf16[3072,1024]{1,0:T(8,128)(2,1)} %all-gather.3.cloned.1.call-done) | copy-start | bytes 18874372
  88.3 11.2 %copy-start.1 = (bf16[3072,1024]{1,0:T(8,128)(2,1)S(1)}, bf16[3072,1024]{1,0:T(8,128)(2,1)}, u32[]{:S(2)}) copy-start(bf16[3072,1024]{1,0:T(8,128)(2,1)} %all-gather.3.cloned.1.call-done) | copy-start | bytes 18874372
  88.9 1.3 collective-permute-start.1
  92.1 7.4 %collective-permute-start.2 = (f32[48,1024]{1,0:T(8,128)S(1)}, f32[48,1024]{1,0:T(8,128)S(1)}, u32[]{:S(2)}, u32[]{:S(2)}) collective-permute-start(f32[48,1024]{1,0:T(8,128)S(1)} %shard_map.100.own_ref), channel_id=1, source_target_pairs={{0,32},{16,48},{32,0},{48,16},{64,96},{80,112},{96,64},{112,80},{1... | collective-permute-start | bytes 589832 | tf_op jit(solution)/shard_map/ppermute | solution.py:243
  100.0 1.3 collective-permute-start.3
  102.6 8.4 %collective-permute-start.4 = (f32[32,1024]{1,0:T(8,128)S(1)}, f32[32,1024]{1,0:T(8,128)S(1)}, u32[]{:S(2)}, u32[]{:S(2)}) collective-permute-start(f32[32,1024]{1,0:T(8,128)S(1)} %shard_map.102.own_ref), channel_id=1, source_target_pairs={{0,64},{16,80},{32,96},{48,112},{64,0},{80,16},{96,32},{112,48},{1... | collective-permute-start | bytes 393224 | tf_op jit(solution)/shard_map/ppermute | solution.py:243
  111.6 1.3 collective-permute-start.5
  113.6 8.0 %collective-permute-start.6 = (f32[16,1024]{1,0:T(8,128)S(1)}, f32[16,1024]{1,0:T(8,128)S(1)}, u32[]{:S(2)}, u32[]{:S(2)}) collective-permute-start(f32[16,1024]{1,0:T(8,128)S(1)} %shard_map.104.own_ref), channel_id=1, source_target_pairs={{0,192},{16,208},{32,224},{48,240},{64,128},{80,144},{96,160},{112... | collective-permute-start | bytes 196616 | tf_op jit(solution)/shard_map/ppermute | solution.py:243
  122.5 18.6 %all-to-all-start.2 = ((bf16[16,16,1408]{2,1,0:T(8,128)(2,1)}), bf16[16,16,1408]{2,1,0:T(8,128)(2,1)S(1)}, u32[]{:S(2)}, u32[]{:S(2)}) async-start(bf16[16,16,1408]{2,1,0:T(8,128)(2,1)} %shard_map.108), calls=%async_computation.2 | async-start | bytes 1441792 | tf_op jit(solution)/shard_map/all_to_all | solution.py:319
Sparse Core Ops, SparseCore 0:
  16.5 68.9 all-gather.2

commit v2 on v1

v2 whole, which is shorter than its diff:
```python
import functools

import jax
import jax.numpy as jnp
from jax import lax
from jax.experimental import pallas as pl
from jax.experimental.pallas import tpu as pltpu
from jax.sharding import PartitionSpec as P

BF = jnp.bfloat16
F32 = jnp.float32
FRONTS = 16
COLS = 16
WIDTHS = (8, 4, 2, 1)
STARTS = (0, 8, 12, 14)

VMEM = pl.BlockSpec(memory_space=pltpu.VMEM)
SMEM = pl.BlockSpec(memory_space=pltpu.SMEM)
HBM = pl.BlockSpec(memory_space=pltpu.HBM)


def nt(a, b):
    return lax.dot_general(a, b, (((1,), (1,)), ((), ())), preferred_element_type=F32)


def nn(a, b):
    return jnp.dot(a, b, preferred_element_type=F32)


def halves(value):
    high = value.astype(BF)
    low = (value - high.astype(F32)).astype(BF)
    return high, low


def iota(shape, dim):
    return lax.broadcasted_iota(jnp.int32, shape, dim)


def params(mib=16):
    return pltpu.CompilerParams(vmem_limit_bytes=mib * 2**20)


def call(kernel, outs, specs, args, flops=10**8, bytes_accessed=10**6):
    many = isinstance(outs, (tuple, list))
    return pl.pallas_call(
        kernel,
        out_shape=outs,
        in_specs=specs,
        out_specs=tuple(VMEM for _ in outs) if many else VMEM,
        compiler_params=params(),
        cost_estimate=pl.CostEstimate(
            flops=flops, bytes_accessed=bytes_accessed, transcendentals=0
        ),
    )(*args)


def weights_kernel(place, inv_ref, off_ref, out_ref, held, sems):
    level = pl.program_id(0)
    node = place[level]
    at = pl.ds(pl.multiple_of(place[8] * 32, 32), 32)
    copies = [
        pltpu.make_async_copy(inv_ref.at[node - 1, at, :], held.at[0], sems.at[0]),
        pltpu.make_async_copy(off_ref.at[node - 2, at, :], held.at[1], sems.at[1]),
    ]
    for copy in copies:
        copy.start()
    for copy in copies:
        copy.wait()
    for f in range(FRONTS):
        out_ref[f, :32, :] = held[0]
        out_ref[f, 32:, :] = held[1]


def path_weights(place, inv_top, off_top, levels):
    return pl.pallas_call(
        weights_kernel,
        grid=(levels,),
        out_shape=jax.ShapeDtypeStruct((FRONTS, levels * 64, 1024), BF),
        in_specs=[SMEM, HBM, HBM],
        out_specs=pl.BlockSpec((FRONTS, 64, 1024), lambda i: (0, i, 0)),
        scratch_shapes=[pltpu.VMEM((2, 32, 1024), BF), pltpu.SemaphoreType.DMA((2,))],
        compiler_params=params(60),
    )(place, inv_top, off_top)


def shares_kernel(place, rhs_ref, out_ref, held, sems):
    copies = [
        pltpu.make_async_copy(rhs_ref.at[place[a] - 1], held.at[a], sems.at[a]) for a in range(4)
    ]
    for copy in copies:
        copy.start()
    for copy in copies:
        copy.wait()
    total = jnp.zeros((256, 128), F32)
    to = iota((256, 256), 0)
    come = iota((256, 256), 1)
    slot = to % 16
    for a in range(4):
        sub = place[4 + a]
        width, start = WIDTHS[a], STARTS[a]
        from_col = (to - slot) + sub * width + (slot - start)
        chosen = (slot >= start) & (slot < start + width) & (come == from_col)
        stacked = jnp.concatenate(halves(held[a]), axis=0)
        total = total + nt(jnp.where(chosen, 1.0, 0.0).astype(BF), stacked)
    out_ref[...] = total.astype(BF).reshape(4, 64, 128)


def rhs_shares(place, rhs_top):
    return pl.pallas_call(
        shares_kernel,
        out_shape=jax.ShapeDtypeStruct((4, 64, 128), BF),
        in_specs=[SMEM, HBM],
        out_specs=VMEM,
        scratch_shapes=[pltpu.VMEM((4, 64, 256), F32), pltpu.SemaphoreType.DMA((4,))],
        compiler_params=params(60),
    )(place, rhs_top)


def leaf_solve_kernel(place, inv_ref, r0, r1, r2, r3, off_ref, shares_ref, *refs):
    x_ref, outs, right_ref, update_ref = refs[0], refs[1:5], refs[5], refs[6]
    front_x, front_y = place[9], place[10]
    for t, r in enumerate((r0, r1, r2, r3)):
        for s in range(4):
            right_ref[(front_x ^ t) * 4 + (front_y ^ s)] = r[s]
    right = right_ref[...].reshape(1024, 256)
    x = nn(inv_ref[0], right)
    x_ref[...] = x
    xt = x.T.astype(BF)
    update_ref[...] = nn(xt, off_ref[0]).astype(BF).reshape(4, 64, 1024)
    for t, out_ref in enumerate(outs):
        to = front_x ^ t
        out_ref[:, :1024] = update_ref[to]
        out_ref[:, 1024:] = shares_ref[to]


def fold_kernel(place, r0, r1, r2, r3, *outs):
    front_x, front_y = place[9], place[10]
    refs = (r0, r1, r2, r3)
    for s, out_ref in enumerate(outs):
        at = pl.ds(pl.multiple_of((front_y ^ s) * 16, 16), 16)
        total = refs[0][at, :1024].astype(F32)
        for r in refs[1:]:
            total = total + r[at, :1024].astype(F32)
        out_ref[:, :1024] = total
        for t, r in enumerate(refs):
            both = r[at, 1024:].astype(F32)
            share = both + pltpu.roll(both, 64, 1)
            lanes = pl.ds(pl.multiple_of((1024 + (front_x ^ t) * 128), 128), 128)
            out_ref[:, lanes] = share


def push(update, idx, count):
    high, low = halves(update)
    both = jnp.concatenate([high, low], axis=0)
    blocks = []
    step = 512
    for a in range(count):
        parts = []
        for t in range(1024 // step):
            hit = iota((step, 1024), 0) + (a * 1024 + t * step) == idx
            got = nt(both, jnp.where(hit, 1.0, 0.0).astype(BF))
            parts.append(got[:16] + got[16:])
        blocks.append(jnp.concatenate(parts, axis=1))
    return blocks


def leaf_update_kernel(place, r0, r1, r2, r3, idx_ref, out_ref, held):
    front_y = place[10]
    refs = (r0, r1, r2, r3)
    update = refs[0][:, :1024]
    for r in refs[1:]:
        update = update + r[:, :1024]
    pending = push(update, idx_ref[...], 4)
    for s, r in enumerate(refs):
        held[front_y ^ s] = r[:, 1024:]
    pieces = []
    left_half = iota((16, 128), 1) < 64
    for x in range(4):
        at = slice(x * 128, (x + 1) * 128)
        for y in (0, 2):
            pieces.append(jnp.where(left_half, held[y][:, at], held[y + 1][:, at]))
    shares = jnp.concatenate(pieces, axis=1)
    high, low = halves(shares)
    row = iota((16, 16), 0)
    slot = iota((16, 16), 1)
    for a in range(4):
        width, start = WIDTHS[a], STARTS[a]
        put = (slot >= start) & (slot < start + width)
        put = put & (row == place[4 + a] * width + slot - start)
        put = jnp.where(put, 1.0, 0.0).astype(BF)
        out_ref[a * 16 : (a + 1) * 16, :] = nn(put, high) + nn(put, low) - pending[a]


def solve_kernel(own_ref, other_ref, weights_ref, ux_ref, rest_ref):
    total = own_ref[...] + other_ref[...]
    right = total[:16].astype(BF)
    inverse = weights_ref[:, :32, :].reshape(512, 1024)
    off = weights_ref[:, 32:, :].reshape(512, 1024)
    x = nt(right, inverse)
    ux_ref[:, :1024] = nn(x.astype(BF), off)
    ux_ref[:, 1024:] = x
    rest_ref[...] = total[16:]


def top_solve(own, other, weights, level):
    left = own.shape[0] - 16
    whole = pl.BlockSpec(own.shape, lambda i: (0, 0))
    return pl.pallas_call(
        solve_kernel,
        grid=(1,),
        in_specs=[whole, whole, pl.BlockSpec((FRONTS, 64, 1024), lambda i: (0, level, 0))],
        out_specs=(
            pl.BlockSpec((16, 1536), lambda i: (0, 0)),
            pl.BlockSpec((left, 1024), lambda i: (0, 0)),
        ),
        out_shape=(jax.ShapeDtypeStruct((16, 1536), F32), jax.ShapeDtypeStruct((left, 1024), F32)),
        compiler_params=params(),
    )(own, other, weights)


def update_kernel(level, place, own_ref, other_ref, rest_ref, idx_ref, out_ref):
    update = own_ref[:, :1024] + other_ref[:, :1024]
    count = out_ref.shape[0] // 16
    idx = idx_ref[pl.ds(place[level] - 2, 1), :]
    for a, block in enumerate(push(update, idx, count)):
        out_ref[a * 16 : (a + 1) * 16, :] = rest_ref[a * 16 : (a + 1) * 16, :] - block


def ship_kernel(place, own_ref, other_ref, out_ref):
    first = place[8] == 0
    own = own_ref[:, 1024:]
    other = other_ref[:, 1024:]
    low_core = jnp.where(first, own, other)
    high_core = jnp.where(first, other, own)
    for f in range(FRONTS):
        at = slice(f * 32, (f + 1) * 32)
        value = jnp.concatenate([low_core[:, at], high_core[:, at]], axis=1)
        high = value.astype(BF).astype(F32)
        low = value - high
        out_ref[f] = jnp.concatenate([high, low], axis=1).astype(BF)


def root_right_kernel(own_ref, other_ref, s3_ref, s2_ref, s1_ref, out_ref):
    right = (own_ref[...] + other_ref[...]).astype(BF)
    for f in range(FRONTS):
        out_ref[f, :, :1024] = right
    out_ref[:, :, 1024:1152] = s3_ref[...]
    out_ref[:, :, 1152:1280] = s2_ref[...]
    out_ref[:, :, 1280:] = s1_ref[...]


def root_kernel(got_ref, inv_ref, out_ref):
    right = got_ref[:, :, :1024].reshape(256, 1024)
    out_ref[3] = nt(inv_ref[0], right)
    for a in range(3):
        at = 1024 + a * 128
        both = got_ref[:, :, at : at + 128].reshape(256, 128).astype(F32).T
        out_ref[a] = both[:64] + both[64:]


def swap(block, pairs):
    return lax.ppermute(block, "leaf", pairs)


def along(block, bits):
    return lax.ppermute(block, "front", [(i, i ^ bits) for i in range(FRONTS)])


def core_pairs():
    return [(i, i ^ 1) for i in range(16)]


def chip_pairs(level):
    pairs = []
    for i in range(16):
        z, core = i // 2, i % 2
        if level == 0:
            to = z ^ 1
        elif level == 1:
            to = z ^ 2
        else:
            to = (6, 7, 4, 5, 2, 3, 0, 1)[z]
        pairs.append((i, 2 * to + core))
    return pairs


def local(rhs_leaf, rhs_top, inv_leaf, inv_top, off_leaf, off_top, idx_leaf, idx_top):
    leaf = lax.axis_index("leaf")
    front = lax.axis_index("front")
    nodes = [jnp.right_shift(16 + leaf, a + 1) for a in range(4)]
    subs = [leaf & (2 ** (a + 1) - 1) for a in range(4)]
    place = nodes + subs + [leaf & 1, front // 4, front % 4]
    place = jnp.stack(place).astype(jnp.int32)
    off_top = jnp.swapaxes(off_top, 1, 2)
    off_leaf = jnp.swapaxes(off_leaf, 1, 2)

    weights = lax.all_to_all(path_weights(place, inv_top, off_top, 3), "front", 0, 0)
    right = rhs_leaf[0].astype(BF)
    one, three, two = [along(right, s) for s in (1, 3, 2)]
    right = jnp.stack([right, one, two, three])
    right = [right] + [along(right, 4 * t) for t in (1, 3, 2)]
    shares = rhs_shares(place, rhs_top)
    piece = jax.ShapeDtypeStruct((64, 1152), BF)
    leaf_x, *sent = pl.pallas_call(
        leaf_solve_kernel,
        out_shape=(jax.ShapeDtypeStruct((64, 256), F32), piece, piece, piece, piece),
        in_specs=[SMEM] + [VMEM] * 7,
        out_specs=(VMEM,) * 5,
        scratch_shapes=[pltpu.VMEM((16, 64, 256), BF), pltpu.VMEM((4, 64, 1024), BF)],
        compiler_params=params(),
    )(place, inv_leaf, right[0], right[1], right[3], right[2], off_leaf, shares)
    got = [sent[0]] + [along(sent[t], 4 * t) for t in (1, 2, 3)]
    piece = jax.ShapeDtypeStruct((16, 1536), F32)
    sent = call(fold_kernel, (piece,) * 4, [SMEM] + [VMEM] * 4, (place, *got))
    got = [sent[0]] + [along(sent[s], s) for s in (1, 2, 3)]
    state = pl.pallas_call(
        leaf_update_kernel,
        out_shape=jax.ShapeDtypeStruct((64, 1024), F32),
        in_specs=[SMEM] + [VMEM] * 5,
        out_specs=VMEM,
        scratch_shapes=[pltpu.VMEM((4, 16, 512), F32)],
        compiler_params=params(),
    )(place, *got, idx_leaf)
    other = swap(state, core_pairs())
    ships = []
    for level in range(3):
        ux, rest = top_solve(state, other, weights, level)
        ux_other = swap(ux, core_pairs())
        state = call(
            functools.partial(update_kernel, level),
            jax.ShapeDtypeStruct(rest.shape, F32),
            [SMEM] + [VMEM] * 4,
            (place, ux, ux_other, rest, idx_top),
        )
        other = swap(state, chip_pairs(level))
        ships.append(
            call(
                ship_kernel,
                jax.ShapeDtypeStruct((16, 16, 128), BF),
                [SMEM, VMEM, VMEM],
                (place, ux, ux_other),
            )
        )
    sent = call(
        root_right_kernel,
        jax.ShapeDtypeStruct((16, 16, 1408), BF),
        [VMEM] * 5,
        (state, other, *ships),
    )
    got = lax.all_to_all(sent, "front", 0, 0)
    ancestors = call(
        root_kernel,
        jax.ShapeDtypeStruct((4, 64, 256), F32),
        [VMEM] * 2,
        (got, inv_top[:1]),
    )
    return (leaf_x[None], ancestors[None])


def solution(mesh):
    placed = (
        P("leaf", "front", None),
        P(None, "front", None),
        P("leaf", "front", None),
        P(None, "front", None),
        P("leaf", None, "front"),
        P(None, None, "front"),
        P("leaf", None),
        P(),
    )
    return jax.shard_map(
        local,
        mesh=mesh,
        in_specs=placed,
        out_specs=(P("leaf", "front", None), P("leaf", None, "front", None)),
        check_vma=False,
    )
```

time: 150 us -> 213 us (1.42)
  waiting for transfers between devices: 66.3 us -> 118 us
  starting transfers between devices: 19.6 us -> 61.2 us
  blocking collectives: 14.9 us -> 0 us
  local copies, waits for them, and re-layouts: 16.7 us -> 2.45 us
  between operations: 14.2 us -> 0.85 us
  Pallas kernels: 17.3 us -> 29.7 us
    ppermute x0 -> x12, waiting for transfers between devices: none -> 86.8 us  [along(): return lax.ppermute(block, 'front', [(i, i ^ bits) for i in range(FRONTS)])]
    ppermute x0 -> x12, starting transfers between devices: none -> 40.4 us  [along(): return lax.ppermute(block, 'front', [(i, i ^ bits) for i in range(FRONTS)])]
    all_gather x1 -> x0, waiting for transfers between devices: 26.1 us -> none  [local(): weights = lax.all_gather(path, 'front', axis=0, tiled=False)]
    all_to_all x1 -> x0, blocking collectives: 14.9 us -> none  [local(): got = lax.all_to_all(sent, 'front', 0, 0)]
    pallas_call x5 -> x7, Pallas kernels: 5.01 us -> 19.4 us  [the longest x3 6.61 us: top_solve(): pl.pallas_call(solve_kernel, grid=(1,), in_specs=[whole, whole, pl.BlockS...]
    unnamed x24 -> x14, local copies, waits for them, and re-layouts: 14.7 us -> 0.87 us
    all_to_all x1, waiting for transfers between devices: 8.17 us -> 0.01 us  [local(): lax.all_to_all(path_weights(place, inv_top, off_top, 3), 'front', 0, 0)]
    ppermute x7, starting transfers between devices: 7.33 us -> 9.65 us  [swap(): return lax.ppermute(block, 'leaf', pairs)]
  transfers between devices with their start and end apart: 10 -> 21, of which waited for: 10 -> 16; matrix products, arithmetic and copies ran while one was open for 2% -> 0% of each run, Pallas kernels for 5% -> 5%
where the time goes in v2:
time: 213 us; the launch traced here: 212 us
  waiting for transfers between devices  118 us (55%)
  starting transfers between devices  61.2 us (29%)
  Pallas kernels  29.7 us (14%)
  local copies, waits for them, and re-layouts  2.45 us (1%)
    ppermute x12, waiting for transfers between devices, along(): return lax.ppermute(block, 'front', [(i, i ^ bits) for i in range(FRONTS)])  86.8 us
    ppermute x12, starting transfers between devices, along(): return lax.ppermute(block, 'front', [(i, i ^ bits) for i in range(FRONTS)])  40.4 us
    ppermute x7, waiting for transfers between devices, swap(): return lax.ppermute(block, 'leaf', pairs)  18.2 us
    all_to_all x1, waiting for transfers between devices, local(): got = lax.all_to_all(sent, 'front', 0, 0)  12.7 us
    pallas_call x9, Pallas kernels, call(): pl.pallas_call(kernel, out_shape=outs, in_specs=specs, out_specs=tuple((V...  10.3 us
    ppermute x7, starting transfers between devices, swap(): return lax.ppermute(block, 'leaf', pairs)  9.65 us
    all_to_all x1, starting transfers between devices, local(): lax.all_to_all(path_weights(place, inv_top, off_top, 3), 'front', 0, 0)  7.22 us
    pallas_call x3, Pallas kernels, top_solve(): pl.pallas_call(solve_kernel, grid=(1,), in_specs=[whole, whole, pl.BlockS...  6.61 us
  transfers between devices with their start and end apart: 21, of which 16 were waited for; matrix products, arithmetic and copies ran while one was open for 0% of the time, Pallas kernels for 5%

profile of v2, /device:TPU:32, one launch (start us, length us, event | category | flops | bytes accessed | tf_op | source)
XLA Modules:
  0.0 212.1 jit_solution(11059691355120832906)
XLA Ops:
  1.3 5.6 %shard_map.99 = bf16[16,192,1024]{2,1,0:T(8,128)(2,1)} custom-call(s32[11]{0:T(128)} %stack.57.place, bf16[15,64,1024]{2,1,0:T(8,128)(2,1)} %inv_ref.3, bf16[14,64,1024]{2,1,0:T(8,128)(2,1)} %bitcast.20), custom_call_target="tpu_custom_call" | custom-call | tf_op jit(solution)/shard_map/pallas_call | solution.py:76
  6.9 7.2 %all-to-all-start = ((bf16[16,192,1024]{2,1,0:T(8,128)(2,1)}), bf16[16,192,1024]{2,1,0:T(8,128)(2,1)}, u32[]{:S(2)}, u32[]{:S(2)}) async-start(bf16[16,192,1024]{2,1,0:T(8,128)(2,1)} %shard_map.99), calls=%async_computation | async-start | bytes 12582912 | tf_op jit(solution)/shard_map/all_to_all | solution.py:298
  14.2 2.0 collective-permute-start
  16.2 2.7 %collective-permute-start.1 = (bf16[64,256]{1,0:T(8,128)(2,1)S(1)}, bf16[64,256]{1,0:T(8,128)(2,1)S(1)}, u32[]{:S(2)}, u32[]{:S(2)}) collective-permute-start(bf16[64,256]{1,0:T(8,128)(2,1)S(1)} %convert_bitcast_fusion), channel_id=1, source_target_pairs={{0,2},{1,3},{2,0},{3,1},{4,6},{5,7},{6,4},{7,5},{8,10},{9,11},{10,... | collective-permute-start | bytes 98312 | tf_op jit(solution)/shard_map/ppermute | solution.py:267
  19.0 58.8 %collective-permute-done = bf16[64,256]{1,0:T(8,128)(2,1)S(1)} collective-permute-done((bf16[64,256]{1,0:T(8,128)(2,1)S(1)}, bf16[64,256]{1,0:T(8,128)(2,1)S(1)}, u32[]{:S(2)}, u32[]{:S(2)}) %collective-permute-start) | collective-permute-done | bytes 32800 | tf_op jit(solution)/shard_map/ppermute | solution.py:267
  77.9 19.1 %collective-permute-start.3 = (bf16[4,64,256]{2,1,0:T(8,128)(2,1)S(1)}, bf16[4,64,256]{2,1,0:T(8,128)(2,1)S(1)}, u32[]{:S(2)}, u32[]{:S(2)}) collective-permute-start(bf16[4,64,256]{2,1,0:T(8,128)(2,1)S(1)} %pad_maximum_fusion.r0), channel_id=1, source_target_pairs={{0,4},{1,5},{2,6},{3,7},{4,0},{5,1},{6,2},{7,3},{8,12},{9,13},{10,... | collective-permute-start | bytes 393224 | tf_op jit(solution)/shard_map/ppermute | solution.py:267
  97.0 2.6 %collective-permute-start.4 = (bf16[4,64,256]{2,1,0:T(8,128)(2,1)S(1)}, bf16[4,64,256]{2,1,0:T(8,128)(2,1)S(1)}, u32[]{:S(2)}, u32[]{:S(2)}) collective-permute-start(bf16[4,64,256]{2,1,0:T(8,128)(2,1)S(1)} %pad_maximum_fusion.r0), channel_id=1, source_target_pairs={{0,8},{1,9},{2,10},{3,11},{4,12},{5,13},{6,14},{7,15},{8,0},{9,1},... | collective-permute-start | bytes 393224 | tf_op jit(solution)/shard_map/ppermute | solution.py:267
  99.7 2.6 %shard_map.95.shares_ref = bf16[4,64,128]{2,1,0:T(8,128)(2,1)} custom-call(s32[11]{0:T(128)} %stack.57.place, f32[15,64,256]{2,1,0:T(8,128)} %rhs_ref.1), custom_call_target="tpu_custom_call" | custom-call | tf_op jit(solution)/shard_map/pallas_call | solution.py:110
  102.3 17.1 %collective-permute-done.3.r1 = bf16[4,64,256]{2,1,0:T(8,128)(2,1)S(1)} collective-permute-done((bf16[4,64,256]{2,1,0:T(8,128)(2,1)S(1)}, bf16[4,64,256]{2,1,0:T(8,128)(2,1)S(1)}, u32[]{:S(2)}, u32[]{:S(2)}) %collective-permute-start.3) | collective-permute-done | bytes 131104 | tf_op jit(solution)/shard_map/ppermute | solution.py:267
  119.4 1.7 collective-permute-done.4.r2
  122.0 1.6 shard_map.96
  123.5 7.6 %collective-permute-start.6 = (bf16[64,1152]{1,0:T(8,128)(2,1)S(1)}, bf16[64,1152]{1,0:T(8,128)(2,1)S(1)}, u32[]{:S(2)}, u32[]{:S(2)}) collective-permute-start(bf16[64,1152]{1,0:T(8,128)(2,1)S(1)} %get-tuple-element.19), channel_id=1, source_target_pairs={{0,4},{1,5},{2,6},{3,7},{4,0},{5,1},{6,2},{7,3},{8,12},{9,13},{10,... | collective-permute-start | bytes 442376 | tf_op jit(solution)/shard_map/ppermute | solution.py:267
  131.2 2.5 %collective-permute-start.8 = (bf16[64,1152]{1,0:T(8,128)(2,1)S(1)}, bf16[64,1152]{1,0:T(8,128)(2,1)S(1)}, u32[]{:S(2)}, u32[]{:S(2)}) collective-permute-start(bf16[64,1152]{1,0:T(8,128)(2,1)S(1)} %get-tuple-element.21), channel_id=1, source_target_pairs={{0,12},{1,13},{2,14},{3,15},{4,8},{5,9},{6,10},{7,11},{8,4},{9,5},... | collective-permute-start | bytes 442376 | tf_op jit(solution)/shard_map/ppermute | solution.py:267
  133.8 1.3 collective-permute-done.6.r1
  135.1 2.7 %collective-permute-done.7.r2 = bf16[64,1152]{1,0:T(8,128)(2,1)S(1)} collective-permute-done((bf16[64,1152]{1,0:T(8,128)(2,1)S(1)}, bf16[64,1152]{1,0:T(8,128)(2,1)S(1)}, u32[]{:S(2)}, u32[]{:S(2)}) %collective-permute-start.7) | collective-permute-done | bytes 147488 | tf_op jit(solution)/shard_map/ppermute | solution.py:267
  137.8 1.7 collective-permute-done.8.r3
  140.4 3.4 %collective-permute-start.9 = (f32[16,1536]{1,0:T(8,128)S(1)}, f32[16,1536]{1,0:T(8,128)S(1)}, u32[]{:S(2)}, u32[]{:S(2)}) collective-permute-start(f32[16,1536]{1,0:T(8,128)S(1)} %get-tuple-element.23), channel_id=1, source_target_pairs={{0,1},{1,0},{2,3},{3,2},{4,5},{5,4},{6,7},{7,6},{8,9},{9,8},{10,11... | collective-permute-start | bytes 294920 | tf_op jit(solution)/shard_map/ppermute | solution.py:267
  143.7 2.7 %collective-permute-done.10.r2 = f32[16,1536]{1,0:T(8,128)S(1)} collective-permute-done((f32[16,1536]{1,0:T(8,128)S(1)}, f32[16,1536]{1,0:T(8,128)S(1)}, u32[]{:S(2)}, u32[]{:S(2)}) %collective-permute-start.10) | collective-permute-done | bytes 98336 | tf_op jit(solution)/shard_map/ppermute | solution.py:267
  147.2 3.1 %shard_map.98.own_ref = f32[64,1024]{1,0:T(8,128)S(1)} custom-call(s32[11]{0:T(128)S(1)} %copy-done.4, f32[16,1536]{1,0:T(8,128)S(1)} %get-tuple-element.22.r0, f32[16,1536]{1,0:T(8,128)S(1)} %collective-permute-done.9.r1, f32[16,1536]{1,0:T(8,128)S(1)} %collective-permute-done.10.r2, f32[16,1536]{1,0:T(8,128)S(1)} %collective-permute-done.11.r3, ...), custom_call_target="tpu_custom_call" | custom-call | tf_op jit(solution)/shard_map/pallas_call | solution.py:317
  150.4 1.5 collective-permute-done.12.other_ref
  152.0 2.2 %shard_map.100 = (f32[16,1536]{1,0:T(8,128)S(1)}, f32[48,1024]{1,0:T(8,128)S(1)}) custom-call(f32[64,1024]{1,0:T(8,128)S(1)} %shard_map.98.own_ref, f32[64,1024]{1,0:T(8,128)S(1)} %collective-permute-done.12.other_ref, bf16[16,192,1024]{2,1,0:T(8,128)(2,1)} %all-to-all-done.weights_ref), custom_call_target="tpu_custom_call" | custom-call | tf_op jit(solution)/shard_map/pallas_call | solution.py:209
  155.7 2.4 %shard_map.101.own_ref = f32[48,1024]{1,0:T(8,128)S(1)} custom-call(s32[11]{0:T(128)S(1)} %copy-done.4, f32[16,1536]{1,0:T(8,128)S(1)} %get-tuple-element.26.own_ref, f32[16,1536]{1,0:T(8,128)S(1)} %collective-permute-done.13.other_ref, f32[48,1024]{1,0:T(8,128)S(1)} %get-tuple-element.27.rest_ref, s32[14,1024]{1,0:T(8,128)S(1)} %copy-done), custom_call_target="tpu_custom_call" | custom-call | flops 100000000 | bytes 1000000 | tf_op jit(solution)/shard_map/pallas_call | solution.py:46
  158.2 6.8 %collective-permute-done.14.other_ref = f32[48,1024]{1,0:T(8,128)S(1)} collective-permute-done((f32[48,1024]{1,0:T(8,128)S(1)}, f32[48,1024]{1,0:T(8,128)S(1)}, u32[]{:S(2)}, u32[]{:S(2)}) %collective-permute-start.14) | collective-permute-done | bytes 196640 | tf_op jit(solution)/shard_map/ppermute | solution.py:263
  165.1 2.2 %shard_map.102 = (f32[16,1536]{1,0:T(8,128)S(1)}, f32[32,1024]{1,0:T(8,128)S(1)}) custom-call(f32[48,1024]{1,0:T(8,128)S(1)} %shard_map.101.own_ref, f32[48,1024]{1,0:T(8,128)S(1)} %collective-permute-done.14.other_ref, bf16[16,192,1024]{2,1,0:T(8,128)(2,1)} %all-to-all-done.weights_ref), custom_call_target="tpu_custom_call" | custom-call | tf_op jit(solution)/shard_map/pallas_call | solution.py:209
  167.3 1.3 collective-permute-done.15.other_ref
  168.6 1.8 shard_map.103.own_ref
  170.4 3.3 %collective-permute-start.16 = (f32[32,1024]{1,0:T(8,128)S(1)}, f32[32,1024]{1,0:T(8,128)S(1)}, u32[]{:S(2)}, u32[]{:S(2)}) collective-permute-start(f32[32,1024]{1,0:T(8,128)S(1)} %shard_map.103.own_ref), channel_id=1, source_target_pairs={{0,64},{16,80},{32,96},{48,112},{64,0},{80,16},{96,32},{112,48},{1... | collective-permute-start | bytes 393224 | tf_op jit(solution)/shard_map/ppermute | solution.py:263
  173.7 5.6 %collective-permute-done.16.other_ref = f32[32,1024]{1,0:T(8,128)S(1)} collective-permute-done((f32[32,1024]{1,0:T(8,128)S(1)}, f32[32,1024]{1,0:T(8,128)S(1)}, u32[]{:S(2)}, u32[]{:S(2)}) %collective-permute-start.16) | collective-permute-done | bytes 131104 | tf_op jit(solution)/shard_map/ppermute | solution.py:263
  179.3 2.2 %shard_map.104 = (f32[16,1536]{1,0:T(8,128)S(1)}, f32[16,1024]{1,0:T(8,128)S(1)}) custom-call(f32[32,1024]{1,0:T(8,128)S(1)} %shard_map.103.own_ref, f32[32,1024]{1,0:T(8,128)S(1)} %collective-permute-done.16.other_ref, bf16[16,192,1024]{2,1,0:T(8,128)(2,1)} %all-to-all-done.weights_ref), custom_call_target="tpu_custom_call" | custom-call | tf_op jit(solution)/shard_map/pallas_call | solution.py:209
  184.1 5.8 %collective-permute-start.18 = (f32[16,1024]{1,0:T(8,128)S(1)}, f32[16,1024]{1,0:T(8,128)S(1)}, u32[]{:S(2)}, u32[]{:S(2)}) collective-permute-start(f32[16,1024]{1,0:T(8,128)S(1)} %shard_map.105.own_ref), channel_id=1, source_target_pairs={{0,192},{16,208},{32,224},{48,240},{64,128},{80,144},{96,160},{112... | collective-permute-start | bytes 196616 | tf_op jit(solution)/shard_map/ppermute | solution.py:263
  193.5 3.9 %all-to-all-start.1 = ((bf16[16,16,1408]{2,1,0:T(8,128)(2,1)}), bf16[16,16,1408]{2,1,0:T(8,128)(2,1)S(1)}, u32[]{:S(2)}, u32[]{:S(2)}) async-start(bf16[16,16,1408]{2,1,0:T(8,128)(2,1)} %shard_map.109), calls=%async_computation.1 | async-start | bytes 1441792 | tf_op jit(solution)/shard_map/all_to_all | solution.py:351
  198.3 12.7 %all-to-all-done.1.got_ref = bf16[16,16,1408]{2,1,0:T(8,128)(2,1)S(1)} async-done(((bf16[16,16,1408]{2,1,0:T(8,128)(2,1)}), bf16[16,16,1408]{2,1,0:T(8,128)(2,1)S(1)}, u32[]{:S(2)}, u32[]{:S(2)}) %all-to-all-start.1) | async-done | bytes 720928 | tf_op jit(solution)/shard_map/all_to_all | solution.py:351
  (45 shorter events, 13.5 us)
Async XLA Ops:
  6.9 7.3 %copy-start.6 = (f32[1,64,256]{2,1,0:T(8,128)S(1)}, f32[1,64,256]{2,1,0:T(8,128)}, u32[]{:S(2)}) copy-start(f32[1,64,256]{2,1,0:T(8,128)} %param.8) | copy-start | bytes 196612
  6.9 114.2 %copy-start.2 = (bf16[1,64,1024]{2,1,0:T(8,128)(2,1)S(1)}, bf16[1,64,1024]{2,1,0:T(8,128)(2,1)}, u32[]{:S(2)}) copy-start(bf16[1,64,1024]{2,1,0:T(8,128)(2,1)} %inv_ref.2) | copy-start | bytes 393220
  6.9 114.2 %copy-start.3 = (bf16[1,1024,64]{1,2,0:T(8,128)(2,1)S(1)}, bf16[1,1024,64]{1,2,0:T(8,128)(2,1)}, u32[]{:S(2)}) copy-start(bf16[1,1024,64]{1,2,0:T(8,128)(2,1)} %param.12) | copy-start | bytes 393220
  6.9 114.2 %copy-start.4 = (s32[11]{0:T(128)S(1)}, s32[11]{0:T(128)}, u32[]{:S(2)}) copy-start(s32[11]{0:T(128)} %stack.57.place) | copy-start | bytes 136
  6.9 140.3 %copy-start.5 = (s32[1,1024]{1,0:T(1,128)S(1)}, s32[1,1024]{1,0:T(1,128)}, u32[]{:S(2)}) copy-start(s32[1,1024]{1,0:T(1,128)} %idx_ref.4) | copy-start | bytes 12292
  6.9 145.0 %all-to-all-start = ((bf16[16,192,1024]{2,1,0:T(8,128)(2,1)}), bf16[16,192,1024]{2,1,0:T(8,128)(2,1)}, u32[]{:S(2)}, u32[]{:S(2)}) async-start(bf16[16,192,1024]{2,1,0:T(8,128)(2,1)} %shard_map.99), calls=%async_computation | async-start | bytes 12582912 | tf_op jit(solution)/shard_map/all_to_all | solution.py:298
  14.2 141.5 %copy-start = (s32[14,1024]{1,0:T(8,128)S(1)}, s32[14,1024]{1,0:T(8,128)}, u32[]{:S(2)}) copy-start(s32[14,1024]{1,0:T(8,128)} %idx_ref.7) | copy-start | bytes 172036
  14.2 63.6 %collective-permute-start = (bf16[64,256]{1,0:T(8,128)(2,1)S(1)}, bf16[64,256]{1,0:T(8,128)(2,1)S(1)}, u32[]{:S(2)}, u32[]{:S(2)}) collective-permute-start(bf16[64,256]{1,0:T(8,128)(2,1)S(1)} %convert_bitcast_fusion), channel_id=1, source_target_pairs={{0,1},{1,0},{2,3},{3,2},{4,5},{5,4},{6,7},{7,6},{8,9},{9,8},{10,11... | collective-permute-start | bytes 98312 | tf_op jit(solution)/shard_map/ppermute | solution.py:267
  16.2 61.7 %collective-permute-start.1 = (bf16[64,256]{1,0:T(8,128)(2,1)S(1)}, bf16[64,256]{1,0:T(8,128)(2,1)S(1)}, u32[]{:S(2)}, u32[]{:S(2)}) collective-permute-start(bf16[64,256]{1,0:T(8,128)(2,1)S(1)} %convert_bitcast_fusion), channel_id=1, source_target_pairs={{0,2},{1,3},{2,0},{3,1},{4,6},{5,7},{6,4},{7,5},{8,10},{9,11},{10,... | collective-permute-start | bytes 98312 | tf_op jit(solution)/shard_map/ppermute | solution.py:267
  18.8 59.0 %collective-permute-start.2 = (bf16[64,256]{1,0:T(8,128)(2,1)S(1)}, bf16[64,256]{1,0:T(8,128)(2,1)S(1)}, u32[]{:S(2)}, u32[]{:S(2)}) collective-permute-start(bf16[64,256]{1,0:T(8,128)(2,1)S(1)} %convert_bitcast_fusion), channel_id=1, source_target_pairs={{0,3},{1,2},{2,1},{3,0},{4,7},{5,6},{6,5},{7,4},{8,11},{9,10},{10,... | collective-permute-start | bytes 98312 | tf_op jit(solution)/shard_map/ppermute | solution.py:267
  77.9 41.6 %collective-permute-start.3 = (bf16[4,64,256]{2,1,0:T(8,128)(2,1)S(1)}, bf16[4,64,256]{2,1,0:T(8,128)(2,1)S(1)}, u32[]{:S(2)}, u32[]{:S(2)}) collective-permute-start(bf16[4,64,256]{2,1,0:T(8,128)(2,1)S(1)} %pad_maximum_fusion.r0), channel_id=1, source_target_pairs={{0,4},{1,5},{2,6},{3,7},{4,0},{5,1},{6,2},{7,3},{8,12},{9,13},{10,... | collective-permute-start | bytes 393224 | tf_op jit(solution)/shard_map/ppermute | solution.py:267
  97.0 24.1 %collective-permute-start.4 = (bf16[4,64,256]{2,1,0:T(8,128)(2,1)S(1)}, bf16[4,64,256]{2,1,0:T(8,128)(2,1)S(1)}, u32[]{:S(2)}, u32[]{:S(2)}) collective-permute-start(bf16[4,64,256]{2,1,0:T(8,128)(2,1)S(1)} %pad_maximum_fusion.r0), channel_id=1, source_target_pairs={{0,8},{1,9},{2,10},{3,11},{4,12},{5,13},{6,14},{7,15},{8,0},{9,1},... | collective-permute-start | bytes 393224 | tf_op jit(solution)/shard_map/ppermute | solution.py:267
  99.5 21.6 %collective-permute-start.5 = (bf16[4,64,256]{2,1,0:T(8,128)(2,1)S(1)}, bf16[4,64,256]{2,1,0:T(8,128)(2,1)S(1)}, u32[]{:S(2)}, u32[]{:S(2)}) collective-permute-start(bf16[4,64,256]{2,1,0:T(8,128)(2,1)S(1)} %pad_maximum_fusion.r0), channel_id=1, source_target_pairs={{0,12},{1,13},{2,14},{3,15},{4,8},{5,9},{6,10},{7,11},{8,4},{9,5},... | collective-permute-start | bytes 393224 | tf_op jit(solution)/shard_map/ppermute | solution.py:267
  121.1 0.8 copy-start.1
  123.5 11.6 %collective-permute-start.6 = (bf16[64,1152]{1,0:T(8,128)(2,1)S(1)}, bf16[64,1152]{1,0:T(8,128)(2,1)S(1)}, u32[]{:S(2)}, u32[]{:S(2)}) collective-permute-start(bf16[64,1152]{1,0:T(8,128)(2,1)S(1)} %get-tuple-element.19), channel_id=1, source_target_pairs={{0,4},{1,5},{2,6},{3,7},{4,0},{5,1},{6,2},{7,3},{8,12},{9,13},{10,... | collective-permute-start | bytes 442376 | tf_op jit(solution)/shard_map/ppermute | solution.py:267
  131.1 6.7 %collective-permute-start.7 = (bf16[64,1152]{1,0:T(8,128)(2,1)S(1)}, bf16[64,1152]{1,0:T(8,128)(2,1)S(1)}, u32[]{:S(2)}, u32[]{:S(2)}) collective-permute-start(bf16[64,1152]{1,0:T(8,128)(2,1)S(1)} %get-tuple-element.20), channel_id=1, source_target_pairs={{0,8},{1,9},{2,10},{3,11},{4,12},{5,13},{6,14},{7,15},{8,0},{9,1},... | collective-permute-start | bytes 442376 | tf_op jit(solution)/shard_map/ppermute | solution.py:267
  131.2 8.3 %collective-permute-start.8 = (bf16[64,1152]{1,0:T(8,128)(2,1)S(1)}, bf16[64,1152]{1,0:T(8,128)(2,1)S(1)}, u32[]{:S(2)}, u32[]{:S(2)}) collective-permute-start(bf16[64,1152]{1,0:T(8,128)(2,1)S(1)} %get-tuple-element.21), channel_id=1, source_target_pairs={{0,12},{1,13},{2,14},{3,15},{4,8},{5,9},{6,10},{7,11},{8,4},{9,5},... | collective-permute-start | bytes 442376 | tf_op jit(solution)/shard_map/ppermute | solution.py:267
  140.2 6.3 %collective-permute-start.10 = (f32[16,1536]{1,0:T(8,128)S(1)}, f32[16,1536]{1,0:T(8,128)S(1)}, u32[]{:S(2)}, u32[]{:S(2)}) collective-permute-start(f32[16,1536]{1,0:T(8,128)S(1)} %get-tuple-element.24), channel_id=1, source_target_pairs={{0,2},{1,3},{2,0},{3,1},{4,6},{5,7},{6,4},{7,5},{8,10},{9,11},{10,... | collective-permute-start | bytes 294920 | tf_op jit(solution)/shard_map/ppermute | solution.py:267
  140.3 7.0 %collective-permute-start.11 = (f32[16,1536]{1,0:T(8,128)S(1)}, f32[16,1536]{1,0:T(8,128)S(1)}, u32[]{:S(2)}, u32[]{:S(2)}) collective-permute-start(f32[16,1536]{1,0:T(8,128)S(1)} %get-tuple-element.25), channel_id=1, source_target_pairs={{0,3},{1,2},{2,1},{3,0},{4,7},{5,6},{6,5},{7,4},{8,11},{9,10},{10,... | collective-permute-start | bytes 294920 | tf_op jit(solution)/shard_map/ppermute | solution.py:267
  140.4 6.9 %collective-permute-start.9 = (f32[16,1536]{1,0:T(8,128)S(1)}, f32[16,1536]{1,0:T(8,128)S(1)}, u32[]{:S(2)}, u32[]{:S(2)}) collective-permute-start(f32[16,1536]{1,0:T(8,128)S(1)} %get-tuple-element.23), channel_id=1, source_target_pairs={{0,1},{1,0},{2,3},{3,2},{4,5},{5,4},{6,7},{7,6},{8,9},{9,8},{10,11... | collective-permute-start | bytes 294920 | tf_op jit(solution)/shard_map/ppermute | solution.py:267
  150.3 1.6 collective-permute-start.12
  154.2 1.5 collective-permute-start.13
  158.1 7.0 %collective-permute-start.14 = (f32[48,1024]{1,0:T(8,128)S(1)}, f32[48,1024]{1,0:T(8,128)S(1)}, u32[]{:S(2)}, u32[]{:S(2)}) collective-permute-start(f32[48,1024]{1,0:T(8,128)S(1)} %shard_map.101.own_ref), channel_id=1, source_target_pairs={{0,32},{16,48},{32,0},{48,16},{64,96},{80,112},{96,64},{112,80},{1... | collective-permute-start | bytes 589832 | tf_op jit(solution)/shard_map/ppermute | solution.py:263
  167.3 1.3 collective-permute-start.15
  170.4 8.9 %collective-permute-start.16 = (f32[32,1024]{1,0:T(8,128)S(1)}, f32[32,1024]{1,0:T(8,128)S(1)}, u32[]{:S(2)}, u32[]{:S(2)}) collective-permute-start(f32[32,1024]{1,0:T(8,128)S(1)} %shard_map.103.own_ref), channel_id=1, source_target_pairs={{0,64},{16,80},{32,96},{48,112},{64,0},{80,16},{96,32},{112,48},{1... | collective-permute-start | bytes 393224 | tf_op jit(solution)/shard_map/ppermute | solution.py:263
  181.5 1.3 collective-permute-start.17
  184.1 8.5 %collective-permute-start.18 = (f32[16,1024]{1,0:T(8,128)S(1)}, f32[16,1024]{1,0:T(8,128)S(1)}, u32[]{:S(2)}, u32[]{:S(2)}) collective-permute-start(f32[16,1024]{1,0:T(8,128)S(1)} %shard_map.105.own_ref), channel_id=1, source_target_pairs={{0,192},{16,208},{32,224},{48,240},{64,128},{80,144},{96,160},{112... | collective-permute-start | bytes 196616 | tf_op jit(solution)/shard_map/ppermute | solution.py:263
  193.5 17.5 %all-to-all-start.1 = ((bf16[16,16,1408]{2,1,0:T(8,128)(2,1)}), bf16[16,16,1408]{2,1,0:T(8,128)(2,1)S(1)}, u32[]{:S(2)}, u32[]{:S(2)}) async-start(bf16[16,16,1408]{2,1,0:T(8,128)(2,1)} %shard_map.109), calls=%async_computation.1 | async-start | bytes 1441792 | tf_op jit(solution)/shard_map/all_to_all | solution.py:351

commit v3 on v1

--- a/solution.py
+++ b/solution.py
@@ -16,6 +16,7 @@
 
 VMEM = pl.BlockSpec(memory_space=pltpu.VMEM)
 SMEM = pl.BlockSpec(memory_space=pltpu.SMEM)
+HBM = pl.BlockSpec(memory_space=pltpu.HBM)
 
 
 def nt(a, b):
@@ -36,8 +37,8 @@
     return lax.broadcasted_iota(jnp.int32, shape, dim)
 
 
-def params():
-    return pltpu.CompilerParams(vmem_limit_bytes=40 * 2**20)
+def params(mib=16):
+    return pltpu.CompilerParams(vmem_limit_bytes=mib * 2**20)
 
 
 def call(kernel, outs, specs, args, flops=10**8, bytes_accessed=10**6):
@@ -54,70 +55,70 @@
     )(*args)
 
 
-def weights_kernel(place, inv_ref, off_ref, out_ref):
-    core = place[8]
-    rows = inv_ref.shape[1]
-    out_ref[:rows, :] = inv_ref[0]
-    pick = (iota((rows, 2 * rows), 1) == iota((rows, 2 * rows), 0) + core * rows).astype(BF)
-    out_ref[rows:, :] = nt(pick, off_ref[0]).astype(BF)
-
-
-def path_weights(place, inv_top, off_top, levels):
-    width = inv_top.shape[2]
-    rows = inv_top.shape[1] // 2
+def weights_kernel(place, inv_ref, off_ref, out_ref, sems):
+    at = pl.ds(pl.multiple_of(place[8] * 32, 32), 32)
+    copies = []
+    for level in range(3):
+        node, to = place[level], level * 64
+        for ref, index, to in ((inv_ref, node - 1, to), (off_ref, node - 2, to + 32)):
+            copies.append(
+                pltpu.make_async_copy(
+                    ref.at[index, at, :], out_ref.at[pl.ds(to, 32), :], sems.at[len(copies)]
+                )
+            )
+    for copy in copies:
+        copy.start()
+    for copy in copies:
+        copy.wait()
+
+
+def path_weights(place, inv_top, off_top):
     return pl.pallas_call(
         weights_kernel,
-        grid_spec=pltpu.PrefetchScalarGridSpec(
-            num_scalar_prefetch=1,
-            grid=(levels,),
-            in_specs=[
-                pl.BlockSpec((1, rows, width), lambda a, s: (s[a] - 1, s[8], 0)),
-                pl.BlockSpec((1, width, 2 * rows), lambda a, s: (s[a] - 2, 0, 0)),
-            ],
-            out_specs=pl.BlockSpec((2 * rows, width), lambda a, s: (a, 0)),
-        ),
-        out_shape=jax.ShapeDtypeStruct((levels * 2 * rows, width), BF),
-        compiler_params=params(),
+        out_shape=jax.ShapeDtypeStruct((192, 1024), BF),
+        in_specs=[SMEM, HBM, HBM],
+        out_specs=HBM,
+        scratch_shapes=[pltpu.SemaphoreType.DMA((6,))],
+        compiler_params=params(60),
     )(place, inv_top, off_top)
 
 
-def shares_kernel(place, *refs):
-    rhs_refs, out_ref = refs[:4], refs[4]
-    parity = place[9]
-    total = jnp.zeros(out_ref.shape, F32)
+def shares_kernel(place, rhs_ref, out_ref, held, sems):
+    copies = [
+        pltpu.make_async_copy(rhs_ref.at[place[a] - 1], held.at[a], sems.at[a]) for a in range(4)
+    ]
+    for copy in copies:
+        copy.start()
+    for copy in copies:
+        copy.wait()
+    total = jnp.zeros((256, 256), F32)
     to = iota((256, 256), 0)
     come = iota((256, 256), 1)
     slot = to % 16
+    odd = place[9].astype(F32)
+    even = 1.0 - odd
     for a in range(4):
         sub = place[4 + a]
         width, start = WIDTHS[a], STARTS[a]
         from_col = (to - slot) + sub * width + (slot - start)
         chosen = (slot >= start) & (slot < start + width) & (come == from_col)
-        high, low = halves(rhs_refs[a][0])
+        high, low = halves(held[a])
         high = high.astype(F32)
         low = low.astype(F32)
-        even = (parity == 0).astype(F32)
-        odd = 1.0 - even
         stacked = jnp.concatenate([high * even, high * odd, low * even, low * odd], axis=0)
-        total = total + nt(chosen.astype(BF), stacked.astype(BF))
-    out_ref[...] = total.astype(BF)
+        total = total + nt(jnp.where(chosen, 1.0, 0.0).astype(BF), stacked.astype(BF))
+    out_ref[...] = total.astype(BF).reshape(16, 16, 256)
 
 
 def rhs_shares(place, rhs_top):
-    rows, cols = rhs_top.shape[1:]
     return pl.pallas_call(
         shares_kernel,
-        grid_spec=pltpu.PrefetchScalarGridSpec(
-            num_scalar_prefetch=1,
-            grid=(1,),
-            in_specs=[
-                pl.BlockSpec((1, rows, cols), lambda i, s, a=a: (s[a] - 1, 0, 0)) for a in range(4)
-            ],
-            out_specs=pl.BlockSpec((256, 256), lambda i, s: (0, 0)),
-        ),
-        out_shape=jax.ShapeDtypeStruct((256, 256), BF),
-        compiler_params=params(),
-    )(place, rhs_top, rhs_top, rhs_top, rhs_top)
+        out_shape=jax.ShapeDtypeStruct((16, 16, 256), BF),
+        in_specs=[SMEM, HBM],
+        out_specs=VMEM,
+        scratch_shapes=[pltpu.VMEM((4, 64, 256), F32), pltpu.SemaphoreType.DMA((4,))],
+        compiler_params=params(60),
+    )(place, rhs_top)
 
 
 def leaf_solve_kernel(inv_ref, rhs_ref, off_ref, shares_ref, x_ref, out_ref):
@@ -125,9 +126,9 @@
     x = nn(inv_ref[0], right)
     x_ref[...] = x
     xt = x.T.astype(BF)
-    update = nt(xt, off_ref[0])
+    update = nn(xt, off_ref[0])
     out_ref[:, :, :1024] = update.astype(BF).reshape(16, 16, 1024)
-    out_ref[:, :, 1024:] = shares_ref[...].reshape(16, 16, 256)
+    out_ref[:, :, 1024:] = shares_ref[...]
 
 
 def push(update, idx, count):
@@ -167,43 +168,54 @@
         out_ref[a * 16 : (a + 1) * 16, :] = nn(put, high) + nn(put, low) - pending[a]
 
 
-def solve_kernel(left, own_ref, other_ref, weights_ref, ux_ref, *rest):
+def solve_kernel(level, own_ref, other_ref, weights_ref, ux_ref, rest_ref, held, sems):
+    copies = []
+    for part in range(2):
+        for half in range(2):
+            fronts = pl.ds(half * 8, 8)
+            rows = pl.ds(level * 64 + part * 32, 32)
+            copies.append(
+                pltpu.make_async_copy(
+                    weights_ref.at[fronts, rows, :],
+                    held.at[part, fronts],
+                    sems.at[len(copies)],
+                )
+            )
+    for copy in copies:
+        copy.start()
     total = own_ref[...] + other_ref[...]
+    rest_ref[...] = total[16:]
     right = total[:16].astype(BF)
-    inverse = weights_ref[:, :32, :].reshape(512, 1024)
-    off = weights_ref[:, 32:, :].reshape(512, 1024)
-    x = nt(right, inverse)
-    ux_ref[:, :1024] = nn(x.astype(BF), off)
-    ux_ref[:, 1024:] = x
-    rest[0][...] = total[16:]
+    update = jnp.zeros((16, 1024), F32)
+    xs = []
+    for half in range(2):
+        copies[half].wait()
+        xs.append(nt(right, held[0, half * 8 : half * 8 + 8].reshape(256, 1024)))
+    for half in range(2):
+        copies[2 + half].wait()
+        off = held[1, half * 8 : half * 8 + 8].reshape(256, 1024)
+        update = update + nn(xs[half].astype(BF), off)
+        ux_ref[:, 1024 + half * 256 : 1280 + half * 256] = xs[half]
+    ux_ref[:, :1024] = update
 
 
 def top_solve(own, other, weights, level):
-    left = own.shape[0] // 16 - 1
+    left = own.shape[0] - 16
     return pl.pallas_call(
-        functools.partial(solve_kernel, left),
-        grid=(1,),
-        in_specs=[
-            pl.BlockSpec(own.shape, lambda i: (0, 0)),
-            pl.BlockSpec(own.shape, lambda i: (0, 0)),
-            pl.BlockSpec((16, 64, 1024), lambda i: (0, level, 0)),
-        ],
-        out_specs=(
-            pl.BlockSpec((16, 1536), lambda i: (0, 0)),
-            pl.BlockSpec((left * 16, 1024), lambda i: (0, 0)),
-        ),
-        out_shape=(
-            jax.ShapeDtypeStruct((16, 1536), F32),
-            jax.ShapeDtypeStruct((left * 16, 1024), F32),
-        ),
-        compiler_params=params(),
+        functools.partial(solve_kernel, level),
+        in_specs=[VMEM, VMEM, HBM],
+        out_specs=(VMEM, VMEM),
+        out_shape=(jax.ShapeDtypeStruct((16, 1536), F32), jax.ShapeDtypeStruct((left, 1024), F32)),
+        scratch_shapes=[pltpu.VMEM((2, 16, 32, 1024), BF), pltpu.SemaphoreType.DMA((4,))],
+        compiler_params=params(60 if level == 0 else 16),
     )(own, other, weights)
 
 
-def update_kernel(own_ref, other_ref, rest_ref, idx_ref, out_ref):
+def update_kernel(level, place, own_ref, other_ref, rest_ref, idx_ref, out_ref):
     update = own_ref[:, :1024] + other_ref[:, :1024]
     count = out_ref.shape[0] // 16
-    for a, block in enumerate(push(update, idx_ref[...], count)):
+    idx = idx_ref[pl.ds(place[level] - 2, 1), :]
+    for a, block in enumerate(push(update, idx, count)):
         out_ref[a * 16 : (a + 1) * 16, :] = rest_ref[a * 16 : (a + 1) * 16, :] - block
 
 
@@ -267,15 +279,13 @@
     nodes = [jnp.right_shift(16 + leaf, a + 1) for a in range(4)]
     subs = [leaf & (2 ** (a + 1) - 1) for a in range(4)]
     place = jnp.stack(nodes + subs + [leaf & 1, front & 1]).astype(jnp.int32)
-
-    rounded = rhs_leaf[0].astype(BF)
-    sent = jnp.broadcast_to(rounded[None], (FRONTS, *rounded.shape))
-    right = lax.all_to_all(sent, "front", 0, 0)
-
-    path = path_weights(place, inv_top, off_top, 3)
-    weights = lax.all_gather(path, "front", axis=0, tiled=False)
+    off_top = jnp.swapaxes(off_top, 1, 2)
+    off_leaf = jnp.swapaxes(off_leaf, 1, 2)
+
+    weights = lax.all_gather(path_weights(place, inv_top, off_top), "front", axis=0)
+    right = rhs_leaf[0].astype(BF)
+    right = lax.all_to_all(jnp.broadcast_to(right, (FRONTS, *right.shape)), "front", 0, 0)
     shares = rhs_shares(place, rhs_top)
-
     leaf_x, sent = call(
         leaf_solve_kernel,
         (jax.ShapeDtypeStruct((64, 256), F32), jax.ShapeDtypeStruct((16, 16, 1280), BF)),
@@ -294,12 +304,11 @@
     for level in range(3):
         ux, rest = top_solve(state, other, weights, level)
         ux_other = swap(ux, core_pairs())
-        rows = lax.dynamic_slice_in_dim(idx_top, nodes[level] - 2, 1, 0)
         state = call(
-            update_kernel,
+            functools.partial(update_kernel, level),
             jax.ShapeDtypeStruct(rest.shape, F32),
-            [VMEM] * 4,
-            (ux, ux_other, rest, rows),
+            [SMEM] + [VMEM] * 4,
+            (place, ux, ux_other, rest, idx_top),
         )
         other = swap(state, chip_pairs(level))
         ships.append(

time: 150 us -> 167 us (1.11)
  Pallas kernels: 17.3 us -> 36.8 us
  local copies, waits for them, and re-layouts: 16.7 us -> 8.03 us
  waiting for transfers between devices: 66.3 us -> 71.1 us
    pallas_call x5, Pallas kernels: 5.01 us -> 22.9 us  [the longest x1 13.9 us: path_weights(): pl.pallas_call(weights_kernel, out_shape=jax.ShapeDtypeStruct((192, 1024)...]
    unnamed x24 -> x28, local copies, waits for them, and re-layouts: 14.7 us -> 5.55 us
    all_gather x1, waiting for transfers between devices: 26.1 us -> 30.3 us  [local(): lax.all_gather(path_weights(place, inv_top, off_top), 'front', axis=0)]
  transfers between devices with their start and end apart: 10 -> 10, of which waited for: 10 -> 10; matrix products, arithmetic and copies ran while one was open for 2% -> 1% of each run, Pallas kernels for 5% -> 6%
where the time goes in v3:
time: 167 us; the launch traced here: 166 us
  waiting for transfers between devices  71.1 us (43%)
  Pallas kernels  36.8 us (22%)
  starting transfers between devices  20.1 us (12%)
  blocking collectives  15.9 us (10%)
  between operations  14.2 us (9%)
  local copies, waits for them, and re-layouts  8.03 us (5%)
    all_gather x1, waiting for transfers between devices, local(): lax.all_gather(path_weights(place, inv_top, off_top), 'front', axis=0)  30.3 us
    ppermute x7, waiting for transfers between devices, swap(): return lax.ppermute(block, 'leaf', pairs)  19.5 us
    all_to_all x1, blocking collectives, local(): got = lax.all_to_all(sent, 'front', 0, 0)  15.9 us
    pallas_call x10, Pallas kernels, call(): pl.pallas_call(kernel, out_shape=outs, in_specs=specs, out_specs=tuple((V...  13.9 us
    pallas_call x1, Pallas kernels, path_weights(): pl.pallas_call(weights_kernel, out_shape=jax.ShapeDtypeStruct((192, 1024)...  13.9 us
    all_to_all x1, waiting for transfers between devices, local(): got = lax.all_to_all(sent, 'front', 0, 0)  12.5 us
    all_to_all x1, waiting for transfers between devices, local(): lax.all_to_all(jnp.broadcast_to(right, (FRONTS, *right.shape)), 'front',...  8.83 us
    ppermute x7, starting transfers between devices, swap(): return lax.ppermute(block, 'leaf', pairs)  7.6 us
  transfers between devices with their start and end apart: 10, of which 10 were waited for; matrix products, arithmetic and copies ran while one was open for 1% of the time, Pallas kernels for 6%

profile of v3, /device:TPU:32, one launch (start us, length us, event | category | flops | bytes accessed | tf_op | source)
XLA Modules:
  0.0 166.1 jit_solution(160010281674470222)
XLA Ops:
  7.9 13.9 %shard_map.98 = bf16[192,1024]{1,0:T(8,128)(2,1)} custom-call(s32[10]{0:T(128)} %stack.40.place, bf16[15,64,1024]{2,1,0:T(8,128)(2,1)} %inv_ref.3, bf16[14,64,1024]{2,1,0:T(8,128)(2,1)} %bitcast.20), custom_call_target="tpu_custom_call" | custom-call | tf_op jit(solution)/shard_map/pallas_call | solution.py:76
  22.7 7.2 %all-to-all-start = ((bf16[16,64,256]{2,1,0:T(8,128)(2,1)}), bf16[16,64,256]{2,1,0:T(8,128)(2,1)S(1)}, u32[]{:S(2)}, u32[]{:S(2)}) async-start(bf16[16,64,256]{2,1,0:T(8,128)(2,1)} %broadcast_in_dim.9), calls=%async_computation | async-start | bytes 1048576 | tf_op jit(solution)/shard_map/all_to_all | solution.py:287
  29.9 2.7 %shard_map.95.shares_ref = bf16[16,16,256]{2,1,0:T(8,128)(2,1)} custom-call(s32[10]{0:T(128)} %stack.40.place, f32[15,64,256]{2,1,0:T(8,128)} %rhs_ref.1), custom_call_target="tpu_custom_call" | custom-call | tf_op jit(solution)/shard_map/pallas_call | solution.py:114
  32.6 8.8 %all-to-all-done.rhs_ref = bf16[16,64,256]{2,1,0:T(8,128)(2,1)S(1)} async-done(((bf16[16,64,256]{2,1,0:T(8,128)(2,1)}), bf16[16,64,256]{2,1,0:T(8,128)(2,1)S(1)}, u32[]{:S(2)}, u32[]{:S(2)}) %all-to-all-start) | async-done | bytes 524320 | tf_op jit(solution)/shard_map/all_to_all | solution.py:287
  41.4 0.9 copy-done.4
  42.3 1.2 shard_map.96
  43.5 15.9 %all_to_all.15.got_ref = bf16[16,16,1280]{2,1,0:T(8,128)(2,1)S(1)} all-to-all(bf16[16,16,1280]{2,1,0:T(8,128)(2,1)S(1)} %get-tuple-element.11), channel_id=1, replica_groups=mesh['leaf'=16,'front'=16] {'front'}, dimensions={0} | all-to-all | bytes 1310720 | tf_op jit(solution)/shard_map/all_to_all | solution.py:295
  59.5 3.1 %shard_map.97.own_ref = f32[64,1024]{1,0:T(8,128)S(1)} custom-call(s32[10]{0:T(128)S(1)} %copy-done.10, bf16[16,16,1280]{2,1,0:T(8,128)(2,1)S(1)} %all_to_all.15.got_ref, s32[1,1024]{1,0:T(1,128)S(1)} %copy-done.11), custom_call_target="tpu_custom_call" | custom-call | flops 100000000 | bytes 1000000 | tf_op jit(solution)/shard_map/pallas_call | solution.py:46
  62.7 1.5 collective-permute-done.other_ref
  64.2 30.3 %all-gather.3.cloned.1.call-done = bf16[3072,1024]{1,0:T(8,128)(2,1)} async-done(((bf16[192,1024]{1,0:T(8,128)(2,1)}), bf16[3072,1024]{1,0:T(8,128)(2,1)}) %all-gather.3.cloned.1.call-update) | async-done | bytes 6291472 | tf_op jit(solution)/shard_map/all_gather | solution.py:285
  94.5 3.8 %shard_map.99 = (f32[16,1536]{1,0:T(8,128)}, f32[48,1024]{1,0:T(8,128)}) custom-call(f32[64,1024]{1,0:T(8,128)} %copy-done.2, f32[64,1024]{1,0:T(8,128)} %copy-done.12, bf16[16,192,1024]{2,1,0:T(8,128)(2,1)} %bitcast.16), custom_call_target="tpu_custom_call" | custom-call | tf_op jit(solution)/shard_map/pallas_call | solution.py:204
  98.5 1.5 collective-permute-done.1.other_ref
  100.0 0.9 copy-done.5
  100.9 0.9 copy-done.8
  101.8 2.4 %shard_map.100.own_ref = f32[48,1024]{1,0:T(8,128)S(1)} custom-call(s32[10]{0:T(128)S(1)} %copy-done.10, f32[16,1536]{1,0:T(8,128)S(1)} %copy-done.8, f32[16,1536]{1,0:T(8,128)S(1)} %collective-permute-done.1.other_ref, f32[48,1024]{1,0:T(8,128)S(1)} %copy-done.5, s32[14,1024]{1,0:T(8,128)S(1)} %copy-done.3), custom_call_target="tpu_custom_call" | custom-call | flops 100000000 | bytes 1000000 | tf_op jit(solution)/shard_map/pallas_call | solution.py:46
  104.7 6.5 %collective-permute-done.2.other_ref = f32[48,1024]{1,0:T(8,128)S(1)} collective-permute-done((f32[48,1024]{1,0:T(8,128)S(1)}, f32[48,1024]{1,0:T(8,128)S(1)}, u32[]{:S(2)}, u32[]{:S(2)}) %collective-permute-start.2) | collective-permute-done | bytes 196640 | tf_op jit(solution)/shard_map/ppermute | solution.py:255
  111.2 2.8 %copy-done = bf16[3072,1024]{1,0:T(8,128)(2,1)S(1)} copy-done((bf16[3072,1024]{1,0:T(8,128)(2,1)S(1)}, bf16[3072,1024]{1,0:T(8,128)(2,1)}, u32[]{:S(2)}) %copy-start) | copy-done | bytes 6291480
  114.0 1.3 shard_map.101
  115.4 1.3 collective-permute-done.3.other_ref
  116.7 1.8 %shard_map.102.own_ref = f32[32,1024]{1,0:T(8,128)S(1)} custom-call(s32[10]{0:T(128)S(1)} %copy-done.10, f32[16,1536]{1,0:T(8,128)S(1)} %get-tuple-element.14.own_ref, f32[16,1536]{1,0:T(8,128)S(1)} %collective-permute-done.3.other_ref, f32[32,1024]{1,0:T(8,128)S(1)} %get-tuple-element.15.rest_ref, s32[14,1024]{1,0:T(8,128)S(1)} %copy-done.3), custom_call_target="tpu_custom_call" | custom-call | flops 100000000 | bytes 1000000 | tf_op jit(solution)/shard_map/pallas_call | solution.py:46
  118.5 2.6 %collective-permute-start.4 = (f32[32,1024]{1,0:T(8,128)S(1)}, f32[32,1024]{1,0:T(8,128)S(1)}, u32[]{:S(2)}, u32[]{:S(2)}) collective-permute-start(f32[32,1024]{1,0:T(8,128)S(1)} %shard_map.102.own_ref), channel_id=1, source_target_pairs={{0,64},{16,80},{32,96},{48,112},{64,0},{80,16},{96,32},{112,48},{1... | collective-permute-start | bytes 393224 | tf_op jit(solution)/shard_map/ppermute | solution.py:255
  121.1 5.8 %collective-permute-done.4.other_ref = f32[32,1024]{1,0:T(8,128)S(1)} collective-permute-done((f32[32,1024]{1,0:T(8,128)S(1)}, f32[32,1024]{1,0:T(8,128)S(1)}, u32[]{:S(2)}, u32[]{:S(2)}) %collective-permute-start.4) | collective-permute-done | bytes 131104 | tf_op jit(solution)/shard_map/ppermute | solution.py:255
  126.9 1.3 shard_map.103
  128.2 1.3 collective-permute-done.5.other_ref
  129.5 1.2 shard_map.104.own_ref
  130.7 4.2 %collective-permute-start.6 = (f32[16,1024]{1,0:T(8,128)S(1)}, f32[16,1024]{1,0:T(8,128)S(1)}, u32[]{:S(2)}, u32[]{:S(2)}) collective-permute-start(f32[16,1024]{1,0:T(8,128)S(1)} %shard_map.104.own_ref), channel_id=1, source_target_pairs={{0,192},{16,208},{32,224},{48,240},{64,128},{80,144},{96,160},{112... | collective-permute-start | bytes 196616 | tf_op jit(solution)/shard_map/ppermute | solution.py:255
  137.1 1.6 collective-permute-done.6.other_ref
  138.7 0.9 shard_map.108
  139.6 5.3 %all-to-all-start.2 = ((bf16[16,16,1408]{2,1,0:T(8,128)(2,1)}), bf16[16,16,1408]{2,1,0:T(8,128)(2,1)S(1)}, u32[]{:S(2)}, u32[]{:S(2)}) async-start(bf16[16,16,1408]{2,1,0:T(8,128)(2,1)} %shard_map.108), calls=%async_computation.2 | async-start | bytes 1441792 | tf_op jit(solution)/shard_map/all_to_all | solution.py:328
  144.9 0.9 slice.3.inv_ref
  145.8 12.5 %all-to-all-done.2.got_ref = bf16[16,16,1408]{2,1,0:T(8,128)(2,1)S(1)} async-done(((bf16[16,16,1408]{2,1,0:T(8,128)(2,1)}), bf16[16,16,1408]{2,1,0:T(8,128)(2,1)S(1)}, u32[]{:S(2)}, u32[]{:S(2)}) %all-to-all-start.2) | async-done | bytes 720928 | tf_op jit(solution)/shard_map/all_to_all | solution.py:328
  158.3 1.0 shard_map.109
  (37 shorter events, 4.8 us)
Async XLA Ops:
  7.2 87.4 %all-gather.3.cloned.1.call-start = ((), (), s32[]{:S(2)}) async-start(), calls=%async_computation.3 | async-start | bytes 6684672 | tf_op jit(solution)/shard_map/all_gather | solution.py:285
  7.9 13.9 %copy-start.13 = (f32[1,64,256]{2,1,0:T(8,128)S(1)}, f32[1,64,256]{2,1,0:T(8,128)}, u32[]{:S(2)}) copy-start(f32[1,64,256]{2,1,0:T(8,128)} %param.8) | copy-start | bytes 196612
  21.8 19.6 %copy-start.6 = (bf16[1,64,1024]{2,1,0:T(8,128)(2,1)S(1)}, bf16[1,64,1024]{2,1,0:T(8,128)(2,1)}, u32[]{:S(2)}) copy-start(bf16[1,64,1024]{2,1,0:T(8,128)(2,1)} %inv_ref.2) | copy-start | bytes 393220
  21.8 19.6 %copy-start.7 = (bf16[1,1024,64]{1,2,0:T(8,128)(2,1)S(1)}, bf16[1,1024,64]{1,2,0:T(8,128)(2,1)}, u32[]{:S(2)}) copy-start(bf16[1,1024,64]{1,2,0:T(8,128)(2,1)} %param.12) | copy-start | bytes 393220
  22.7 36.7 %copy-start.10 = (s32[10]{0:T(128)S(1)}, s32[10]{0:T(128)}, u32[]{:S(2)}) copy-start(s32[10]{0:T(128)} %stack.40.place) | copy-start | bytes 124
  22.7 36.7 %copy-start.11 = (s32[1,1024]{1,0:T(1,128)S(1)}, s32[1,1024]{1,0:T(1,128)}, u32[]{:S(2)}) copy-start(s32[1,1024]{1,0:T(1,128)} %idx_ref.4) | copy-start | bytes 12292
  22.7 18.7 %all-to-all-start = ((bf16[16,64,256]{2,1,0:T(8,128)(2,1)}), bf16[16,64,256]{2,1,0:T(8,128)(2,1)S(1)}, u32[]{:S(2)}, u32[]{:S(2)}) async-start(bf16[16,64,256]{2,1,0:T(8,128)(2,1)} %broadcast_in_dim.9), calls=%async_computation | async-start | bytes 1048576 | tf_op jit(solution)/shard_map/all_to_all | solution.py:287
  41.4 0.9 copy-start.4
  62.6 32.0 %copy-start.2 = (f32[64,1024]{1,0:T(8,128)}, f32[64,1024]{1,0:T(8,128)S(1)}, u32[]{:S(2)}) copy-start(f32[64,1024]{1,0:T(8,128)S(1)} %shard_map.97.own_ref) | copy-start | bytes 786436
  62.6 1.6 collective-permute-start
  64.2 30.3 %copy-start.12 = (f32[64,1024]{1,0:T(8,128)}, f32[64,1024]{1,0:T(8,128)S(1)}, u32[]{:S(2)}) copy-start(f32[64,1024]{1,0:T(8,128)S(1)} %collective-permute-done.other_ref) | copy-start | bytes 786436
  94.5 5.4 %copy-start.3 = (s32[14,1024]{1,0:T(8,128)S(1)}, s32[14,1024]{1,0:T(8,128)}, u32[]{:S(2)}) copy-start(s32[14,1024]{1,0:T(8,128)} %idx_ref.7) | copy-start | bytes 172036
  98.4 1.6 collective-permute-start.1
  100.0 0.9 copy-start.5
  100.9 0.9 copy-start.8
  104.2 7.0 %collective-permute-start.2 = (f32[48,1024]{1,0:T(8,128)S(1)}, f32[48,1024]{1,0:T(8,128)S(1)}, u32[]{:S(2)}, u32[]{:S(2)}) collective-permute-start(f32[48,1024]{1,0:T(8,128)S(1)} %shard_map.100.own_ref), channel_id=1, source_target_pairs={{0,32},{16,48},{32,0},{48,16},{64,96},{80,112},{96,64},{112,80},{1... | collective-permute-start | bytes 589832 | tf_op jit(solution)/shard_map/ppermute | solution.py:255
  111.2 2.8 %copy-start = (bf16[3072,1024]{1,0:T(8,128)(2,1)S(1)}, bf16[3072,1024]{1,0:T(8,128)(2,1)}, u32[]{:S(2)}) copy-start(bf16[3072,1024]{1,0:T(8,128)(2,1)} %all-gather.3.cloned.1.call-done) | copy-start | bytes 18874372
  114.0 12.9 %copy-start.1 = (bf16[3072,1024]{1,0:T(8,128)(2,1)S(1)}, bf16[3072,1024]{1,0:T(8,128)(2,1)}, u32[]{:S(2)}) copy-start(bf16[3072,1024]{1,0:T(8,128)(2,1)} %all-gather.3.cloned.1.call-done) | copy-start | bytes 18874372
  115.3 1.4 collective-permute-start.3
  118.5 16.4 %copy-start.9 = (f32[16,1536]{1,0:T(8,128)S(1)}, f32[16,1536]{1,0:T(8,128)}, u32[]{:S(2)}) copy-start(f32[16,1536]{1,0:T(8,128)} %get-tuple-element.12.own_ref) | copy-start | bytes 294916
  118.5 8.4 %collective-permute-start.4 = (f32[32,1024]{1,0:T(8,128)S(1)}, f32[32,1024]{1,0:T(8,128)S(1)}, u32[]{:S(2)}, u32[]{:S(2)}) collective-permute-start(f32[32,1024]{1,0:T(8,128)S(1)} %shard_map.102.own_ref), channel_id=1, source_target_pairs={{0,64},{16,80},{32,96},{48,112},{64,0},{80,16},{96,32},{112,48},{1... | collective-permute-start | bytes 393224 | tf_op jit(solution)/shard_map/ppermute | solution.py:255
  128.1 1.4 collective-permute-start.5
  130.7 8.0 %collective-permute-start.6 = (f32[16,1024]{1,0:T(8,128)S(1)}, f32[16,1024]{1,0:T(8,128)S(1)}, u32[]{:S(2)}, u32[]{:S(2)}) collective-permute-start(f32[16,1024]{1,0:T(8,128)S(1)} %shard_map.104.own_ref), channel_id=1, source_target_pairs={{0,192},{16,208},{32,224},{48,240},{64,128},{80,144},{96,160},{112... | collective-permute-start | bytes 196616 | tf_op jit(solution)/shard_map/ppermute | solution.py:255
  139.6 18.7 %all-to-all-start.2 = ((bf16[16,16,1408]{2,1,0:T(8,128)(2,1)}), bf16[16,16,1408]{2,1,0:T(8,128)(2,1)S(1)}, u32[]{:S(2)}, u32[]{:S(2)}) async-start(bf16[16,16,1408]{2,1,0:T(8,128)(2,1)} %shard_map.108), calls=%async_computation.2 | async-start | bytes 1441792 | tf_op jit(solution)/shard_map/all_to_all | solution.py:328
Sparse Core Ops, SparseCore 0:
  21.9 72.5 all-gather.2

commit v4 on v3

--- a/solution.py
+++ b/solution.py
@@ -55,40 +55,15 @@
     )(*args)
 
 
-def weights_kernel(place, inv_ref, off_ref, out_ref, sems):
-    at = pl.ds(pl.multiple_of(place[8] * 32, 32), 32)
-    copies = []
-    for level in range(3):
-        node, to = place[level], level * 64
-        for ref, index, to in ((inv_ref, node - 1, to), (off_ref, node - 2, to + 32)):
-            copies.append(
-                pltpu.make_async_copy(
-                    ref.at[index, at, :], out_ref.at[pl.ds(to, 32), :], sems.at[len(copies)]
-                )
-            )
-    for copy in copies:
-        copy.start()
-    for copy in copies:
-        copy.wait()
-
-
-def path_weights(place, inv_top, off_top):
-    return pl.pallas_call(
-        weights_kernel,
-        out_shape=jax.ShapeDtypeStruct((192, 1024), BF),
-        in_specs=[SMEM, HBM, HBM],
-        out_specs=HBM,
-        scratch_shapes=[pltpu.SemaphoreType.DMA((6,))],
-        compiler_params=params(60),
-    )(place, inv_top, off_top)
-
-
-def shares_kernel(place, rhs_ref, out_ref, held, sems):
+def first_kernel(place, leaf_ref, rhs_ref, out_ref, held, sems):
     copies = [
         pltpu.make_async_copy(rhs_ref.at[place[a] - 1], held.at[a], sems.at[a]) for a in range(4)
     ]
     for copy in copies:
         copy.start()
+    right = leaf_ref[0].astype(BF)
+    for f in range(FRONTS):
+        out_ref[f, :64, :] = right
     for copy in copies:
         copy.wait()
     total = jnp.zeros((256, 256), F32)
@@ -107,28 +82,79 @@
         low = low.astype(F32)
         stacked = jnp.concatenate([high * even, high * odd, low * even, low * odd], axis=0)
         total = total + nt(jnp.where(chosen, 1.0, 0.0).astype(BF), stacked.astype(BF))
-    out_ref[...] = total.astype(BF).reshape(16, 16, 256)
-
-
-def rhs_shares(place, rhs_top):
+    out_ref[:, 64:, :] = total.astype(BF).reshape(16, 16, 256)
+
+
+def first_payload(place, rhs_leaf, rhs_top):
     return pl.pallas_call(
-        shares_kernel,
-        out_shape=jax.ShapeDtypeStruct((16, 16, 256), BF),
-        in_specs=[SMEM, HBM],
+        first_kernel,
+        out_shape=jax.ShapeDtypeStruct((FRONTS, 80, 256), BF),
+        in_specs=[SMEM, VMEM, HBM],
         out_specs=VMEM,
         scratch_shapes=[pltpu.VMEM((4, 64, 256), F32), pltpu.SemaphoreType.DMA((4,))],
         compiler_params=params(60),
-    )(place, rhs_top)
-
-
-def leaf_solve_kernel(inv_ref, rhs_ref, off_ref, shares_ref, x_ref, out_ref):
-    right = rhs_ref[...].reshape(1024, 256)
+    )(place, rhs_leaf, rhs_top)
+
+
+def weights_kernel(place, inv_ref, off_ref, *refs):
+    outs, sems = refs[:3], refs[3]
+    at = pl.ds(pl.multiple_of(place[8] * 32, 32), 32)
+    copies = []
+    for level, out_ref in enumerate(outs):
+        node = place[level]
+        for part, (ref, index) in enumerate(((inv_ref, node - 1), (off_ref, node - 2))):
+            copies.append(
+                pltpu.make_async_copy(
+                    ref.at[index, at, :],
+                    out_ref.at[pl.ds(part * 32, 32), :],
+                    sems.at[len(copies)],
+                )
+            )
+    for copy in copies:
+        copy.start()
+    for copy in copies:
+        copy.wait()
+
+
+def path_weights(place, inv_top, off_top):
+    piece = jax.ShapeDtypeStruct((64, 1024), BF)
+    return pl.pallas_call(
+        weights_kernel,
+        out_shape=(piece,) * 3,
+        in_specs=[SMEM, HBM, HBM],
+        out_specs=(VMEM,) * 3,
+        scratch_shapes=[pltpu.SemaphoreType.DMA((6,))],
+        compiler_params=params(60),
+    )(place, inv_top, off_top)
+
+
+def turn(block, dx, dy):
+    route = [(i, (i // 4 + dx) % 4 * 4 + (i % 4 + dy) % 4) for i in range(FRONTS)]
+    return lax.ppermute(block, "front", route)
+
+
+def ring(block, axis):
+    half = block.shape[0] // 2
+    step = (1, 0) if axis == "x" else (0, 1)
+    back = tuple(-d for d in step)
+    before = turn(block, *step)
+    after = turn(block, *back)
+    return block, before, after, turn(after[:half], *back), turn(before[half:], *step)
+
+
+def spread(block, first, second):
+    return ring(jnp.concatenate(ring(block, first), axis=0), second)
+
+
+def leaf_solve_kernel(inv_ref, rhs_ref, off_ref, weights_ref, x_ref, out_ref):
+    right = rhs_ref[:, :64, :].reshape(1024, 256)
     x = nn(inv_ref[0], right)
     x_ref[...] = x
     xt = x.T.astype(BF)
     update = nn(xt, off_ref[0])
-    out_ref[:, :, :1024] = update.astype(BF).reshape(16, 16, 1024)
-    out_ref[:, :, 1024:] = shares_ref[...]
+    out_ref[:, :16, :] = update.astype(BF).reshape(16, 16, 1024)
+    for f in range(FRONTS):
+        out_ref[f, 16:, :] = weights_ref[...]
 
 
 def push(update, idx, count):
@@ -146,14 +172,14 @@
     return blocks
 
 
-def leaf_update_kernel(place, got_ref, idx_ref, out_ref):
+def leaf_update_kernel(place, first_ref, got_ref, idx_ref, out_ref):
     update = jnp.zeros((16, 1024), F32)
     for s in range(FRONTS):
-        update = update + got_ref[s, :, :1024].astype(F32)
+        update = update + got_ref[s, :16, :].astype(F32)
     pending = push(update, idx_ref[...], 4)
     high, low = [], []
     for g in range(FRONTS // 2):
-        pair = got_ref[2 * g, :, 1024:].astype(F32) + got_ref[2 * g + 1, :, 1024:].astype(F32)
+        pair = first_ref[2 * g, 64:, :].astype(F32) + first_ref[2 * g + 1, 64:, :].astype(F32)
         high.append(pair[:, :128])
         low.append(pair[:, 128:])
     high = jnp.concatenate(high, axis=1).astype(BF)
@@ -168,47 +194,32 @@
         out_ref[a * 16 : (a + 1) * 16, :] = nn(put, high) + nn(put, low) - pending[a]
 
 
-def solve_kernel(level, own_ref, other_ref, weights_ref, ux_ref, rest_ref, held, sems):
-    copies = []
-    for part in range(2):
-        for half in range(2):
-            fronts = pl.ds(half * 8, 8)
-            rows = pl.ds(level * 64 + part * 32, 32)
-            copies.append(
-                pltpu.make_async_copy(
-                    weights_ref.at[fronts, rows, :],
-                    held.at[part, fronts],
-                    sems.at[len(copies)],
-                )
-            )
-    for copy in copies:
-        copy.start()
+def solve_kernel(start, own_ref, other_ref, *refs):
+    weights, ux_ref, rest_ref = refs[:-2], refs[-2], refs[-1]
     total = own_ref[...] + other_ref[...]
     rest_ref[...] = total[16:]
     right = total[:16].astype(BF)
     update = jnp.zeros((16, 1024), F32)
-    xs = []
-    for half in range(2):
-        copies[half].wait()
-        xs.append(nt(right, held[0, half * 8 : half * 8 + 8].reshape(256, 1024)))
-    for half in range(2):
-        copies[2 + half].wait()
-        off = held[1, half * 8 : half * 8 + 8].reshape(256, 1024)
-        update = update + nn(xs[half].astype(BF), off)
-        ux_ref[:, 1024 + half * 256 : 1280 + half * 256] = xs[half]
+    at = 1024
+    for ref in weights:
+        blocks = ref.shape[0]
+        rows = blocks * 32
+        x = nt(right, ref[:, start : start + 32, :].reshape(rows, 1024))
+        off = ref[:, start + 32 : start + 64, :].reshape(rows, 1024)
+        update = update + nn(x.astype(BF), off)
+        ux_ref[:, at : at + rows] = x
+        at += rows
     ux_ref[:, :1024] = update
 
 
-def top_solve(own, other, weights, level):
+def top_solve(own, other, weights, start):
     left = own.shape[0] - 16
-    return pl.pallas_call(
-        functools.partial(solve_kernel, level),
-        in_specs=[VMEM, VMEM, HBM],
-        out_specs=(VMEM, VMEM),
-        out_shape=(jax.ShapeDtypeStruct((16, 1536), F32), jax.ShapeDtypeStruct((left, 1024), F32)),
-        scratch_shapes=[pltpu.VMEM((2, 16, 32, 1024), BF), pltpu.SemaphoreType.DMA((4,))],
-        compiler_params=params(60 if level == 0 else 16),
-    )(own, other, weights)
+    return call(
+        functools.partial(solve_kernel, start),
+        (jax.ShapeDtypeStruct((16, 1536), F32), jax.ShapeDtypeStruct((left, 1024), F32)),
+        [VMEM] * (2 + len(weights)),
+        (own, other, *weights),
+    )
 
 
 def update_kernel(level, place, own_ref, other_ref, rest_ref, idx_ref, out_ref):
@@ -219,18 +230,25 @@
         out_ref[a * 16 : (a + 1) * 16, :] = rest_ref[a * 16 : (a + 1) * 16, :] - block
 
 
-def ship_kernel(place, own_ref, other_ref, out_ref):
+def ship_kernel(order, place, own_ref, other_ref, out_ref):
     first = place[8] == 0
     own = own_ref[:, 1024:]
     other = other_ref[:, 1024:]
     low_core = jnp.where(first, own, other)
     high_core = jnp.where(first, other, own)
-    for f in range(FRONTS):
-        at = slice(f * 32, (f + 1) * 32)
+    for k in range(FRONTS):
+        outer, inner = (0, 3, 1, 2)[k // 4], (0, 3, 1, 2)[k % 4]
+        if order == "yx":
+            to = (place[10] + outer) % 4 * 4 + (place[11] + inner) % 4
+        elif order == "xy":
+            to = (place[10] + inner) % 4 * 4 + (place[11] + outer) % 4
+        else:
+            to = k
+        at = slice(k * 32, (k + 1) * 32)
         value = jnp.concatenate([low_core[:, at], high_core[:, at]], axis=1)
         high = value.astype(BF).astype(F32)
         low = value - high
-        out_ref[f] = jnp.concatenate([high, low], axis=1).astype(BF)
+        out_ref[to] = jnp.concatenate([high, low], axis=1).astype(BF)
 
 
 def root_right_kernel(own_ref, other_ref, s3_ref, s2_ref, s1_ref, out_ref):
@@ -278,31 +296,34 @@
     front = lax.axis_index("front")
     nodes = [jnp.right_shift(16 + leaf, a + 1) for a in range(4)]
     subs = [leaf & (2 ** (a + 1) - 1) for a in range(4)]
-    place = jnp.stack(nodes + subs + [leaf & 1, front & 1]).astype(jnp.int32)
+    place = nodes + subs + [leaf & 1, front & 1, front // 4, front % 4]
+    place = jnp.stack(place).astype(jnp.int32)
     off_top = jnp.swapaxes(off_top, 1, 2)
     off_leaf = jnp.swapaxes(off_leaf, 1, 2)
 
-    weights = lax.all_gather(path_weights(place, inv_top, off_top), "front", axis=0)
-    right = rhs_leaf[0].astype(BF)
-    right = lax.all_to_all(jnp.broadcast_to(right, (FRONTS, *right.shape)), "front", 0, 0)
-    shares = rhs_shares(place, rhs_top)
+    first = lax.all_to_all(first_payload(place, rhs_leaf, rhs_top), "front", 0, 0)
+    third, second, lowest = path_weights(place, inv_top, off_top)
     leaf_x, sent = call(
         leaf_solve_kernel,
-        (jax.ShapeDtypeStruct((64, 256), F32), jax.ShapeDtypeStruct((16, 16, 1280), BF)),
+        (jax.ShapeDtypeStruct((64, 256), F32), jax.ShapeDtypeStruct((FRONTS, 80, 1024), BF)),
         [VMEM] * 4,
-        (inv_leaf, right, off_leaf, shares),
+        (inv_leaf, first, off_leaf, third),
     )
     got = lax.all_to_all(sent, "front", 0, 0)
+    weights = [(got,)]
+    for block, axes in ((second, "yx"), (lowest, "xy")):
+        parts = spread(block, *axes)
+        weights.append([part.reshape(-1, 64, 1024) for part in parts])
     state = call(
         leaf_update_kernel,
         jax.ShapeDtypeStruct((64, 1024), F32),
-        [SMEM, VMEM, VMEM],
-        (place, got, idx_leaf),
+        [SMEM] + [VMEM] * 3,
+        (place, first, got, idx_leaf),
     )
     other = swap(state, core_pairs())
     ships = []
     for level in range(3):
-        ux, rest = top_solve(state, other, weights, level)
+        ux, rest = top_solve(state, other, weights[level], 0 if level else 16)
         ux_other = swap(ux, core_pairs())
         state = call(
             functools.partial(update_kernel, level),
@@ -313,7 +334,7 @@
         other = swap(state, chip_pairs(level))
         ships.append(
             call(
-                ship_kernel,
+                functools.partial(ship_kernel, (None, "yx", "xy")[level]),
                 jax.ShapeDtypeStruct((16, 16, 128), BF),
                 [SMEM, VMEM, VMEM],
                 (place, ux, ux_other),

time: 167 us -> 151 us (0.904)
  starting transfers between devices: 20.1 us -> 52.3 us
  blocking collectives: 15.9 us -> 0 us
  between operations: 14.2 us -> 0.9 us
  Pallas kernels: 36.8 us -> 24.3 us
  waiting for transfers between devices: 71.1 us -> 61.1 us
  local copies, waits for them, and re-layouts: 8.03 us -> 11.8 us
    all_gather x1 -> x0, waiting for transfers between devices: 30.3 us -> none  [local(): lax.all_gather(path_weights(place, inv_top, off_top), 'front', axis=0)]
    ppermute x0 -> x16, waiting for transfers between devices: none -> 29.5 us  [turn(): return lax.ppermute(block, 'front', route)]
    ppermute x0 -> x16, starting transfers between devices: none -> 23.8 us  [turn(): return lax.ppermute(block, 'front', route)]
    pallas_call x5 -> x2, Pallas kernels: 22.9 us -> 5.48 us  [the longest x1 3.03 us: first_payload(): pl.pallas_call(first_kernel, out_shape=jax.ShapeDtypeStruct((FRONTS, 80,...]
    all_to_all x1 -> x0, blocking collectives: 15.9 us -> none  [local(): got = lax.all_to_all(sent, 'front', 0, 0)]
    ppermute x7, waiting for transfers between devices: 19.5 us -> 8.45 us  [swap(): return lax.ppermute(block, 'leaf', pairs)]
    all_to_all x1 -> x2, starting transfers between devices: 5.25 us -> 11.5 us  [local(): got = lax.all_to_all(sent, 'front', 0, 0)]
    pallas_call x10 -> x13, Pallas kernels: 13.9 us -> 18.8 us  [call(): pl.pallas_call(kernel, out_shape=outs, in_specs=specs, out_specs=tuple((V...]
  transfers between devices with their start and end apart: 10 -> 26, of which waited for: 10 -> 10; matrix products, arithmetic and copies ran while one was open for 1% -> 6% of each run, Pallas kernels for 6% -> 10%
where the time goes in v4:
time: 151 us; the launch traced here: 150 us
  waiting for transfers between devices  61.1 us (40%)
  starting transfers between devices  52.3 us (35%)
  Pallas kernels  24.3 us (16%)
  local copies, waits for them, and re-layouts  11.8 us (8%)
    ppermute x16, waiting for transfers between devices, turn(): return lax.ppermute(block, 'front', route)  29.5 us
    ppermute x16, starting transfers between devices, turn(): return lax.ppermute(block, 'front', route)  23.8 us
    pallas_call x13, Pallas kernels, call(): pl.pallas_call(kernel, out_shape=outs, in_specs=specs, out_specs=tuple((V...  18.8 us
    all_to_all x2, waiting for transfers between devices, local(): got = lax.all_to_all(sent, 'front', 0, 0)  12.6 us
    all_to_all x2, starting transfers between devices, local(): got = lax.all_to_all(sent, 'front', 0, 0)  11.5 us
    all_to_all x1, waiting for transfers between devices, local(): lax.all_to_all(first_payload(place, rhs_leaf, rhs_top), 'front', 0, 0)  10.4 us
    ppermute x7, starting transfers between devices, swap(): return lax.ppermute(block, 'leaf', pairs)  9.77 us
    ppermute x7, waiting for transfers between devices, swap(): return lax.ppermute(block, 'leaf', pairs)  8.45 us
  transfers between devices with their start and end apart: 26, of which 10 were waited for; matrix products, arithmetic and copies ran while one was open for 6% of the time, Pallas kernels for 10%

profile of v4, /device:TPU:32, one launch (start us, length us, event | category | flops | bytes accessed | tf_op | source)
XLA Modules:
  0.0 150.4 jit_solution(2029439764686947593)
XLA Ops:
  1.3 3.0 %shard_map.95 = bf16[16,80,256]{2,1,0:T(8,128)(2,1)} custom-call(s32[12]{0:T(128)} %stack.48.place, f32[1,64,256]{2,1,0:T(8,128)} %leaf_ref.1, f32[15,64,256]{2,1,0:T(8,128)} %rhs_ref.1), custom_call_target="tpu_custom_call" | custom-call | tf_op jit(solution)/shard_map/pallas_call | solution.py:89
  4.4 7.2 %all-to-all-start = ((bf16[16,80,256]{2,1,0:T(8,128)(2,1)}), bf16[16,80,256]{2,1,0:T(8,128)(2,1)S(1)}, u32[]{:S(2)}, u32[]{:S(2)}) async-start(bf16[16,80,256]{2,1,0:T(8,128)(2,1)} %shard_map.95), calls=%async_computation | async-start | bytes 1310720 | tf_op jit(solution)/shard_map/all_to_all | solution.py:304
  11.6 2.5 %shard_map.96 = (bf16[64,1024]{1,0:T(8,128)(2,1)}, bf16[64,1024]{1,0:T(8,128)(2,1)}, bf16[64,1024]{1,0:T(8,128)(2,1)}) custom-call(s32[12]{0:T(128)} %stack.48.place, bf16[15,64,1024]{2,1,0:T(8,128)(2,1)} %inv_ref.2, bf16[14,64,1024]{2,1,0:T(8,128)(2,1)} %bitcast.32), custom_call_target="tpu_custom_call" | custom-call | tf_op jit(solution)/shard_map/pallas_call | solution.py:121
  14.0 10.4 %all-to-all-done.rhs_ref.first_ref = bf16[16,80,256]{2,1,0:T(8,128)(2,1)S(1)} async-done(((bf16[16,80,256]{2,1,0:T(8,128)(2,1)}), bf16[16,80,256]{2,1,0:T(8,128)(2,1)S(1)}, u32[]{:S(2)}, u32[]{:S(2)}) %all-to-all-start) | async-done | bytes 655392 | tf_op jit(solution)/shard_map/all_to_all | solution.py:304
  26.3 1.5 copy-done
  27.8 3.9 %all-to-all-start.1 = ((bf16[16,80,1024]{2,1,0:T(8,128)(2,1)}), bf16[16,80,1024]{2,1,0:T(8,128)(2,1)S(1)}, u32[]{:S(2)}, u32[]{:S(2)}) async-start(bf16[16,80,1024]{2,1,0:T(8,128)(2,1)} %copy-done), calls=%async_computation.1 | async-start | bytes 5242880 | tf_op jit(solution)/shard_map/all_to_all | solution.py:312
  31.7 3.1 %collective-permute-start.4 = (bf16[64,1024]{1,0:T(8,128)(2,1)S(1)}, bf16[64,1024]{1,0:T(8,128)(2,1)S(1)}, u32[]{:S(2)}, u32[]{:S(2)}) collective-permute-start(bf16[64,1024]{1,0:T(8,128)(2,1)S(1)} %copy-done.8), channel_id=1, source_target_pairs={{0,3},{1,0},{2,1},{3,2},{4,7},{5,4},{6,5},{7,6},{8,11},{9,8},{10,9... | collective-permute-start | bytes 393224 | tf_op jit(solution)/shard_map/ppermute | solution.py:133
  34.8 2.8 %collective-permute-start.14 = (bf16[64,1024]{1,0:T(8,128)(2,1)S(1)}, bf16[64,1024]{1,0:T(8,128)(2,1)S(1)}, u32[]{:S(2)}, u32[]{:S(2)}) collective-permute-start(bf16[64,1024]{1,0:T(8,128)(2,1)S(1)} %copy-done.7), channel_id=1, source_target_pairs={{0,12},{1,13},{2,14},{3,15},{4,0},{5,1},{6,2},{7,3},{8,4},{9,5},{1... | collective-permute-start | bytes 393224 | tf_op jit(solution)/shard_map/ppermute | solution.py:133
  38.2 26.6 %collective-permute-done.4 = bf16[64,1024]{1,0:T(8,128)(2,1)S(1)} collective-permute-done((bf16[64,1024]{1,0:T(8,128)(2,1)S(1)}, bf16[64,1024]{1,0:T(8,128)(2,1)S(1)}, u32[]{:S(2)}, u32[]{:S(2)}) %collective-permute-start.4) | collective-permute-done | bytes 131104 | tf_op jit(solution)/shard_map/ppermute | solution.py:133
  64.8 2.1 %collective-permute-start.6 = (bf16[32,1024]{1,0:T(8,128)(2,1)S(1)}, bf16[32,1024]{1,0:T(8,128)(2,1)S(1)}, u32[]{:S(2)}, u32[]{:S(2)}) collective-permute-start(bf16[32,1024]{1,0:T(8,128)(2,1)S(1)} %slice.37), channel_id=1, source_target_pairs={{0,1},{1,2},{2,3},{3,0},{4,5},{5,6},{6,7},{7,4},{8,9},{9,10},{10,1... | collective-permute-start | bytes 196616 | tf_op jit(solution)/shard_map/ppermute | solution.py:133
  66.9 1.7 %collective-permute-start.15 = (bf16[32,1024]{1,0:T(8,128)(2,1)S(1)}, bf16[32,1024]{1,0:T(8,128)(2,1)S(1)}, u32[]{:S(2)}, u32[]{:S(2)}) collective-permute-start(bf16[32,1024]{1,0:T(8,128)(2,1)S(1)} %slice.40), channel_id=1, source_target_pairs={{0,12},{1,13},{2,14},{3,15},{4,0},{5,1},{6,2},{7,3},{8,4},{9,5},{1... | collective-permute-start | bytes 196616 | tf_op jit(solution)/shard_map/ppermute | solution.py:133
  72.4 1.8 %collective-permute-start.7 = (bf16[256,1024]{1,0:T(8,128)(2,1)}, bf16[256,1024]{1,0:T(8,128)(2,1)}, u32[]{:S(2)}, u32[]{:S(2)}) collective-permute-start(bf16[256,1024]{1,0:T(8,128)(2,1)} %constant_dynamic-update-slice_fusion), channel_id=1, source_target_pairs={{0,4},{1,5},{2,6},{3,7},{4,8},{5,9},{6,10},{7,11},{8,12},{9,13},{1... | collective-permute-start | bytes 1572872 | tf_op jit(solution)/shard_map/ppermute | solution.py:133
  74.2 1.4 collective-permute-start.8
  76.9 3.1 %shard_map.98.own_ref = f32[64,1024]{1,0:T(8,128)S(1)} custom-call(s32[12]{0:T(128)S(1)} %copy-done.5, bf16[16,80,256]{2,1,0:T(8,128)(2,1)S(1)} %all-to-all-done.rhs_ref.first_ref, bf16[16,80,1024]{2,1,0:T(8,128)(2,1)S(1)} %all-to-all-done.1.got_ref.refs_0_, s32[1,1024]{1,0:T(1,128)S(1)} %copy-done.6), custom_call_target="tpu_custom_call" | custom-call | flops 100000000 | bytes 1000000 | tf_op jit(solution)/shard_map/pallas_call | solution.py:46
  80.8 2.8 %collective-permute-start.18 = (bf16[256,1024]{1,0:T(8,128)(2,1)}, bf16[256,1024]{1,0:T(8,128)(2,1)S(1)}, u32[]{:S(2)}, u32[]{:S(2)}) collective-permute-start(bf16[256,1024]{1,0:T(8,128)(2,1)} %constant_dynamic-update-slice_fusion.5), channel_id=1, source_target_pairs={{0,3},{1,0},{2,1},{3,2},{4,7},{5,4},{6,5},{7,6},{8,11},{9,8},{10,9... | collective-permute-start | bytes 1572872 | tf_op jit(solution)/shard_map/ppermute | solution.py:133
  84.4 1.3 collective-permute-done.8
  86.7 3.8 %collective-permute-start.9 = (bf16[128,1024]{1,0:T(8,128)(2,1)S(1)}, bf16[128,1024]{1,0:T(8,128)(2,1)S(1)}, u32[]{:S(2)}, u32[]{:S(2)}) collective-permute-start(bf16[128,1024]{1,0:T(8,128)(2,1)S(1)} %slice.38), channel_id=1, source_target_pairs={{0,12},{1,13},{2,14},{3,15},{4,0},{5,1},{6,2},{7,3},{8,4},{9,5},{1... | collective-permute-start | bytes 786440 | tf_op jit(solution)/shard_map/ppermute | solution.py:133
  91.6 2.4 %shard_map.100.own_ref = f32[48,1024]{1,0:T(8,128)S(1)} custom-call(s32[12]{0:T(128)S(1)} %copy-done.5, f32[16,1536]{1,0:T(8,128)S(1)} %get-tuple-element.16.own_ref, f32[16,1536]{1,0:T(8,128)S(1)} %collective-permute-done.1.other_ref, f32[48,1024]{1,0:T(8,128)S(1)} %get-tuple-element.17.rest_ref, s32[14,1024]{1,0:T(8,128)S(1)} %copy-done.1), custom_call_target="tpu_custom_call" | custom-call | flops 100000000 | bytes 1000000 | tf_op jit(solution)/shard_map/pallas_call | solution.py:46
  94.1 1.6 %collective-permute-done.18 = bf16[256,1024]{1,0:T(8,128)(2,1)S(1)} collective-permute-done((bf16[256,1024]{1,0:T(8,128)(2,1)}, bf16[256,1024]{1,0:T(8,128)(2,1)S(1)}, u32[]{:S(2)}, u32[]{:S(2)}) %collective-permute-start.18) | collective-permute-done | bytes 524320 | tf_op jit(solution)/shard_map/ppermute | solution.py:133
  95.8 3.7 %collective-permute-start.19 = (bf16[128,1024]{1,0:T(8,128)(2,1)S(1)}, bf16[128,1024]{1,0:T(8,128)(2,1)S(1)}, u32[]{:S(2)}, u32[]{:S(2)}) collective-permute-start(bf16[128,1024]{1,0:T(8,128)(2,1)S(1)} %slice.42), channel_id=1, source_target_pairs={{0,3},{1,0},{2,1},{3,2},{4,7},{5,4},{6,5},{7,6},{8,11},{9,8},{10,9... | collective-permute-start | bytes 786440 | tf_op jit(solution)/shard_map/ppermute | solution.py:133
  99.7 2.4 %shard_map.101 = (f32[16,1536]{1,0:T(8,128)S(1)}, f32[32,1024]{1,0:T(8,128)S(1)}) custom-call(f32[48,1024]{1,0:T(8,128)S(1)} %shard_map.100.own_ref, f32[48,1024]{1,0:T(8,128)S(1)} %collective-permute-done.2.other_ref, bf16[4,64,1024]{2,1,0:T(8,128)(2,1)} %bitcast.14.refs_0_, bf16[4,64,1024]{2,1,0:T(8,128)(2,1)} %bitcast.15.refs_1_, ...), custom_call_target="tpu_custom_call" | custom-call | flops 100000000 | bytes 1000000 | tf_op jit(solution)/shard_map/pallas_call | solution.py:46
  102.2 1.3 collective-permute-done.11.other_ref
  103.5 1.8 %shard_map.102.own_ref = f32[32,1024]{1,0:T(8,128)S(1)} custom-call(s32[12]{0:T(128)S(1)} %copy-done.5, f32[16,1536]{1,0:T(8,128)S(1)} %get-tuple-element.19.own_ref, f32[16,1536]{1,0:T(8,128)S(1)} %collective-permute-done.11.other_ref, f32[32,1024]{1,0:T(8,128)S(1)} %get-tuple-element.20.rest_ref, s32[14,1024]{1,0:T(8,128)S(1)} %copy-done.1), custom_call_target="tpu_custom_call" | custom-call | flops 100000000 | bytes 1000000 | tf_op jit(solution)/shard_map/pallas_call | solution.py:46
  105.3 3.3 %collective-permute-start.12 = (f32[32,1024]{1,0:T(8,128)S(1)}, f32[32,1024]{1,0:T(8,128)S(1)}, u32[]{:S(2)}, u32[]{:S(2)}) collective-permute-start(f32[32,1024]{1,0:T(8,128)S(1)} %shard_map.102.own_ref), channel_id=1, source_target_pairs={{0,64},{16,80},{32,96},{48,112},{64,0},{80,16},{96,32},{112,48},{1... | collective-permute-start | bytes 393224 | tf_op jit(solution)/shard_map/ppermute | solution.py:273
  108.6 5.4 %collective-permute-done.12.other_ref = f32[32,1024]{1,0:T(8,128)S(1)} collective-permute-done((f32[32,1024]{1,0:T(8,128)S(1)}, f32[32,1024]{1,0:T(8,128)S(1)}, u32[]{:S(2)}, u32[]{:S(2)}) %collective-permute-start.12) | collective-permute-done | bytes 131104 | tf_op jit(solution)/shard_map/ppermute | solution.py:273
  114.0 2.1 %shard_map.103 = (f32[16,1536]{1,0:T(8,128)S(1)}, f32[16,1024]{1,0:T(8,128)S(1)}) custom-call(f32[32,1024]{1,0:T(8,128)S(1)} %shard_map.102.own_ref, f32[32,1024]{1,0:T(8,128)S(1)} %collective-permute-done.12.other_ref, bf16[4,64,1024]{2,1,0:T(8,128)(2,1)} %bitcast.19.refs_0_, bf16[4,64,1024]{2,1,0:T(8,128)(2,1)S(1)} %bitcast.26, ...), custom_call_target="tpu_custom_call" | custom-call | flops 100000000 | bytes 1000000 | tf_op jit(solution)/shard_map/pallas_call | solution.py:46
  116.2 1.3 collective-permute-done.21.other_ref
  117.5 1.2 shard_map.104.own_ref
  118.7 6.0 %collective-permute-start.22 = (f32[16,1024]{1,0:T(8,128)S(1)}, f32[16,1024]{1,0:T(8,128)S(1)}, u32[]{:S(2)}, u32[]{:S(2)}) collective-permute-start(f32[16,1024]{1,0:T(8,128)S(1)} %shard_map.104.own_ref), channel_id=1, source_target_pairs={{0,192},{16,208},{32,224},{48,240},{64,128},{80,144},{96,160},{112... | collective-permute-start | bytes 196616 | tf_op jit(solution)/shard_map/ppermute | solution.py:273
  128.2 7.7 %all-to-all-start.2 = ((bf16[16,16,1408]{2,1,0:T(8,128)(2,1)}), bf16[16,16,1408]{2,1,0:T(8,128)(2,1)S(1)}, u32[]{:S(2)}, u32[]{:S(2)}) async-start(bf16[16,16,1408]{2,1,0:T(8,128)(2,1)} %shard_map.108), calls=%async_computation.2 | async-start | bytes 1441792 | tf_op jit(solution)/shard_map/all_to_all | solution.py:349
  136.8 12.6 %all-to-all-done.2.got_ref = bf16[16,16,1408]{2,1,0:T(8,128)(2,1)S(1)} async-done(((bf16[16,16,1408]{2,1,0:T(8,128)(2,1)}), bf16[16,16,1408]{2,1,0:T(8,128)(2,1)S(1)}, u32[]{:S(2)}, u32[]{:S(2)}) %all-to-all-start.2) | async-done | bytes 720928 | tf_op jit(solution)/shard_map/all_to_all | solution.py:349
  149.4 1.0 shard_map.109
  (72 shorter events, 16.7 us)
Async XLA Ops:
  4.4 20.1 %copy-start.2 = (bf16[1,64,1024]{2,1,0:T(8,128)(2,1)S(1)}, bf16[1,64,1024]{2,1,0:T(8,128)(2,1)}, u32[]{:S(2)}) copy-start(bf16[1,64,1024]{2,1,0:T(8,128)(2,1)} %inv_ref.3) | copy-start | bytes 393220
  4.4 20.1 %copy-start.3 = (bf16[1,1024,64]{1,2,0:T(8,128)(2,1)S(1)}, bf16[1,1024,64]{1,2,0:T(8,128)(2,1)}, u32[]{:S(2)}) copy-start(bf16[1,1024,64]{1,2,0:T(8,128)(2,1)} %param.12) | copy-start | bytes 393220
  4.4 20.1 %all-to-all-start = ((bf16[16,80,256]{2,1,0:T(8,128)(2,1)}), bf16[16,80,256]{2,1,0:T(8,128)(2,1)S(1)}, u32[]{:S(2)}, u32[]{:S(2)}) async-start(bf16[16,80,256]{2,1,0:T(8,128)(2,1)} %shard_map.95), calls=%async_computation | async-start | bytes 1310720 | tf_op jit(solution)/shard_map/all_to_all | solution.py:304
  27.8 7.0 %copy-start.7 = (bf16[64,1024]{1,0:T(8,128)(2,1)S(1)}, bf16[64,1024]{1,0:T(8,128)(2,1)}, u32[]{:S(2)}) copy-start(bf16[64,1024]{1,0:T(8,128)(2,1)} %get-tuple-element.21) | copy-start | bytes 393220
  27.8 49.1 %copy-start.5 = (s32[12]{0:T(128)S(1)}, s32[12]{0:T(128)}, u32[]{:S(2)}) copy-start(s32[12]{0:T(128)} %stack.48.place) | copy-start | bytes 148
  27.8 49.1 %copy-start.6 = (s32[1,1024]{1,0:T(1,128)S(1)}, s32[1,1024]{1,0:T(1,128)}, u32[]{:S(2)}) copy-start(s32[1,1024]{1,0:T(1,128)} %idx_ref.4) | copy-start | bytes 12292
  27.8 49.1 %all-to-all-start.1 = ((bf16[16,80,1024]{2,1,0:T(8,128)(2,1)}), bf16[16,80,1024]{2,1,0:T(8,128)(2,1)S(1)}, u32[]{:S(2)}, u32[]{:S(2)}) async-start(bf16[16,80,1024]{2,1,0:T(8,128)(2,1)} %copy-done), calls=%async_computation.1 | async-start | bytes 5242880 | tf_op jit(solution)/shard_map/all_to_all | solution.py:312
  31.7 33.1 %collective-permute-start.4 = (bf16[64,1024]{1,0:T(8,128)(2,1)S(1)}, bf16[64,1024]{1,0:T(8,128)(2,1)S(1)}, u32[]{:S(2)}, u32[]{:S(2)}) collective-permute-start(bf16[64,1024]{1,0:T(8,128)(2,1)S(1)} %copy-done.8), channel_id=1, source_target_pairs={{0,3},{1,0},{2,1},{3,2},{4,7},{5,4},{6,5},{7,6},{8,11},{9,8},{10,9... | collective-permute-start | bytes 393224 | tf_op jit(solution)/shard_map/ppermute | solution.py:133
  34.8 30.1 %collective-permute-start.3 = (bf16[64,1024]{1,0:T(8,128)(2,1)S(1)}, bf16[64,1024]{1,0:T(8,128)(2,1)S(1)}, u32[]{:S(2)}, u32[]{:S(2)}) collective-permute-start(bf16[64,1024]{1,0:T(8,128)(2,1)S(1)} %copy-done.8), channel_id=1, source_target_pairs={{0,1},{1,2},{2,3},{3,0},{4,5},{5,6},{6,7},{7,4},{8,9},{9,10},{10,1... | collective-permute-start | bytes 393224 | tf_op jit(solution)/shard_map/ppermute | solution.py:133
  34.8 32.2 %collective-permute-start.14 = (bf16[64,1024]{1,0:T(8,128)(2,1)S(1)}, bf16[64,1024]{1,0:T(8,128)(2,1)S(1)}, u32[]{:S(2)}, u32[]{:S(2)}) collective-permute-start(bf16[64,1024]{1,0:T(8,128)(2,1)S(1)} %copy-done.7), channel_id=1, source_target_pairs={{0,12},{1,13},{2,14},{3,15},{4,0},{5,1},{6,2},{7,3},{8,4},{9,5},{1... | collective-permute-start | bytes 393224 | tf_op jit(solution)/shard_map/ppermute | solution.py:133
  37.5 31.1 %collective-permute-start.13 = (bf16[64,1024]{1,0:T(8,128)(2,1)S(1)}, bf16[64,1024]{1,0:T(8,128)(2,1)S(1)}, u32[]{:S(2)}, u32[]{:S(2)}) collective-permute-start(bf16[64,1024]{1,0:T(8,128)(2,1)S(1)} %copy-done.7), channel_id=1, source_target_pairs={{0,4},{1,5},{2,6},{3,7},{4,8},{5,9},{6,10},{7,11},{8,12},{9,13},{1... | collective-permute-start | bytes 393224 | tf_op jit(solution)/shard_map/ppermute | solution.py:133
  64.8 6.3 %collective-permute-start.5 = (bf16[32,1024]{1,0:T(8,128)(2,1)S(1)}, bf16[32,1024]{1,0:T(8,128)(2,1)S(1)}, u32[]{:S(2)}, u32[]{:S(2)}) collective-permute-start(bf16[32,1024]{1,0:T(8,128)(2,1)S(1)} %slice.36), channel_id=1, source_target_pairs={{0,3},{1,0},{2,1},{3,2},{4,7},{5,4},{6,5},{7,6},{8,11},{9,8},{10,9... | collective-permute-start | bytes 196616 | tf_op jit(solution)/shard_map/ppermute | solution.py:133
  64.8 6.9 %collective-permute-start.6 = (bf16[32,1024]{1,0:T(8,128)(2,1)S(1)}, bf16[32,1024]{1,0:T(8,128)(2,1)S(1)}, u32[]{:S(2)}, u32[]{:S(2)}) collective-permute-start(bf16[32,1024]{1,0:T(8,128)(2,1)S(1)} %slice.37), channel_id=1, source_target_pairs={{0,1},{1,2},{2,3},{3,0},{4,5},{5,6},{6,7},{7,4},{8,9},{9,10},{10,1... | collective-permute-start | bytes 196616 | tf_op jit(solution)/shard_map/ppermute | solution.py:133
  66.9 9.3 %collective-permute-start.15 = (bf16[32,1024]{1,0:T(8,128)(2,1)S(1)}, bf16[32,1024]{1,0:T(8,128)(2,1)S(1)}, u32[]{:S(2)}, u32[]{:S(2)}) collective-permute-start(bf16[32,1024]{1,0:T(8,128)(2,1)S(1)} %slice.40), channel_id=1, source_target_pairs={{0,12},{1,13},{2,14},{3,15},{4,0},{5,1},{6,2},{7,3},{8,4},{9,5},{1... | collective-permute-start | bytes 196616 | tf_op jit(solution)/shard_map/ppermute | solution.py:133
  68.7 11.5 %collective-permute-start.16 = (bf16[32,1024]{1,0:T(8,128)(2,1)S(1)}, bf16[32,1024]{1,0:T(8,128)(2,1)S(1)}, u32[]{:S(2)}, u32[]{:S(2)}) collective-permute-start(bf16[32,1024]{1,0:T(8,128)(2,1)S(1)} %slice.41), channel_id=1, source_target_pairs={{0,4},{1,5},{2,6},{3,7},{4,8},{5,9},{6,10},{7,11},{8,12},{9,13},{1... | collective-permute-start | bytes 196616 | tf_op jit(solution)/shard_map/ppermute | solution.py:133
  72.4 18.1 %collective-permute-start.7 = (bf16[256,1024]{1,0:T(8,128)(2,1)}, bf16[256,1024]{1,0:T(8,128)(2,1)}, u32[]{:S(2)}, u32[]{:S(2)}) collective-permute-start(bf16[256,1024]{1,0:T(8,128)(2,1)} %constant_dynamic-update-slice_fusion), channel_id=1, source_target_pairs={{0,4},{1,5},{2,6},{3,7},{4,8},{5,9},{6,10},{7,11},{8,12},{9,13},{1... | collective-permute-start | bytes 1572872 | tf_op jit(solution)/shard_map/ppermute | solution.py:133
  74.2 11.5 %collective-permute-start.8 = (bf16[256,1024]{1,0:T(8,128)(2,1)}, bf16[256,1024]{1,0:T(8,128)(2,1)}, u32[]{:S(2)}, u32[]{:S(2)}) collective-permute-start(bf16[256,1024]{1,0:T(8,128)(2,1)} %constant_dynamic-update-slice_fusion), channel_id=1, source_target_pairs={{0,12},{1,13},{2,14},{3,15},{4,0},{5,1},{6,2},{7,3},{8,4},{9,5},{1... | collective-permute-start | bytes 1572872 | tf_op jit(solution)/shard_map/ppermute | solution.py:133
  80.0 11.5 %copy-start.1 = (s32[14,1024]{1,0:T(8,128)S(1)}, s32[14,1024]{1,0:T(8,128)}, u32[]{:S(2)}) copy-start(s32[14,1024]{1,0:T(8,128)} %idx_ref.7) | copy-start | bytes 172036
  80.0 3.6 %collective-permute-start = (f32[64,1024]{1,0:T(8,128)S(1)}, f32[64,1024]{1,0:T(8,128)S(1)}, u32[]{:S(2)}, u32[]{:S(2)}) collective-permute-start(f32[64,1024]{1,0:T(8,128)S(1)} %shard_map.98.own_ref), channel_id=1, source_target_pairs={{0,16},{16,0},{32,48},{48,32},{64,80},{80,64},{96,112},{112,96},{1... | collective-permute-start | bytes 786440 | tf_op jit(solution)/shard_map/ppermute | solution.py:273
  80.8 15.0 %collective-permute-start.18 = (bf16[256,1024]{1,0:T(8,128)(2,1)}, bf16[256,1024]{1,0:T(8,128)(2,1)S(1)}, u32[]{:S(2)}, u32[]{:S(2)}) collective-permute-start(bf16[256,1024]{1,0:T(8,128)(2,1)} %constant_dynamic-update-slice_fusion.5), channel_id=1, source_target_pairs={{0,3},{1,0},{2,1},{3,2},{4,7},{5,4},{6,5},{7,6},{8,11},{9,8},{10,9... | collective-permute-start | bytes 1572872 | tf_op jit(solution)/shard_map/ppermute | solution.py:133
  83.6 15.8 %collective-permute-start.17 = (bf16[256,1024]{1,0:T(8,128)(2,1)}, bf16[256,1024]{1,0:T(8,128)(2,1)S(1)}, u32[]{:S(2)}, u32[]{:S(2)}) collective-permute-start(bf16[256,1024]{1,0:T(8,128)(2,1)} %constant_dynamic-update-slice_fusion.5), channel_id=1, source_target_pairs={{0,1},{1,2},{2,3},{3,0},{4,5},{5,6},{6,7},{7,4},{8,9},{9,10},{10,1... | collective-permute-start | bytes 1572872 | tf_op jit(solution)/shard_map/ppermute | solution.py:133
  84.2 7.3 %collective-permute-start.1 = (f32[16,1536]{1,0:T(8,128)S(1)}, f32[16,1536]{1,0:T(8,128)S(1)}, u32[]{:S(2)}, u32[]{:S(2)}) collective-permute-start(f32[16,1536]{1,0:T(8,128)S(1)} %get-tuple-element.16.own_ref), channel_id=1, source_target_pairs={{0,16},{16,0},{32,48},{48,32},{64,80},{80,64},{96,112},{112,96},{1... | collective-permute-start | bytes 294920 | tf_op jit(solution)/shard_map/ppermute | solution.py:273
  86.7 12.9 %collective-permute-start.9 = (bf16[128,1024]{1,0:T(8,128)(2,1)S(1)}, bf16[128,1024]{1,0:T(8,128)(2,1)S(1)}, u32[]{:S(2)}, u32[]{:S(2)}) collective-permute-start(bf16[128,1024]{1,0:T(8,128)(2,1)S(1)} %slice.38), channel_id=1, source_target_pairs={{0,12},{1,13},{2,14},{3,15},{4,0},{5,1},{6,2},{7,3},{8,4},{9,5},{1... | collective-permute-start | bytes 786440 | tf_op jit(solution)/shard_map/ppermute | solution.py:133
  91.5 8.1 %collective-permute-start.10 = (bf16[128,1024]{1,0:T(8,128)(2,1)S(1)}, bf16[128,1024]{1,0:T(8,128)(2,1)S(1)}, u32[]{:S(2)}, u32[]{:S(2)}) collective-permute-start(bf16[128,1024]{1,0:T(8,128)(2,1)S(1)} %slice.39), channel_id=1, source_target_pairs={{0,4},{1,5},{2,6},{3,7},{4,8},{5,9},{6,10},{7,11},{8,12},{9,13},{1... | collective-permute-start | bytes 786440 | tf_op jit(solution)/shard_map/ppermute | solution.py:133
  94.0 5.7 %collective-permute-start.2 = (f32[48,1024]{1,0:T(8,128)S(1)}, f32[48,1024]{1,0:T(8,128)S(1)}, u32[]{:S(2)}, u32[]{:S(2)}) collective-permute-start(f32[48,1024]{1,0:T(8,128)S(1)} %shard_map.100.own_ref), channel_id=1, source_target_pairs={{0,32},{16,48},{32,0},{48,16},{64,96},{80,112},{96,64},{112,80},{1... | collective-permute-start | bytes 589832 | tf_op jit(solution)/shard_map/ppermute | solution.py:273
  95.8 12.8 %collective-permute-start.19 = (bf16[128,1024]{1,0:T(8,128)(2,1)S(1)}, bf16[128,1024]{1,0:T(8,128)(2,1)S(1)}, u32[]{:S(2)}, u32[]{:S(2)}) collective-permute-start(bf16[128,1024]{1,0:T(8,128)(2,1)S(1)} %slice.42), channel_id=1, source_target_pairs={{0,3},{1,0},{2,1},{3,2},{4,7},{5,4},{6,5},{7,6},{8,11},{9,8},{10,9... | collective-permute-start | bytes 786440 | tf_op jit(solution)/shard_map/ppermute | solution.py:133
  99.5 9.1 %collective-permute-start.20 = (bf16[128,1024]{1,0:T(8,128)(2,1)S(1)}, bf16[128,1024]{1,0:T(8,128)(2,1)S(1)}, u32[]{:S(2)}, u32[]{:S(2)}) collective-permute-start(bf16[128,1024]{1,0:T(8,128)(2,1)S(1)} %slice.43), channel_id=1, source_target_pairs={{0,1},{1,2},{2,3},{3,0},{4,5},{5,6},{6,7},{7,4},{8,9},{9,10},{10,1... | collective-permute-start | bytes 786440 | tf_op jit(solution)/shard_map/ppermute | solution.py:133
  102.1 1.3 collective-permute-start.11
  105.3 8.7 %collective-permute-start.12 = (f32[32,1024]{1,0:T(8,128)S(1)}, f32[32,1024]{1,0:T(8,128)S(1)}, u32[]{:S(2)}, u32[]{:S(2)}) collective-permute-start(f32[32,1024]{1,0:T(8,128)S(1)} %shard_map.102.own_ref), channel_id=1, source_target_pairs={{0,64},{16,80},{32,96},{48,112},{64,0},{80,16},{96,32},{112,48},{1... | collective-permute-start | bytes 393224 | tf_op jit(solution)/shard_map/ppermute | solution.py:273
  116.2 1.3 collective-permute-start.21
  118.7 8.5 %collective-permute-start.22 = (f32[16,1024]{1,0:T(8,128)S(1)}, f32[16,1024]{1,0:T(8,128)S(1)}, u32[]{:S(2)}, u32[]{:S(2)}) collective-permute-start(f32[16,1024]{1,0:T(8,128)S(1)} %shard_map.104.own_ref), channel_id=1, source_target_pairs={{0,192},{16,208},{32,224},{48,240},{64,128},{80,144},{96,160},{112... | collective-permute-start | bytes 196616 | tf_op jit(solution)/shard_map/ppermute | solution.py:273
  128.2 21.2 %all-to-all-start.2 = ((bf16[16,16,1408]{2,1,0:T(8,128)(2,1)}), bf16[16,16,1408]{2,1,0:T(8,128)(2,1)S(1)}, u32[]{:S(2)}, u32[]{:S(2)}) async-start(bf16[16,16,1408]{2,1,0:T(8,128)(2,1)} %shard_map.108), calls=%async_computation.2 | async-start | bytes 1441792 | tf_op jit(solution)/shard_map/all_to_all | solution.py:349
  (3 other events, 6.3 us)

commit v5 on v4

--- a/solution.py
+++ b/solution.py
@@ -37,7 +37,7 @@
     return lax.broadcasted_iota(jnp.int32, shape, dim)
 
 
-def params(mib=16):
+def params(mib=12):
     return pltpu.CompilerParams(vmem_limit_bytes=mib * 2**20)
 
 
@@ -55,10 +55,22 @@
     )(*args)
 
 
-def first_kernel(place, leaf_ref, rhs_ref, out_ref, held, sems):
+def first_kernel(place, leaf_ref, rhs_ref, inv_ref, off_ref, out_ref, *refs):
+    pieces, held, sems = refs[:3], refs[3], refs[4]
     copies = [
         pltpu.make_async_copy(rhs_ref.at[place[a] - 1], held.at[a], sems.at[a]) for a in range(4)
     ]
+    at = pl.ds(pl.multiple_of(place[8] * 32, 32), 32)
+    for level, piece in enumerate(pieces):
+        node = place[level]
+        for part, (ref, index) in enumerate(((inv_ref, node - 1), (off_ref, node - 2))):
+            copies.append(
+                pltpu.make_async_copy(
+                    ref.at[index, at, :],
+                    piece.at[pl.ds(part * 32, 32), :],
+                    sems.at[len(copies)],
+                )
+            )
     for copy in copies:
         copy.start()
     right = leaf_ref[0].astype(BF)
@@ -85,47 +97,31 @@
     out_ref[:, 64:, :] = total.astype(BF).reshape(16, 16, 256)
 
 
-def first_payload(place, rhs_leaf, rhs_top):
+def first_payload(place, rhs_leaf, rhs_top, inv_top, off_top):
+    piece = jax.ShapeDtypeStruct((64, 1024), BF)
     return pl.pallas_call(
         first_kernel,
-        out_shape=jax.ShapeDtypeStruct((FRONTS, 80, 256), BF),
-        in_specs=[SMEM, VMEM, HBM],
-        out_specs=VMEM,
-        scratch_shapes=[pltpu.VMEM((4, 64, 256), F32), pltpu.SemaphoreType.DMA((4,))],
+        out_shape=(jax.ShapeDtypeStruct((FRONTS, 80, 256), BF), piece, piece, piece),
+        in_specs=[SMEM, VMEM, HBM, HBM, HBM],
+        out_specs=(VMEM,) * 4,
+        scratch_shapes=[pltpu.VMEM((4, 64, 256), F32), pltpu.SemaphoreType.DMA((10,))],
         compiler_params=params(60),
-    )(place, rhs_leaf, rhs_top)
-
-
-def weights_kernel(place, inv_ref, off_ref, *refs):
-    outs, sems = refs[:3], refs[3]
-    at = pl.ds(pl.multiple_of(place[8] * 32, 32), 32)
-    copies = []
-    for level, out_ref in enumerate(outs):
-        node = place[level]
-        for part, (ref, index) in enumerate(((inv_ref, node - 1), (off_ref, node - 2))):
-            copies.append(
-                pltpu.make_async_copy(
-                    ref.at[index, at, :],
-                    out_ref.at[pl.ds(part * 32, 32), :],
-                    sems.at[len(copies)],
-                )
-            )
-    for copy in copies:
-        copy.start()
-    for copy in copies:
-        copy.wait()
-
-
-def path_weights(place, inv_top, off_top):
-    piece = jax.ShapeDtypeStruct((64, 1024), BF)
-    return pl.pallas_call(
-        weights_kernel,
-        out_shape=(piece,) * 3,
-        in_specs=[SMEM, HBM, HBM],
-        out_specs=(VMEM,) * 3,
-        scratch_shapes=[pltpu.SemaphoreType.DMA((6,))],
-        compiler_params=params(60),
-    )(place, inv_top, off_top)
+    )(place, rhs_leaf, rhs_top, inv_top, off_top)
+
+
+def stack_kernel(*refs):
+    at = 0
+    for ref in refs[:-1]:
+        rows = ref.shape[0]
+        refs[-1][at : at + rows, :] = ref[...]
+        at += rows
+
+
+def stack(parts):
+    rows = sum(part.shape[0] for part in parts)
+    return call(
+        stack_kernel, jax.ShapeDtypeStruct((rows, 1024), BF), [VMEM] * len(parts), tuple(parts)
+    )
 
 
 def turn(block, dx, dy):
@@ -133,28 +129,29 @@
     return lax.ppermute(block, "front", route)
 
 
-def ring(block, axis):
-    half = block.shape[0] // 2
-    step = (1, 0) if axis == "x" else (0, 1)
-    back = tuple(-d for d in step)
-    before = turn(block, *step)
-    after = turn(block, *back)
-    return block, before, after, turn(after[:half], *back), turn(before[half:], *step)
-
-
-def spread(block, first, second):
-    return ring(jnp.concatenate(ring(block, first), axis=0), second)
-
-
-def leaf_solve_kernel(inv_ref, rhs_ref, off_ref, weights_ref, x_ref, out_ref):
+def step_of(axis):
+    return (1, 0) if axis == "x" else (0, 1)
+
+
+def near(block, axis):
+    dx, dy = step_of(axis)
+    return turn(block, dx, dy), turn(block, -dx, -dy)
+
+
+def far(pair, axis):
+    dx, dy = step_of(axis)
+    before, after = pair
+    half = before.shape[0] // 2
+    return turn(after[:half], -dx, -dy), turn(before[half:], dx, dy)
+
+
+def leaf_solve_kernel(inv_ref, rhs_ref, off_ref, x_ref, out_ref):
     right = rhs_ref[:, :64, :].reshape(1024, 256)
     x = nn(inv_ref[0], right)
     x_ref[...] = x
     xt = x.T.astype(BF)
     update = nn(xt, off_ref[0])
-    out_ref[:, :16, :] = update.astype(BF).reshape(16, 16, 1024)
-    for f in range(FRONTS):
-        out_ref[f, 16:, :] = weights_ref[...]
+    out_ref[...] = update.astype(BF).reshape(16, 16, 1024)
 
 
 def push(update, idx, count):
@@ -175,7 +172,7 @@
 def leaf_update_kernel(place, first_ref, got_ref, idx_ref, out_ref):
     update = jnp.zeros((16, 1024), F32)
     for s in range(FRONTS):
-        update = update + got_ref[s, :16, :].astype(F32)
+        update = update + got_ref[s].astype(F32)
     pending = push(update, idx_ref[...], 4)
     high, low = [], []
     for g in range(FRONTS // 2):
@@ -194,7 +191,7 @@
         out_ref[a * 16 : (a + 1) * 16, :] = nn(put, high) + nn(put, low) - pending[a]
 
 
-def solve_kernel(start, own_ref, other_ref, *refs):
+def solve_kernel(own_ref, other_ref, *refs):
     weights, ux_ref, rest_ref = refs[:-2], refs[-2], refs[-1]
     total = own_ref[...] + other_ref[...]
     rest_ref[...] = total[16:]
@@ -204,18 +201,18 @@
     for ref in weights:
         blocks = ref.shape[0]
         rows = blocks * 32
-        x = nt(right, ref[:, start : start + 32, :].reshape(rows, 1024))
-        off = ref[:, start + 32 : start + 64, :].reshape(rows, 1024)
+        x = nt(right, ref[:, :32, :].reshape(rows, 1024))
+        off = ref[:, 32:, :].reshape(rows, 1024)
         update = update + nn(x.astype(BF), off)
         ux_ref[:, at : at + rows] = x
         at += rows
     ux_ref[:, :1024] = update
 
 
-def top_solve(own, other, weights, start):
+def top_solve(own, other, weights):
     left = own.shape[0] - 16
     return call(
-        functools.partial(solve_kernel, start),
+        solve_kernel,
         (jax.ShapeDtypeStruct((16, 1536), F32), jax.ShapeDtypeStruct((left, 1024), F32)),
         [VMEM] * (2 + len(weights)),
         (own, other, *weights),
@@ -240,10 +237,8 @@
         outer, inner = (0, 3, 1, 2)[k // 4], (0, 3, 1, 2)[k % 4]
         if order == "yx":
             to = (place[10] + outer) % 4 * 4 + (place[11] + inner) % 4
-        elif order == "xy":
+        else:
             to = (place[10] + inner) % 4 * 4 + (place[11] + outer) % 4
-        else:
-            to = k
         at = slice(k * 32, (k + 1) * 32)
         value = jnp.concatenate([low_core[:, at], high_core[:, at]], axis=1)
         high = value.astype(BF).astype(F32)
@@ -301,29 +296,44 @@
     off_top = jnp.swapaxes(off_top, 1, 2)
     off_leaf = jnp.swapaxes(off_leaf, 1, 2)
 
-    first = lax.all_to_all(first_payload(place, rhs_leaf, rhs_top), "front", 0, 0)
-    third, second, lowest = path_weights(place, inv_top, off_top)
+    sent, third, second, lowest = first_payload(place, rhs_leaf, rhs_top, inv_top, off_top)
+    first = lax.all_to_all(sent, "front", 0, 0)
+    third_near, second_near, lowest_near = near(third, "y"), near(second, "x"), near(lowest, "y")
+    third = (third, *third_near, *far(third_near, "y"))
+    second = (second, *second_near, *far(second_near, "x"))
+    lowest = (lowest, *lowest_near, *far(lowest_near, "y"))
     leaf_x, sent = call(
         leaf_solve_kernel,
-        (jax.ShapeDtypeStruct((64, 256), F32), jax.ShapeDtypeStruct((FRONTS, 80, 1024), BF)),
-        [VMEM] * 4,
-        (inv_leaf, first, off_leaf, third),
-    )
+        (jax.ShapeDtypeStruct((64, 256), F32), jax.ShapeDtypeStruct((FRONTS, 16, 1024), BF)),
+        [VMEM] * 3,
+        (inv_leaf, first, off_leaf),
+    )
+    sent, third, second, lowest = lax.optimization_barrier((sent, third, second, lowest))
     got = lax.all_to_all(sent, "front", 0, 0)
-    weights = [(got,)]
-    for block, axes in ((second, "yx"), (lowest, "xy")):
-        parts = spread(block, *axes)
-        weights.append([part.reshape(-1, 64, 1024) for part in parts])
+    third, second = stack(third), stack(second)
+    third_near, second_near = near(third, "x"), near(second, "y")
     state = call(
         leaf_update_kernel,
         jax.ShapeDtypeStruct((64, 1024), F32),
         [SMEM] + [VMEM] * 3,
         (place, first, got, idx_leaf),
     )
+    state, third_near, second_near = lax.optimization_barrier((state, third_near, second_near))
+    third_far, second_far = far(third_near, "x"), far(second_near, "y")
     other = swap(state, core_pairs())
     ships = []
     for level in range(3):
-        ux, rest = top_solve(state, other, weights[level], 0 if level else 16)
+        if level == 0:
+            parts = (third, *third_near, *third_far)
+        elif level == 1:
+            parts = (second, *second_near, *second_far)
+        else:
+            parts = (lowest, *lowest_near, *lowest_far)
+        ux, rest = top_solve(state, other, [part.reshape(-1, 64, 1024) for part in parts])
+        if level == 0:
+            ux, lowest, second_far = lax.optimization_barrier((ux, lowest, second_far))
+            lowest = stack(lowest)
+            lowest_near = near(lowest, "x")
         ux_other = swap(ux, core_pairs())
         state = call(
             functools.partial(update_kernel, level),
@@ -332,9 +342,12 @@
             (place, ux, ux_other, rest, idx_top),
         )
         other = swap(state, chip_pairs(level))
+        if level == 0:
+            other, lowest_near = lax.optimization_barrier((other, lowest_near))
+            lowest_far = far(lowest_near, "x")
         ships.append(
             call(
-                functools.partial(ship_kernel, (None, "yx", "xy")[level]),
+                functools.partial(ship_kernel, ("yx", "xy", "yx")[level]),
                 jax.ShapeDtypeStruct((16, 16, 128), BF),
                 [SMEM, VMEM, VMEM],
                 (place, ux, ux_other),

time: 151 us -> 142 us (0.940)
  waiting for transfers between devices: 61.1 us -> 46.6 us
  blocking collectives: 0 us -> 13.4 us
  local copies, waits for them, and re-layouts: 11.8 us -> 1.74 us
  starting transfers between devices: 52.3 us -> 58.3 us
  Pallas kernels: 24.3 us -> 20.3 us
    all_to_all x0 -> x1, blocking collectives: none -> 13.4 us  [local(): got = lax.all_to_all(sent, 'front', 0, 0)]
    ppermute x16 -> x24, starting transfers between devices: 23.8 us -> 36.1 us  [turn(): return lax.ppermute(block, 'front', route)]
    ppermute x16 -> x24, waiting for transfers between devices: 29.5 us -> 17.4 us  [turn(): return lax.ppermute(block, 'front', route)]
    all_to_all x1, waiting for transfers between devices: 10.4 us -> 0.01 us  [local(): first = lax.all_to_all(sent, 'front', 0, 0)]
    ppermute x7, waiting for transfers between devices: 8.45 us -> 16.5 us  [swap(): return lax.ppermute(block, 'leaf', pairs)]
    unnamed x25 -> x16, local copies, waits for them, and re-layouts: 7.02 us -> 0.04 us
    all_to_all x2 -> x1, starting transfers between devices: 11.5 us -> 5.54 us  [local(): got = lax.all_to_all(sent, 'front', 0, 0)]
    pallas_call x2 -> x1, Pallas kernels: 5.48 us -> 3.27 us  [first_payload(): pl.pallas_call(first_kernel, out_shape=(jax.ShapeDtypeStruct((FRONTS, 80,...]
  transfers between devices with their start and end apart: 26 -> 33, of which waited for: 10 -> 14; matrix products, arithmetic and copies ran while one was open for 6% -> 1% of each run, Pallas kernels for 10% -> 9%
where the time goes in v5:
time: 142 us; the launch traced here: 141 us
  starting transfers between devices  58.3 us (41%)
  waiting for transfers between devices  46.6 us (33%)
  Pallas kernels  20.3 us (14%)
  blocking collectives  13.4 us (9%)
  local copies, waits for them, and re-layouts  1.74 us (1%)
    ppermute x24, starting transfers between devices, turn(): return lax.ppermute(block, 'front', route)  36.1 us
    ppermute x24, waiting for transfers between devices, turn(): return lax.ppermute(block, 'front', route)  17.4 us
    pallas_call x16, Pallas kernels, call(): pl.pallas_call(kernel, out_shape=outs, in_specs=specs, out_specs=tuple((V...  17 us
    ppermute x7, waiting for transfers between devices, swap(): return lax.ppermute(block, 'leaf', pairs)  16.5 us
    all_to_all x1, blocking collectives, local(): got = lax.all_to_all(sent, 'front', 0, 0)  13.4 us
    all_to_all x1, waiting for transfers between devices, local(): got = lax.all_to_all(sent, 'front', 0, 0)  12.6 us
    ppermute x7, starting transfers between devices, swap(): return lax.ppermute(block, 'leaf', pairs)  9.52 us
    all_to_all x1, starting transfers between devices, local(): first = lax.all_to_all(sent, 'front', 0, 0)  7.18 us
  transfers between devices with their start and end apart: 33, of which 14 were waited for; matrix products, arithmetic and copies ran while one was open for 1% of the time, Pallas kernels for 9%

profile of v5, /device:TPU:32, one launch (start us, length us, event | category | flops | bytes accessed | tf_op | source)
XLA Modules:
  0.0 141.3 jit_solution(7321897253299883779)
XLA Ops:
  1.3 3.3 %shard_map.95 = (bf16[16,80,256]{2,1,0:T(8,128)(2,1)}, bf16[64,1024]{1,0:T(8,128)(2,1)}, bf16[64,1024]{1,0:T(8,128)(2,1)}, bf16[64,1024]{1,0:T(8,128)(2,1)}) custom-call(s32[12]{0:T(128)} %stack.48.place, f32[1,64,256]{2,1,0:T(8,128)} %leaf_ref.1, f32[15,64,256]{2,1,0:T(8,128)} %rhs_ref.1, bf16[15,64,1024]{2,1,0:T(8,128)(2,1)} %inv_ref.2, ...), custom_call_target="tpu_custom_call" | custom-call | tf_op jit(solution)/shard_map/pallas_call | solution.py:102
  4.6 7.2 %all-to-all-start = ((bf16[16,80,256]{2,1,0:T(8,128)(2,1)}), bf16[16,80,256]{2,1,0:T(8,128)(2,1)S(1)}, u32[]{:S(2)}, u32[]{:S(2)}) async-start(bf16[16,80,256]{2,1,0:T(8,128)(2,1)} %get-tuple-element.46), calls=%async_computation | async-start | bytes 1310720 | tf_op jit(solution)/shard_map/all_to_all | solution.py:300
  11.8 3.1 %collective-permute-start.1 = (bf16[64,1024]{1,0:T(8,128)(2,1)}, bf16[64,1024]{1,0:T(8,128)(2,1)S(1)}, u32[]{:S(2)}, u32[]{:S(2)}) collective-permute-start(bf16[64,1024]{1,0:T(8,128)(2,1)} %get-tuple-element.53.refs_0_), channel_id=1, source_target_pairs={{0,3},{1,0},{2,1},{3,2},{4,7},{5,4},{6,5},{7,6},{8,11},{9,8},{10,9... | collective-permute-start | bytes 393224 | tf_op jit(solution)/shard_map/ppermute | solution.py:129
  14.9 2.7 %collective-permute-start.5 = (bf16[64,1024]{1,0:T(8,128)(2,1)}, bf16[64,1024]{1,0:T(8,128)(2,1)S(1)}, u32[]{:S(2)}, u32[]{:S(2)}) collective-permute-start(bf16[64,1024]{1,0:T(8,128)(2,1)} %get-tuple-element.58.refs_0_), channel_id=1, source_target_pairs={{0,12},{1,13},{2,14},{3,15},{4,0},{5,1},{6,2},{7,3},{8,4},{9,5},{1... | collective-permute-start | bytes 393224 | tf_op jit(solution)/shard_map/ppermute | solution.py:129
  17.6 3.2 %collective-permute-start.9 = (bf16[64,1024]{1,0:T(8,128)(2,1)}, bf16[64,1024]{1,0:T(8,128)(2,1)S(1)}, u32[]{:S(2)}, u32[]{:S(2)}) collective-permute-start(bf16[64,1024]{1,0:T(8,128)(2,1)} %get-tuple-element.76.refs_0_), channel_id=1, source_target_pairs={{0,3},{1,0},{2,1},{3,2},{4,7},{5,4},{6,5},{7,6},{8,11},{9,8},{10,9... | collective-permute-start | bytes 393224 | tf_op jit(solution)/shard_map/ppermute | solution.py:129
  20.9 4.4 %collective-permute-done.1.refs_2_ = bf16[64,1024]{1,0:T(8,128)(2,1)S(1)} collective-permute-done((bf16[64,1024]{1,0:T(8,128)(2,1)}, bf16[64,1024]{1,0:T(8,128)(2,1)S(1)}, u32[]{:S(2)}, u32[]{:S(2)}) %collective-permute-start.1) | collective-permute-done | bytes 131104 | tf_op jit(solution)/shard_map/ppermute | solution.py:129
  26.4 2.2 %collective-permute-start.2 = (bf16[32,1024]{1,0:T(8,128)(2,1)S(1)}, bf16[32,1024]{1,0:T(8,128)(2,1)S(1)}, u32[]{:S(2)}, u32[]{:S(2)}) collective-permute-start(bf16[32,1024]{1,0:T(8,128)(2,1)S(1)} %slice.52), channel_id=1, source_target_pairs={{0,3},{1,0},{2,1},{3,2},{4,7},{5,4},{6,5},{7,6},{8,11},{9,8},{10,9... | collective-permute-start | bytes 196616 | tf_op jit(solution)/shard_map/ppermute | solution.py:129
  28.7 2.3 %collective-permute-start.6 = (bf16[32,1024]{1,0:T(8,128)(2,1)S(1)}, bf16[32,1024]{1,0:T(8,128)(2,1)S(1)}, u32[]{:S(2)}, u32[]{:S(2)}) collective-permute-start(bf16[32,1024]{1,0:T(8,128)(2,1)S(1)} %slice.54), channel_id=1, source_target_pairs={{0,12},{1,13},{2,14},{3,15},{4,0},{5,1},{6,2},{7,3},{8,4},{9,5},{1... | collective-permute-start | bytes 196616 | tf_op jit(solution)/shard_map/ppermute | solution.py:129
  31.7 2.6 %collective-permute-start.10 = (bf16[32,1024]{1,0:T(8,128)(2,1)S(1)}, bf16[32,1024]{1,0:T(8,128)(2,1)S(1)}, u32[]{:S(2)}, u32[]{:S(2)}) collective-permute-start(bf16[32,1024]{1,0:T(8,128)(2,1)S(1)} %slice.56), channel_id=1, source_target_pairs={{0,3},{1,0},{2,1},{3,2},{4,7},{5,4},{6,5},{7,6},{8,11},{9,8},{10,9... | collective-permute-start | bytes 196616 | tf_op jit(solution)/shard_map/ppermute | solution.py:129
  35.3 1.3 collective-permute-done.7.refs_4_
  36.6 3.2 %collective-permute-done.11.refs_4_ = bf16[32,1024]{1,0:T(8,128)(2,1)S(1)} collective-permute-done((bf16[32,1024]{1,0:T(8,128)(2,1)S(1)}, bf16[32,1024]{1,0:T(8,128)(2,1)S(1)}, u32[]{:S(2)}, u32[]{:S(2)}) %collective-permute-start.11) | collective-permute-done | bytes 65568 | tf_op jit(solution)/shard_map/ppermute | solution.py:129
  40.9 2.2 %collective-permute-start.13 = (bf16[256,1024]{1,0:T(8,128)(2,1)S(1)}, bf16[256,1024]{1,0:T(8,128)(2,1)S(1)}, u32[]{:S(2)}, u32[]{:S(2)}) collective-permute-start(bf16[256,1024]{1,0:T(8,128)(2,1)S(1)} %shard_map.98), channel_id=1, source_target_pairs={{0,12},{1,13},{2,14},{3,15},{4,0},{5,1},{6,2},{7,3},{8,4},{9,5},{1... | collective-permute-start | bytes 1572872 | tf_op jit(solution)/shard_map/ppermute | solution.py:129
  43.5 3.2 %collective-permute-start.15 = (bf16[256,1024]{1,0:T(8,128)(2,1)S(1)}, bf16[256,1024]{1,0:T(8,128)(2,1)S(1)}, u32[]{:S(2)}, u32[]{:S(2)}) collective-permute-start(bf16[256,1024]{1,0:T(8,128)(2,1)S(1)} %shard_map.99), channel_id=1, source_target_pairs={{0,3},{1,0},{2,1},{3,2},{4,7},{5,4},{6,5},{7,6},{8,11},{9,8},{10,9... | collective-permute-start | bytes 1572872 | tf_op jit(solution)/shard_map/ppermute | solution.py:129
  46.7 13.4 %all_to_all.15.got_ref = bf16[16,16,1024]{2,1,0:T(8,128)(2,1)S(1)} all-to-all(bf16[16,16,1024]{2,1,0:T(8,128)(2,1)S(1)} %get-tuple-element.52), channel_id=1, replica_groups=mesh['leaf'=16,'front'=16] {'front'}, dimensions={0} | all-to-all | bytes 1048576 | tf_op jit(solution)/shard_map/all_to_all | solution.py:312
  60.1 3.1 %shard_map.97.own_ref = f32[64,1024]{1,0:T(8,128)S(1)} custom-call(s32[12]{0:T(128)S(1)} %copy-done.6, bf16[16,80,256]{2,1,0:T(8,128)(2,1)S(1)} %all-to-all-done.rhs_ref.first_ref, bf16[16,16,1024]{2,1,0:T(8,128)(2,1)S(1)} %all_to_all.15.got_ref, s32[1,1024]{1,0:T(1,128)S(1)} %copy-done.7), custom_call_target="tpu_custom_call" | custom-call | flops 100000000 | bytes 1000000 | tf_op jit(solution)/shard_map/pallas_call | solution.py:46
  63.4 1.5 %collective-permute-start.17 = (bf16[128,1024]{1,0:T(8,128)(2,1)S(1)}, bf16[128,1024]{1,0:T(8,128)(2,1)S(1)}, u32[]{:S(2)}, u32[]{:S(2)}) collective-permute-start(bf16[128,1024]{1,0:T(8,128)(2,1)S(1)} %slice.45), channel_id=1, source_target_pairs={{0,12},{1,13},{2,14},{3,15},{4,0},{5,1},{6,2},{7,3},{8,4},{9,5},{1... | collective-permute-start | bytes 786440 | tf_op jit(solution)/shard_map/ppermute | solution.py:129
  65.6 3.0 %collective-permute-start.19 = (bf16[128,1024]{1,0:T(8,128)(2,1)S(1)}, bf16[128,1024]{1,0:T(8,128)(2,1)S(1)}, u32[]{:S(2)}, u32[]{:S(2)}) collective-permute-start(bf16[128,1024]{1,0:T(8,128)(2,1)S(1)} %slice.47), channel_id=1, source_target_pairs={{0,3},{1,0},{2,1},{3,2},{4,7},{5,4},{6,5},{7,6},{8,11},{9,8},{10,9... | collective-permute-start | bytes 786440 | tf_op jit(solution)/shard_map/ppermute | solution.py:129
  68.8 3.4 %collective-permute-done.17 = bf16[128,1024]{1,0:T(8,128)(2,1)S(1)} collective-permute-done((bf16[128,1024]{1,0:T(8,128)(2,1)S(1)}, bf16[128,1024]{1,0:T(8,128)(2,1)S(1)}, u32[]{:S(2)}, u32[]{:S(2)}) %collective-permute-start.17) | collective-permute-done | bytes 262176 | tf_op jit(solution)/shard_map/ppermute | solution.py:129
  72.2 2.5 %collective-permute-done.18 = bf16[128,1024]{1,0:T(8,128)(2,1)S(1)} collective-permute-done((bf16[128,1024]{1,0:T(8,128)(2,1)S(1)}, bf16[128,1024]{1,0:T(8,128)(2,1)S(1)}, u32[]{:S(2)}, u32[]{:S(2)}) %collective-permute-start.18) | collective-permute-done | bytes 262176 | tf_op jit(solution)/shard_map/ppermute | solution.py:129
  75.7 2.1 %collective-permute-done.20 = bf16[128,1024]{1,0:T(8,128)(2,1)S(1)} collective-permute-done((bf16[128,1024]{1,0:T(8,128)(2,1)S(1)}, bf16[128,1024]{1,0:T(8,128)(2,1)S(1)}, u32[]{:S(2)}, u32[]{:S(2)}) %collective-permute-start.20) | collective-permute-done | bytes 262176 | tf_op jit(solution)/shard_map/ppermute | solution.py:129
  78.3 2.9 %collective-permute-start.24 = (bf16[256,1024]{1,0:T(8,128)(2,1)S(1)}, bf16[256,1024]{1,0:T(8,128)(2,1)S(1)}, u32[]{:S(2)}, u32[]{:S(2)}) collective-permute-start(bf16[256,1024]{1,0:T(8,128)(2,1)S(1)} %shard_map.102), channel_id=1, source_target_pairs={{0,12},{1,13},{2,14},{3,15},{4,0},{5,1},{6,2},{7,3},{8,4},{9,5},{1... | collective-permute-start | bytes 1572872 | tf_op jit(solution)/shard_map/ppermute | solution.py:129
  81.2 1.3 collective-permute-done.21.other_ref
  82.5 2.4 %shard_map.101.own_ref = f32[48,1024]{1,0:T(8,128)S(1)} custom-call(s32[12]{0:T(128)S(1)} %copy-done.6, f32[16,1536]{1,0:T(8,128)S(1)} %get-tuple-element.74.own_ref, f32[16,1536]{1,0:T(8,128)S(1)} %collective-permute-done.21.other_ref, f32[48,1024]{1,0:T(8,128)S(1)} %get-tuple-element.75.rest_ref, s32[14,1024]{1,0:T(8,128)S(1)} %copy-done), custom_call_target="tpu_custom_call" | custom-call | flops 100000000 | bytes 1000000 | tf_op jit(solution)/shard_map/pallas_call | solution.py:46
  85.1 6.8 %collective-permute-done.22.other_ref = f32[48,1024]{1,0:T(8,128)S(1)} collective-permute-done((f32[48,1024]{1,0:T(8,128)S(1)}, f32[48,1024]{1,0:T(8,128)S(1)}, u32[]{:S(2)}, u32[]{:S(2)}) %collective-permute-start.22) | collective-permute-done | bytes 196640 | tf_op jit(solution)/shard_map/ppermute | solution.py:268
  92.0 2.9 %collective-permute-start.27 = (bf16[128,1024]{1,0:T(8,128)(2,1)S(1)}, bf16[128,1024]{1,0:T(8,128)(2,1)S(1)}, u32[]{:S(2)}, u32[]{:S(2)}) collective-permute-start(bf16[128,1024]{1,0:T(8,128)(2,1)S(1)} %slice.49), channel_id=1, source_target_pairs={{0,12},{1,13},{2,14},{3,15},{4,0},{5,1},{6,2},{7,3},{8,4},{9,5},{1... | collective-permute-start | bytes 786440 | tf_op jit(solution)/shard_map/ppermute | solution.py:129
  96.3 1.3 collective-permute-done.25.other_ref
  97.5 1.8 %shard_map.104.own_ref = f32[32,1024]{1,0:T(8,128)S(1)} custom-call(s32[12]{0:T(128)S(1)} %copy-done.6, f32[16,1536]{1,0:T(8,128)S(1)} %get-tuple-element.84.own_ref, f32[16,1536]{1,0:T(8,128)S(1)} %collective-permute-done.25.other_ref, f32[32,1024]{1,0:T(8,128)S(1)} %get-tuple-element.85.rest_ref, s32[14,1024]{1,0:T(8,128)S(1)} %copy-done), custom_call_target="tpu_custom_call" | custom-call | flops 100000000 | bytes 1000000 | tf_op jit(solution)/shard_map/pallas_call | solution.py:46
  99.4 3.3 %collective-permute-start.26 = (f32[32,1024]{1,0:T(8,128)S(1)}, f32[32,1024]{1,0:T(8,128)S(1)}, u32[]{:S(2)}, u32[]{:S(2)}) collective-permute-start(f32[32,1024]{1,0:T(8,128)S(1)} %shard_map.104.own_ref), channel_id=1, source_target_pairs={{0,64},{16,80},{32,96},{48,112},{64,0},{80,16},{96,32},{112,48},{1... | collective-permute-start | bytes 393224 | tf_op jit(solution)/shard_map/ppermute | solution.py:268
  102.7 5.5 %collective-permute-done.26.other_ref = f32[32,1024]{1,0:T(8,128)S(1)} collective-permute-done((f32[32,1024]{1,0:T(8,128)S(1)}, f32[32,1024]{1,0:T(8,128)S(1)}, u32[]{:S(2)}, u32[]{:S(2)}) %collective-permute-start.26) | collective-permute-done | bytes 131104 | tf_op jit(solution)/shard_map/ppermute | solution.py:268
  111.8 6.0 %collective-permute-start.30 = (f32[16,1024]{1,0:T(8,128)S(1)}, f32[16,1024]{1,0:T(8,128)S(1)}, u32[]{:S(2)}, u32[]{:S(2)}) collective-permute-start(f32[16,1024]{1,0:T(8,128)S(1)} %shard_map.106.own_ref), channel_id=1, source_target_pairs={{0,192},{16,208},{32,224},{48,240},{64,128},{80,144},{96,160},{112... | collective-permute-start | bytes 196616 | tf_op jit(solution)/shard_map/ppermute | solution.py:268
  121.2 5.5 %all-to-all-start.2 = ((bf16[16,16,1408]{2,1,0:T(8,128)(2,1)}), bf16[16,16,1408]{2,1,0:T(8,128)(2,1)S(1)}, u32[]{:S(2)}, u32[]{:S(2)}) async-start(bf16[16,16,1408]{2,1,0:T(8,128)(2,1)} %shard_map.110), calls=%async_computation.2 | async-start | bytes 1441792 | tf_op jit(solution)/shard_map/all_to_all | solution.py:362
  127.7 12.6 %all-to-all-done.2.got_ref = bf16[16,16,1408]{2,1,0:T(8,128)(2,1)S(1)} async-done(((bf16[16,16,1408]{2,1,0:T(8,128)(2,1)}), bf16[16,16,1408]{2,1,0:T(8,128)(2,1)S(1)}, u32[]{:S(2)}, u32[]{:S(2)}) %all-to-all-start.2) | async-done | bytes 720928 | tf_op jit(solution)/shard_map/all_to_all | solution.py:362
  (82 shorter events, 18.0 us)
Async XLA Ops:
  4.6 29.7 %all-to-all-start = ((bf16[16,80,256]{2,1,0:T(8,128)(2,1)}), bf16[16,80,256]{2,1,0:T(8,128)(2,1)S(1)}, u32[]{:S(2)}, u32[]{:S(2)}) async-start(bf16[16,80,256]{2,1,0:T(8,128)(2,1)} %get-tuple-element.46), calls=%async_computation | async-start | bytes 1310720 | tf_op jit(solution)/shard_map/all_to_all | solution.py:300
  11.8 13.5 %collective-permute-start.1 = (bf16[64,1024]{1,0:T(8,128)(2,1)}, bf16[64,1024]{1,0:T(8,128)(2,1)S(1)}, u32[]{:S(2)}, u32[]{:S(2)}) collective-permute-start(bf16[64,1024]{1,0:T(8,128)(2,1)} %get-tuple-element.53.refs_0_), channel_id=1, source_target_pairs={{0,3},{1,0},{2,1},{3,2},{4,7},{5,4},{6,5},{7,6},{8,11},{9,8},{10,9... | collective-permute-start | bytes 393224 | tf_op jit(solution)/shard_map/ppermute | solution.py:129
  14.9 11.5 %collective-permute-start = (bf16[64,1024]{1,0:T(8,128)(2,1)}, bf16[64,1024]{1,0:T(8,128)(2,1)S(1)}, u32[]{:S(2)}, u32[]{:S(2)}) collective-permute-start(bf16[64,1024]{1,0:T(8,128)(2,1)} %get-tuple-element.53.refs_0_), channel_id=1, source_target_pairs={{0,1},{1,2},{2,3},{3,0},{4,5},{5,6},{6,7},{7,4},{8,9},{9,10},{10,1... | collective-permute-start | bytes 393224 | tf_op jit(solution)/shard_map/ppermute | solution.py:129
  14.9 13.7 %collective-permute-start.5 = (bf16[64,1024]{1,0:T(8,128)(2,1)}, bf16[64,1024]{1,0:T(8,128)(2,1)S(1)}, u32[]{:S(2)}, u32[]{:S(2)}) collective-permute-start(bf16[64,1024]{1,0:T(8,128)(2,1)} %get-tuple-element.58.refs_0_), channel_id=1, source_target_pairs={{0,12},{1,13},{2,14},{3,15},{4,0},{5,1},{6,2},{7,3},{8,4},{9,5},{1... | collective-permute-start | bytes 393224 | tf_op jit(solution)/shard_map/ppermute | solution.py:129
  17.6 11.1 %collective-permute-start.4 = (bf16[64,1024]{1,0:T(8,128)(2,1)}, bf16[64,1024]{1,0:T(8,128)(2,1)S(1)}, u32[]{:S(2)}, u32[]{:S(2)}) collective-permute-start(bf16[64,1024]{1,0:T(8,128)(2,1)} %get-tuple-element.58.refs_0_), channel_id=1, source_target_pairs={{0,4},{1,5},{2,6},{3,7},{4,8},{5,9},{6,10},{7,11},{8,12},{9,13},{1... | collective-permute-start | bytes 393224 | tf_op jit(solution)/shard_map/ppermute | solution.py:129
  17.6 13.5 %collective-permute-start.9 = (bf16[64,1024]{1,0:T(8,128)(2,1)}, bf16[64,1024]{1,0:T(8,128)(2,1)S(1)}, u32[]{:S(2)}, u32[]{:S(2)}) collective-permute-start(bf16[64,1024]{1,0:T(8,128)(2,1)} %get-tuple-element.76.refs_0_), channel_id=1, source_target_pairs={{0,3},{1,0},{2,1},{3,2},{4,7},{5,4},{6,5},{7,6},{8,11},{9,8},{10,9... | collective-permute-start | bytes 393224 | tf_op jit(solution)/shard_map/ppermute | solution.py:129
  25.3 6.4 %collective-permute-start.8 = (bf16[64,1024]{1,0:T(8,128)(2,1)}, bf16[64,1024]{1,0:T(8,128)(2,1)S(1)}, u32[]{:S(2)}, u32[]{:S(2)}) collective-permute-start(bf16[64,1024]{1,0:T(8,128)(2,1)} %get-tuple-element.76.refs_0_), channel_id=1, source_target_pairs={{0,1},{1,2},{2,3},{3,0},{4,5},{5,6},{6,7},{7,4},{8,9},{9,10},{10,1... | collective-permute-start | bytes 393224 | tf_op jit(solution)/shard_map/ppermute | solution.py:129
  26.4 7.9 %collective-permute-start.2 = (bf16[32,1024]{1,0:T(8,128)(2,1)S(1)}, bf16[32,1024]{1,0:T(8,128)(2,1)S(1)}, u32[]{:S(2)}, u32[]{:S(2)}) collective-permute-start(bf16[32,1024]{1,0:T(8,128)(2,1)S(1)} %slice.52), channel_id=1, source_target_pairs={{0,3},{1,0},{2,1},{3,2},{4,7},{5,4},{6,5},{7,6},{8,11},{9,8},{10,9... | collective-permute-start | bytes 196616 | tf_op jit(solution)/shard_map/ppermute | solution.py:129
  28.6 6.7 %collective-permute-start.3 = (bf16[32,1024]{1,0:T(8,128)(2,1)S(1)}, bf16[32,1024]{1,0:T(8,128)(2,1)S(1)}, u32[]{:S(2)}, u32[]{:S(2)}) collective-permute-start(bf16[32,1024]{1,0:T(8,128)(2,1)S(1)} %slice.53), channel_id=1, source_target_pairs={{0,1},{1,2},{2,3},{3,0},{4,5},{5,6},{6,7},{7,4},{8,9},{9,10},{10,1... | collective-permute-start | bytes 196616 | tf_op jit(solution)/shard_map/ppermute | solution.py:129
  28.7 6.6 %collective-permute-start.6 = (bf16[32,1024]{1,0:T(8,128)(2,1)S(1)}, bf16[32,1024]{1,0:T(8,128)(2,1)S(1)}, u32[]{:S(2)}, u32[]{:S(2)}) collective-permute-start(bf16[32,1024]{1,0:T(8,128)(2,1)S(1)} %slice.54), channel_id=1, source_target_pairs={{0,12},{1,13},{2,14},{3,15},{4,0},{5,1},{6,2},{7,3},{8,4},{9,5},{1... | collective-permute-start | bytes 196616 | tf_op jit(solution)/shard_map/ppermute | solution.py:129
  31.1 5.6 %collective-permute-start.7 = (bf16[32,1024]{1,0:T(8,128)(2,1)S(1)}, bf16[32,1024]{1,0:T(8,128)(2,1)S(1)}, u32[]{:S(2)}, u32[]{:S(2)}) collective-permute-start(bf16[32,1024]{1,0:T(8,128)(2,1)S(1)} %slice.55), channel_id=1, source_target_pairs={{0,4},{1,5},{2,6},{3,7},{4,8},{5,9},{6,10},{7,11},{8,12},{9,13},{1... | collective-permute-start | bytes 196616 | tf_op jit(solution)/shard_map/ppermute | solution.py:129
  31.7 5.0 %collective-permute-start.10 = (bf16[32,1024]{1,0:T(8,128)(2,1)S(1)}, bf16[32,1024]{1,0:T(8,128)(2,1)S(1)}, u32[]{:S(2)}, u32[]{:S(2)}) collective-permute-start(bf16[32,1024]{1,0:T(8,128)(2,1)S(1)} %slice.56), channel_id=1, source_target_pairs={{0,3},{1,0},{2,1},{3,2},{4,7},{5,4},{6,5},{7,6},{8,11},{9,8},{10,9... | collective-permute-start | bytes 196616 | tf_op jit(solution)/shard_map/ppermute | solution.py:129
  34.2 5.6 %collective-permute-start.11 = (bf16[32,1024]{1,0:T(8,128)(2,1)S(1)}, bf16[32,1024]{1,0:T(8,128)(2,1)S(1)}, u32[]{:S(2)}, u32[]{:S(2)}) collective-permute-start(bf16[32,1024]{1,0:T(8,128)(2,1)S(1)} %slice.57), channel_id=1, source_target_pairs={{0,1},{1,2},{2,3},{3,0},{4,5},{5,6},{6,7},{7,4},{8,9},{9,10},{10,1... | collective-permute-start | bytes 196616 | tf_op jit(solution)/shard_map/ppermute | solution.py:129
  39.8 23.4 %collective-permute-start.12 = (bf16[256,1024]{1,0:T(8,128)(2,1)S(1)}, bf16[256,1024]{1,0:T(8,128)(2,1)S(1)}, u32[]{:S(2)}, u32[]{:S(2)}) collective-permute-start(bf16[256,1024]{1,0:T(8,128)(2,1)S(1)} %shard_map.98), channel_id=1, source_target_pairs={{0,4},{1,5},{2,6},{3,7},{4,8},{5,9},{6,10},{7,11},{8,12},{9,13},{1... | collective-permute-start | bytes 1572872 | tf_op jit(solution)/shard_map/ppermute | solution.py:129
  40.9 22.3 %collective-permute-start.13 = (bf16[256,1024]{1,0:T(8,128)(2,1)S(1)}, bf16[256,1024]{1,0:T(8,128)(2,1)S(1)}, u32[]{:S(2)}, u32[]{:S(2)}) collective-permute-start(bf16[256,1024]{1,0:T(8,128)(2,1)S(1)} %shard_map.98), channel_id=1, source_target_pairs={{0,12},{1,13},{2,14},{3,15},{4,0},{5,1},{6,2},{7,3},{8,4},{9,5},{1... | collective-permute-start | bytes 1572872 | tf_op jit(solution)/shard_map/ppermute | solution.py:129
  43.2 20.1 %collective-permute-start.14 = (bf16[256,1024]{1,0:T(8,128)(2,1)S(1)}, bf16[256,1024]{1,0:T(8,128)(2,1)S(1)}, u32[]{:S(2)}, u32[]{:S(2)}) collective-permute-start(bf16[256,1024]{1,0:T(8,128)(2,1)S(1)} %shard_map.99), channel_id=1, source_target_pairs={{0,1},{1,2},{2,3},{3,0},{4,5},{5,6},{6,7},{7,4},{8,9},{9,10},{10,1... | collective-permute-start | bytes 1572872 | tf_op jit(solution)/shard_map/ppermute | solution.py:129
  43.5 19.8 %collective-permute-start.15 = (bf16[256,1024]{1,0:T(8,128)(2,1)S(1)}, bf16[256,1024]{1,0:T(8,128)(2,1)S(1)}, u32[]{:S(2)}, u32[]{:S(2)}) collective-permute-start(bf16[256,1024]{1,0:T(8,128)(2,1)S(1)} %shard_map.99), channel_id=1, source_target_pairs={{0,3},{1,0},{2,1},{3,2},{4,7},{5,4},{6,5},{7,6},{8,11},{9,8},{10,9... | collective-permute-start | bytes 1572872 | tf_op jit(solution)/shard_map/ppermute | solution.py:129
  63.3 5.5 %collective-permute-start.16 = (f32[64,1024]{1,0:T(8,128)S(1)}, f32[64,1024]{1,0:T(8,128)S(1)}, u32[]{:S(2)}, u32[]{:S(2)}) collective-permute-start(f32[64,1024]{1,0:T(8,128)S(1)} %shard_map.97.own_ref), channel_id=1, source_target_pairs={{0,16},{16,0},{32,48},{48,32},{64,80},{80,64},{96,112},{112,96},{1... | collective-permute-start | bytes 786440 | tf_op jit(solution)/shard_map/ppermute | solution.py:268
  63.4 8.8 %collective-permute-start.17 = (bf16[128,1024]{1,0:T(8,128)(2,1)S(1)}, bf16[128,1024]{1,0:T(8,128)(2,1)S(1)}, u32[]{:S(2)}, u32[]{:S(2)}) collective-permute-start(bf16[128,1024]{1,0:T(8,128)(2,1)S(1)} %slice.45), channel_id=1, source_target_pairs={{0,12},{1,13},{2,14},{3,15},{4,0},{5,1},{6,2},{7,3},{8,4},{9,5},{1... | collective-permute-start | bytes 786440 | tf_op jit(solution)/shard_map/ppermute | solution.py:129
  64.9 9.7 %collective-permute-start.18 = (bf16[128,1024]{1,0:T(8,128)(2,1)S(1)}, bf16[128,1024]{1,0:T(8,128)(2,1)S(1)}, u32[]{:S(2)}, u32[]{:S(2)}) collective-permute-start(bf16[128,1024]{1,0:T(8,128)(2,1)S(1)} %slice.46), channel_id=1, source_target_pairs={{0,4},{1,5},{2,6},{3,7},{4,8},{5,9},{6,10},{7,11},{8,12},{9,13},{1... | collective-permute-start | bytes 786440 | tf_op jit(solution)/shard_map/ppermute | solution.py:129
  65.6 10.1 %collective-permute-start.19 = (bf16[128,1024]{1,0:T(8,128)(2,1)S(1)}, bf16[128,1024]{1,0:T(8,128)(2,1)S(1)}, u32[]{:S(2)}, u32[]{:S(2)}) collective-permute-start(bf16[128,1024]{1,0:T(8,128)(2,1)S(1)} %slice.47), channel_id=1, source_target_pairs={{0,3},{1,0},{2,1},{3,2},{4,7},{5,4},{6,5},{7,6},{8,11},{9,8},{10,9... | collective-permute-start | bytes 786440 | tf_op jit(solution)/shard_map/ppermute | solution.py:129
  68.7 9.2 %collective-permute-start.20 = (bf16[128,1024]{1,0:T(8,128)(2,1)S(1)}, bf16[128,1024]{1,0:T(8,128)(2,1)S(1)}, u32[]{:S(2)}, u32[]{:S(2)}) collective-permute-start(bf16[128,1024]{1,0:T(8,128)(2,1)S(1)} %slice.48), channel_id=1, source_target_pairs={{0,1},{1,2},{2,3},{3,0},{4,5},{5,6},{6,7},{7,4},{8,9},{9,10},{10,1... | collective-permute-start | bytes 786440 | tf_op jit(solution)/shard_map/ppermute | solution.py:129
  77.9 14.0 %collective-permute-start.23 = (bf16[256,1024]{1,0:T(8,128)(2,1)S(1)}, bf16[256,1024]{1,0:T(8,128)(2,1)S(1)}, u32[]{:S(2)}, u32[]{:S(2)}) collective-permute-start(bf16[256,1024]{1,0:T(8,128)(2,1)S(1)} %shard_map.102), channel_id=1, source_target_pairs={{0,4},{1,5},{2,6},{3,7},{4,8},{5,9},{6,10},{7,11},{8,12},{9,13},{1... | collective-permute-start | bytes 1572872 | tf_op jit(solution)/shard_map/ppermute | solution.py:129
  78.3 13.7 %collective-permute-start.24 = (bf16[256,1024]{1,0:T(8,128)(2,1)S(1)}, bf16[256,1024]{1,0:T(8,128)(2,1)S(1)}, u32[]{:S(2)}, u32[]{:S(2)}) collective-permute-start(bf16[256,1024]{1,0:T(8,128)(2,1)S(1)} %shard_map.102), channel_id=1, source_target_pairs={{0,12},{1,13},{2,14},{3,15},{4,0},{5,1},{6,2},{7,3},{8,4},{9,5},{1... | collective-permute-start | bytes 1572872 | tf_op jit(solution)/shard_map/ppermute | solution.py:129
  84.9 7.0 %collective-permute-start.22 = (f32[48,1024]{1,0:T(8,128)S(1)}, f32[48,1024]{1,0:T(8,128)S(1)}, u32[]{:S(2)}, u32[]{:S(2)}) collective-permute-start(f32[48,1024]{1,0:T(8,128)S(1)} %shard_map.101.own_ref), channel_id=1, source_target_pairs={{0,32},{16,48},{32,0},{48,16},{64,96},{80,112},{96,64},{112,80},{1... | collective-permute-start | bytes 589832 | tf_op jit(solution)/shard_map/ppermute | solution.py:268
  92.0 16.2 %collective-permute-start.27 = (bf16[128,1024]{1,0:T(8,128)(2,1)S(1)}, bf16[128,1024]{1,0:T(8,128)(2,1)S(1)}, u32[]{:S(2)}, u32[]{:S(2)}) collective-permute-start(bf16[128,1024]{1,0:T(8,128)(2,1)S(1)} %slice.49), channel_id=1, source_target_pairs={{0,12},{1,13},{2,14},{3,15},{4,0},{5,1},{6,2},{7,3},{8,4},{9,5},{1... | collective-permute-start | bytes 786440 | tf_op jit(solution)/shard_map/ppermute | solution.py:129
  94.8 13.3 %collective-permute-start.28 = (bf16[128,1024]{1,0:T(8,128)(2,1)S(1)}, bf16[128,1024]{1,0:T(8,128)(2,1)S(1)}, u32[]{:S(2)}, u32[]{:S(2)}) collective-permute-start(bf16[128,1024]{1,0:T(8,128)(2,1)S(1)} %slice.50), channel_id=1, source_target_pairs={{0,4},{1,5},{2,6},{3,7},{4,8},{5,9},{6,10},{7,11},{8,12},{9,13},{1... | collective-permute-start | bytes 786440 | tf_op jit(solution)/shard_map/ppermute | solution.py:129
  96.2 1.3 collective-permute-start.25
  99.4 8.7 %collective-permute-start.26 = (f32[32,1024]{1,0:T(8,128)S(1)}, f32[32,1024]{1,0:T(8,128)S(1)}, u32[]{:S(2)}, u32[]{:S(2)}) collective-permute-start(f32[32,1024]{1,0:T(8,128)S(1)} %shard_map.104.own_ref), channel_id=1, source_target_pairs={{0,64},{16,80},{32,96},{48,112},{64,0},{80,16},{96,32},{112,48},{1... | collective-permute-start | bytes 393224 | tf_op jit(solution)/shard_map/ppermute | solution.py:268
  109.2 1.3 collective-permute-start.29
  111.8 8.5 %collective-permute-start.30 = (f32[16,1024]{1,0:T(8,128)S(1)}, f32[16,1024]{1,0:T(8,128)S(1)}, u32[]{:S(2)}, u32[]{:S(2)}) collective-permute-start(f32[16,1024]{1,0:T(8,128)S(1)} %shard_map.106.own_ref), channel_id=1, source_target_pairs={{0,192},{16,208},{32,224},{48,240},{64,128},{80,144},{96,160},{112... | collective-permute-start | bytes 196616 | tf_op jit(solution)/shard_map/ppermute | solution.py:268
  121.2 19.1 %all-to-all-start.2 = ((bf16[16,16,1408]{2,1,0:T(8,128)(2,1)}), bf16[16,16,1408]{2,1,0:T(8,128)(2,1)S(1)}, u32[]{:S(2)}, u32[]{:S(2)}) async-start(bf16[16,16,1408]{2,1,0:T(8,128)(2,1)} %shard_map.110), calls=%async_computation.2 | async-start | bytes 1441792 | tf_op jit(solution)/shard_map/all_to_all | solution.py:362
  (9 other events, 212.9 us)

commit v6 on v5

--- a/solution.py
+++ b/solution.py
@@ -56,18 +56,18 @@
 
 
 def first_kernel(place, leaf_ref, rhs_ref, inv_ref, off_ref, out_ref, *refs):
-    pieces, held, sems = refs[:3], refs[3], refs[4]
+    ends_ref, middle_ref, held, sems = refs
     copies = [
         pltpu.make_async_copy(rhs_ref.at[place[a] - 1], held.at[a], sems.at[a]) for a in range(4)
     ]
     at = pl.ds(pl.multiple_of(place[8] * 32, 32), 32)
-    for level, piece in enumerate(pieces):
+    for level, (piece, start) in enumerate(((ends_ref, 0), (middle_ref, 0), (ends_ref, 64))):
         node = place[level]
         for part, (ref, index) in enumerate(((inv_ref, node - 1), (off_ref, node - 2))):
             copies.append(
                 pltpu.make_async_copy(
                     ref.at[index, at, :],
-                    piece.at[pl.ds(part * 32, 32), :],
+                    piece.at[pl.ds(start + part * 32, 32), :],
                     sems.at[len(copies)],
                 )
             )
@@ -98,29 +98,32 @@
 
 
 def first_payload(place, rhs_leaf, rhs_top, inv_top, off_top):
-    piece = jax.ShapeDtypeStruct((64, 1024), BF)
     return pl.pallas_call(
         first_kernel,
-        out_shape=(jax.ShapeDtypeStruct((FRONTS, 80, 256), BF), piece, piece, piece),
+        out_shape=(
+            jax.ShapeDtypeStruct((FRONTS, 80, 256), BF),
+            jax.ShapeDtypeStruct((128, 1024), BF),
+            jax.ShapeDtypeStruct((64, 1024), BF),
+        ),
         in_specs=[SMEM, VMEM, HBM, HBM, HBM],
-        out_specs=(VMEM,) * 4,
+        out_specs=(VMEM,) * 3,
         scratch_shapes=[pltpu.VMEM((4, 64, 256), F32), pltpu.SemaphoreType.DMA((10,))],
         compiler_params=params(60),
     )(place, rhs_leaf, rhs_top, inv_top, off_top)
 
 
-def stack_kernel(*refs):
-    at = 0
-    for ref in refs[:-1]:
-        rows = ref.shape[0]
-        refs[-1][at : at + rows, :] = ref[...]
-        at += rows
-
-
-def stack(parts):
-    rows = sum(part.shape[0] for part in parts)
+def stack_kernel(start, *refs):
+    for k, ref in enumerate(refs[:-1]):
+        refs[-1][k * 64 : (k + 1) * 64, :] = ref[start : start + 64, :]
+
+
+def stack(parts, start):
+    rows = 64 * len(parts)
     return call(
-        stack_kernel, jax.ShapeDtypeStruct((rows, 1024), BF), [VMEM] * len(parts), tuple(parts)
+        functools.partial(stack_kernel, start),
+        jax.ShapeDtypeStruct((rows, 1024), BF),
+        [VMEM] * len(parts),
+        tuple(parts),
     )
 
 
@@ -136,6 +139,12 @@
 def near(block, axis):
     dx, dy = step_of(axis)
     return turn(block, dx, dy), turn(block, -dx, -dy)
+
+
+def around(block, axis):
+    dx, dy = step_of(axis)
+    opposite = turn(block, 2 * dx, 2 * dy)
+    return (block, *near(block, axis), opposite)
 
 
 def far(pair, axis):
@@ -296,30 +305,30 @@
     off_top = jnp.swapaxes(off_top, 1, 2)
     off_leaf = jnp.swapaxes(off_leaf, 1, 2)
 
-    sent, third, second, lowest = first_payload(place, rhs_leaf, rhs_top, inv_top, off_top)
+    sent, ends, middle = first_payload(place, rhs_leaf, rhs_top, inv_top, off_top)
     first = lax.all_to_all(sent, "front", 0, 0)
-    third_near, second_near, lowest_near = near(third, "y"), near(second, "x"), near(lowest, "y")
-    third = (third, *third_near, *far(third_near, "y"))
-    second = (second, *second_near, *far(second_near, "x"))
-    lowest = (lowest, *lowest_near, *far(lowest_near, "y"))
+    ends, middle = around(ends, "y"), around(middle, "x")
     leaf_x, sent = call(
         leaf_solve_kernel,
         (jax.ShapeDtypeStruct((64, 256), F32), jax.ShapeDtypeStruct((FRONTS, 16, 1024), BF)),
         [VMEM] * 3,
         (inv_leaf, first, off_leaf),
     )
-    sent, third, second, lowest = lax.optimization_barrier((sent, third, second, lowest))
+    sent, ends, middle = lax.optimization_barrier((sent, ends, middle))
     got = lax.all_to_all(sent, "front", 0, 0)
-    third, second = stack(third), stack(second)
+    third, second, lowest = stack(ends, 0), stack(middle, 0), stack(ends, 64)
     third_near, second_near = near(third, "x"), near(second, "y")
+    third_far, second_far = far(third_near, "x"), far(second_near, "y")
+    got, third_far, second_far, lowest = lax.optimization_barrier(
+        (got, third_far, second_far, lowest)
+    )
+    lowest_near = near(lowest, "x")
     state = call(
         leaf_update_kernel,
         jax.ShapeDtypeStruct((64, 1024), F32),
         [SMEM] + [VMEM] * 3,
         (place, first, got, idx_leaf),
     )
-    state, third_near, second_near = lax.optimization_barrier((state, third_near, second_near))
-    third_far, second_far = far(third_near, "x"), far(second_near, "y")
     other = swap(state, core_pairs())
     ships = []
     for level in range(3):
@@ -330,10 +339,6 @@
         else:
             parts = (lowest, *lowest_near, *lowest_far)
         ux, rest = top_solve(state, other, [part.reshape(-1, 64, 1024) for part in parts])
-        if level == 0:
-            ux, lowest, second_far = lax.optimization_barrier((ux, lowest, second_far))
-            lowest = stack(lowest)
-            lowest_near = near(lowest, "x")
         ux_other = swap(ux, core_pairs())
         state = call(
             functools.partial(update_kernel, level),

time: 142 us -> 138 us (0.972)
  blocking collectives: 13.4 us -> 0 us
  local copies, waits for them, and re-layouts: 1.74 us -> 6.65 us
  waiting for transfers between devices: 46.6 us -> 50.3 us
  Pallas kernels: 20.3 us -> 22.8 us
  starting transfers between devices: 58.3 us -> 56.6 us
    all_to_all x1 -> x0, blocking collectives: 13.4 us -> none  [local(): got = lax.all_to_all(sent, 'front', 0, 0)]
    ppermute x24 -> x18, waiting for transfers between devices: 17.4 us -> 27.9 us  [turn(): return lax.ppermute(block, 'front', route)]
    ppermute x7, waiting for transfers between devices: 16.5 us -> 9.63 us  [swap(): return lax.ppermute(block, 'leaf', pairs)]
    ppermute x24 -> x18, starting transfers between devices: 36.1 us -> 29.4 us  [turn(): return lax.ppermute(block, 'front', route)]
    all_to_all x1 -> x2, starting transfers between devices: 5.54 us -> 10.4 us  [local(): got = lax.all_to_all(sent, 'front', 0, 0)]
    slice x12 -> x6, local copies, waits for them, and re-layouts: 0.14 us -> 4.86 us  [far(): return (turn(after[:half], -dx, -dy), turn(before[half:], dx, dy))]
    pallas_call x16, Pallas kernels: 17 us -> 19.5 us  [call(): pl.pallas_call(kernel, out_shape=outs, in_specs=specs, out_specs=tuple((V...]
    all_to_all x1 -> x2, waiting for transfers between devices: 12.6 us -> 12.7 us  [local(): got = lax.all_to_all(sent, 'front', 0, 0)]
  transfers between devices with their start and end apart: 33 -> 28, of which waited for: 14 -> 15; matrix products, arithmetic and copies ran while one was open for 1% -> 4% of each run, Pallas kernels for 9% -> 9%
where the time goes in v6:
time: 138 us; the launch traced here: 137 us
  starting transfers between devices  56.6 us (41%)
  waiting for transfers between devices  50.3 us (36%)
  Pallas kernels  22.8 us (17%)
  local copies, waits for them, and re-layouts  6.65 us (5%)
    ppermute x18, starting transfers between devices, turn(): return lax.ppermute(block, 'front', route)  29.4 us
    ppermute x18, waiting for transfers between devices, turn(): return lax.ppermute(block, 'front', route)  27.9 us
    pallas_call x16, Pallas kernels, call(): pl.pallas_call(kernel, out_shape=outs, in_specs=specs, out_specs=tuple((V...  19.5 us
    all_to_all x2, waiting for transfers between devices, local(): got = lax.all_to_all(sent, 'front', 0, 0)  12.7 us
    all_to_all x2, starting transfers between devices, local(): got = lax.all_to_all(sent, 'front', 0, 0)  10.4 us
    ppermute x7, waiting for transfers between devices, swap(): return lax.ppermute(block, 'leaf', pairs)  9.63 us
    ppermute x7, starting transfers between devices, swap(): return lax.ppermute(block, 'leaf', pairs)  9.63 us
    all_to_all x1, starting transfers between devices, local(): first = lax.all_to_all(sent, 'front', 0, 0)  7.18 us
  transfers between devices with their start and end apart: 28, of which 15 were waited for; matrix products, arithmetic and copies ran while one was open for 4% of the time, Pallas kernels for 9%

profile of v6, /device:TPU:32, one launch (start us, length us, event | category | flops | bytes accessed | tf_op | source)
XLA Modules:
  0.0 137.2 jit_solution(2989896831970970537)
XLA Ops:
  1.3 3.3 %shard_map.95 = (bf16[16,80,256]{2,1,0:T(8,128)(2,1)}, bf16[128,1024]{1,0:T(8,128)(2,1)}, bf16[64,1024]{1,0:T(8,128)(2,1)}) custom-call(s32[12]{0:T(128)} %stack.48.place, f32[1,64,256]{2,1,0:T(8,128)} %leaf_ref.1, f32[15,64,256]{2,1,0:T(8,128)} %rhs_ref.1, bf16[15,64,1024]{2,1,0:T(8,128)(2,1)} %inv_ref.2, bf16[14,64,1024]{2,1,0:T(8,128)(2,1)} %bitcast.40), custom_call_target="tpu_custom_call" | custom-call | tf_op jit(solution)/shard_map/pallas_call | solution.py:101
  4.7 7.2 %all-to-all-start = ((bf16[16,80,256]{2,1,0:T(8,128)(2,1)}), bf16[16,80,256]{2,1,0:T(8,128)(2,1)S(1)}, u32[]{:S(2)}, u32[]{:S(2)}) async-start(bf16[16,80,256]{2,1,0:T(8,128)(2,1)} %get-tuple-element.31), calls=%async_computation | async-start | bytes 1310720 | tf_op jit(solution)/shard_map/all_to_all | solution.py:309
  11.9 3.4 %collective-permute-start.5 = (bf16[64,1024]{1,0:T(8,128)(2,1)}, bf16[64,1024]{1,0:T(8,128)(2,1)S(1)}, u32[]{:S(2)}, u32[]{:S(2)}) collective-permute-start(bf16[64,1024]{1,0:T(8,128)(2,1)} %get-tuple-element.41.refs_0_), channel_id=1, source_target_pairs={{0,8},{1,9},{2,10},{3,11},{4,12},{5,13},{6,14},{7,15},{8,0},{9,1},... | collective-permute-start | bytes 393224 | tf_op jit(solution)/shard_map/ppermute | solution.py:132
  15.3 3.0 %collective-permute-start.2 = (bf16[128,1024]{1,0:T(8,128)(2,1)}, bf16[128,1024]{1,0:T(8,128)(2,1)S(1)}, u32[]{:S(2)}, u32[]{:S(2)}) collective-permute-start(bf16[128,1024]{1,0:T(8,128)(2,1)} %get-tuple-element.37.refs_0_), channel_id=1, source_target_pairs={{0,2},{1,3},{2,0},{3,1},{4,6},{5,7},{6,4},{7,5},{8,10},{9,11},{10,... | collective-permute-start | bytes 786440 | tf_op jit(solution)/shard_map/ppermute | solution.py:132
  21.5 4.0 %collective-permute-done.5.refs_3_ = bf16[64,1024]{1,0:T(8,128)(2,1)S(1)} collective-permute-done((bf16[64,1024]{1,0:T(8,128)(2,1)}, bf16[64,1024]{1,0:T(8,128)(2,1)S(1)}, u32[]{:S(2)}, u32[]{:S(2)}) %collective-permute-start.5) | collective-permute-done | bytes 131104 | tf_op jit(solution)/shard_map/ppermute | solution.py:132
  25.5 2.0 %collective-permute-start.3 = (bf16[64,1024]{1,0:T(8,128)(2,1)}, bf16[64,1024]{1,0:T(8,128)(2,1)S(1)}, u32[]{:S(2)}, u32[]{:S(2)}) collective-permute-start(bf16[64,1024]{1,0:T(8,128)(2,1)} %get-tuple-element.41.refs_0_), channel_id=1, source_target_pairs={{0,4},{1,5},{2,6},{3,7},{4,8},{5,9},{6,10},{7,11},{8,12},{9,13},{1... | collective-permute-start | bytes 393224 | tf_op jit(solution)/shard_map/ppermute | solution.py:132
  28.5 3.4 %collective-permute-done.3.refs_1_ = bf16[64,1024]{1,0:T(8,128)(2,1)S(1)} collective-permute-done((bf16[64,1024]{1,0:T(8,128)(2,1)}, bf16[64,1024]{1,0:T(8,128)(2,1)S(1)}, u32[]{:S(2)}, u32[]{:S(2)}) %collective-permute-start.3) | collective-permute-done | bytes 131104 | tf_op jit(solution)/shard_map/ppermute | solution.py:132
  31.9 1.7 %collective-permute-done.1.refs_2_ = bf16[128,1024]{1,0:T(8,128)(2,1)S(1)} collective-permute-done((bf16[128,1024]{1,0:T(8,128)(2,1)}, bf16[128,1024]{1,0:T(8,128)(2,1)S(1)}, u32[]{:S(2)}, u32[]{:S(2)}) %collective-permute-start.1) | collective-permute-done | bytes 262176 | tf_op jit(solution)/shard_map/ppermute | solution.py:132
  35.5 2.3 %collective-permute-start.6 = (bf16[256,1024]{1,0:T(8,128)(2,1)S(1)}, bf16[256,1024]{1,0:T(8,128)(2,1)}, u32[]{:S(2)}, u32[]{:S(2)}) collective-permute-start(bf16[256,1024]{1,0:T(8,128)(2,1)S(1)} %shard_map.97), channel_id=1, source_target_pairs={{0,12},{1,13},{2,14},{3,15},{4,0},{5,1},{6,2},{7,3},{8,4},{9,5},{1... | collective-permute-start | bytes 1572872 | tf_op jit(solution)/shard_map/ppermute | solution.py:132
  38.9 2.3 %collective-permute-start.10 = (bf16[256,1024]{1,0:T(8,128)(2,1)S(1)}, bf16[256,1024]{1,0:T(8,128)(2,1)S(1)}, u32[]{:S(2)}, u32[]{:S(2)}) collective-permute-start(bf16[256,1024]{1,0:T(8,128)(2,1)S(1)} %shard_map.98), channel_id=1, source_target_pairs={{0,3},{1,0},{2,1},{3,2},{4,7},{5,4},{6,5},{7,6},{8,11},{9,8},{10,9... | collective-permute-start | bytes 1572872 | tf_op jit(solution)/shard_map/ppermute | solution.py:132
  41.2 3.6 %all-to-all-start.1 = ((bf16[16,16,1024]{2,1,0:T(8,128)(2,1)}), bf16[16,16,1024]{2,1,0:T(8,128)(2,1)S(1)}, u32[]{:S(2)}, u32[]{:S(2)}) async-start(bf16[16,16,1024]{2,1,0:T(8,128)(2,1)} %copy-done.10), calls=%async_computation.1 | async-start | bytes 1048576 | tf_op jit(solution)/shard_map/all_to_all | solution.py:318
  44.8 6.6 %collective-permute-done.8 = bf16[256,1024]{1,0:T(8,128)(2,1)} collective-permute-done((bf16[256,1024]{1,0:T(8,128)(2,1)S(1)}, bf16[256,1024]{1,0:T(8,128)(2,1)}, u32[]{:S(2)}, u32[]{:S(2)}) %collective-permute-start.8) | collective-permute-done | bytes 524320 | tf_op jit(solution)/shard_map/ppermute | solution.py:132
  51.4 1.7 %slice.29 = bf16[128,1024]{1,0:T(8,128)(2,1)} slice(bf16[256,1024]{1,0:T(8,128)(2,1)} %collective-permute-done.8), slice={[128:256], [0:1024]} | slice | bytes 524288 | tf_op jit(solution)/shard_map/slice | solution.py:154
  53.1 1.7 %slice.28 = bf16[128,1024]{1,0:T(8,128)(2,1)} slice(bf16[256,1024]{1,0:T(8,128)(2,1)} %collective-permute-done.6), slice={[0:128], [0:1024]} | slice | bytes 524288 | tf_op jit(solution)/shard_map/slice | solution.py:154
  54.7 3.7 %collective-permute-start.7 = (bf16[128,1024]{1,0:T(8,128)(2,1)}, bf16[128,1024]{1,0:T(8,128)(2,1)}, u32[]{:S(2)}, u32[]{:S(2)}) collective-permute-start(bf16[128,1024]{1,0:T(8,128)(2,1)} %slice.28), channel_id=1, source_target_pairs={{0,12},{1,13},{2,14},{3,15},{4,0},{5,1},{6,2},{7,3},{8,4},{9,5},{1... | collective-permute-start | bytes 786440 | tf_op jit(solution)/shard_map/ppermute | solution.py:132
  61.0 2.3 %collective-permute-start.11 = (bf16[128,1024]{1,0:T(8,128)(2,1)}, bf16[128,1024]{1,0:T(8,128)(2,1)}, u32[]{:S(2)}, u32[]{:S(2)}) collective-permute-start(bf16[128,1024]{1,0:T(8,128)(2,1)} %slice.30), channel_id=1, source_target_pairs={{0,3},{1,0},{2,1},{3,2},{4,7},{5,4},{6,5},{7,6},{8,11},{9,8},{10,9... | collective-permute-start | bytes 786440 | tf_op jit(solution)/shard_map/ppermute | solution.py:132
  63.4 3.7 %collective-permute-done.13 = bf16[128,1024]{1,0:T(8,128)(2,1)} collective-permute-done((bf16[128,1024]{1,0:T(8,128)(2,1)}, bf16[128,1024]{1,0:T(8,128)(2,1)}, u32[]{:S(2)}, u32[]{:S(2)}) %collective-permute-start.13) | collective-permute-done | bytes 262176 | tf_op jit(solution)/shard_map/ppermute | solution.py:132
  67.7 3.1 %shard_map.100.own_ref = f32[64,1024]{1,0:T(8,128)S(1)} custom-call(s32[12]{0:T(128)S(1)} %copy-done.14, bf16[16,80,256]{2,1,0:T(8,128)(2,1)S(1)} %all-to-all-done.rhs_ref.first_ref, bf16[16,16,1024]{2,1,0:T(8,128)(2,1)S(1)} %all-to-all-done.1.got_ref, s32[1,1024]{1,0:T(1,128)S(1)} %copy-done.15), custom_call_target="tpu_custom_call" | custom-call | flops 100000000 | bytes 1000000 | tf_op jit(solution)/shard_map/pallas_call | solution.py:46
  71.0 2.0 %collective-permute-start.17 = (bf16[256,1024]{1,0:T(8,128)(2,1)S(1)}, bf16[256,1024]{1,0:T(8,128)(2,1)S(1)}, u32[]{:S(2)}, u32[]{:S(2)}) collective-permute-start(bf16[256,1024]{1,0:T(8,128)(2,1)S(1)} %shard_map.99), channel_id=1, source_target_pairs={{0,4},{1,5},{2,6},{3,7},{4,8},{5,9},{6,10},{7,11},{8,12},{9,13},{1... | collective-permute-start | bytes 1572872 | tf_op jit(solution)/shard_map/ppermute | solution.py:132
  73.0 2.5 %shard_map.101 = (f32[16,1536]{1,0:T(8,128)S(1)}, f32[48,1024]{1,0:T(8,128)S(1)}) custom-call(f32[64,1024]{1,0:T(8,128)S(1)} %shard_map.100.own_ref, f32[64,1024]{1,0:T(8,128)S(1)} %collective-permute-done.14.other_ref, bf16[4,64,1024]{2,1,0:T(8,128)(2,1)S(1)} %bitcast.30, bf16[4,64,1024]{2,1,0:T(8,128)(2,1)} %bitcast.15.refs_1_, ...), custom_call_target="tpu_custom_call" | custom-call | flops 100000000 | bytes 1000000 | tf_op jit(solution)/shard_map/pallas_call | solution.py:46
  75.6 1.3 collective-permute-done.15.other_ref
  76.9 2.4 %shard_map.102.own_ref = f32[48,1024]{1,0:T(8,128)S(1)} custom-call(s32[12]{0:T(128)S(1)} %copy-done.14, f32[16,1536]{1,0:T(8,128)S(1)} %get-tuple-element.48.own_ref, f32[16,1536]{1,0:T(8,128)S(1)} %collective-permute-done.15.other_ref, f32[48,1024]{1,0:T(8,128)S(1)} %get-tuple-element.49.rest_ref, s32[14,1024]{1,0:T(8,128)S(1)} %copy-done.9), custom_call_target="tpu_custom_call" | custom-call | flops 100000000 | bytes 1000000 | tf_op jit(solution)/shard_map/pallas_call | solution.py:46
  79.4 5.8 %collective-permute-done.18 = bf16[256,1024]{1,0:T(8,128)(2,1)S(1)} collective-permute-done((bf16[256,1024]{1,0:T(8,128)(2,1)S(1)}, bf16[256,1024]{1,0:T(8,128)(2,1)S(1)}, u32[]{:S(2)}, u32[]{:S(2)}) %collective-permute-start.18) | collective-permute-done | bytes 524320 | tf_op jit(solution)/shard_map/ppermute | solution.py:132
  88.6 2.1 %shard_map.103 = (f32[16,1536]{1,0:T(8,128)S(1)}, f32[32,1024]{1,0:T(8,128)S(1)}) custom-call(f32[48,1024]{1,0:T(8,128)S(1)} %shard_map.102.own_ref, f32[48,1024]{1,0:T(8,128)S(1)} %collective-permute-done.16.other_ref, bf16[4,64,1024]{2,1,0:T(8,128)(2,1)S(1)} %bitcast.31, bf16[4,64,1024]{2,1,0:T(8,128)(2,1)S(1)} %bitcast.33, ...), custom_call_target="tpu_custom_call" | custom-call | flops 100000000 | bytes 1000000 | tf_op jit(solution)/shard_map/pallas_call | solution.py:46
  90.8 1.3 collective-permute-done.19.other_ref
  92.1 1.8 %shard_map.104.own_ref = f32[32,1024]{1,0:T(8,128)S(1)} custom-call(s32[12]{0:T(128)S(1)} %copy-done.14, f32[16,1536]{1,0:T(8,128)S(1)} %get-tuple-element.54.own_ref, f32[16,1536]{1,0:T(8,128)S(1)} %collective-permute-done.19.other_ref, f32[32,1024]{1,0:T(8,128)S(1)} %get-tuple-element.55.rest_ref, s32[14,1024]{1,0:T(8,128)S(1)} %copy-done.9), custom_call_target="tpu_custom_call" | custom-call | flops 100000000 | bytes 1000000 | tf_op jit(solution)/shard_map/pallas_call | solution.py:46
  93.9 3.3 %collective-permute-start.20 = (f32[32,1024]{1,0:T(8,128)S(1)}, f32[32,1024]{1,0:T(8,128)S(1)}, u32[]{:S(2)}, u32[]{:S(2)}) collective-permute-start(f32[32,1024]{1,0:T(8,128)S(1)} %shard_map.104.own_ref), channel_id=1, source_target_pairs={{0,64},{16,80},{32,96},{48,112},{64,0},{80,16},{96,32},{112,48},{1... | collective-permute-start | bytes 393224 | tf_op jit(solution)/shard_map/ppermute | solution.py:277
  97.2 5.4 %collective-permute-done.20.other_ref = f32[32,1024]{1,0:T(8,128)S(1)} collective-permute-done((f32[32,1024]{1,0:T(8,128)S(1)}, f32[32,1024]{1,0:T(8,128)S(1)}, u32[]{:S(2)}, u32[]{:S(2)}) %collective-permute-start.20) | collective-permute-done | bytes 131104 | tf_op jit(solution)/shard_map/ppermute | solution.py:277
  103.8 1.3 collective-permute-done.23.other_ref
  106.3 6.0 %collective-permute-start.24 = (f32[16,1024]{1,0:T(8,128)S(1)}, f32[16,1024]{1,0:T(8,128)S(1)}, u32[]{:S(2)}, u32[]{:S(2)}) collective-permute-start(f32[16,1024]{1,0:T(8,128)S(1)} %shard_map.106.own_ref), channel_id=1, source_target_pairs={{0,192},{16,208},{32,224},{48,240},{64,128},{80,144},{96,160},{112... | collective-permute-start | bytes 196616 | tf_op jit(solution)/shard_map/ppermute | solution.py:277
  115.7 6.8 %all-to-all-start.2 = ((bf16[16,16,1408]{2,1,0:T(8,128)(2,1)}), bf16[16,16,1408]{2,1,0:T(8,128)(2,1)S(1)}, u32[]{:S(2)}, u32[]{:S(2)}) async-start(bf16[16,16,1408]{2,1,0:T(8,128)(2,1)} %shard_map.110), calls=%async_computation.2 | async-start | bytes 1441792 | tf_op jit(solution)/shard_map/all_to_all | solution.py:367
  123.5 12.7 %all-to-all-done.2.got_ref = bf16[16,16,1408]{2,1,0:T(8,128)(2,1)S(1)} async-done(((bf16[16,16,1408]{2,1,0:T(8,128)(2,1)}), bf16[16,16,1408]{2,1,0:T(8,128)(2,1)S(1)}, u32[]{:S(2)}, u32[]{:S(2)}) %all-to-all-start.2) | async-done | bytes 720928 | tf_op jit(solution)/shard_map/all_to_all | solution.py:367
  (81 shorter events, 22.5 us)
Async XLA Ops:
  1.3 26.2 %copy-start.11 = (bf16[1,64,1024]{2,1,0:T(8,128)(2,1)S(1)}, bf16[1,64,1024]{2,1,0:T(8,128)(2,1)}, u32[]{:S(2)}) copy-start(bf16[1,64,1024]{2,1,0:T(8,128)(2,1)} %inv_ref.3) | copy-start | bytes 393220
  1.3 26.2 %copy-start.12 = (bf16[1,1024,64]{1,2,0:T(8,128)(2,1)S(1)}, bf16[1,1024,64]{1,2,0:T(8,128)(2,1)}, u32[]{:S(2)}) copy-start(bf16[1,1024,64]{1,2,0:T(8,128)(2,1)} %param.12) | copy-start | bytes 393220
  4.7 29.8 %copy-start.2 = (bf16[128,1024]{1,0:T(8,128)(2,1)S(1)}, bf16[128,1024]{1,0:T(8,128)(2,1)}, u32[]{:S(2)}) copy-start(bf16[128,1024]{1,0:T(8,128)(2,1)} %get-tuple-element.37.refs_0_) | copy-start | bytes 786436
  4.7 33.2 %copy-start.13 = (bf16[64,1024]{1,0:T(8,128)(2,1)S(1)}, bf16[64,1024]{1,0:T(8,128)(2,1)}, u32[]{:S(2)}) copy-start(bf16[64,1024]{1,0:T(8,128)(2,1)} %get-tuple-element.41.refs_0_) | copy-start | bytes 393220
  4.7 22.8 %all-to-all-start = ((bf16[16,80,256]{2,1,0:T(8,128)(2,1)}), bf16[16,80,256]{2,1,0:T(8,128)(2,1)S(1)}, u32[]{:S(2)}, u32[]{:S(2)}) async-start(bf16[16,80,256]{2,1,0:T(8,128)(2,1)} %get-tuple-element.31), calls=%async_computation | async-start | bytes 1310720 | tf_op jit(solution)/shard_map/all_to_all | solution.py:309
  11.9 13.6 %collective-permute-start.5 = (bf16[64,1024]{1,0:T(8,128)(2,1)}, bf16[64,1024]{1,0:T(8,128)(2,1)S(1)}, u32[]{:S(2)}, u32[]{:S(2)}) collective-permute-start(bf16[64,1024]{1,0:T(8,128)(2,1)} %get-tuple-element.41.refs_0_), channel_id=1, source_target_pairs={{0,8},{1,9},{2,10},{3,11},{4,12},{5,13},{6,14},{7,15},{8,0},{9,1},... | collective-permute-start | bytes 393224 | tf_op jit(solution)/shard_map/ppermute | solution.py:132
  15.3 16.6 %collective-permute-start.2 = (bf16[128,1024]{1,0:T(8,128)(2,1)}, bf16[128,1024]{1,0:T(8,128)(2,1)S(1)}, u32[]{:S(2)}, u32[]{:S(2)}) collective-permute-start(bf16[128,1024]{1,0:T(8,128)(2,1)} %get-tuple-element.37.refs_0_), channel_id=1, source_target_pairs={{0,2},{1,3},{2,0},{3,1},{4,6},{5,7},{6,4},{7,5},{8,10},{9,11},{10,... | collective-permute-start | bytes 786440 | tf_op jit(solution)/shard_map/ppermute | solution.py:132
  18.3 15.3 %collective-permute-start.1 = (bf16[128,1024]{1,0:T(8,128)(2,1)}, bf16[128,1024]{1,0:T(8,128)(2,1)S(1)}, u32[]{:S(2)}, u32[]{:S(2)}) collective-permute-start(bf16[128,1024]{1,0:T(8,128)(2,1)} %get-tuple-element.37.refs_0_), channel_id=1, source_target_pairs={{0,3},{1,0},{2,1},{3,2},{4,7},{5,4},{6,5},{7,6},{8,11},{9,8},{10,9... | collective-permute-start | bytes 786440 | tf_op jit(solution)/shard_map/ppermute | solution.py:132
  19.5 15.0 %collective-permute-start = (bf16[128,1024]{1,0:T(8,128)(2,1)}, bf16[128,1024]{1,0:T(8,128)(2,1)S(1)}, u32[]{:S(2)}, u32[]{:S(2)}) collective-permute-start(bf16[128,1024]{1,0:T(8,128)(2,1)} %get-tuple-element.37.refs_0_), channel_id=1, source_target_pairs={{0,1},{1,2},{2,3},{3,0},{4,5},{5,6},{6,7},{7,4},{8,9},{9,10},{10,1... | collective-permute-start | bytes 786440 | tf_op jit(solution)/shard_map/ppermute | solution.py:132
  20.3 8.1 %collective-permute-start.4 = (bf16[64,1024]{1,0:T(8,128)(2,1)}, bf16[64,1024]{1,0:T(8,128)(2,1)S(1)}, u32[]{:S(2)}, u32[]{:S(2)}) collective-permute-start(bf16[64,1024]{1,0:T(8,128)(2,1)} %get-tuple-element.41.refs_0_), channel_id=1, source_target_pairs={{0,12},{1,13},{2,14},{3,15},{4,0},{5,1},{6,2},{7,3},{8,4},{9,5},{1... | collective-permute-start | bytes 393224 | tf_op jit(solution)/shard_map/ppermute | solution.py:132
  25.5 6.4 %collective-permute-start.3 = (bf16[64,1024]{1,0:T(8,128)(2,1)}, bf16[64,1024]{1,0:T(8,128)(2,1)S(1)}, u32[]{:S(2)}, u32[]{:S(2)}) collective-permute-start(bf16[64,1024]{1,0:T(8,128)(2,1)} %get-tuple-element.41.refs_0_), channel_id=1, source_target_pairs={{0,4},{1,5},{2,6},{3,7},{4,8},{5,9},{6,10},{7,11},{8,12},{9,13},{1... | collective-permute-start | bytes 393224 | tf_op jit(solution)/shard_map/ppermute | solution.py:132
  34.5 16.9 %collective-permute-start.8 = (bf16[256,1024]{1,0:T(8,128)(2,1)S(1)}, bf16[256,1024]{1,0:T(8,128)(2,1)}, u32[]{:S(2)}, u32[]{:S(2)}) collective-permute-start(bf16[256,1024]{1,0:T(8,128)(2,1)S(1)} %shard_map.97), channel_id=1, source_target_pairs={{0,4},{1,5},{2,6},{3,7},{4,8},{5,9},{6,10},{7,11},{8,12},{9,13},{1... | collective-permute-start | bytes 1572872 | tf_op jit(solution)/shard_map/ppermute | solution.py:132
  35.5 17.6 %collective-permute-start.6 = (bf16[256,1024]{1,0:T(8,128)(2,1)S(1)}, bf16[256,1024]{1,0:T(8,128)(2,1)}, u32[]{:S(2)}, u32[]{:S(2)}) collective-permute-start(bf16[256,1024]{1,0:T(8,128)(2,1)S(1)} %shard_map.97), channel_id=1, source_target_pairs={{0,12},{1,13},{2,14},{3,15},{4,0},{5,1},{6,2},{7,3},{8,4},{9,5},{1... | collective-permute-start | bytes 1572872 | tf_op jit(solution)/shard_map/ppermute | solution.py:132
  37.9 20.6 %collective-permute-start.12 = (bf16[256,1024]{1,0:T(8,128)(2,1)S(1)}, bf16[256,1024]{1,0:T(8,128)(2,1)S(1)}, u32[]{:S(2)}, u32[]{:S(2)}) collective-permute-start(bf16[256,1024]{1,0:T(8,128)(2,1)S(1)} %shard_map.98), channel_id=1, source_target_pairs={{0,1},{1,2},{2,3},{3,0},{4,5},{5,6},{6,7},{7,4},{8,9},{9,10},{10,1... | collective-permute-start | bytes 1572872 | tf_op jit(solution)/shard_map/ppermute | solution.py:132
  38.9 21.2 %collective-permute-start.10 = (bf16[256,1024]{1,0:T(8,128)(2,1)S(1)}, bf16[256,1024]{1,0:T(8,128)(2,1)S(1)}, u32[]{:S(2)}, u32[]{:S(2)}) collective-permute-start(bf16[256,1024]{1,0:T(8,128)(2,1)S(1)} %shard_map.98), channel_id=1, source_target_pairs={{0,3},{1,0},{2,1},{3,2},{4,7},{5,4},{6,5},{7,6},{8,11},{9,8},{10,9... | collective-permute-start | bytes 1572872 | tf_op jit(solution)/shard_map/ppermute | solution.py:132
  41.2 22.1 %all-to-all-start.1 = ((bf16[16,16,1024]{2,1,0:T(8,128)(2,1)}), bf16[16,16,1024]{2,1,0:T(8,128)(2,1)S(1)}, u32[]{:S(2)}, u32[]{:S(2)}) async-start(bf16[16,16,1024]{2,1,0:T(8,128)(2,1)} %copy-done.10), calls=%async_computation.1 | async-start | bytes 1048576 | tf_op jit(solution)/shard_map/all_to_all | solution.py:318
  53.1 10.3 %collective-permute-start.9 = (bf16[128,1024]{1,0:T(8,128)(2,1)}, bf16[128,1024]{1,0:T(8,128)(2,1)}, u32[]{:S(2)}, u32[]{:S(2)}) collective-permute-start(bf16[128,1024]{1,0:T(8,128)(2,1)} %slice.29), channel_id=1, source_target_pairs={{0,4},{1,5},{2,6},{3,7},{4,8},{5,9},{6,10},{7,11},{8,12},{9,13},{1... | collective-permute-start | bytes 786440 | tf_op jit(solution)/shard_map/ppermute | solution.py:132
  54.7 8.6 %collective-permute-start.7 = (bf16[128,1024]{1,0:T(8,128)(2,1)}, bf16[128,1024]{1,0:T(8,128)(2,1)}, u32[]{:S(2)}, u32[]{:S(2)}) collective-permute-start(bf16[128,1024]{1,0:T(8,128)(2,1)} %slice.28), channel_id=1, source_target_pairs={{0,12},{1,13},{2,14},{3,15},{4,0},{5,1},{6,2},{7,3},{8,4},{9,5},{1... | collective-permute-start | bytes 786440 | tf_op jit(solution)/shard_map/ppermute | solution.py:132
  59.2 7.9 %collective-permute-start.13 = (bf16[128,1024]{1,0:T(8,128)(2,1)}, bf16[128,1024]{1,0:T(8,128)(2,1)}, u32[]{:S(2)}, u32[]{:S(2)}) collective-permute-start(bf16[128,1024]{1,0:T(8,128)(2,1)} %slice.31), channel_id=1, source_target_pairs={{0,1},{1,2},{2,3},{3,0},{4,5},{5,6},{6,7},{7,4},{8,9},{9,10},{10,1... | collective-permute-start | bytes 786440 | tf_op jit(solution)/shard_map/ppermute | solution.py:132
  61.0 6.7 %collective-permute-start.11 = (bf16[128,1024]{1,0:T(8,128)(2,1)}, bf16[128,1024]{1,0:T(8,128)(2,1)}, u32[]{:S(2)}, u32[]{:S(2)}) collective-permute-start(bf16[128,1024]{1,0:T(8,128)(2,1)} %slice.30), channel_id=1, source_target_pairs={{0,3},{1,0},{2,1},{3,2},{4,7},{5,4},{6,5},{7,6},{8,11},{9,8},{10,9... | collective-permute-start | bytes 786440 | tf_op jit(solution)/shard_map/ppermute | solution.py:132
  70.8 2.2 %collective-permute-start.14 = (f32[64,1024]{1,0:T(8,128)S(1)}, f32[64,1024]{1,0:T(8,128)S(1)}, u32[]{:S(2)}, u32[]{:S(2)}) collective-permute-start(f32[64,1024]{1,0:T(8,128)S(1)} %shard_map.100.own_ref), channel_id=1, source_target_pairs={{0,16},{16,0},{32,48},{48,32},{64,80},{80,64},{96,112},{112,96},{1... | collective-permute-start | bytes 786440 | tf_op jit(solution)/shard_map/ppermute | solution.py:277
  70.9 14.3 %collective-permute-start.18 = (bf16[256,1024]{1,0:T(8,128)(2,1)S(1)}, bf16[256,1024]{1,0:T(8,128)(2,1)S(1)}, u32[]{:S(2)}, u32[]{:S(2)}) collective-permute-start(bf16[256,1024]{1,0:T(8,128)(2,1)S(1)} %shard_map.99), channel_id=1, source_target_pairs={{0,12},{1,13},{2,14},{3,15},{4,0},{5,1},{6,2},{7,3},{8,4},{9,5},{1... | collective-permute-start | bytes 1572872 | tf_op jit(solution)/shard_map/ppermute | solution.py:132
  71.0 15.4 %collective-permute-start.17 = (bf16[256,1024]{1,0:T(8,128)(2,1)S(1)}, bf16[256,1024]{1,0:T(8,128)(2,1)S(1)}, u32[]{:S(2)}, u32[]{:S(2)}) collective-permute-start(bf16[256,1024]{1,0:T(8,128)(2,1)S(1)} %shard_map.99), channel_id=1, source_target_pairs={{0,4},{1,5},{2,6},{3,7},{4,8},{5,9},{6,10},{7,11},{8,12},{9,13},{1... | collective-permute-start | bytes 1572872 | tf_op jit(solution)/shard_map/ppermute | solution.py:132
  75.5 1.4 collective-permute-start.15
  79.3 7.1 %collective-permute-start.16 = (f32[48,1024]{1,0:T(8,128)S(1)}, f32[48,1024]{1,0:T(8,128)S(1)}, u32[]{:S(2)}, u32[]{:S(2)}) collective-permute-start(f32[48,1024]{1,0:T(8,128)S(1)} %shard_map.102.own_ref), channel_id=1, source_target_pairs={{0,32},{16,48},{32,0},{48,16},{64,96},{80,112},{96,64},{112,80},{1... | collective-permute-start | bytes 589832 | tf_op jit(solution)/shard_map/ppermute | solution.py:277
  86.5 16.1 %collective-permute-start.21 = (bf16[128,1024]{1,0:T(8,128)(2,1)S(1)}, bf16[128,1024]{1,0:T(8,128)(2,1)S(1)}, u32[]{:S(2)}, u32[]{:S(2)}) collective-permute-start(bf16[128,1024]{1,0:T(8,128)(2,1)S(1)} %slice.25), channel_id=1, source_target_pairs={{0,12},{1,13},{2,14},{3,15},{4,0},{5,1},{6,2},{7,3},{8,4},{9,5},{1... | collective-permute-start | bytes 786440 | tf_op jit(solution)/shard_map/ppermute | solution.py:132
  87.7 14.9 %collective-permute-start.22 = (bf16[128,1024]{1,0:T(8,128)(2,1)S(1)}, bf16[128,1024]{1,0:T(8,128)(2,1)S(1)}, u32[]{:S(2)}, u32[]{:S(2)}) collective-permute-start(bf16[128,1024]{1,0:T(8,128)(2,1)S(1)} %slice.26), channel_id=1, source_target_pairs={{0,4},{1,5},{2,6},{3,7},{4,8},{5,9},{6,10},{7,11},{8,12},{9,13},{1... | collective-permute-start | bytes 786440 | tf_op jit(solution)/shard_map/ppermute | solution.py:132
  90.7 1.3 collective-permute-start.19
  93.9 8.7 %collective-permute-start.20 = (f32[32,1024]{1,0:T(8,128)S(1)}, f32[32,1024]{1,0:T(8,128)S(1)}, u32[]{:S(2)}, u32[]{:S(2)}) collective-permute-start(f32[32,1024]{1,0:T(8,128)S(1)} %shard_map.104.own_ref), channel_id=1, source_target_pairs={{0,64},{16,80},{32,96},{48,112},{64,0},{80,16},{96,32},{112,48},{1... | collective-permute-start | bytes 393224 | tf_op jit(solution)/shard_map/ppermute | solution.py:277
  103.7 1.3 collective-permute-start.23
  106.3 8.5 %collective-permute-start.24 = (f32[16,1024]{1,0:T(8,128)S(1)}, f32[16,1024]{1,0:T(8,128)S(1)}, u32[]{:S(2)}, u32[]{:S(2)}) collective-permute-start(f32[16,1024]{1,0:T(8,128)S(1)} %shard_map.106.own_ref), channel_id=1, source_target_pairs={{0,192},{16,208},{32,224},{48,240},{64,128},{80,144},{96,160},{112... | collective-permute-start | bytes 196616 | tf_op jit(solution)/shard_map/ppermute | solution.py:277
  115.7 20.5 %all-to-all-start.2 = ((bf16[16,16,1408]{2,1,0:T(8,128)(2,1)}), bf16[16,16,1408]{2,1,0:T(8,128)(2,1)S(1)}, u32[]{:S(2)}, u32[]{:S(2)}) async-start(bf16[16,16,1408]{2,1,0:T(8,128)(2,1)} %shard_map.110), calls=%async_computation.2 | async-start | bytes 1441792 | tf_op jit(solution)/shard_map/all_to_all | solution.py:367
  (12 other events, 146.1 us)

commit v7 on v6

--- a/solution.py
+++ b/solution.py
@@ -56,12 +56,12 @@
 
 
 def first_kernel(place, leaf_ref, rhs_ref, inv_ref, off_ref, out_ref, *refs):
-    ends_ref, middle_ref, held, sems = refs
+    third_ref, pair_ref, held, sems = refs
     copies = [
         pltpu.make_async_copy(rhs_ref.at[place[a] - 1], held.at[a], sems.at[a]) for a in range(4)
     ]
     at = pl.ds(pl.multiple_of(place[8] * 32, 32), 32)
-    for level, (piece, start) in enumerate(((ends_ref, 0), (middle_ref, 0), (ends_ref, 64))):
+    for level, (piece, start) in enumerate(((third_ref, 0), (pair_ref, 0), (pair_ref, 64))):
         node = place[level]
         for part, (ref, index) in enumerate(((inv_ref, node - 1), (off_ref, node - 2))):
             copies.append(
@@ -102,8 +102,8 @@
         first_kernel,
         out_shape=(
             jax.ShapeDtypeStruct((FRONTS, 80, 256), BF),
+            jax.ShapeDtypeStruct((64, 1024), BF),
             jax.ShapeDtypeStruct((128, 1024), BF),
-            jax.ShapeDtypeStruct((64, 1024), BF),
         ),
         in_specs=[SMEM, VMEM, HBM, HBM, HBM],
         out_specs=(VMEM,) * 3,
@@ -112,19 +112,17 @@
     )(place, rhs_leaf, rhs_top, inv_top, off_top)
 
 
-def stack_kernel(start, *refs):
-    for k, ref in enumerate(refs[:-1]):
-        refs[-1][k * 64 : (k + 1) * 64, :] = ref[start : start + 64, :]
-
-
-def stack(parts, start):
-    rows = 64 * len(parts)
-    return call(
-        functools.partial(stack_kernel, start),
-        jax.ShapeDtypeStruct((rows, 1024), BF),
-        [VMEM] * len(parts),
-        tuple(parts),
-    )
+def stack_kernel(own_ref, before_ref, after_ref, second_ref, lowest_ref, *outs):
+    for level, (opposite_ref, out_ref) in enumerate(zip((second_ref, lowest_ref), outs)):
+        at = slice(level * 64, (level + 1) * 64)
+        for k, ref in enumerate((own_ref, before_ref, after_ref)):
+            out_ref[k * 64 : (k + 1) * 64, :] = ref[at, :]
+        out_ref[192:, :] = opposite_ref[...]
+
+
+def stack(parts):
+    piece = jax.ShapeDtypeStruct((256, 1024), BF)
+    return call(stack_kernel, (piece, piece), [VMEM] * 5, parts)
 
 
 def turn(block, dx, dy):
@@ -139,12 +137,6 @@
 def near(block, axis):
     dx, dy = step_of(axis)
     return turn(block, dx, dy), turn(block, -dx, -dy)
-
-
-def around(block, axis):
-    dx, dy = step_of(axis)
-    opposite = turn(block, 2 * dx, 2 * dy)
-    return (block, *near(block, axis), opposite)
 
 
 def far(pair, axis):
@@ -154,13 +146,15 @@
     return turn(after[:half], -dx, -dy), turn(before[half:], dx, dy)
 
 
-def leaf_solve_kernel(inv_ref, rhs_ref, off_ref, x_ref, out_ref):
+def leaf_solve_kernel(inv_ref, rhs_ref, off_ref, third_ref, x_ref, out_ref):
     right = rhs_ref[:, :64, :].reshape(1024, 256)
     x = nn(inv_ref[0], right)
     x_ref[...] = x
     xt = x.T.astype(BF)
     update = nn(xt, off_ref[0])
-    out_ref[...] = update.astype(BF).reshape(16, 16, 1024)
+    out_ref[:, :16, :] = update.astype(BF).reshape(16, 16, 1024)
+    for f in range(FRONTS):
+        out_ref[f, 16:, :] = third_ref[...]
 
 
 def push(update, idx, count):
@@ -181,7 +175,7 @@
 def leaf_update_kernel(place, first_ref, got_ref, idx_ref, out_ref):
     update = jnp.zeros((16, 1024), F32)
     for s in range(FRONTS):
-        update = update + got_ref[s].astype(F32)
+        update = update + got_ref[s, :16, :].astype(F32)
     pending = push(update, idx_ref[...], 4)
     high, low = [], []
     for g in range(FRONTS // 2):
@@ -200,7 +194,7 @@
         out_ref[a * 16 : (a + 1) * 16, :] = nn(put, high) + nn(put, low) - pending[a]
 
 
-def solve_kernel(own_ref, other_ref, *refs):
+def solve_kernel(start, own_ref, other_ref, *refs):
     weights, ux_ref, rest_ref = refs[:-2], refs[-2], refs[-1]
     total = own_ref[...] + other_ref[...]
     rest_ref[...] = total[16:]
@@ -210,8 +204,8 @@
     for ref in weights:
         blocks = ref.shape[0]
         rows = blocks * 32
-        x = nt(right, ref[:, :32, :].reshape(rows, 1024))
-        off = ref[:, 32:, :].reshape(rows, 1024)
+        x = nt(right, ref[:, start : start + 32, :].reshape(rows, 1024))
+        off = ref[:, start + 32 : start + 64, :].reshape(rows, 1024)
         update = update + nn(x.astype(BF), off)
         ux_ref[:, at : at + rows] = x
         at += rows
@@ -220,8 +214,9 @@
 
 def top_solve(own, other, weights):
     left = own.shape[0] - 16
+    start = weights[0].shape[1] - 64
     return call(
-        solve_kernel,
+        functools.partial(solve_kernel, start),
         (jax.ShapeDtypeStruct((16, 1536), F32), jax.ShapeDtypeStruct((left, 1024), F32)),
         [VMEM] * (2 + len(weights)),
         (own, other, *weights),
@@ -236,7 +231,7 @@
         out_ref[a * 16 : (a + 1) * 16, :] = rest_ref[a * 16 : (a + 1) * 16, :] - block
 
 
-def ship_kernel(order, place, own_ref, other_ref, out_ref):
+def ship_kernel(turned, place, own_ref, other_ref, out_ref):
     first = place[8] == 0
     own = own_ref[:, 1024:]
     other = other_ref[:, 1024:]
@@ -244,10 +239,9 @@
     high_core = jnp.where(first, other, own)
     for k in range(FRONTS):
         outer, inner = (0, 3, 1, 2)[k // 4], (0, 3, 1, 2)[k % 4]
-        if order == "yx":
+        to = k
+        if turned:
             to = (place[10] + outer) % 4 * 4 + (place[11] + inner) % 4
-        else:
-            to = (place[10] + inner) % 4 * 4 + (place[11] + outer) % 4
         at = slice(k * 32, (k + 1) * 32)
         value = jnp.concatenate([low_core[:, at], high_core[:, at]], axis=1)
         high = value.astype(BF).astype(F32)
@@ -305,24 +299,21 @@
     off_top = jnp.swapaxes(off_top, 1, 2)
     off_leaf = jnp.swapaxes(off_leaf, 1, 2)
 
-    sent, ends, middle = first_payload(place, rhs_leaf, rhs_top, inv_top, off_top)
+    sent, third, pair = first_payload(place, rhs_leaf, rhs_top, inv_top, off_top)
     first = lax.all_to_all(sent, "front", 0, 0)
-    ends, middle = around(ends, "y"), around(middle, "x")
+    pair_near = near(pair, "y")
+    pair_far = far(pair_near, "y")
     leaf_x, sent = call(
         leaf_solve_kernel,
-        (jax.ShapeDtypeStruct((64, 256), F32), jax.ShapeDtypeStruct((FRONTS, 16, 1024), BF)),
-        [VMEM] * 3,
-        (inv_leaf, first, off_leaf),
-    )
-    sent, ends, middle = lax.optimization_barrier((sent, ends, middle))
+        (jax.ShapeDtypeStruct((64, 256), F32), jax.ShapeDtypeStruct((FRONTS, 80, 1024), BF)),
+        [VMEM] * 4,
+        (inv_leaf, first, off_leaf, third),
+    )
+    second, lowest = stack((pair, *pair_near, *pair_far))
+    sent, second, lowest = lax.optimization_barrier((sent, second, lowest))
     got = lax.all_to_all(sent, "front", 0, 0)
-    third, second, lowest = stack(ends, 0), stack(middle, 0), stack(ends, 64)
-    third_near, second_near = near(third, "x"), near(second, "y")
-    third_far, second_far = far(third_near, "x"), far(second_near, "y")
-    got, third_far, second_far, lowest = lax.optimization_barrier(
-        (got, third_far, second_far, lowest)
-    )
-    lowest_near = near(lowest, "x")
+    got, second = lax.optimization_barrier((got, second))
+    second_near = near(second, "x")
     state = call(
         leaf_update_kernel,
         jax.ShapeDtypeStruct((64, 1024), F32),
@@ -333,12 +324,12 @@
     ships = []
     for level in range(3):
         if level == 0:
-            parts = (third, *third_near, *third_far)
+            parts = (got,)
         elif level == 1:
             parts = (second, *second_near, *second_far)
         else:
             parts = (lowest, *lowest_near, *lowest_far)
-        ux, rest = top_solve(state, other, [part.reshape(-1, 64, 1024) for part in parts])
+        ux, rest = top_solve(state, other, [part.reshape(-1, 80 if level == 0 else 64, 1024) for part in parts])
         ux_other = swap(ux, core_pairs())
         state = call(
             functools.partial(update_kernel, level),
@@ -346,13 +337,17 @@
             [SMEM] + [VMEM] * 4,
             (place, ux, ux_other, rest, idx_top),
         )
+        if level == 0:
+            state, second_near = lax.optimization_barrier((state, second_near))
+            second_far = far(second_near, "x")
         other = swap(state, chip_pairs(level))
         if level == 0:
-            other, lowest_near = lax.optimization_barrier((other, lowest_near))
+            other, lowest = lax.optimization_barrier((other, lowest))
+            lowest_near = near(lowest, "x")
             lowest_far = far(lowest_near, "x")
         ships.append(
             call(
-                functools.partial(ship_kernel, ("yx", "xy", "yx")[level]),
+                functools.partial(ship_kernel, level > 0),
                 jax.ShapeDtypeStruct((16, 16, 128), BF),
                 [SMEM, VMEM, VMEM],
                 (place, ux, ux_other),

time: 138 us -> 162 us (1.17)
  blocking collectives: 0 us -> 36.6 us
  starting transfers between devices: 56.6 us -> 37.7 us
  waiting for transfers between devices: 50.3 us -> 64.5 us
  local copies, waits for them, and re-layouts: 6.65 us -> 2.62 us
  Pallas kernels: 22.8 us -> 19.8 us
    all_to_all x0 -> x1, blocking collectives: none -> 36.6 us  [local(): got = lax.all_to_all(sent, 'front', 0, 0)]
    ppermute x18 -> x12, starting transfers between devices: 29.4 us -> 17.6 us  [turn(): return lax.ppermute(block, 'front', route)]
    ppermute x7, waiting for transfers between devices: 9.63 us -> 18.6 us  [swap(): return lax.ppermute(block, 'leaf', pairs)]
    all_to_all x2 -> x1, starting transfers between devices: 10.4 us -> 3.6 us  [local(): got = lax.all_to_all(sent, 'front', 0, 0)]
    slice x6, local copies, waits for them, and re-layouts: 4.86 us -> 0.09 us  [far(): return (turn(after[:half], -dx, -dy), turn(before[half:], dx, dy))]
    ppermute x18 -> x12, waiting for transfers between devices: 27.9 us -> 32.5 us  [turn(): return lax.ppermute(block, 'front', route)]
    pallas_call x16 -> x14, Pallas kernels: 19.5 us -> 16.5 us  [call(): pl.pallas_call(kernel, out_shape=outs, in_specs=specs, out_specs=tuple((V...]
    all_to_all x2 -> x1, waiting for transfers between devices: 12.7 us -> 13.4 us  [local(): got = lax.all_to_all(sent, 'front', 0, 0)]
  transfers between devices with their start and end apart: 28 -> 21, of which waited for: 15 -> 15; matrix products, arithmetic and copies ran while one was open for 4% -> 1% of each run, Pallas kernels for 9% -> 7%
where the time goes in v7:
time: 162 us
  waiting for transfers between devices  64.5 us (40%)
  starting transfers between devices  37.7 us (23%)
  blocking collectives  36.6 us (23%)
  Pallas kernels  19.8 us (12%)
  local copies, waits for them, and re-layouts  2.62 us (2%)
    all_to_all x1, blocking collectives, local(): got = lax.all_to_all(sent, 'front', 0, 0)  36.6 us
    ppermute x12, waiting for transfers between devices, turn(): return lax.ppermute(block, 'front', route)  32.5 us
    ppermute x7, waiting for transfers between devices, swap(): return lax.ppermute(block, 'leaf', pairs)  18.6 us
    ppermute x12, starting transfers between devices, turn(): return lax.ppermute(block, 'front', route)  17.6 us
    pallas_call x14, Pallas kernels, call(): pl.pallas_call(kernel, out_shape=outs, in_specs=specs, out_specs=tuple((V...  16.5 us
    all_to_all x1, waiting for transfers between devices, local(): got = lax.all_to_all(sent, 'front', 0, 0)  13.4 us
    ppermute x7, starting transfers between devices, swap(): return lax.ppermute(block, 'leaf', pairs)  9.29 us
    all_to_all x1, starting transfers between devices, local(): first = lax.all_to_all(sent, 'front', 0, 0)  7.18 us
  transfers between devices with their start and end apart: 21, of which 15 were waited for; matrix products, arithmetic and copies ran while one was open for 1% of the time, Pallas kernels for 7%

profile of v7, /device:TPU:32, one launch (start us, length us, event | category | flops | bytes accessed | tf_op | source)
XLA Modules:
  0.0 162.0 jit_solution(13516552020318670836)
XLA Ops:
  1.3 3.3 %shard_map.95 = (bf16[16,80,256]{2,1,0:T(8,128)(2,1)}, bf16[64,1024]{1,0:T(8,128)(2,1)}, bf16[128,1024]{1,0:T(8,128)(2,1)}) custom-call(s32[12]{0:T(128)} %stack.48.place, f32[1,64,256]{2,1,0:T(8,128)} %leaf_ref.1, f32[15,64,256]{2,1,0:T(8,128)} %rhs_ref.1, bf16[15,64,1024]{2,1,0:T(8,128)(2,1)} %inv_ref.2, bf16[14,64,1024]{2,1,0:T(8,128)(2,1)} %bitcast.36), custom_call_target="tpu_custom_call" | custom-call | tf_op jit(solution)/shard_map/pallas_call | solution.py:101
  4.6 7.2 %all-to-all-start = ((bf16[16,80,256]{2,1,0:T(8,128)(2,1)}), bf16[16,80,256]{2,1,0:T(8,128)(2,1)S(1)}, u32[]{:S(2)}, u32[]{:S(2)}) async-start(bf16[16,80,256]{2,1,0:T(8,128)(2,1)} %get-tuple-element.25), calls=%async_computation | async-start | bytes 1310720 | tf_op jit(solution)/shard_map/all_to_all | solution.py:303
  11.8 3.1 %collective-permute-start.1 = (bf16[128,1024]{1,0:T(8,128)(2,1)}, bf16[128,1024]{1,0:T(8,128)(2,1)S(1)}, u32[]{:S(2)}, u32[]{:S(2)}) collective-permute-start(bf16[128,1024]{1,0:T(8,128)(2,1)} %get-tuple-element.29.own_ref), channel_id=1, source_target_pairs={{0,3},{1,0},{2,1},{3,2},{4,7},{5,4},{6,5},{7,6},{8,11},{9,8},{10,9... | collective-permute-start | bytes 786440 | tf_op jit(solution)/shard_map/ppermute | solution.py:130
  14.9 11.8 %collective-permute-done.1.after_ref = bf16[128,1024]{1,0:T(8,128)(2,1)S(1)} collective-permute-done((bf16[128,1024]{1,0:T(8,128)(2,1)}, bf16[128,1024]{1,0:T(8,128)(2,1)S(1)}, u32[]{:S(2)}, u32[]{:S(2)}) %collective-permute-start.1) | collective-permute-done | bytes 262176 | tf_op jit(solution)/shard_map/ppermute | solution.py:130
  26.7 2.9 %collective-permute-start.2 = (bf16[64,1024]{1,0:T(8,128)(2,1)S(1)}, bf16[64,1024]{1,0:T(8,128)(2,1)S(1)}, u32[]{:S(2)}, u32[]{:S(2)}) collective-permute-start(bf16[64,1024]{1,0:T(8,128)(2,1)S(1)} %slice.28), channel_id=1, source_target_pairs={{0,3},{1,0},{2,1},{3,2},{4,7},{5,4},{6,5},{7,6},{8,11},{9,8},{10,9... | collective-permute-start | bytes 393224 | tf_op jit(solution)/shard_map/ppermute | solution.py:130
  29.7 2.4 %collective-permute-done.2.second_ref = bf16[64,1024]{1,0:T(8,128)(2,1)S(1)} collective-permute-done((bf16[64,1024]{1,0:T(8,128)(2,1)S(1)}, bf16[64,1024]{1,0:T(8,128)(2,1)S(1)}, u32[]{:S(2)}, u32[]{:S(2)}) %collective-permute-start.2) | collective-permute-done | bytes 131104 | tf_op jit(solution)/shard_map/ppermute | solution.py:130
  32.1 3.8 %collective-permute-done.3.lowest_ref = bf16[64,1024]{1,0:T(8,128)(2,1)S(1)} collective-permute-done((bf16[64,1024]{1,0:T(8,128)(2,1)S(1)}, bf16[64,1024]{1,0:T(8,128)(2,1)S(1)}, u32[]{:S(2)}, u32[]{:S(2)}) %collective-permute-start.3) | collective-permute-done | bytes 131104 | tf_op jit(solution)/shard_map/ppermute | solution.py:130
  37.9 36.6 %all_to_all.15.got_ref.refs_0_ = bf16[16,80,1024]{2,1,0:T(8,128)(2,1)S(1)} all-to-all(bf16[16,80,1024]{2,1,0:T(8,128)(2,1)S(1)} %get-tuple-element.32), channel_id=1, replica_groups=mesh['leaf'=16,'front'=16] {'front'}, dimensions={0} | all-to-all | bytes 5242880 | tf_op jit(solution)/shard_map/all_to_all | solution.py:314
  75.0 2.7 %collective-permute-start.7 = (bf16[256,1024]{1,0:T(8,128)(2,1)S(1)}, bf16[256,1024]{1,0:T(8,128)(2,1)S(1)}, u32[]{:S(2)}, u32[]{:S(2)}) collective-permute-start(bf16[256,1024]{1,0:T(8,128)(2,1)S(1)} %get-tuple-element.37), channel_id=1, source_target_pairs={{0,12},{1,13},{2,14},{3,15},{4,0},{5,1},{6,2},{7,3},{8,4},{9,5},{1... | collective-permute-start | bytes 1572872 | tf_op jit(solution)/shard_map/ppermute | solution.py:130
  77.7 3.1 %shard_map.98.own_ref = f32[64,1024]{1,0:T(8,128)S(1)} custom-call(s32[12]{0:T(128)S(1)} %copy-done.5, bf16[16,80,256]{2,1,0:T(8,128)(2,1)S(1)} %all-to-all-done.rhs_ref.first_ref, bf16[16,80,1024]{2,1,0:T(8,128)(2,1)S(1)} %all_to_all.15.got_ref.refs_0_, s32[1,1024]{1,0:T(1,128)S(1)} %copy-done.6), custom_call_target="tpu_custom_call" | custom-call | flops 100000000 | bytes 1000000 | tf_op jit(solution)/shard_map/pallas_call | solution.py:46
  80.9 1.5 collective-permute-done.4.other_ref
  83.2 1.2 collective-permute-done.5.other_ref
  84.4 2.4 %shard_map.100.own_ref = f32[48,1024]{1,0:T(8,128)S(1)} custom-call(s32[12]{0:T(128)S(1)} %copy-done.5, f32[16,1536]{1,0:T(8,128)S(1)} %get-tuple-element.35.own_ref, f32[16,1536]{1,0:T(8,128)S(1)} %collective-permute-done.5.other_ref, f32[48,1024]{1,0:T(8,128)S(1)} %get-tuple-element.36.rest_ref, s32[14,1024]{1,0:T(8,128)S(1)} %copy-done), custom_call_target="tpu_custom_call" | custom-call | flops 100000000 | bytes 1000000 | tf_op jit(solution)/shard_map/pallas_call | solution.py:46
  87.1 6.8 %collective-permute-done.8.other_ref = f32[48,1024]{1,0:T(8,128)S(1)} collective-permute-done((f32[48,1024]{1,0:T(8,128)S(1)}, f32[48,1024]{1,0:T(8,128)S(1)}, u32[]{:S(2)}, u32[]{:S(2)}) %collective-permute-start.8) | collective-permute-done | bytes 196640 | tf_op jit(solution)/shard_map/ppermute | solution.py:271
  93.9 1.7 %collective-permute-start.14 = (bf16[256,1024]{1,0:T(8,128)(2,1)S(1)}, bf16[256,1024]{1,0:T(8,128)(2,1)S(1)}, u32[]{:S(2)}, u32[]{:S(2)}) collective-permute-start(bf16[256,1024]{1,0:T(8,128)(2,1)S(1)} %get-tuple-element.45), channel_id=1, source_target_pairs={{0,12},{1,13},{2,14},{3,15},{4,0},{5,1},{6,2},{7,3},{8,4},{9,5},{1... | collective-permute-start | bytes 1572872 | tf_op jit(solution)/shard_map/ppermute | solution.py:130
  95.9 3.0 %collective-permute-start.9 = (bf16[128,1024]{1,0:T(8,128)(2,1)S(1)}, bf16[128,1024]{1,0:T(8,128)(2,1)S(1)}, u32[]{:S(2)}, u32[]{:S(2)}) collective-permute-start(bf16[128,1024]{1,0:T(8,128)(2,1)S(1)} %slice.23), channel_id=1, source_target_pairs={{0,12},{1,13},{2,14},{3,15},{4,0},{5,1},{6,2},{7,3},{8,4},{9,5},{1... | collective-permute-start | bytes 786440 | tf_op jit(solution)/shard_map/ppermute | solution.py:130
  99.0 9.7 %collective-permute-done.14 = bf16[256,1024]{1,0:T(8,128)(2,1)S(1)} collective-permute-done((bf16[256,1024]{1,0:T(8,128)(2,1)S(1)}, bf16[256,1024]{1,0:T(8,128)(2,1)S(1)}, u32[]{:S(2)}, u32[]{:S(2)}) %collective-permute-start.14) | collective-permute-done | bytes 524320 | tf_op jit(solution)/shard_map/ppermute | solution.py:130
  108.7 3.0 %collective-permute-start.15 = (bf16[128,1024]{1,0:T(8,128)(2,1)S(1)}, bf16[128,1024]{1,0:T(8,128)(2,1)S(1)}, u32[]{:S(2)}, u32[]{:S(2)}) collective-permute-start(bf16[128,1024]{1,0:T(8,128)(2,1)S(1)} %slice.30), channel_id=1, source_target_pairs={{0,12},{1,13},{2,14},{3,15},{4,0},{5,1},{6,2},{7,3},{8,4},{9,5},{1... | collective-permute-start | bytes 786440 | tf_op jit(solution)/shard_map/ppermute | solution.py:130
  111.9 2.5 %collective-permute-done.9 = bf16[128,1024]{1,0:T(8,128)(2,1)S(1)} collective-permute-done((bf16[128,1024]{1,0:T(8,128)(2,1)S(1)}, bf16[128,1024]{1,0:T(8,128)(2,1)S(1)}, u32[]{:S(2)}, u32[]{:S(2)}) %collective-permute-start.9) | collective-permute-done | bytes 262176 | tf_op jit(solution)/shard_map/ppermute | solution.py:130
  114.3 2.3 %collective-permute-done.10 = bf16[128,1024]{1,0:T(8,128)(2,1)S(1)} collective-permute-done((bf16[128,1024]{1,0:T(8,128)(2,1)S(1)}, bf16[128,1024]{1,0:T(8,128)(2,1)S(1)}, u32[]{:S(2)}, u32[]{:S(2)}) %collective-permute-start.10) | collective-permute-done | bytes 262176 | tf_op jit(solution)/shard_map/ppermute | solution.py:130
  116.6 1.1 shard_map.101
  117.7 1.3 collective-permute-done.11.other_ref
  119.0 1.8 %shard_map.102.own_ref = f32[32,1024]{1,0:T(8,128)S(1)} custom-call(s32[12]{0:T(128)S(1)} %copy-done.5, f32[16,1536]{1,0:T(8,128)S(1)} %get-tuple-element.43.own_ref, f32[16,1536]{1,0:T(8,128)S(1)} %collective-permute-done.11.other_ref, f32[32,1024]{1,0:T(8,128)S(1)} %get-tuple-element.44.rest_ref, s32[14,1024]{1,0:T(8,128)S(1)} %copy-done), custom_call_target="tpu_custom_call" | custom-call | flops 100000000 | bytes 1000000 | tf_op jit(solution)/shard_map/pallas_call | solution.py:46
  120.8 3.3 %collective-permute-start.12 = (f32[32,1024]{1,0:T(8,128)S(1)}, f32[32,1024]{1,0:T(8,128)S(1)}, u32[]{:S(2)}, u32[]{:S(2)}) collective-permute-start(f32[32,1024]{1,0:T(8,128)S(1)} %shard_map.102.own_ref), channel_id=1, source_target_pairs={{0,64},{16,80},{32,96},{48,112},{64,0},{80,16},{96,32},{112,48},{1... | collective-permute-start | bytes 393224 | tf_op jit(solution)/shard_map/ppermute | solution.py:271
  124.1 5.8 %collective-permute-done.12.other_ref = f32[32,1024]{1,0:T(8,128)S(1)} collective-permute-done((f32[32,1024]{1,0:T(8,128)S(1)}, f32[32,1024]{1,0:T(8,128)S(1)}, u32[]{:S(2)}, u32[]{:S(2)}) %collective-permute-start.12) | collective-permute-done | bytes 131104 | tf_op jit(solution)/shard_map/ppermute | solution.py:271
  130.0 1.1 shard_map.103
  131.1 1.3 collective-permute-done.17.other_ref
  132.4 1.2 shard_map.104.own_ref
  133.6 5.6 %collective-permute-start.18 = (f32[16,1024]{1,0:T(8,128)S(1)}, f32[16,1024]{1,0:T(8,128)S(1)}, u32[]{:S(2)}, u32[]{:S(2)}) collective-permute-start(f32[16,1024]{1,0:T(8,128)S(1)} %shard_map.104.own_ref), channel_id=1, source_target_pairs={{0,192},{16,208},{32,224},{48,240},{64,128},{80,144},{96,160},{112... | collective-permute-start | bytes 196616 | tf_op jit(solution)/shard_map/ppermute | solution.py:271
  143.1 3.6 %all-to-all-start.2 = ((bf16[16,16,1408]{2,1,0:T(8,128)(2,1)}), bf16[16,16,1408]{2,1,0:T(8,128)(2,1)S(1)}, u32[]{:S(2)}, u32[]{:S(2)}) async-start(bf16[16,16,1408]{2,1,0:T(8,128)(2,1)} %shard_map.108), calls=%async_computation.2 | async-start | bytes 1441792 | tf_op jit(solution)/shard_map/all_to_all | solution.py:362
  147.6 13.4 %all-to-all-done.2.got_ref = bf16[16,16,1408]{2,1,0:T(8,128)(2,1)S(1)} async-done(((bf16[16,16,1408]{2,1,0:T(8,128)(2,1)}), bf16[16,16,1408]{2,1,0:T(8,128)(2,1)S(1)}, u32[]{:S(2)}, u32[]{:S(2)}) %all-to-all-start.2) | async-done | bytes 720928 | tf_op jit(solution)/shard_map/all_to_all | solution.py:362
  161.0 1.0 shard_map.109
  (48 shorter events, 9.7 us)
Async XLA Ops:
  4.6 32.4 %copy-start.2 = (bf16[1,64,1024]{2,1,0:T(8,128)(2,1)S(1)}, bf16[1,64,1024]{2,1,0:T(8,128)(2,1)}, u32[]{:S(2)}) copy-start(bf16[1,64,1024]{2,1,0:T(8,128)(2,1)} %inv_ref.3) | copy-start | bytes 393220
  4.6 32.4 %copy-start.3 = (bf16[1,1024,64]{1,2,0:T(8,128)(2,1)S(1)}, bf16[1,1024,64]{1,2,0:T(8,128)(2,1)}, u32[]{:S(2)}) copy-start(bf16[1,1024,64]{1,2,0:T(8,128)(2,1)} %param.12) | copy-start | bytes 393220
  4.6 32.4 %copy-start.4 = (bf16[64,1024]{1,0:T(8,128)(2,1)S(1)}, bf16[64,1024]{1,0:T(8,128)(2,1)}, u32[]{:S(2)}) copy-start(bf16[64,1024]{1,0:T(8,128)(2,1)} %get-tuple-element.26.third_ref) | copy-start | bytes 393220
  4.6 32.3 %all-to-all-start = ((bf16[16,80,256]{2,1,0:T(8,128)(2,1)}), bf16[16,80,256]{2,1,0:T(8,128)(2,1)S(1)}, u32[]{:S(2)}, u32[]{:S(2)}) async-start(bf16[16,80,256]{2,1,0:T(8,128)(2,1)} %get-tuple-element.25), calls=%async_computation | async-start | bytes 1310720 | tf_op jit(solution)/shard_map/all_to_all | solution.py:303
  11.8 14.9 %collective-permute-start.1 = (bf16[128,1024]{1,0:T(8,128)(2,1)}, bf16[128,1024]{1,0:T(8,128)(2,1)S(1)}, u32[]{:S(2)}, u32[]{:S(2)}) collective-permute-start(bf16[128,1024]{1,0:T(8,128)(2,1)} %get-tuple-element.29.own_ref), channel_id=1, source_target_pairs={{0,3},{1,0},{2,1},{3,2},{4,7},{5,4},{6,5},{7,6},{8,11},{9,8},{10,9... | collective-permute-start | bytes 786440 | tf_op jit(solution)/shard_map/ppermute | solution.py:130
  14.9 14.7 %collective-permute-start = (bf16[128,1024]{1,0:T(8,128)(2,1)}, bf16[128,1024]{1,0:T(8,128)(2,1)S(1)}, u32[]{:S(2)}, u32[]{:S(2)}) collective-permute-start(bf16[128,1024]{1,0:T(8,128)(2,1)} %get-tuple-element.29.own_ref), channel_id=1, source_target_pairs={{0,1},{1,2},{2,3},{3,0},{4,5},{5,6},{6,7},{7,4},{8,9},{9,10},{10,1... | collective-permute-start | bytes 786440 | tf_op jit(solution)/shard_map/ppermute | solution.py:130
  26.7 5.5 %collective-permute-start.2 = (bf16[64,1024]{1,0:T(8,128)(2,1)S(1)}, bf16[64,1024]{1,0:T(8,128)(2,1)S(1)}, u32[]{:S(2)}, u32[]{:S(2)}) collective-permute-start(bf16[64,1024]{1,0:T(8,128)(2,1)S(1)} %slice.28), channel_id=1, source_target_pairs={{0,3},{1,0},{2,1},{3,2},{4,7},{5,4},{6,5},{7,6},{8,11},{9,8},{10,9... | collective-permute-start | bytes 393224 | tf_op jit(solution)/shard_map/ppermute | solution.py:130
  29.6 6.3 %collective-permute-start.3 = (bf16[64,1024]{1,0:T(8,128)(2,1)S(1)}, bf16[64,1024]{1,0:T(8,128)(2,1)S(1)}, u32[]{:S(2)}, u32[]{:S(2)}) collective-permute-start(bf16[64,1024]{1,0:T(8,128)(2,1)S(1)} %slice.29), channel_id=1, source_target_pairs={{0,1},{1,2},{2,3},{3,0},{4,5},{5,6},{6,7},{7,4},{8,9},{9,10},{10,1... | collective-permute-start | bytes 393224 | tf_op jit(solution)/shard_map/ppermute | solution.py:130
  35.9 1.0 copy-start.1
  37.9 39.8 %copy-start.5 = (s32[12]{0:T(128)S(1)}, s32[12]{0:T(128)}, u32[]{:S(2)}) copy-start(s32[12]{0:T(128)} %stack.48.place) | copy-start | bytes 148
  37.9 39.8 %copy-start.6 = (s32[1,1024]{1,0:T(1,128)S(1)}, s32[1,1024]{1,0:T(1,128)}, u32[]{:S(2)}) copy-start(s32[1,1024]{1,0:T(1,128)} %idx_ref.4) | copy-start | bytes 12292
  74.5 9.9 %copy-start = (s32[14,1024]{1,0:T(8,128)S(1)}, s32[14,1024]{1,0:T(8,128)}, u32[]{:S(2)}) copy-start(s32[14,1024]{1,0:T(8,128)} %idx_ref.7) | copy-start | bytes 172036
  74.5 12.5 %collective-permute-start.6 = (bf16[256,1024]{1,0:T(8,128)(2,1)S(1)}, bf16[256,1024]{1,0:T(8,128)(2,1)S(1)}, u32[]{:S(2)}, u32[]{:S(2)}) collective-permute-start(bf16[256,1024]{1,0:T(8,128)(2,1)S(1)} %get-tuple-element.37), channel_id=1, source_target_pairs={{0,4},{1,5},{2,6},{3,7},{4,8},{5,9},{6,10},{7,11},{8,12},{9,13},{1... | collective-permute-start | bytes 1572872 | tf_op jit(solution)/shard_map/ppermute | solution.py:130
  75.0 11.9 %collective-permute-start.7 = (bf16[256,1024]{1,0:T(8,128)(2,1)S(1)}, bf16[256,1024]{1,0:T(8,128)(2,1)S(1)}, u32[]{:S(2)}, u32[]{:S(2)}) collective-permute-start(bf16[256,1024]{1,0:T(8,128)(2,1)S(1)} %get-tuple-element.37), channel_id=1, source_target_pairs={{0,12},{1,13},{2,14},{3,15},{4,0},{5,1},{6,2},{7,3},{8,4},{9,5},{1... | collective-permute-start | bytes 1572872 | tf_op jit(solution)/shard_map/ppermute | solution.py:130
  80.8 1.6 %collective-permute-start.4 = (f32[64,1024]{1,0:T(8,128)S(1)}, f32[64,1024]{1,0:T(8,128)S(1)}, u32[]{:S(2)}, u32[]{:S(2)}) collective-permute-start(f32[64,1024]{1,0:T(8,128)S(1)} %shard_map.98.own_ref), channel_id=1, source_target_pairs={{0,16},{16,0},{32,48},{48,32},{64,80},{80,64},{96,112},{112,96},{1... | collective-permute-start | bytes 786440 | tf_op jit(solution)/shard_map/ppermute | solution.py:271
  83.0 1.3 collective-permute-start.5
  86.9 6.9 %collective-permute-start.8 = (f32[48,1024]{1,0:T(8,128)S(1)}, f32[48,1024]{1,0:T(8,128)S(1)}, u32[]{:S(2)}, u32[]{:S(2)}) collective-permute-start(f32[48,1024]{1,0:T(8,128)S(1)} %shard_map.100.own_ref), channel_id=1, source_target_pairs={{0,32},{16,48},{32,0},{48,16},{64,96},{80,112},{96,64},{112,80},{1... | collective-permute-start | bytes 589832 | tf_op jit(solution)/shard_map/ppermute | solution.py:271
  93.9 14.9 %collective-permute-start.14 = (bf16[256,1024]{1,0:T(8,128)(2,1)S(1)}, bf16[256,1024]{1,0:T(8,128)(2,1)S(1)}, u32[]{:S(2)}, u32[]{:S(2)}) collective-permute-start(bf16[256,1024]{1,0:T(8,128)(2,1)S(1)} %get-tuple-element.45), channel_id=1, source_target_pairs={{0,12},{1,13},{2,14},{3,15},{4,0},{5,1},{6,2},{7,3},{8,4},{9,5},{1... | collective-permute-start | bytes 1572872 | tf_op jit(solution)/shard_map/ppermute | solution.py:130
  95.6 16.2 %collective-permute-start.13 = (bf16[256,1024]{1,0:T(8,128)(2,1)S(1)}, bf16[256,1024]{1,0:T(8,128)(2,1)S(1)}, u32[]{:S(2)}, u32[]{:S(2)}) collective-permute-start(bf16[256,1024]{1,0:T(8,128)(2,1)S(1)} %get-tuple-element.45), channel_id=1, source_target_pairs={{0,4},{1,5},{2,6},{3,7},{4,8},{5,9},{6,10},{7,11},{8,12},{9,13},{1... | collective-permute-start | bytes 1572872 | tf_op jit(solution)/shard_map/ppermute | solution.py:130
  95.9 18.4 %collective-permute-start.9 = (bf16[128,1024]{1,0:T(8,128)(2,1)S(1)}, bf16[128,1024]{1,0:T(8,128)(2,1)S(1)}, u32[]{:S(2)}, u32[]{:S(2)}) collective-permute-start(bf16[128,1024]{1,0:T(8,128)(2,1)S(1)} %slice.23), channel_id=1, source_target_pairs={{0,12},{1,13},{2,14},{3,15},{4,0},{5,1},{6,2},{7,3},{8,4},{9,5},{1... | collective-permute-start | bytes 786440 | tf_op jit(solution)/shard_map/ppermute | solution.py:130
  98.9 17.7 %collective-permute-start.10 = (bf16[128,1024]{1,0:T(8,128)(2,1)S(1)}, bf16[128,1024]{1,0:T(8,128)(2,1)S(1)}, u32[]{:S(2)}, u32[]{:S(2)}) collective-permute-start(bf16[128,1024]{1,0:T(8,128)(2,1)S(1)} %slice.24), channel_id=1, source_target_pairs={{0,4},{1,5},{2,6},{3,7},{4,8},{5,9},{6,10},{7,11},{8,12},{9,13},{1... | collective-permute-start | bytes 786440 | tf_op jit(solution)/shard_map/ppermute | solution.py:130
  108.7 21.2 %collective-permute-start.15 = (bf16[128,1024]{1,0:T(8,128)(2,1)S(1)}, bf16[128,1024]{1,0:T(8,128)(2,1)S(1)}, u32[]{:S(2)}, u32[]{:S(2)}) collective-permute-start(bf16[128,1024]{1,0:T(8,128)(2,1)S(1)} %slice.30), channel_id=1, source_target_pairs={{0,12},{1,13},{2,14},{3,15},{4,0},{5,1},{6,2},{7,3},{8,4},{9,5},{1... | collective-permute-start | bytes 786440 | tf_op jit(solution)/shard_map/ppermute | solution.py:130
  111.8 18.2 %collective-permute-start.16 = (bf16[128,1024]{1,0:T(8,128)(2,1)S(1)}, bf16[128,1024]{1,0:T(8,128)(2,1)S(1)}, u32[]{:S(2)}, u32[]{:S(2)}) collective-permute-start(bf16[128,1024]{1,0:T(8,128)(2,1)S(1)} %slice.31), channel_id=1, source_target_pairs={{0,4},{1,5},{2,6},{3,7},{4,8},{5,9},{6,10},{7,11},{8,12},{9,13},{1... | collective-permute-start | bytes 786440 | tf_op jit(solution)/shard_map/ppermute | solution.py:130
  117.7 1.3 collective-permute-start.11
  120.8 9.1 %collective-permute-start.12 = (f32[32,1024]{1,0:T(8,128)S(1)}, f32[32,1024]{1,0:T(8,128)S(1)}, u32[]{:S(2)}, u32[]{:S(2)}) collective-permute-start(f32[32,1024]{1,0:T(8,128)S(1)} %shard_map.102.own_ref), channel_id=1, source_target_pairs={{0,64},{16,80},{32,96},{48,112},{64,0},{80,16},{96,32},{112,48},{1... | collective-permute-start | bytes 393224 | tf_op jit(solution)/shard_map/ppermute | solution.py:271
  131.0 1.3 collective-permute-start.17
  133.6 8.5 %collective-permute-start.18 = (f32[16,1024]{1,0:T(8,128)S(1)}, f32[16,1024]{1,0:T(8,128)S(1)}, u32[]{:S(2)}, u32[]{:S(2)}) collective-permute-start(f32[16,1024]{1,0:T(8,128)S(1)} %shard_map.104.own_ref), channel_id=1, source_target_pairs={{0,192},{16,208},{32,224},{48,240},{64,128},{80,144},{96,160},{112... | collective-permute-start | bytes 196616 | tf_op jit(solution)/shard_map/ppermute | solution.py:271
  143.1 17.9 %all-to-all-start.2 = ((bf16[16,16,1408]{2,1,0:T(8,128)(2,1)}), bf16[16,16,1408]{2,1,0:T(8,128)(2,1)S(1)}, u32[]{:S(2)}, u32[]{:S(2)}) async-start(bf16[16,16,1408]{2,1,0:T(8,128)(2,1)} %shard_map.108), calls=%async_computation.2 | async-start | bytes 1441792 | tf_op jit(solution)/shard_map/all_to_all | solution.py:362

commit v8 on v6

--- a/solution.py
+++ b/solution.py
@@ -56,12 +56,12 @@
 
 
 def first_kernel(place, leaf_ref, rhs_ref, inv_ref, off_ref, out_ref, *refs):
-    ends_ref, middle_ref, held, sems = refs
+    third_ref, pair_ref, held, sems = refs
     copies = [
         pltpu.make_async_copy(rhs_ref.at[place[a] - 1], held.at[a], sems.at[a]) for a in range(4)
     ]
     at = pl.ds(pl.multiple_of(place[8] * 32, 32), 32)
-    for level, (piece, start) in enumerate(((ends_ref, 0), (middle_ref, 0), (ends_ref, 64))):
+    for level, (piece, start) in enumerate(((third_ref, 0), (pair_ref, 0), (pair_ref, 64))):
         node = place[level]
         for part, (ref, index) in enumerate(((inv_ref, node - 1), (off_ref, node - 2))):
             copies.append(
@@ -102,8 +102,8 @@
         first_kernel,
         out_shape=(
             jax.ShapeDtypeStruct((FRONTS, 80, 256), BF),
+            jax.ShapeDtypeStruct((64, 1024), BF),
             jax.ShapeDtypeStruct((128, 1024), BF),
-            jax.ShapeDtypeStruct((64, 1024), BF),
         ),
         in_specs=[SMEM, VMEM, HBM, HBM, HBM],
         out_specs=(VMEM,) * 3,
@@ -112,17 +112,16 @@
     )(place, rhs_leaf, rhs_top, inv_top, off_top)
 
 
-def stack_kernel(start, *refs):
-    for k, ref in enumerate(refs[:-1]):
+def stack_kernel(starts, *refs):
+    for k, (start, ref) in enumerate(zip(starts, refs)):
         refs[-1][k * 64 : (k + 1) * 64, :] = ref[start : start + 64, :]
 
 
-def stack(parts, start):
-    rows = 64 * len(parts)
+def stack(parts, starts):
     return call(
-        functools.partial(stack_kernel, start),
-        jax.ShapeDtypeStruct((rows, 1024), BF),
-        [VMEM] * len(parts),
+        functools.partial(stack_kernel, starts),
+        jax.ShapeDtypeStruct((256, 1024), BF),
+        [VMEM] * 4,
         tuple(parts),
     )
 
@@ -141,10 +140,9 @@
     return turn(block, dx, dy), turn(block, -dx, -dy)
 
 
-def around(block, axis):
+def opposite(block, axis):
     dx, dy = step_of(axis)
-    opposite = turn(block, 2 * dx, 2 * dy)
-    return (block, *near(block, axis), opposite)
+    return turn(block, 2 * dx, 2 * dy)
 
 
 def far(pair, axis):
@@ -178,7 +176,7 @@
     return blocks
 
 
-def leaf_update_kernel(place, first_ref, got_ref, idx_ref, out_ref):
+def leaf_update_kernel(place, first_ref, got_ref, idx_ref, next_ref, rest_ref):
     update = jnp.zeros((16, 1024), F32)
     for s in range(FRONTS):
         update = update + got_ref[s].astype(F32)
@@ -197,43 +195,60 @@
         put = (slot >= start) & (slot < start + width)
         put = put & (row == place[4 + a] * width + slot - start)
         put = jnp.where(put, 1.0, 0.0).astype(BF)
-        out_ref[a * 16 : (a + 1) * 16, :] = nn(put, high) + nn(put, low) - pending[a]
+        block = nn(put, high) + nn(put, low) - pending[a]
+        if a == 0:
+            next_ref[...] = block
+        else:
+            rest_ref[(a - 1) * 16 : a * 16, :] = block
 
 
 def solve_kernel(own_ref, other_ref, *refs):
-    weights, ux_ref, rest_ref = refs[:-2], refs[-2], refs[-1]
-    total = own_ref[...] + other_ref[...]
-    rest_ref[...] = total[16:]
-    right = total[:16].astype(BF)
+    weights, ux_ref = refs[:-1], refs[-1]
+    right = (own_ref[...] + other_ref[...]).astype(BF)
     update = jnp.zeros((16, 1024), F32)
     at = 1024
     for ref in weights:
-        blocks = ref.shape[0]
-        rows = blocks * 32
+        rows = ref.shape[0] * 32
         x = nt(right, ref[:, :32, :].reshape(rows, 1024))
-        off = ref[:, 32:, :].reshape(rows, 1024)
-        update = update + nn(x.astype(BF), off)
+        update = update + nn(x.astype(BF), ref[:, 32:, :].reshape(rows, 1024))
         ux_ref[:, at : at + rows] = x
         at += rows
     ux_ref[:, :1024] = update
 
 
 def top_solve(own, other, weights):
-    left = own.shape[0] - 16
+    weights = [part.reshape(-1, 64, 1024) for part in weights]
     return call(
         solve_kernel,
-        (jax.ShapeDtypeStruct((16, 1536), F32), jax.ShapeDtypeStruct((left, 1024), F32)),
+        jax.ShapeDtypeStruct((16, 1536), F32),
         [VMEM] * (2 + len(weights)),
         (own, other, *weights),
     )
 
 
-def update_kernel(level, place, own_ref, other_ref, rest_ref, idx_ref, out_ref):
+def update_kernel(level, place, own_ref, other_ref, left_ref, left_other_ref, idx_ref, *outs):
     update = own_ref[:, :1024] + other_ref[:, :1024]
-    count = out_ref.shape[0] // 16
+    count = left_ref.shape[0] // 16
     idx = idx_ref[pl.ds(place[level] - 2, 1), :]
     for a, block in enumerate(push(update, idx, count)):
-        out_ref[a * 16 : (a + 1) * 16, :] = rest_ref[a * 16 : (a + 1) * 16, :] - block
+        at = slice(a * 16, (a + 1) * 16)
+        block = left_ref[at, :] + left_other_ref[at, :] - block
+        if a == 0:
+            outs[0][...] = block
+        else:
+            outs[1][(a - 1) * 16 : a * 16, :] = block
+
+
+def top_update(level, place, ux, ux_other, left, left_other, idx_top):
+    shapes = [jax.ShapeDtypeStruct((16, 1024), F32)]
+    if left.shape[0] > 16:
+        shapes.append(jax.ShapeDtypeStruct((left.shape[0] - 16, 1024), F32))
+    return call(
+        functools.partial(update_kernel, level),
+        tuple(shapes),
+        [SMEM] + [VMEM] * 5,
+        (place, ux, ux_other, left, left_other, idx_top),
+    )
 
 
 def ship_kernel(order, place, own_ref, other_ref, out_ref):
@@ -305,31 +320,36 @@
     off_top = jnp.swapaxes(off_top, 1, 2)
     off_leaf = jnp.swapaxes(off_leaf, 1, 2)
 
-    sent, ends, middle = first_payload(place, rhs_leaf, rhs_top, inv_top, off_top)
+    sent, third, pair = first_payload(place, rhs_leaf, rhs_top, inv_top, off_top)
     first = lax.all_to_all(sent, "front", 0, 0)
-    ends, middle = around(ends, "y"), around(middle, "x")
+    third = (third, *near(third, "y"), opposite(third, "y"))
+    pair = (pair, *near(pair, "x"))
+    second = opposite(pair[0][:64], "x")
     leaf_x, sent = call(
         leaf_solve_kernel,
         (jax.ShapeDtypeStruct((64, 256), F32), jax.ShapeDtypeStruct((FRONTS, 16, 1024), BF)),
         [VMEM] * 3,
         (inv_leaf, first, off_leaf),
     )
-    sent, ends, middle = lax.optimization_barrier((sent, ends, middle))
+    sent, third, pair, second = lax.optimization_barrier((sent, third, pair, second))
     got = lax.all_to_all(sent, "front", 0, 0)
-    third, second, lowest = stack(ends, 0), stack(middle, 0), stack(ends, 64)
+    third = stack(third, (0, 0, 0, 0))
+    second = stack((*pair, second), (0, 0, 0, 0))
     third_near, second_near = near(third, "x"), near(second, "y")
+    lowest = turn(pair[2][64:], -1, 0)
     third_far, second_far = far(third_near, "x"), far(second_near, "y")
+    lowest = stack((*pair, lowest), (64, 64, 64, 0))
     got, third_far, second_far, lowest = lax.optimization_barrier(
         (got, third_far, second_far, lowest)
     )
-    lowest_near = near(lowest, "x")
-    state = call(
+    lowest_near = near(lowest, "y")
+    state, left = call(
         leaf_update_kernel,
-        jax.ShapeDtypeStruct((64, 1024), F32),
+        (jax.ShapeDtypeStruct((16, 1024), F32), jax.ShapeDtypeStruct((48, 1024), F32)),
         [SMEM] + [VMEM] * 3,
         (place, first, got, idx_leaf),
     )
-    other = swap(state, core_pairs())
+    other, left_other = swap(state, core_pairs()), swap(left, core_pairs())
     ships = []
     for level in range(3):
         if level == 0:
@@ -338,21 +358,20 @@
             parts = (second, *second_near, *second_far)
         else:
             parts = (lowest, *lowest_near, *lowest_far)
-        ux, rest = top_solve(state, other, [part.reshape(-1, 64, 1024) for part in parts])
+        ux = top_solve(state, other, parts)
+        if level == 2:
+            ux, left_other = lax.optimization_barrier((ux, left_other))
         ux_other = swap(ux, core_pairs())
-        state = call(
-            functools.partial(update_kernel, level),
-            jax.ShapeDtypeStruct(rest.shape, F32),
-            [SMEM] + [VMEM] * 4,
-            (place, ux, ux_other, rest, idx_top),
-        )
+        state, *more = top_update(level, place, ux, ux_other, left, left_other, idx_top)
         other = swap(state, chip_pairs(level))
         if level == 0:
             other, lowest_near = lax.optimization_barrier((other, lowest_near))
-            lowest_far = far(lowest_near, "x")
+            lowest_far = far(lowest_near, "y")
+        if more:
+            left, left_other = more[0], swap(more[0], chip_pairs(level))
         ships.append(
             call(
-                functools.partial(ship_kernel, ("yx", "xy", "yx")[level]),
+                functools.partial(ship_kernel, ("yx", "xy", "xy")[level]),
                 jax.ShapeDtypeStruct((16, 16, 128), BF),
                 [SMEM, VMEM, VMEM],
                 (place, ux, ux_other),

time: 138 us -> 139 us (level)
  waiting for transfers between devices: 50.3 us -> 48 us
  local copies, waits for them, and re-layouts: 6.65 us -> 8.38 us
    ppermute x18 -> x19, waiting for transfers between devices: 27.9 us -> 20.8 us  [turn(): return lax.ppermute(block, 'front', route)]
    ppermute x7 -> x10, waiting for transfers between devices: 9.63 us -> 14.4 us  [swap(): return lax.ppermute(block, 'leaf', pairs)]
    all_to_all x2, starting transfers between devices: 10.4 us -> 8.19 us  [local(): got = lax.all_to_all(sent, 'front', 0, 0)]
    ppermute x18 -> x19, starting transfers between devices: 29.4 us -> 31.5 us  [turn(): return lax.ppermute(block, 'front', route)]
    ppermute x7 -> x10, starting transfers between devices: 9.63 us -> 11 us  [swap(): return lax.ppermute(block, 'leaf', pairs)]
  transfers between devices with their start and end apart: 28 -> 32, of which waited for: 15 -> 14; matrix products, arithmetic and copies ran while one was open for 4% -> 6% of each run, Pallas kernels for 9% -> 12%
where the time goes in v8:
time: 139 us; the launch traced here: 138 us
  starting transfers between devices  57.8 us (42%)
  waiting for transfers between devices  48 us (35%)
  Pallas kernels  22.9 us (16%)
  local copies, waits for them, and re-layouts  8.38 us (6%)
    ppermute x19, starting transfers between devices, turn(): return lax.ppermute(block, 'front', route)  31.5 us
    ppermute x19, waiting for transfers between devices, turn(): return lax.ppermute(block, 'front', route)  20.8 us
    pallas_call x16, Pallas kernels, call(): pl.pallas_call(kernel, out_shape=outs, in_specs=specs, out_specs=tuple((V...  19.6 us
    ppermute x10, waiting for transfers between devices, swap(): return lax.ppermute(block, 'leaf', pairs)  14.4 us
    all_to_all x2, waiting for transfers between devices, local(): got = lax.all_to_all(sent, 'front', 0, 0)  12.8 us
    ppermute x10, starting transfers between devices, swap(): return lax.ppermute(block, 'leaf', pairs)  11 us
    all_to_all x2, starting transfers between devices, local(): got = lax.all_to_all(sent, 'front', 0, 0)  8.19 us
    all_to_all x1, starting transfers between devices, local(): first = lax.all_to_all(sent, 'front', 0, 0)  7.18 us
  transfers between devices with their start and end apart: 32, of which 14 were waited for; matrix products, arithmetic and copies ran while one was open for 6% of the time, Pallas kernels for 12%

profile of v8, /device:TPU:32, one launch (start us, length us, event | category | flops | bytes accessed | tf_op | source)
XLA Modules:
  0.0 138.0 jit_solution(11722674254428961225)
XLA Ops:
  1.3 3.3 %shard_map.95 = (bf16[16,80,256]{2,1,0:T(8,128)(2,1)}, bf16[64,1024]{1,0:T(8,128)(2,1)}, bf16[128,1024]{1,0:T(8,128)(2,1)}) custom-call(s32[12]{0:T(128)} %stack.48.place, f32[1,64,256]{2,1,0:T(8,128)} %leaf_ref.1, f32[15,64,256]{2,1,0:T(8,128)} %rhs_ref.1, bf16[15,64,1024]{2,1,0:T(8,128)(2,1)} %inv_ref.2, bf16[14,64,1024]{2,1,0:T(8,128)(2,1)} %bitcast.39), custom_call_target="tpu_custom_call" | custom-call | tf_op jit(solution)/shard_map/pallas_call | solution.py:101
  4.7 7.2 %all-to-all-start = ((bf16[16,80,256]{2,1,0:T(8,128)(2,1)}), bf16[16,80,256]{2,1,0:T(8,128)(2,1)S(1)}, u32[]{:S(2)}, u32[]{:S(2)}) async-start(bf16[16,80,256]{2,1,0:T(8,128)(2,1)} %get-tuple-element.33), calls=%async_computation | async-start | bytes 1310720 | tf_op jit(solution)/shard_map/all_to_all | solution.py:324
  12.8 3.5 %collective-permute-start.5 = (bf16[64,1024]{1,0:T(8,128)(2,1)S(1)}, bf16[64,1024]{1,0:T(8,128)(2,1)S(1)}, u32[]{:S(2)}, u32[]{:S(2)}) collective-permute-start(bf16[64,1024]{1,0:T(8,128)(2,1)S(1)} %slice.27), channel_id=1, source_target_pairs={{0,8},{1,9},{2,10},{3,11},{4,12},{5,13},{6,14},{7,15},{8,0},{9,1},... | collective-permute-start | bytes 393224 | tf_op jit(solution)/shard_map/ppermute | solution.py:131
  18.3 3.0 %collective-permute-start.2 = (bf16[64,1024]{1,0:T(8,128)(2,1)}, bf16[64,1024]{1,0:T(8,128)(2,1)S(1)}, u32[]{:S(2)}, u32[]{:S(2)}) collective-permute-start(bf16[64,1024]{1,0:T(8,128)(2,1)} %get-tuple-element.39.refs_0_), channel_id=1, source_target_pairs={{0,2},{1,3},{2,0},{3,1},{4,6},{5,7},{6,4},{7,5},{8,10},{9,11},{10,... | collective-permute-start | bytes 393224 | tf_op jit(solution)/shard_map/ppermute | solution.py:131
  22.5 4.5 %collective-permute-done.5.refs_3_ = bf16[64,1024]{1,0:T(8,128)(2,1)S(1)} collective-permute-done((bf16[64,1024]{1,0:T(8,128)(2,1)S(1)}, bf16[64,1024]{1,0:T(8,128)(2,1)S(1)}, u32[]{:S(2)}, u32[]{:S(2)}) %collective-permute-start.5) | collective-permute-done | bytes 131104 | tf_op jit(solution)/shard_map/ppermute | solution.py:131
  27.0 1.5 %collective-permute-start = (bf16[64,1024]{1,0:T(8,128)(2,1)}, bf16[64,1024]{1,0:T(8,128)(2,1)S(1)}, u32[]{:S(2)}, u32[]{:S(2)}) collective-permute-start(bf16[64,1024]{1,0:T(8,128)(2,1)} %get-tuple-element.39.refs_0_), channel_id=1, source_target_pairs={{0,1},{1,2},{2,3},{3,0},{4,5},{5,6},{6,7},{7,4},{8,9},{9,10},{10,1... | collective-permute-start | bytes 393224 | tf_op jit(solution)/shard_map/ppermute | solution.py:131
  29.4 4.0 %collective-permute-done.refs_1_ = bf16[64,1024]{1,0:T(8,128)(2,1)S(1)} collective-permute-done((bf16[64,1024]{1,0:T(8,128)(2,1)}, bf16[64,1024]{1,0:T(8,128)(2,1)S(1)}, u32[]{:S(2)}, u32[]{:S(2)}) %collective-permute-start) | collective-permute-done | bytes 131104 | tf_op jit(solution)/shard_map/ppermute | solution.py:131
  34.1 2.6 %collective-permute-start.6 = (bf16[256,1024]{1,0:T(8,128)(2,1)S(1)}, bf16[256,1024]{1,0:T(8,128)(2,1)}, u32[]{:S(2)}, u32[]{:S(2)}) collective-permute-start(bf16[256,1024]{1,0:T(8,128)(2,1)S(1)} %shard_map.97), channel_id=1, source_target_pairs={{0,12},{1,13},{2,14},{3,15},{4,0},{5,1},{6,2},{7,3},{8,4},{9,5},{1... | collective-permute-start | bytes 1572872 | tf_op jit(solution)/shard_map/ppermute | solution.py:131
  37.1 3.0 %collective-permute-start.10 = (bf16[256,1024]{1,0:T(8,128)(2,1)S(1)}, bf16[256,1024]{1,0:T(8,128)(2,1)}, u32[]{:S(2)}, u32[]{:S(2)}) collective-permute-start(bf16[256,1024]{1,0:T(8,128)(2,1)S(1)} %shard_map.98), channel_id=1, source_target_pairs={{0,3},{1,0},{2,1},{3,2},{4,7},{5,4},{6,5},{7,6},{8,11},{9,8},{10,9... | collective-permute-start | bytes 1572872 | tf_op jit(solution)/shard_map/ppermute | solution.py:131
  40.1 3.6 %all-to-all-start.1 = ((bf16[16,16,1024]{2,1,0:T(8,128)(2,1)}), bf16[16,16,1024]{2,1,0:T(8,128)(2,1)S(1)}, u32[]{:S(2)}, u32[]{:S(2)}) async-start(bf16[16,16,1024]{2,1,0:T(8,128)(2,1)} %copy-done.4), calls=%async_computation.1 | async-start | bytes 1048576 | tf_op jit(solution)/shard_map/all_to_all | solution.py:335
  43.7 5.5 %collective-permute-done.8 = bf16[256,1024]{1,0:T(8,128)(2,1)} collective-permute-done((bf16[256,1024]{1,0:T(8,128)(2,1)S(1)}, bf16[256,1024]{1,0:T(8,128)(2,1)}, u32[]{:S(2)}, u32[]{:S(2)}) %collective-permute-start.8) | collective-permute-done | bytes 524320 | tf_op jit(solution)/shard_map/ppermute | solution.py:131
  49.2 1.7 %slice.37 = bf16[128,1024]{1,0:T(8,128)(2,1)} slice(bf16[256,1024]{1,0:T(8,128)(2,1)} %collective-permute-done.8), slice={[128:256], [0:1024]} | slice | bytes 524288 | tf_op jit(solution)/shard_map/slice | solution.py:152
  50.9 1.7 %slice.36 = bf16[128,1024]{1,0:T(8,128)(2,1)} slice(bf16[256,1024]{1,0:T(8,128)(2,1)} %collective-permute-done.6), slice={[0:128], [0:1024]} | slice | bytes 524288 | tf_op jit(solution)/shard_map/slice | solution.py:152
  52.6 3.2 %collective-permute-start.7 = (bf16[128,1024]{1,0:T(8,128)(2,1)}, bf16[128,1024]{1,0:T(8,128)(2,1)}, u32[]{:S(2)}, u32[]{:S(2)}) collective-permute-start(bf16[128,1024]{1,0:T(8,128)(2,1)} %slice.36), channel_id=1, source_target_pairs={{0,12},{1,13},{2,14},{3,15},{4,0},{5,1},{6,2},{7,3},{8,4},{9,5},{1... | collective-permute-start | bytes 786440 | tf_op jit(solution)/shard_map/ppermute | solution.py:131
  57.4 1.7 %slice.38 = bf16[128,1024]{1,0:T(8,128)(2,1)} slice(bf16[256,1024]{1,0:T(8,128)(2,1)} %collective-permute-done.10), slice={[0:128], [0:1024]} | slice | bytes 524288 | tf_op jit(solution)/shard_map/slice | solution.py:152
  59.0 2.4 %collective-permute-start.11 = (bf16[128,1024]{1,0:T(8,128)(2,1)}, bf16[128,1024]{1,0:T(8,128)(2,1)}, u32[]{:S(2)}, u32[]{:S(2)}) collective-permute-start(bf16[128,1024]{1,0:T(8,128)(2,1)} %slice.38), channel_id=1, source_target_pairs={{0,3},{1,0},{2,1},{3,2},{4,7},{5,4},{6,5},{7,6},{8,11},{9,8},{10,9... | collective-permute-start | bytes 786440 | tf_op jit(solution)/shard_map/ppermute | solution.py:131
  61.8 4.9 %collective-permute-done.14.refs_3_ = bf16[64,1024]{1,0:T(8,128)(2,1)S(1)} collective-permute-done((bf16[64,1024]{1,0:T(8,128)(2,1)S(1)}, bf16[64,1024]{1,0:T(8,128)(2,1)S(1)}, u32[]{:S(2)}, u32[]{:S(2)}) %collective-permute-start.14) | collective-permute-done | bytes 131104 | tf_op jit(solution)/shard_map/ppermute | solution.py:131
  66.8 1.8 %collective-permute-done.11 = bf16[128,1024]{1,0:T(8,128)(2,1)} collective-permute-done((bf16[128,1024]{1,0:T(8,128)(2,1)}, bf16[128,1024]{1,0:T(8,128)(2,1)}, u32[]{:S(2)}, u32[]{:S(2)}) %collective-permute-start.11) | collective-permute-done | bytes 262176 | tf_op jit(solution)/shard_map/ppermute | solution.py:131
  68.6 3.7 %collective-permute-start.20 = (bf16[256,1024]{1,0:T(8,128)(2,1)S(1)}, bf16[256,1024]{1,0:T(8,128)(2,1)S(1)}, u32[]{:S(2)}, u32[]{:S(2)}) collective-permute-start(bf16[256,1024]{1,0:T(8,128)(2,1)S(1)} %shard_map.99), channel_id=1, source_target_pairs={{0,3},{1,0},{2,1},{3,2},{4,7},{5,4},{6,5},{7,6},{8,11},{9,8},{10,9... | collective-permute-start | bytes 1572872 | tf_op jit(solution)/shard_map/ppermute | solution.py:131
  72.3 3.1 %shard_map.100 = (f32[16,1024]{1,0:T(8,128)S(1)}, f32[48,1024]{1,0:T(8,128)S(1)}) custom-call(s32[12]{0:T(128)S(1)} %copy-done.8, bf16[16,80,256]{2,1,0:T(8,128)(2,1)S(1)} %all-to-all-done.rhs_ref.first_ref, bf16[16,16,1024]{2,1,0:T(8,128)(2,1)S(1)} %all-to-all-done.1.got_ref, s32[1,1024]{1,0:T(1,128)S(1)} %copy-done.9), custom_call_target="tpu_custom_call" | custom-call | flops 100000000 | bytes 1000000 | tf_op jit(solution)/shard_map/pallas_call | solution.py:46
  77.0 2.5 %shard_map.101.own_ref = f32[16,1536]{1,0:T(8,128)S(1)} custom-call(f32[16,1024]{1,0:T(8,128)S(1)} %get-tuple-element.48.own_ref, f32[16,1024]{1,0:T(8,128)S(1)} %collective-permute-done.15.other_ref, bf16[4,64,1024]{2,1,0:T(8,128)(2,1)S(1)} %bitcast.30, bf16[4,64,1024]{2,1,0:T(8,128)(2,1)} %bitcast.15.refs_1_, bf16[4,64,1024]{2,1,0:T(8,128)(2,1)} %bitcast.16.refs_2_, ...), custom_call_target="tpu_custom_call" | custom-call | flops 100000000 | bytes 1000000 | tf_op jit(solution)/shard_map/pallas_call | solution.py:46
  80.8 2.4 %shard_map.102 = (f32[16,1024]{1,0:T(8,128)S(1)}, f32[32,1024]{1,0:T(8,128)S(1)}) custom-call(s32[12]{0:T(128)S(1)} %copy-done.8, f32[16,1536]{1,0:T(8,128)S(1)} %shard_map.101.own_ref, f32[16,1536]{1,0:T(8,128)S(1)} %collective-permute-done.16.other_ref, f32[48,1024]{1,0:T(8,128)S(1)} %get-tuple-element.51.left_ref, ...), custom_call_target="tpu_custom_call" | custom-call | flops 100000000 | bytes 1000000 | tf_op jit(solution)/shard_map/pallas_call | solution.py:46
  83.4 4.2 %collective-permute-done.18.other_ref = f32[16,1024]{1,0:T(8,128)S(1)} collective-permute-done((f32[16,1024]{1,0:T(8,128)S(1)}, f32[16,1024]{1,0:T(8,128)S(1)}, u32[]{:S(2)}, u32[]{:S(2)}) %collective-permute-start.18) | collective-permute-done | bytes 65568 | tf_op jit(solution)/shard_map/ppermute | solution.py:292
  87.6 3.3 %collective-permute-start.24 = (bf16[128,1024]{1,0:T(8,128)(2,1)S(1)}, bf16[128,1024]{1,0:T(8,128)(2,1)S(1)}, u32[]{:S(2)}, u32[]{:S(2)}) collective-permute-start(bf16[128,1024]{1,0:T(8,128)(2,1)S(1)} %slice.33), channel_id=1, source_target_pairs={{0,3},{1,0},{2,1},{3,2},{4,7},{5,4},{6,5},{7,6},{8,11},{9,8},{10,9... | collective-permute-start | bytes 786440 | tf_op jit(solution)/shard_map/ppermute | solution.py:131
  91.2 2.3 %shard_map.103.own_ref = f32[16,1536]{1,0:T(8,128)S(1)} custom-call(f32[16,1024]{1,0:T(8,128)S(1)} %get-tuple-element.52.own_ref, f32[16,1024]{1,0:T(8,128)S(1)} %collective-permute-done.18.other_ref, bf16[4,64,1024]{2,1,0:T(8,128)(2,1)S(1)} %bitcast.31, bf16[4,64,1024]{2,1,0:T(8,128)(2,1)S(1)} %bitcast.33, bf16[4,64,1024]{2,1,0:T(8,128)(2,1)} %bitcast.21.refs_2_, ...), custom_call_target="tpu_custom_call" | custom-call | flops 100000000 | bytes 1000000 | tf_op jit(solution)/shard_map/pallas_call | solution.py:46
  93.5 2.4 %collective-permute-done.22.left_other_ref = f32[32,1024]{1,0:T(8,128)S(1)} collective-permute-done((f32[32,1024]{1,0:T(8,128)S(1)}, f32[32,1024]{1,0:T(8,128)S(1)}, u32[]{:S(2)}, u32[]{:S(2)}) %collective-permute-start.22) | collective-permute-done | bytes 131104 | tf_op jit(solution)/shard_map/ppermute | solution.py:292
  95.9 1.8 %shard_map.104 = (f32[16,1024]{1,0:T(8,128)S(1)}, f32[16,1024]{1,0:T(8,128)S(1)}) custom-call(s32[12]{0:T(128)S(1)} %copy-done.8, f32[16,1536]{1,0:T(8,128)S(1)} %shard_map.103.own_ref, f32[16,1536]{1,0:T(8,128)S(1)} %collective-permute-done.21.other_ref, f32[32,1024]{1,0:T(8,128)S(1)} %get-tuple-element.57.left_ref, ...), custom_call_target="tpu_custom_call" | custom-call | flops 100000000 | bytes 1000000 | tf_op jit(solution)/shard_map/pallas_call | solution.py:46
  97.7 3.3 %collective-permute-start.23 = (f32[16,1024]{1,0:T(8,128)S(1)}, f32[16,1024]{1,0:T(8,128)S(1)}, u32[]{:S(2)}, u32[]{:S(2)}) collective-permute-start(f32[16,1024]{1,0:T(8,128)S(1)} %get-tuple-element.58.own_ref), channel_id=1, source_target_pairs={{0,64},{16,80},{32,96},{48,112},{64,0},{80,16},{96,32},{112,48},{1... | collective-permute-start | bytes 196616 | tf_op jit(solution)/shard_map/ppermute | solution.py:292
  101.3 3.8 %collective-permute-done.23.other_ref = f32[16,1024]{1,0:T(8,128)S(1)} collective-permute-done((f32[16,1024]{1,0:T(8,128)S(1)}, f32[16,1024]{1,0:T(8,128)S(1)}, u32[]{:S(2)}, u32[]{:S(2)}) %collective-permute-start.23) | collective-permute-done | bytes 65568 | tf_op jit(solution)/shard_map/ppermute | solution.py:292
  108.8 6.1 %collective-permute-start.28 = (f32[16,1024]{1,0:T(8,128)S(1)}, f32[16,1024]{1,0:T(8,128)S(1)}, u32[]{:S(2)}, u32[]{:S(2)}) collective-permute-start(f32[16,1024]{1,0:T(8,128)S(1)} %shard_map.106.own_ref), channel_id=1, source_target_pairs={{0,192},{16,208},{32,224},{48,240},{64,128},{80,144},{96,160},{112... | collective-permute-start | bytes 196616 | tf_op jit(solution)/shard_map/ppermute | solution.py:292
  118.7 4.6 %all-to-all-start.2 = ((bf16[16,16,1408]{2,1,0:T(8,128)(2,1)}), bf16[16,16,1408]{2,1,0:T(8,128)(2,1)S(1)}, u32[]{:S(2)}, u32[]{:S(2)}) async-start(bf16[16,16,1408]{2,1,0:T(8,128)(2,1)} %shard_map.110), calls=%async_computation.2 | async-start | bytes 1441792 | tf_op jit(solution)/shard_map/all_to_all | solution.py:386
  124.2 12.8 %all-to-all-done.2.got_ref = bf16[16,16,1408]{2,1,0:T(8,128)(2,1)S(1)} async-done(((bf16[16,16,1408]{2,1,0:T(8,128)(2,1)}), bf16[16,16,1408]{2,1,0:T(8,128)(2,1)S(1)}, u32[]{:S(2)}, u32[]{:S(2)}) %all-to-all-start.2) | async-done | bytes 720928 | tf_op jit(solution)/shard_map/all_to_all | solution.py:386
  (79 shorter events, 21.9 us)
Async XLA Ops:
  4.7 23.8 %all-to-all-start = ((bf16[16,80,256]{2,1,0:T(8,128)(2,1)}), bf16[16,80,256]{2,1,0:T(8,128)(2,1)S(1)}, u32[]{:S(2)}, u32[]{:S(2)}) async-start(bf16[16,80,256]{2,1,0:T(8,128)(2,1)} %get-tuple-element.33), calls=%async_computation | async-start | bytes 1310720 | tf_op jit(solution)/shard_map/all_to_all | solution.py:324
  12.8 14.2 %collective-permute-start.5 = (bf16[64,1024]{1,0:T(8,128)(2,1)S(1)}, bf16[64,1024]{1,0:T(8,128)(2,1)S(1)}, u32[]{:S(2)}, u32[]{:S(2)}) collective-permute-start(bf16[64,1024]{1,0:T(8,128)(2,1)S(1)} %slice.27), channel_id=1, source_target_pairs={{0,8},{1,9},{2,10},{3,11},{4,12},{5,13},{6,14},{7,15},{8,0},{9,1},... | collective-permute-start | bytes 393224 | tf_op jit(solution)/shard_map/ppermute | solution.py:131
  16.3 17.1 %collective-permute-start.4 = (bf16[128,1024]{1,0:T(8,128)(2,1)}, bf16[128,1024]{1,0:T(8,128)(2,1)S(1)}, u32[]{:S(2)}, u32[]{:S(2)}) collective-permute-start(bf16[128,1024]{1,0:T(8,128)(2,1)} %get-tuple-element.43.refs_0_), channel_id=1, source_target_pairs={{0,12},{1,13},{2,14},{3,15},{4,0},{5,1},{6,2},{7,3},{8,4},{9,5},{1... | collective-permute-start | bytes 786440 | tf_op jit(solution)/shard_map/ppermute | solution.py:131
  17.5 15.9 %collective-permute-start.3 = (bf16[128,1024]{1,0:T(8,128)(2,1)}, bf16[128,1024]{1,0:T(8,128)(2,1)S(1)}, u32[]{:S(2)}, u32[]{:S(2)}) collective-permute-start(bf16[128,1024]{1,0:T(8,128)(2,1)} %get-tuple-element.43.refs_0_), channel_id=1, source_target_pairs={{0,4},{1,5},{2,6},{3,7},{4,8},{5,9},{6,10},{7,11},{8,12},{9,13},{1... | collective-permute-start | bytes 786440 | tf_op jit(solution)/shard_map/ppermute | solution.py:131
  18.3 11.0 %collective-permute-start.2 = (bf16[64,1024]{1,0:T(8,128)(2,1)}, bf16[64,1024]{1,0:T(8,128)(2,1)S(1)}, u32[]{:S(2)}, u32[]{:S(2)}) collective-permute-start(bf16[64,1024]{1,0:T(8,128)(2,1)} %get-tuple-element.39.refs_0_), channel_id=1, source_target_pairs={{0,2},{1,3},{2,0},{3,1},{4,6},{5,7},{6,4},{7,5},{8,10},{9,11},{10,... | collective-permute-start | bytes 393224 | tf_op jit(solution)/shard_map/ppermute | solution.py:131
  21.3 8.1 %collective-permute-start.1 = (bf16[64,1024]{1,0:T(8,128)(2,1)}, bf16[64,1024]{1,0:T(8,128)(2,1)S(1)}, u32[]{:S(2)}, u32[]{:S(2)}) collective-permute-start(bf16[64,1024]{1,0:T(8,128)(2,1)} %get-tuple-element.39.refs_0_), channel_id=1, source_target_pairs={{0,3},{1,0},{2,1},{3,2},{4,7},{5,4},{6,5},{7,6},{8,11},{9,8},{10,9... | collective-permute-start | bytes 393224 | tf_op jit(solution)/shard_map/ppermute | solution.py:131
  27.0 6.4 %collective-permute-start = (bf16[64,1024]{1,0:T(8,128)(2,1)}, bf16[64,1024]{1,0:T(8,128)(2,1)S(1)}, u32[]{:S(2)}, u32[]{:S(2)}) collective-permute-start(bf16[64,1024]{1,0:T(8,128)(2,1)} %get-tuple-element.39.refs_0_), channel_id=1, source_target_pairs={{0,1},{1,2},{2,3},{3,0},{4,5},{5,6},{6,7},{7,4},{8,9},{9,10},{10,1... | collective-permute-start | bytes 393224 | tf_op jit(solution)/shard_map/ppermute | solution.py:131
  33.4 15.8 %collective-permute-start.8 = (bf16[256,1024]{1,0:T(8,128)(2,1)S(1)}, bf16[256,1024]{1,0:T(8,128)(2,1)}, u32[]{:S(2)}, u32[]{:S(2)}) collective-permute-start(bf16[256,1024]{1,0:T(8,128)(2,1)S(1)} %shard_map.97), channel_id=1, source_target_pairs={{0,4},{1,5},{2,6},{3,7},{4,8},{5,9},{6,10},{7,11},{8,12},{9,13},{1... | collective-permute-start | bytes 1572872 | tf_op jit(solution)/shard_map/ppermute | solution.py:131
  34.1 16.8 %collective-permute-start.6 = (bf16[256,1024]{1,0:T(8,128)(2,1)S(1)}, bf16[256,1024]{1,0:T(8,128)(2,1)}, u32[]{:S(2)}, u32[]{:S(2)}) collective-permute-start(bf16[256,1024]{1,0:T(8,128)(2,1)S(1)} %shard_map.97), channel_id=1, source_target_pairs={{0,12},{1,13},{2,14},{3,15},{4,0},{5,1},{6,2},{7,3},{8,4},{9,5},{1... | collective-permute-start | bytes 1572872 | tf_op jit(solution)/shard_map/ppermute | solution.py:131
  36.8 19.0 %collective-permute-start.12 = (bf16[256,1024]{1,0:T(8,128)(2,1)S(1)}, bf16[256,1024]{1,0:T(8,128)(2,1)S(1)}, u32[]{:S(2)}, u32[]{:S(2)}) collective-permute-start(bf16[256,1024]{1,0:T(8,128)(2,1)S(1)} %shard_map.98), channel_id=1, source_target_pairs={{0,1},{1,2},{2,3},{3,0},{4,5},{5,6},{6,7},{7,4},{8,9},{9,10},{10,1... | collective-permute-start | bytes 1572872 | tf_op jit(solution)/shard_map/ppermute | solution.py:131
  37.1 20.2 %collective-permute-start.10 = (bf16[256,1024]{1,0:T(8,128)(2,1)S(1)}, bf16[256,1024]{1,0:T(8,128)(2,1)}, u32[]{:S(2)}, u32[]{:S(2)}) collective-permute-start(bf16[256,1024]{1,0:T(8,128)(2,1)S(1)} %shard_map.98), channel_id=1, source_target_pairs={{0,3},{1,0},{2,1},{3,2},{4,7},{5,4},{6,5},{7,6},{8,11},{9,8},{10,9... | collective-permute-start | bytes 1572872 | tf_op jit(solution)/shard_map/ppermute | solution.py:131
  40.1 26.7 %all-to-all-start.1 = ((bf16[16,16,1024]{2,1,0:T(8,128)(2,1)}), bf16[16,16,1024]{2,1,0:T(8,128)(2,1)S(1)}, u32[]{:S(2)}, u32[]{:S(2)}) async-start(bf16[16,16,1024]{2,1,0:T(8,128)(2,1)} %copy-done.4), calls=%async_computation.1 | async-start | bytes 1048576 | tf_op jit(solution)/shard_map/all_to_all | solution.py:335
  50.9 15.9 %collective-permute-start.9 = (bf16[128,1024]{1,0:T(8,128)(2,1)}, bf16[128,1024]{1,0:T(8,128)(2,1)}, u32[]{:S(2)}, u32[]{:S(2)}) collective-permute-start(bf16[128,1024]{1,0:T(8,128)(2,1)} %slice.37), channel_id=1, source_target_pairs={{0,4},{1,5},{2,6},{3,7},{4,8},{5,9},{6,10},{7,11},{8,12},{9,13},{1... | collective-permute-start | bytes 786440 | tf_op jit(solution)/shard_map/ppermute | solution.py:131
  52.6 14.2 %collective-permute-start.7 = (bf16[128,1024]{1,0:T(8,128)(2,1)}, bf16[128,1024]{1,0:T(8,128)(2,1)}, u32[]{:S(2)}, u32[]{:S(2)}) collective-permute-start(bf16[128,1024]{1,0:T(8,128)(2,1)} %slice.36), channel_id=1, source_target_pairs={{0,12},{1,13},{2,14},{3,15},{4,0},{5,1},{6,2},{7,3},{8,4},{9,5},{1... | collective-permute-start | bytes 786440 | tf_op jit(solution)/shard_map/ppermute | solution.py:131
  56.6 10.2 %collective-permute-start.13 = (bf16[128,1024]{1,0:T(8,128)(2,1)}, bf16[128,1024]{1,0:T(8,128)(2,1)}, u32[]{:S(2)}, u32[]{:S(2)}) collective-permute-start(bf16[128,1024]{1,0:T(8,128)(2,1)} %slice.39), channel_id=1, source_target_pairs={{0,1},{1,2},{2,3},{3,0},{4,5},{5,6},{6,7},{7,4},{8,9},{9,10},{10,1... | collective-permute-start | bytes 786440 | tf_op jit(solution)/shard_map/ppermute | solution.py:131
  59.0 9.5 %collective-permute-start.11 = (bf16[128,1024]{1,0:T(8,128)(2,1)}, bf16[128,1024]{1,0:T(8,128)(2,1)}, u32[]{:S(2)}, u32[]{:S(2)}) collective-permute-start(bf16[128,1024]{1,0:T(8,128)(2,1)} %slice.38), channel_id=1, source_target_pairs={{0,3},{1,0},{2,1},{3,2},{4,7},{5,4},{6,5},{7,6},{8,11},{9,8},{10,9... | collective-permute-start | bytes 786440 | tf_op jit(solution)/shard_map/ppermute | solution.py:131
  61.5 5.2 %collective-permute-start.14 = (bf16[64,1024]{1,0:T(8,128)(2,1)S(1)}, bf16[64,1024]{1,0:T(8,128)(2,1)S(1)}, u32[]{:S(2)}, u32[]{:S(2)}) collective-permute-start(bf16[64,1024]{1,0:T(8,128)(2,1)S(1)} %slice.32), channel_id=1, source_target_pairs={{0,12},{1,13},{2,14},{3,15},{4,0},{5,1},{6,2},{7,3},{8,4},{9,5},{1... | collective-permute-start | bytes 393224 | tf_op jit(solution)/shard_map/ppermute | solution.py:131
  68.6 19.0 %collective-permute-start.20 = (bf16[256,1024]{1,0:T(8,128)(2,1)S(1)}, bf16[256,1024]{1,0:T(8,128)(2,1)S(1)}, u32[]{:S(2)}, u32[]{:S(2)}) collective-permute-start(bf16[256,1024]{1,0:T(8,128)(2,1)S(1)} %shard_map.99), channel_id=1, source_target_pairs={{0,3},{1,0},{2,1},{3,2},{4,7},{5,4},{6,5},{7,6},{8,11},{9,8},{10,9... | collective-permute-start | bytes 1572872 | tf_op jit(solution)/shard_map/ppermute | solution.py:131
  72.2 15.3 %collective-permute-start.19 = (bf16[256,1024]{1,0:T(8,128)(2,1)S(1)}, bf16[256,1024]{1,0:T(8,128)(2,1)S(1)}, u32[]{:S(2)}, u32[]{:S(2)}) collective-permute-start(bf16[256,1024]{1,0:T(8,128)(2,1)S(1)} %shard_map.99), channel_id=1, source_target_pairs={{0,1},{1,2},{2,3},{3,0},{4,5},{5,6},{6,7},{7,4},{8,9},{9,10},{10,1... | collective-permute-start | bytes 1572872 | tf_op jit(solution)/shard_map/ppermute | solution.py:131
  75.4 5.5 %collective-permute-start.17 = (f32[48,1024]{1,0:T(8,128)S(1)}, f32[48,1024]{1,0:T(8,128)S(1)}, u32[]{:S(2)}, u32[]{:S(2)}) collective-permute-start(f32[48,1024]{1,0:T(8,128)S(1)} %get-tuple-element.51.left_ref), channel_id=1, source_target_pairs={{0,16},{16,0},{32,48},{48,32},{64,80},{80,64},{96,112},{112,96},{1... | collective-permute-start | bytes 589832 | tf_op jit(solution)/shard_map/ppermute | solution.py:292
  75.5 1.5 %collective-permute-start.15 = (f32[16,1024]{1,0:T(8,128)S(1)}, f32[16,1024]{1,0:T(8,128)S(1)}, u32[]{:S(2)}, u32[]{:S(2)}) collective-permute-start(f32[16,1024]{1,0:T(8,128)S(1)} %get-tuple-element.48.own_ref), channel_id=1, source_target_pairs={{0,16},{16,0},{32,48},{48,32},{64,80},{80,64},{96,112},{112,96},{1... | collective-permute-start | bytes 196616 | tf_op jit(solution)/shard_map/ppermute | solution.py:292
  79.5 1.4 collective-permute-start.16
  83.3 4.3 %collective-permute-start.18 = (f32[16,1024]{1,0:T(8,128)S(1)}, f32[16,1024]{1,0:T(8,128)S(1)}, u32[]{:S(2)}, u32[]{:S(2)}) collective-permute-start(f32[16,1024]{1,0:T(8,128)S(1)} %get-tuple-element.52.own_ref), channel_id=1, source_target_pairs={{0,32},{16,48},{32,0},{48,16},{64,96},{80,112},{96,64},{112,80},{1... | collective-permute-start | bytes 196616 | tf_op jit(solution)/shard_map/ppermute | solution.py:292
  87.6 17.5 %collective-permute-start.24 = (bf16[128,1024]{1,0:T(8,128)(2,1)S(1)}, bf16[128,1024]{1,0:T(8,128)(2,1)S(1)}, u32[]{:S(2)}, u32[]{:S(2)}) collective-permute-start(bf16[128,1024]{1,0:T(8,128)(2,1)S(1)} %slice.33), channel_id=1, source_target_pairs={{0,3},{1,0},{2,1},{3,2},{4,7},{5,4},{6,5},{7,6},{8,11},{9,8},{10,9... | collective-permute-start | bytes 786440 | tf_op jit(solution)/shard_map/ppermute | solution.py:131
  90.9 14.2 %collective-permute-start.25 = (bf16[128,1024]{1,0:T(8,128)(2,1)S(1)}, bf16[128,1024]{1,0:T(8,128)(2,1)S(1)}, u32[]{:S(2)}, u32[]{:S(2)}) collective-permute-start(bf16[128,1024]{1,0:T(8,128)(2,1)S(1)} %slice.34), channel_id=1, source_target_pairs={{0,1},{1,2},{2,3},{3,0},{4,5},{5,6},{6,7},{7,4},{8,9},{9,10},{10,1... | collective-permute-start | bytes 786440 | tf_op jit(solution)/shard_map/ppermute | solution.py:131
  90.9 5.0 %collective-permute-start.22 = (f32[32,1024]{1,0:T(8,128)S(1)}, f32[32,1024]{1,0:T(8,128)S(1)}, u32[]{:S(2)}, u32[]{:S(2)}) collective-permute-start(f32[32,1024]{1,0:T(8,128)S(1)} %get-tuple-element.57.left_ref), channel_id=1, source_target_pairs={{0,32},{16,48},{32,0},{48,16},{64,96},{80,112},{96,64},{112,80},{1... | collective-permute-start | bytes 393224 | tf_op jit(solution)/shard_map/ppermute | solution.py:292
  93.4 2.5 %collective-permute-start.21 = (f32[16,1536]{1,0:T(8,128)S(1)}, f32[16,1536]{1,0:T(8,128)S(1)}, u32[]{:S(2)}, u32[]{:S(2)}) collective-permute-start(f32[16,1536]{1,0:T(8,128)S(1)} %shard_map.103.own_ref), channel_id=1, source_target_pairs={{0,16},{16,0},{32,48},{48,32},{64,80},{80,64},{96,112},{112,96},{1... | collective-permute-start | bytes 294920 | tf_op jit(solution)/shard_map/ppermute | solution.py:292
  97.7 7.3 %collective-permute-start.23 = (f32[16,1024]{1,0:T(8,128)S(1)}, f32[16,1024]{1,0:T(8,128)S(1)}, u32[]{:S(2)}, u32[]{:S(2)}) collective-permute-start(f32[16,1024]{1,0:T(8,128)S(1)} %get-tuple-element.58.own_ref), channel_id=1, source_target_pairs={{0,64},{16,80},{32,96},{48,112},{64,0},{80,16},{96,32},{112,48},{1... | collective-permute-start | bytes 196616 | tf_op jit(solution)/shard_map/ppermute | solution.py:292
  101.0 5.3 %collective-permute-start.26 = (f32[16,1024]{1,0:T(8,128)S(1)}, f32[16,1024]{1,0:T(8,128)S(1)}, u32[]{:S(2)}, u32[]{:S(2)}) collective-permute-start(f32[16,1024]{1,0:T(8,128)S(1)} %get-tuple-element.61.left_ref), channel_id=1, source_target_pairs={{0,64},{16,80},{32,96},{48,112},{64,0},{80,16},{96,32},{112,48},{1... | collective-permute-start | bytes 196616 | tf_op jit(solution)/shard_map/ppermute | solution.py:292
  106.3 1.3 collective-permute-start.27
  108.8 8.9 %collective-permute-start.28 = (f32[16,1024]{1,0:T(8,128)S(1)}, f32[16,1024]{1,0:T(8,128)S(1)}, u32[]{:S(2)}, u32[]{:S(2)}) collective-permute-start(f32[16,1024]{1,0:T(8,128)S(1)} %shard_map.106.own_ref), channel_id=1, source_target_pairs={{0,192},{16,208},{32,224},{48,240},{64,128},{80,144},{96,160},{112... | collective-permute-start | bytes 196616 | tf_op jit(solution)/shard_map/ppermute | solution.py:292
  118.7 18.4 %all-to-all-start.2 = ((bf16[16,16,1408]{2,1,0:T(8,128)(2,1)}), bf16[16,16,1408]{2,1,0:T(8,128)(2,1)S(1)}, u32[]{:S(2)}, u32[]{:S(2)}) async-start(bf16[16,16,1408]{2,1,0:T(8,128)(2,1)} %shard_map.110), calls=%async_computation.2 | async-start | bytes 1441792 | tf_op jit(solution)/shard_map/all_to_all | solution.py:386
  (10 other events, 210.4 us)

commit v9 on v8

--- a/solution.py
+++ b/solution.py
@@ -112,17 +112,14 @@
     )(place, rhs_leaf, rhs_top, inv_top, off_top)
 
 
-def stack_kernel(starts, *refs):
-    for k, (start, ref) in enumerate(zip(starts, refs)):
-        refs[-1][k * 64 : (k + 1) * 64, :] = ref[start : start + 64, :]
-
-
-def stack(parts, starts):
+def stack_kernel(*refs):
+    for k, ref in enumerate(refs[:-1]):
+        refs[-1][k * 64 : (k + 1) * 64, :] = ref[...]
+
+
+def stack(parts):
     return call(
-        functools.partial(stack_kernel, starts),
-        jax.ShapeDtypeStruct((256, 1024), BF),
-        [VMEM] * 4,
-        tuple(parts),
+        stack_kernel, jax.ShapeDtypeStruct((256, 1024), BF), [VMEM] * 4, tuple(parts)
     )
 
 
@@ -226,6 +223,18 @@
     )
 
 
+def gathered_solve(own, other, weights, level):
+    whole = pl.BlockSpec(own.shape, lambda i: (0, 0))
+    return pl.pallas_call(
+        solve_kernel,
+        grid=(1,),
+        in_specs=[whole, whole, pl.BlockSpec((FRONTS, 64, 1024), lambda i: (0, level, 0))],
+        out_specs=pl.BlockSpec((16, 1536), lambda i: (0, 0)),
+        out_shape=jax.ShapeDtypeStruct((16, 1536), F32),
+        compiler_params=params(),
+    )(own, other, weights)
+
+
 def update_kernel(level, place, own_ref, other_ref, left_ref, left_other_ref, idx_ref, *outs):
     update = own_ref[:, :1024] + other_ref[:, :1024]
     count = left_ref.shape[0] // 16
@@ -251,7 +260,7 @@
     )
 
 
-def ship_kernel(order, place, own_ref, other_ref, out_ref):
+def ship_kernel(turned, place, own_ref, other_ref, out_ref):
     first = place[8] == 0
     own = own_ref[:, 1024:]
     other = other_ref[:, 1024:]
@@ -259,10 +268,9 @@
     high_core = jnp.where(first, other, own)
     for k in range(FRONTS):
         outer, inner = (0, 3, 1, 2)[k // 4], (0, 3, 1, 2)[k % 4]
-        if order == "yx":
+        to = k
+        if turned:
             to = (place[10] + outer) % 4 * 4 + (place[11] + inner) % 4
-        else:
-            to = (place[10] + inner) % 4 * 4 + (place[11] + outer) % 4
         at = slice(k * 32, (k + 1) * 32)
         value = jnp.concatenate([low_core[:, at], high_core[:, at]], axis=1)
         high = value.astype(BF).astype(F32)
@@ -322,27 +330,20 @@
 
     sent, third, pair = first_payload(place, rhs_leaf, rhs_top, inv_top, off_top)
     first = lax.all_to_all(sent, "front", 0, 0)
+    weights = lax.all_gather(pair, "front", axis=0)
     third = (third, *near(third, "y"), opposite(third, "y"))
-    pair = (pair, *near(pair, "x"))
-    second = opposite(pair[0][:64], "x")
     leaf_x, sent = call(
         leaf_solve_kernel,
         (jax.ShapeDtypeStruct((64, 256), F32), jax.ShapeDtypeStruct((FRONTS, 16, 1024), BF)),
         [VMEM] * 3,
         (inv_leaf, first, off_leaf),
     )
-    sent, third, pair, second = lax.optimization_barrier((sent, third, pair, second))
+    sent, third = lax.optimization_barrier((sent, third))
     got = lax.all_to_all(sent, "front", 0, 0)
-    third = stack(third, (0, 0, 0, 0))
-    second = stack((*pair, second), (0, 0, 0, 0))
-    third_near, second_near = near(third, "x"), near(second, "y")
-    lowest = turn(pair[2][64:], -1, 0)
-    third_far, second_far = far(third_near, "x"), far(second_near, "y")
-    lowest = stack((*pair, lowest), (64, 64, 64, 0))
-    got, third_far, second_far, lowest = lax.optimization_barrier(
-        (got, third_far, second_far, lowest)
-    )
-    lowest_near = near(lowest, "y")
+    third = stack(third)
+    third_near = near(third, "x")
+    third_far = far(third_near, "x")
+    got, third_far = lax.optimization_barrier((got, third_far))
     state, left = call(
         leaf_update_kernel,
         (jax.ShapeDtypeStruct((16, 1024), F32), jax.ShapeDtypeStruct((48, 1024), F32)),
@@ -353,25 +354,19 @@
     ships = []
     for level in range(3):
         if level == 0:
-            parts = (third, *third_near, *third_far)
-        elif level == 1:
-            parts = (second, *second_near, *second_far)
+            ux = top_solve(state, other, (third, *third_near, *third_far))
         else:
-            parts = (lowest, *lowest_near, *lowest_far)
-        ux = top_solve(state, other, parts)
+            ux = gathered_solve(state, other, weights, level - 1)
         if level == 2:
             ux, left_other = lax.optimization_barrier((ux, left_other))
         ux_other = swap(ux, core_pairs())
         state, *more = top_update(level, place, ux, ux_other, left, left_other, idx_top)
         other = swap(state, chip_pairs(level))
-        if level == 0:
-            other, lowest_near = lax.optimization_barrier((other, lowest_near))
-            lowest_far = far(lowest_near, "y")
         if more:
             left, left_other = more[0], swap(more[0], chip_pairs(level))
         ships.append(
             call(
-                functools.partial(ship_kernel, ("yx", "xy", "xy")[level]),
+                functools.partial(ship_kernel, level == 0),
                 jax.ShapeDtypeStruct((16, 16, 128), BF),
                 [SMEM, VMEM, VMEM],
                 (place, ux, ux_other),

time: 139 us -> 145 us (1.043)
  waiting for transfers between devices: 48 us -> 62.6 us
  starting transfers between devices: 57.8 us -> 43.2 us
  between operations: 0.89 us -> 14.2 us
  local copies, waits for them, and re-layouts: 8.38 us -> 5.19 us
  Pallas kernels: 22.9 us -> 19.9 us
    ppermute x19 -> x7, starting transfers between devices: 31.5 us -> 12.8 us  [turn(): return lax.ppermute(block, 'front', route)]
    ppermute x19 -> x7, waiting for transfers between devices: 20.8 us -> 28.8 us  [turn(): return lax.ppermute(block, 'front', route)]
    all_to_all x1, waiting for transfers between devices: 0.01 us -> 7.45 us  [local(): first = lax.all_to_all(sent, 'front', 0, 0)]
    slice x6 -> x2, local copies, waits for them, and re-layouts: 5.8 us -> 1.46 us  [far(): return (turn(after[:half], -dx, -dy), turn(before[half:], dx, dy))]
    pallas_call x16 -> x12, Pallas kernels: 19.6 us -> 15.3 us  [call(): pl.pallas_call(kernel, out_shape=outs, in_specs=specs, out_specs=tuple((V...]
    ppermute x10, starting transfers between devices: 11 us -> 14.4 us  [swap(): return lax.ppermute(block, 'leaf', pairs)]
    unnamed x20 -> x16, local copies, waits for them, and re-layouts: 0.05 us -> 2.21 us
    ppermute x10, waiting for transfers between devices: 14.4 us -> 12.3 us  [swap(): return lax.ppermute(block, 'leaf', pairs)]
  transfers between devices with their start and end apart: 32 -> 21, of which waited for: 14 -> 16; matrix products, arithmetic and copies ran while one was open for 6% -> 2% of each run, Pallas kernels for 12% -> 8%
where the time goes in v9:
time: 145 us
  waiting for transfers between devices  62.6 us (43%)
  starting transfers between devices  43.2 us (30%)
  Pallas kernels  19.9 us (14%)
  between operations  14.2 us (10%)
  local copies, waits for them, and re-layouts  5.19 us (4%)
    ppermute x7, waiting for transfers between devices, turn(): return lax.ppermute(block, 'front', route)  28.8 us
    pallas_call x12, Pallas kernels, call(): pl.pallas_call(kernel, out_shape=outs, in_specs=specs, out_specs=tuple((V...  15.3 us
    ppermute x10, starting transfers between devices, swap(): return lax.ppermute(block, 'leaf', pairs)  14.4 us
    all_to_all x2, waiting for transfers between devices, local(): got = lax.all_to_all(sent, 'front', 0, 0)  14.1 us
    ppermute x7, starting transfers between devices, turn(): return lax.ppermute(block, 'front', route)  12.8 us
    ppermute x10, waiting for transfers between devices, swap(): return lax.ppermute(block, 'leaf', pairs)  12.3 us
    all_to_all x2, starting transfers between devices, local(): got = lax.all_to_all(sent, 'front', 0, 0)  8.78 us
    all_to_all x1, waiting for transfers between devices, local(): first = lax.all_to_all(sent, 'front', 0, 0)  7.45 us
  transfers between devices with their start and end apart: 21, of which 16 were waited for; matrix products, arithmetic and copies ran while one was open for 2% of the time, Pallas kernels for 8%

profile of v9, /device:TPU:32, one launch (start us, length us, event | category | flops | bytes accessed | tf_op | source)
XLA Modules:
  0.0 145.0 jit_solution(16728333132918258273)
XLA Ops:
  7.8 3.3 %shard_map.95 = (bf16[16,80,256]{2,1,0:T(8,128)(2,1)}, bf16[64,1024]{1,0:T(8,128)(2,1)}, bf16[128,1024]{1,0:T(8,128)(2,1)}) custom-call(s32[12]{0:T(128)} %stack.48.place, f32[1,64,256]{2,1,0:T(8,128)} %leaf_ref.1, f32[15,64,256]{2,1,0:T(8,128)} %rhs_ref.1, bf16[15,64,1024]{2,1,0:T(8,128)(2,1)} %inv_ref.2, bf16[14,64,1024]{2,1,0:T(8,128)(2,1)} %bitcast.29), custom_call_target="tpu_custom_call" | custom-call | tf_op jit(solution)/shard_map/pallas_call | solution.py:101
  11.2 7.2 %all-to-all-start = ((bf16[16,80,256]{2,1,0:T(8,128)(2,1)}), bf16[16,80,256]{2,1,0:T(8,128)(2,1)S(1)}, u32[]{:S(2)}, u32[]{:S(2)}) async-start(bf16[16,80,256]{2,1,0:T(8,128)(2,1)} %get-tuple-element.23), calls=%async_computation | async-start | bytes 1310720 | tf_op jit(solution)/shard_map/all_to_all | solution.py:332
  18.4 1.9 %collective-permute-start = (bf16[64,1024]{1,0:T(8,128)(2,1)}, bf16[64,1024]{1,0:T(8,128)(2,1)S(1)}, u32[]{:S(2)}, u32[]{:S(2)}) collective-permute-start(bf16[64,1024]{1,0:T(8,128)(2,1)} %get-tuple-element.28.refs_0_), channel_id=1, source_target_pairs={{0,1},{1,2},{2,3},{3,0},{4,5},{5,6},{6,7},{7,4},{8,9},{9,10},{10,1... | collective-permute-start | bytes 393224 | tf_op jit(solution)/shard_map/ppermute | solution.py:128
  20.3 1.4 collective-permute-start.1
  21.7 2.1 %collective-permute-start.2 = (bf16[64,1024]{1,0:T(8,128)(2,1)}, bf16[64,1024]{1,0:T(8,128)(2,1)S(1)}, u32[]{:S(2)}, u32[]{:S(2)}) collective-permute-start(bf16[64,1024]{1,0:T(8,128)(2,1)} %get-tuple-element.28.refs_0_), channel_id=1, source_target_pairs={{0,2},{1,3},{2,0},{3,1},{4,6},{5,7},{6,4},{7,5},{8,10},{9,11},{10,... | collective-permute-start | bytes 393224 | tf_op jit(solution)/shard_map/ppermute | solution.py:128
  23.9 7.5 %all-to-all-done.rhs_ref.first_ref = bf16[16,80,256]{2,1,0:T(8,128)(2,1)S(1)} async-done(((bf16[16,80,256]{2,1,0:T(8,128)(2,1)}), bf16[16,80,256]{2,1,0:T(8,128)(2,1)S(1)}, u32[]{:S(2)}, u32[]{:S(2)}) %all-to-all-start) | async-done | bytes 655392 | tf_op jit(solution)/shard_map/all_to_all | solution.py:332
  31.3 1.5 %shard_map.96 = (f32[64,256]{1,0:T(8,128)}, bf16[16,16,1024]{2,1,0:T(8,128)(2,1)}) custom-call(bf16[1,64,1024]{2,1,0:T(8,128)(2,1)S(1)} %copy-done.3, bf16[16,80,256]{2,1,0:T(8,128)(2,1)S(1)} %all-to-all-done.rhs_ref.first_ref, bf16[1,64,1024]{2,1,0:T(8,128)(2,1)S(1)} %bitcast.28), custom_call_target="tpu_custom_call" | custom-call | flops 100000000 | bytes 1000000 | tf_op jit(solution)/shard_map/pallas_call | solution.py:46
  32.8 1.4 collective-permute-done.refs_1_
  34.2 3.1 %collective-permute-done.2.refs_3_ = bf16[64,1024]{1,0:T(8,128)(2,1)S(1)} collective-permute-done((bf16[64,1024]{1,0:T(8,128)(2,1)}, bf16[64,1024]{1,0:T(8,128)(2,1)S(1)}, u32[]{:S(2)}, u32[]{:S(2)}) %collective-permute-start.2) | collective-permute-done | bytes 131104 | tf_op jit(solution)/shard_map/ppermute | solution.py:128
  37.3 3.1 %collective-permute-start.3 = (bf16[256,1024]{1,0:T(8,128)(2,1)S(1)}, bf16[256,1024]{1,0:T(8,128)(2,1)S(1)}, u32[]{:S(2)}, u32[]{:S(2)}) collective-permute-start(bf16[256,1024]{1,0:T(8,128)(2,1)S(1)} %shard_map.97), channel_id=1, source_target_pairs={{0,12},{1,13},{2,14},{3,15},{4,0},{5,1},{6,2},{7,3},{8,4},{9,5},{1... | collective-permute-start | bytes 1572872 | tf_op jit(solution)/shard_map/ppermute | solution.py:128
  40.5 5.2 %all-to-all-start.1 = ((bf16[16,16,1024]{2,1,0:T(8,128)(2,1)}), bf16[16,16,1024]{2,1,0:T(8,128)(2,1)S(1)}, u32[]{:S(2)}, u32[]{:S(2)}) async-start(bf16[16,16,1024]{2,1,0:T(8,128)(2,1)} %get-tuple-element.27), calls=%async_computation.1 | async-start | bytes 1048576 | tf_op jit(solution)/shard_map/all_to_all | solution.py:342
  45.6 11.4 %collective-permute-done.3 = bf16[256,1024]{1,0:T(8,128)(2,1)S(1)} collective-permute-done((bf16[256,1024]{1,0:T(8,128)(2,1)S(1)}, bf16[256,1024]{1,0:T(8,128)(2,1)S(1)}, u32[]{:S(2)}, u32[]{:S(2)}) %collective-permute-start.3) | collective-permute-done | bytes 524320 | tf_op jit(solution)/shard_map/ppermute | solution.py:128
  57.8 4.2 %collective-permute-start.4 = (bf16[128,1024]{1,0:T(8,128)(2,1)}, bf16[128,1024]{1,0:T(8,128)(2,1)S(1)}, u32[]{:S(2)}, u32[]{:S(2)}) collective-permute-start(bf16[128,1024]{1,0:T(8,128)(2,1)} %slice.12), channel_id=1, source_target_pairs={{0,12},{1,13},{2,14},{3,15},{4,0},{5,1},{6,2},{7,3},{8,4},{9,5},{1... | collective-permute-start | bytes 786440 | tf_op jit(solution)/shard_map/ppermute | solution.py:128
  62.7 1.3 all-to-all-done.1.got_ref
  64.0 8.9 %collective-permute-done.4 = bf16[128,1024]{1,0:T(8,128)(2,1)S(1)} collective-permute-done((bf16[128,1024]{1,0:T(8,128)(2,1)}, bf16[128,1024]{1,0:T(8,128)(2,1)S(1)}, u32[]{:S(2)}, u32[]{:S(2)}) %collective-permute-start.4) | collective-permute-done | bytes 262176 | tf_op jit(solution)/shard_map/ppermute | solution.py:128
  72.9 4.0 %collective-permute-done.6 = bf16[128,1024]{1,0:T(8,128)(2,1)S(1)} collective-permute-done((bf16[128,1024]{1,0:T(8,128)(2,1)}, bf16[128,1024]{1,0:T(8,128)(2,1)S(1)}, u32[]{:S(2)}, u32[]{:S(2)}) %collective-permute-start.6) | collective-permute-done | bytes 262176 | tf_op jit(solution)/shard_map/ppermute | solution.py:128
  76.9 3.1 %shard_map.98 = (f32[16,1024]{1,0:T(8,128)S(1)}, f32[48,1024]{1,0:T(8,128)S(1)}) custom-call(s32[12]{0:T(128)S(1)} %copy-done.6, bf16[16,80,256]{2,1,0:T(8,128)(2,1)S(1)} %all-to-all-done.rhs_ref.first_ref, bf16[16,16,1024]{2,1,0:T(8,128)(2,1)S(1)} %all-to-all-done.1.got_ref, s32[1,1024]{1,0:T(1,128)S(1)} %copy-done.7), custom_call_target="tpu_custom_call" | custom-call | flops 100000000 | bytes 1000000 | tf_op jit(solution)/shard_map/pallas_call | solution.py:46
  81.6 1.1 shard_map.99.own_ref
  83.0 1.1 collective-permute-done.8.other_ref
  84.0 2.4 %shard_map.100 = (f32[16,1024]{1,0:T(8,128)S(1)}, f32[32,1024]{1,0:T(8,128)S(1)}) custom-call(s32[12]{0:T(128)S(1)} %copy-done.6, f32[16,1536]{1,0:T(8,128)S(1)} %shard_map.99.own_ref, f32[16,1536]{1,0:T(8,128)S(1)} %collective-permute-done.8.other_ref, f32[48,1024]{1,0:T(8,128)S(1)} %get-tuple-element.36.left_ref, ...), custom_call_target="tpu_custom_call" | custom-call | flops 100000000 | bytes 1000000 | tf_op jit(solution)/shard_map/pallas_call | solution.py:46
  86.5 2.0 %collective-permute-start.12 = (f32[32,1024]{1,0:T(8,128)S(1)}, f32[32,1024]{1,0:T(8,128)S(1)}, u32[]{:S(2)}, u32[]{:S(2)}) collective-permute-start(f32[32,1024]{1,0:T(8,128)S(1)} %get-tuple-element.39.left_ref), channel_id=1, source_target_pairs={{0,32},{16,48},{32,0},{48,16},{64,96},{80,112},{96,64},{112,80},{1... | collective-permute-start | bytes 393224 | tf_op jit(solution)/shard_map/ppermute | solution.py:300
  88.5 2.9 %collective-permute-done.10.other_ref = f32[16,1024]{1,0:T(8,128)S(1)} collective-permute-done((f32[16,1024]{1,0:T(8,128)S(1)}, f32[16,1024]{1,0:T(8,128)S(1)}, u32[]{:S(2)}, u32[]{:S(2)}) %collective-permute-start.10) | collective-permute-done | bytes 65568 | tf_op jit(solution)/shard_map/ppermute | solution.py:300
  91.4 2.2 %copy-done = bf16[2048,1024]{1,0:T(8,128)(2,1)S(1)} copy-done((bf16[2048,1024]{1,0:T(8,128)(2,1)S(1)}, bf16[2048,1024]{1,0:T(8,128)(2,1)}, u32[]{:S(2)}) %copy-start) | copy-done | bytes 4194328
  94.2 1.3 collective-permute-done.11.other_ref
  95.5 1.8 %shard_map.102 = (f32[16,1024]{1,0:T(8,128)S(1)}, f32[16,1024]{1,0:T(8,128)S(1)}) custom-call(s32[12]{0:T(128)S(1)} %copy-done.6, f32[16,1536]{1,0:T(8,128)S(1)} %shard_map.101.own_ref, f32[16,1536]{1,0:T(8,128)S(1)} %collective-permute-done.11.other_ref, f32[32,1024]{1,0:T(8,128)S(1)} %get-tuple-element.39.left_ref, ...), custom_call_target="tpu_custom_call" | custom-call | flops 100000000 | bytes 1000000 | tf_op jit(solution)/shard_map/pallas_call | solution.py:46
  97.4 4.0 %collective-permute-start.13 = (f32[16,1024]{1,0:T(8,128)S(1)}, f32[16,1024]{1,0:T(8,128)S(1)}, u32[]{:S(2)}, u32[]{:S(2)}) collective-permute-start(f32[16,1024]{1,0:T(8,128)S(1)} %get-tuple-element.40.own_ref), channel_id=1, source_target_pairs={{0,64},{16,80},{32,96},{48,112},{64,0},{80,16},{96,32},{112,48},{1... | collective-permute-start | bytes 196616 | tf_op jit(solution)/shard_map/ppermute | solution.py:300
  101.4 3.5 %collective-permute-done.13.other_ref = f32[16,1024]{1,0:T(8,128)S(1)} collective-permute-done((f32[16,1024]{1,0:T(8,128)S(1)}, f32[16,1024]{1,0:T(8,128)S(1)}, u32[]{:S(2)}, u32[]{:S(2)}) %collective-permute-start.13) | collective-permute-done | bytes 65568 | tf_op jit(solution)/shard_map/ppermute | solution.py:300
  106.5 1.3 collective-permute-done.15.other_ref
  107.8 1.2 shard_map.104.own_ref
  109.1 7.4 %collective-permute-start.16 = (f32[16,1024]{1,0:T(8,128)S(1)}, f32[16,1024]{1,0:T(8,128)S(1)}, u32[]{:S(2)}, u32[]{:S(2)}) collective-permute-start(f32[16,1024]{1,0:T(8,128)S(1)} %shard_map.104.own_ref), channel_id=1, source_target_pairs={{0,192},{16,208},{32,224},{48,240},{64,128},{80,144},{96,160},{112... | collective-permute-start | bytes 196616 | tf_op jit(solution)/shard_map/ppermute | solution.py:300
  119.8 3.6 %all-to-all-start.2 = ((bf16[16,16,1408]{2,1,0:T(8,128)(2,1)}), bf16[16,16,1408]{2,1,0:T(8,128)(2,1)S(1)}, u32[]{:S(2)}, u32[]{:S(2)}) async-start(bf16[16,16,1408]{2,1,0:T(8,128)(2,1)} %shard_map.108), calls=%async_computation.2 | async-start | bytes 1441792 | tf_op jit(solution)/shard_map/all_to_all | solution.py:381
  124.4 12.8 %all-to-all-done.2.got_ref = bf16[16,16,1408]{2,1,0:T(8,128)(2,1)S(1)} async-done(((bf16[16,16,1408]{2,1,0:T(8,128)(2,1)}), bf16[16,16,1408]{2,1,0:T(8,128)(2,1)S(1)}, u32[]{:S(2)}, u32[]{:S(2)}) %all-to-all-start.2) | async-done | bytes 720928 | tf_op jit(solution)/shard_map/all_to_all | solution.py:381
  (46 shorter events, 11.6 us)
Async XLA Ops:
  7.2 84.2 %all-gather.3.cloned.1.call-start = ((), (), s32[]{:S(2)}) async-start(), calls=%async_computation.3 | async-start | bytes 4456448 | tf_op jit(solution)/shard_map/all_gather | solution.py:333
  7.8 23.5 %copy-start.3 = (bf16[1,64,1024]{2,1,0:T(8,128)(2,1)S(1)}, bf16[1,64,1024]{2,1,0:T(8,128)(2,1)}, u32[]{:S(2)}) copy-start(bf16[1,64,1024]{2,1,0:T(8,128)(2,1)} %inv_ref.3) | copy-start | bytes 393220
  7.8 23.5 %copy-start.4 = (bf16[1,1024,64]{1,2,0:T(8,128)(2,1)S(1)}, bf16[1,1024,64]{1,2,0:T(8,128)(2,1)}, u32[]{:S(2)}) copy-start(bf16[1,1024,64]{1,2,0:T(8,128)(2,1)} %param.12) | copy-start | bytes 393220
  11.2 26.1 %copy-start.5 = (bf16[64,1024]{1,0:T(8,128)(2,1)S(1)}, bf16[64,1024]{1,0:T(8,128)(2,1)}, u32[]{:S(2)}) copy-start(bf16[64,1024]{1,0:T(8,128)(2,1)} %get-tuple-element.28.refs_0_) | copy-start | bytes 393220
  11.2 20.1 %all-to-all-start = ((bf16[16,80,256]{2,1,0:T(8,128)(2,1)}), bf16[16,80,256]{2,1,0:T(8,128)(2,1)S(1)}, u32[]{:S(2)}, u32[]{:S(2)}) async-start(bf16[16,80,256]{2,1,0:T(8,128)(2,1)} %get-tuple-element.23), calls=%async_computation | async-start | bytes 1310720 | tf_op jit(solution)/shard_map/all_to_all | solution.py:332
  18.4 15.8 %collective-permute-start = (bf16[64,1024]{1,0:T(8,128)(2,1)}, bf16[64,1024]{1,0:T(8,128)(2,1)S(1)}, u32[]{:S(2)}, u32[]{:S(2)}) collective-permute-start(bf16[64,1024]{1,0:T(8,128)(2,1)} %get-tuple-element.28.refs_0_), channel_id=1, source_target_pairs={{0,1},{1,2},{2,3},{3,0},{4,5},{5,6},{6,7},{7,4},{8,9},{9,10},{10,1... | collective-permute-start | bytes 393224 | tf_op jit(solution)/shard_map/ppermute | solution.py:128
  20.3 13.8 %collective-permute-start.1 = (bf16[64,1024]{1,0:T(8,128)(2,1)}, bf16[64,1024]{1,0:T(8,128)(2,1)S(1)}, u32[]{:S(2)}, u32[]{:S(2)}) collective-permute-start(bf16[64,1024]{1,0:T(8,128)(2,1)} %get-tuple-element.28.refs_0_), channel_id=1, source_target_pairs={{0,3},{1,0},{2,1},{3,2},{4,7},{5,4},{6,5},{7,6},{8,11},{9,8},{10,9... | collective-permute-start | bytes 393224 | tf_op jit(solution)/shard_map/ppermute | solution.py:128
  21.7 15.6 %collective-permute-start.2 = (bf16[64,1024]{1,0:T(8,128)(2,1)}, bf16[64,1024]{1,0:T(8,128)(2,1)S(1)}, u32[]{:S(2)}, u32[]{:S(2)}) collective-permute-start(bf16[64,1024]{1,0:T(8,128)(2,1)} %get-tuple-element.28.refs_0_), channel_id=1, source_target_pairs={{0,2},{1,3},{2,0},{3,1},{4,6},{5,7},{6,4},{7,5},{8,10},{9,11},{10,... | collective-permute-start | bytes 393224 | tf_op jit(solution)/shard_map/ppermute | solution.py:128
  31.3 45.6 %copy-start.6 = (s32[12]{0:T(128)S(1)}, s32[12]{0:T(128)}, u32[]{:S(2)}) copy-start(s32[12]{0:T(128)} %stack.48.place) | copy-start | bytes 148
  31.3 45.6 %copy-start.7 = (s32[1,1024]{1,0:T(1,128)S(1)}, s32[1,1024]{1,0:T(1,128)}, u32[]{:S(2)}) copy-start(s32[1,1024]{1,0:T(1,128)} %idx_ref.4) | copy-start | bytes 12292
  37.3 19.7 %collective-permute-start.3 = (bf16[256,1024]{1,0:T(8,128)(2,1)S(1)}, bf16[256,1024]{1,0:T(8,128)(2,1)S(1)}, u32[]{:S(2)}, u32[]{:S(2)}) collective-permute-start(bf16[256,1024]{1,0:T(8,128)(2,1)S(1)} %shard_map.97), channel_id=1, source_target_pairs={{0,12},{1,13},{2,14},{3,15},{4,0},{5,1},{6,2},{7,3},{8,4},{9,5},{1... | collective-permute-start | bytes 1572872 | tf_op jit(solution)/shard_map/ppermute | solution.py:128
  40.5 21.6 %collective-permute-start.5 = (bf16[256,1024]{1,0:T(8,128)(2,1)S(1)}, bf16[256,1024]{1,0:T(8,128)(2,1)S(1)}, u32[]{:S(2)}, u32[]{:S(2)}) collective-permute-start(bf16[256,1024]{1,0:T(8,128)(2,1)S(1)} %shard_map.97), channel_id=1, source_target_pairs={{0,4},{1,5},{2,6},{3,7},{4,8},{5,9},{6,10},{7,11},{8,12},{9,13},{1... | collective-permute-start | bytes 1572872 | tf_op jit(solution)/shard_map/ppermute | solution.py:128
  40.5 23.6 %all-to-all-start.1 = ((bf16[16,16,1024]{2,1,0:T(8,128)(2,1)}), bf16[16,16,1024]{2,1,0:T(8,128)(2,1)S(1)}, u32[]{:S(2)}, u32[]{:S(2)}) async-start(bf16[16,16,1024]{2,1,0:T(8,128)(2,1)} %get-tuple-element.27), calls=%async_computation.1 | async-start | bytes 1048576 | tf_op jit(solution)/shard_map/all_to_all | solution.py:342
  57.8 26.3 %copy-start.2 = (s32[14,1024]{1,0:T(8,128)S(1)}, s32[14,1024]{1,0:T(8,128)}, u32[]{:S(2)}) copy-start(s32[14,1024]{1,0:T(8,128)} %idx_ref.7) | copy-start | bytes 172036
  57.8 15.2 %collective-permute-start.4 = (bf16[128,1024]{1,0:T(8,128)(2,1)}, bf16[128,1024]{1,0:T(8,128)(2,1)S(1)}, u32[]{:S(2)}, u32[]{:S(2)}) collective-permute-start(bf16[128,1024]{1,0:T(8,128)(2,1)} %slice.12), channel_id=1, source_target_pairs={{0,12},{1,13},{2,14},{3,15},{4,0},{5,1},{6,2},{7,3},{8,4},{9,5},{1... | collective-permute-start | bytes 786440 | tf_op jit(solution)/shard_map/ppermute | solution.py:128
  62.7 14.2 %collective-permute-start.6 = (bf16[128,1024]{1,0:T(8,128)(2,1)}, bf16[128,1024]{1,0:T(8,128)(2,1)S(1)}, u32[]{:S(2)}, u32[]{:S(2)}) collective-permute-start(bf16[128,1024]{1,0:T(8,128)(2,1)} %slice.13), channel_id=1, source_target_pairs={{0,4},{1,5},{2,6},{3,7},{4,8},{5,9},{6,10},{7,11},{8,12},{9,13},{1... | collective-permute-start | bytes 786440 | tf_op jit(solution)/shard_map/ppermute | solution.py:128
  80.0 4.0 %collective-permute-start.9 = (f32[48,1024]{1,0:T(8,128)S(1)}, f32[48,1024]{1,0:T(8,128)S(1)}, u32[]{:S(2)}, u32[]{:S(2)}) collective-permute-start(f32[48,1024]{1,0:T(8,128)S(1)} %get-tuple-element.36.left_ref), channel_id=1, source_target_pairs={{0,16},{16,0},{32,48},{48,32},{64,80},{80,64},{96,112},{112,96},{1... | collective-permute-start | bytes 589832 | tf_op jit(solution)/shard_map/ppermute | solution.py:300
  80.1 1.5 %collective-permute-start.7 = (f32[16,1024]{1,0:T(8,128)S(1)}, f32[16,1024]{1,0:T(8,128)S(1)}, u32[]{:S(2)}, u32[]{:S(2)}) collective-permute-start(f32[16,1024]{1,0:T(8,128)S(1)} %get-tuple-element.33.own_ref), channel_id=1, source_target_pairs={{0,16},{16,0},{32,48},{48,32},{64,80},{80,64},{96,112},{112,96},{1... | collective-permute-start | bytes 196616 | tf_op jit(solution)/shard_map/ppermute | solution.py:300
  82.7 1.3 collective-permute-start.8
  86.5 4.9 %collective-permute-start.10 = (f32[16,1024]{1,0:T(8,128)S(1)}, f32[16,1024]{1,0:T(8,128)S(1)}, u32[]{:S(2)}, u32[]{:S(2)}) collective-permute-start(f32[16,1024]{1,0:T(8,128)S(1)} %get-tuple-element.37.own_ref), channel_id=1, source_target_pairs={{0,32},{16,48},{32,0},{48,16},{64,96},{80,112},{96,64},{112,80},{1... | collective-permute-start | bytes 196616 | tf_op jit(solution)/shard_map/ppermute | solution.py:300
  86.5 7.7 %collective-permute-start.12 = (f32[32,1024]{1,0:T(8,128)S(1)}, f32[32,1024]{1,0:T(8,128)S(1)}, u32[]{:S(2)}, u32[]{:S(2)}) collective-permute-start(f32[32,1024]{1,0:T(8,128)S(1)} %get-tuple-element.39.left_ref), channel_id=1, source_target_pairs={{0,32},{16,48},{32,0},{48,16},{64,96},{80,112},{96,64},{112,80},{1... | collective-permute-start | bytes 393224 | tf_op jit(solution)/shard_map/ppermute | solution.py:300
  91.4 2.2 %copy-start = (bf16[2048,1024]{1,0:T(8,128)(2,1)S(1)}, bf16[2048,1024]{1,0:T(8,128)(2,1)}, u32[]{:S(2)}) copy-start(bf16[2048,1024]{1,0:T(8,128)(2,1)} %all-gather.3.cloned.1.call-done) | copy-start | bytes 12582916
  93.6 11.3 %copy-start.1 = (bf16[2048,1024]{1,0:T(8,128)(2,1)S(1)}, bf16[2048,1024]{1,0:T(8,128)(2,1)}, u32[]{:S(2)}) copy-start(bf16[2048,1024]{1,0:T(8,128)(2,1)} %all-gather.3.cloned.1.call-done) | copy-start | bytes 12582916
  94.2 1.3 collective-permute-start.11
  97.4 7.6 %collective-permute-start.13 = (f32[16,1024]{1,0:T(8,128)S(1)}, f32[16,1024]{1,0:T(8,128)S(1)}, u32[]{:S(2)}, u32[]{:S(2)}) collective-permute-start(f32[16,1024]{1,0:T(8,128)S(1)} %get-tuple-element.40.own_ref), channel_id=1, source_target_pairs={{0,64},{16,80},{32,96},{48,112},{64,0},{80,16},{96,32},{112,48},{1... | collective-permute-start | bytes 196616 | tf_op jit(solution)/shard_map/ppermute | solution.py:300
  101.4 5.2 %collective-permute-start.14 = (f32[16,1024]{1,0:T(8,128)S(1)}, f32[16,1024]{1,0:T(8,128)S(1)}, u32[]{:S(2)}, u32[]{:S(2)}) collective-permute-start(f32[16,1024]{1,0:T(8,128)S(1)} %get-tuple-element.41.left_ref), channel_id=1, source_target_pairs={{0,64},{16,80},{32,96},{48,112},{64,0},{80,16},{96,32},{112,48},{1... | collective-permute-start | bytes 196616 | tf_op jit(solution)/shard_map/ppermute | solution.py:300
  106.5 1.3 collective-permute-start.15
  109.1 9.8 %collective-permute-start.16 = (f32[16,1024]{1,0:T(8,128)S(1)}, f32[16,1024]{1,0:T(8,128)S(1)}, u32[]{:S(2)}, u32[]{:S(2)}) collective-permute-start(f32[16,1024]{1,0:T(8,128)S(1)} %shard_map.104.own_ref), channel_id=1, source_target_pairs={{0,192},{16,208},{32,224},{48,240},{64,128},{80,144},{96,160},{112... | collective-permute-start | bytes 196616 | tf_op jit(solution)/shard_map/ppermute | solution.py:300
  119.8 17.3 %all-to-all-start.2 = ((bf16[16,16,1408]{2,1,0:T(8,128)(2,1)}), bf16[16,16,1408]{2,1,0:T(8,128)(2,1)S(1)}, u32[]{:S(2)}, u32[]{:S(2)}) async-start(bf16[16,16,1408]{2,1,0:T(8,128)(2,1)} %shard_map.108), calls=%async_computation.2 | async-start | bytes 1441792 | tf_op jit(solution)/shard_map/all_to_all | solution.py:381
Sparse Core Ops, SparseCore 0:
  11.3 71.8 all-gather.2

commit v10 on v8

--- a/solution.py
+++ b/solution.py
@@ -56,12 +56,12 @@
 
 
 def first_kernel(place, leaf_ref, rhs_ref, inv_ref, off_ref, out_ref, *refs):
-    third_ref, pair_ref, held, sems = refs
+    second_ref, pair_ref, held, sems = refs
     copies = [
         pltpu.make_async_copy(rhs_ref.at[place[a] - 1], held.at[a], sems.at[a]) for a in range(4)
     ]
     at = pl.ds(pl.multiple_of(place[8] * 32, 32), 32)
-    for level, (piece, start) in enumerate(((third_ref, 0), (pair_ref, 0), (pair_ref, 64))):
+    for level, (piece, start) in enumerate(((pair_ref, 0), (second_ref, 0), (pair_ref, 64))):
         node = place[level]
         for part, (ref, index) in enumerate(((inv_ref, node - 1), (off_ref, node - 2))):
             copies.append(
@@ -320,11 +320,11 @@
     off_top = jnp.swapaxes(off_top, 1, 2)
     off_leaf = jnp.swapaxes(off_leaf, 1, 2)
 
-    sent, third, pair = first_payload(place, rhs_leaf, rhs_top, inv_top, off_top)
+    sent, second, pair = first_payload(place, rhs_leaf, rhs_top, inv_top, off_top)
     first = lax.all_to_all(sent, "front", 0, 0)
-    third = (third, *near(third, "y"), opposite(third, "y"))
-    pair = (pair, *near(pair, "x"))
-    second = opposite(pair[0][:64], "x")
+    pair = (pair, *near(pair, "y"))
+    third = opposite(pair[0][:64], "y")
+    second = (second, *near(second, "x"), opposite(second, "x"))
     leaf_x, sent = call(
         leaf_solve_kernel,
         (jax.ShapeDtypeStruct((64, 256), F32), jax.ShapeDtypeStruct((FRONTS, 16, 1024), BF)),
@@ -333,22 +333,20 @@
     )
     sent, third, pair, second = lax.optimization_barrier((sent, third, pair, second))
     got = lax.all_to_all(sent, "front", 0, 0)
-    third = stack(third, (0, 0, 0, 0))
-    second = stack((*pair, second), (0, 0, 0, 0))
+    third = stack((*pair, third), (0, 0, 0, 0))
+    second = stack(second, (0, 0, 0, 0))
     third_near, second_near = near(third, "x"), near(second, "y")
-    lowest = turn(pair[2][64:], -1, 0)
-    third_far, second_far = far(third_near, "x"), far(second_near, "y")
-    lowest = stack((*pair, lowest), (64, 64, 64, 0))
-    got, third_far, second_far, lowest = lax.optimization_barrier(
-        (got, third_far, second_far, lowest)
-    )
-    lowest_near = near(lowest, "y")
+    got, third_near, second_near = lax.optimization_barrier((got, third_near, second_near))
+    third_far = far(third_near, "x")
     state, left = call(
         leaf_update_kernel,
         (jax.ShapeDtypeStruct((16, 1024), F32), jax.ShapeDtypeStruct((48, 1024), F32)),
         [SMEM] + [VMEM] * 3,
         (place, first, got, idx_leaf),
     )
+    state, second_near, pair = lax.optimization_barrier((state, second_near, pair))
+    second_far = far(second_near, "y")
+    lowest = turn(pair[2][64:], 0, -1)
     other, left_other = swap(state, core_pairs()), swap(left, core_pairs())
     ships = []
     for level in range(3):
@@ -359,6 +357,10 @@
         else:
             parts = (lowest, *lowest_near, *lowest_far)
         ux = top_solve(state, other, parts)
+        if level == 0:
+            ux, lowest = lax.optimization_barrier((ux, lowest))
+            lowest = stack((*pair, lowest), (64, 64, 64, 0))
+            lowest_near = near(lowest, "x")
         if level == 2:
             ux, left_other = lax.optimization_barrier((ux, left_other))
         ux_other = swap(ux, core_pairs())
@@ -366,12 +368,12 @@
         other = swap(state, chip_pairs(level))
         if level == 0:
             other, lowest_near = lax.optimization_barrier((other, lowest_near))
-            lowest_far = far(lowest_near, "y")
+            lowest_far = far(lowest_near, "x")
         if more:
             left, left_other = more[0], swap(more[0], chip_pairs(level))
         ships.append(
             call(
-                functools.partial(ship_kernel, ("yx", "xy", "xy")[level]),
+                functools.partial(ship_kernel, ("yx", "xy", "yx")[level]),
                 jax.ShapeDtypeStruct((16, 16, 128), BF),
                 [SMEM, VMEM, VMEM],
                 (place, ux, ux_other),

time: 139 us -> 131 us (0.942)
  blocking collectives: 0 us -> 14.3 us
  waiting for transfers between devices: 48 us -> 36.7 us
  local copies, waits for them, and re-layouts: 8.38 us -> 2.62 us
  Pallas kernels: 22.9 us -> 20.3 us
  starting transfers between devices: 57.8 us -> 56.1 us
    all_to_all x0 -> x1, blocking collectives: none -> 14.3 us  [local(): got = lax.all_to_all(sent, 'front', 0, 0)]
    ppermute x19, waiting for transfers between devices: 20.8 us -> 7.34 us  [turn(): return lax.ppermute(block, 'front', route)]
    slice x6, local copies, waits for them, and re-layouts: 5.8 us -> 0.11 us  [far(): return (turn(after[:half], -dx, -dy), turn(before[half:], dx, dy))]
    ppermute x19, starting transfers between devices: 31.5 us -> 34.6 us  [turn(): return lax.ppermute(block, 'front', route)]
    all_to_all x2 -> x1, starting transfers between devices: 8.19 us -> 5.44 us  [local(): got = lax.all_to_all(sent, 'front', 0, 0)]
    pallas_call x16, Pallas kernels: 19.6 us -> 17 us  [call(): pl.pallas_call(kernel, out_shape=outs, in_specs=specs, out_specs=tuple((V...]
    ppermute x10, starting transfers between devices: 11 us -> 8.92 us  [swap(): return lax.ppermute(block, 'leaf', pairs)]
    ppermute x10, waiting for transfers between devices: 14.4 us -> 16.4 us  [swap(): return lax.ppermute(block, 'leaf', pairs)]
  transfers between devices with their start and end apart: 32 -> 31, of which waited for: 14 -> 12; matrix products, arithmetic and copies ran while one was open for 6% -> 1% of each run, Pallas kernels for 12% -> 11%
where the time goes in v10:
time: 131 us
  starting transfers between devices  56.1 us (43%)
  waiting for transfers between devices  36.7 us (28%)
  Pallas kernels  20.3 us (15%)
  blocking collectives  14.3 us (11%)
  local copies, waits for them, and re-layouts  2.62 us (2%)
    ppermute x19, starting transfers between devices, turn(): return lax.ppermute(block, 'front', route)  34.6 us
    pallas_call x16, Pallas kernels, call(): pl.pallas_call(kernel, out_shape=outs, in_specs=specs, out_specs=tuple((V...  17 us
    ppermute x10, waiting for transfers between devices, swap(): return lax.ppermute(block, 'leaf', pairs)  16.4 us
    all_to_all x1, blocking collectives, local(): got = lax.all_to_all(sent, 'front', 0, 0)  14.3 us
    all_to_all x1, waiting for transfers between devices, local(): got = lax.all_to_all(sent, 'front', 0, 0)  12.9 us
    ppermute x10, starting transfers between devices, swap(): return lax.ppermute(block, 'leaf', pairs)  8.92 us
    ppermute x19, waiting for transfers between devices, turn(): return lax.ppermute(block, 'front', route)  7.34 us
    all_to_all x1, starting transfers between devices, local(): first = lax.all_to_all(sent, 'front', 0, 0)  7.18 us
  transfers between devices with their start and end apart: 31, of which 12 were waited for; matrix products, arithmetic and copies ran while one was open for 1% of the time, Pallas kernels for 11%

profile of v10, /device:TPU:32, one launch (start us, length us, event | category | flops | bytes accessed | tf_op | source)
XLA Modules:
  0.0 130.9 jit_solution(8383057947693415511)
XLA Ops:
  1.3 3.3 %shard_map.95 = (bf16[16,80,256]{2,1,0:T(8,128)(2,1)}, bf16[64,1024]{1,0:T(8,128)(2,1)}, bf16[128,1024]{1,0:T(8,128)(2,1)}) custom-call(s32[12]{0:T(128)} %stack.48.place, f32[1,64,256]{2,1,0:T(8,128)} %leaf_ref.1, f32[15,64,256]{2,1,0:T(8,128)} %rhs_ref.1, bf16[15,64,1024]{2,1,0:T(8,128)(2,1)} %inv_ref.2, bf16[14,64,1024]{2,1,0:T(8,128)(2,1)} %bitcast.46), custom_call_target="tpu_custom_call" | custom-call | tf_op jit(solution)/shard_map/pallas_call | solution.py:101
  4.6 7.2 %all-to-all-start = ((bf16[16,80,256]{2,1,0:T(8,128)(2,1)}), bf16[16,80,256]{2,1,0:T(8,128)(2,1)S(1)}, u32[]{:S(2)}, u32[]{:S(2)}) async-start(bf16[16,80,256]{2,1,0:T(8,128)(2,1)} %get-tuple-element.40), calls=%async_computation | async-start | bytes 1310720 | tf_op jit(solution)/shard_map/all_to_all | solution.py:324
  12.7 3.5 %collective-permute-start = (bf16[64,1024]{1,0:T(8,128)(2,1)S(1)}, bf16[64,1024]{1,0:T(8,128)(2,1)S(1)}, u32[]{:S(2)}, u32[]{:S(2)}) collective-permute-start(bf16[64,1024]{1,0:T(8,128)(2,1)S(1)} %slice.27), channel_id=1, source_target_pairs={{0,2},{1,3},{2,0},{3,1},{4,6},{5,7},{6,4},{7,5},{8,10},{9,11},{10,... | collective-permute-start | bytes 393224 | tf_op jit(solution)/shard_map/ppermute | solution.py:131
  16.8 2.7 %collective-permute-start.2 = (bf16[128,1024]{1,0:T(8,128)(2,1)}, bf16[128,1024]{1,0:T(8,128)(2,1)S(1)}, u32[]{:S(2)}, u32[]{:S(2)}) collective-permute-start(bf16[128,1024]{1,0:T(8,128)(2,1)} %get-tuple-element.65.refs_0_), channel_id=1, source_target_pairs={{0,3},{1,0},{2,1},{3,2},{4,7},{5,4},{6,5},{7,6},{8,11},{9,8},{10,9... | collective-permute-start | bytes 786440 | tf_op jit(solution)/shard_map/ppermute | solution.py:131
  19.5 1.5 %collective-permute-start.3 = (bf16[64,1024]{1,0:T(8,128)(2,1)}, bf16[64,1024]{1,0:T(8,128)(2,1)S(1)}, u32[]{:S(2)}, u32[]{:S(2)}) collective-permute-start(bf16[64,1024]{1,0:T(8,128)(2,1)} %get-tuple-element.50.refs_0_), channel_id=1, source_target_pairs={{0,4},{1,5},{2,6},{3,7},{4,8},{5,9},{6,10},{7,11},{8,12},{9,13},{1... | collective-permute-start | bytes 393224 | tf_op jit(solution)/shard_map/ppermute | solution.py:131
  21.0 1.8 %collective-permute-start.4 = (bf16[64,1024]{1,0:T(8,128)(2,1)}, bf16[64,1024]{1,0:T(8,128)(2,1)S(1)}, u32[]{:S(2)}, u32[]{:S(2)}) collective-permute-start(bf16[64,1024]{1,0:T(8,128)(2,1)} %get-tuple-element.50.refs_0_), channel_id=1, source_target_pairs={{0,12},{1,13},{2,14},{3,15},{4,0},{5,1},{6,2},{7,3},{8,4},{9,5},{1... | collective-permute-start | bytes 393224 | tf_op jit(solution)/shard_map/ppermute | solution.py:131
  22.7 4.0 %collective-permute-done.refs_3_ = bf16[64,1024]{1,0:T(8,128)(2,1)S(1)} collective-permute-done((bf16[64,1024]{1,0:T(8,128)(2,1)S(1)}, bf16[64,1024]{1,0:T(8,128)(2,1)S(1)}, u32[]{:S(2)}, u32[]{:S(2)}) %collective-permute-start) | collective-permute-done | bytes 131104 | tf_op jit(solution)/shard_map/ppermute | solution.py:131
  26.7 2.7 %collective-permute-start.5 = (bf16[64,1024]{1,0:T(8,128)(2,1)}, bf16[64,1024]{1,0:T(8,128)(2,1)S(1)}, u32[]{:S(2)}, u32[]{:S(2)}) collective-permute-start(bf16[64,1024]{1,0:T(8,128)(2,1)} %get-tuple-element.50.refs_0_), channel_id=1, source_target_pairs={{0,8},{1,9},{2,10},{3,11},{4,12},{5,13},{6,14},{7,15},{8,0},{9,1},... | collective-permute-start | bytes 393224 | tf_op jit(solution)/shard_map/ppermute | solution.py:131
  30.3 3.1 %collective-permute-done.5.refs_3_ = bf16[64,1024]{1,0:T(8,128)(2,1)S(1)} collective-permute-done((bf16[64,1024]{1,0:T(8,128)(2,1)}, bf16[64,1024]{1,0:T(8,128)(2,1)S(1)}, u32[]{:S(2)}, u32[]{:S(2)}) %collective-permute-start.5) | collective-permute-done | bytes 131104 | tf_op jit(solution)/shard_map/ppermute | solution.py:131
  33.5 1.3 %collective-permute-start.6 = (bf16[256,1024]{1,0:T(8,128)(2,1)S(1)}, bf16[256,1024]{1,0:T(8,128)(2,1)S(1)}, u32[]{:S(2)}, u32[]{:S(2)}) collective-permute-start(bf16[256,1024]{1,0:T(8,128)(2,1)S(1)} %shard_map.97), channel_id=1, source_target_pairs={{0,4},{1,5},{2,6},{3,7},{4,8},{5,9},{6,10},{7,11},{8,12},{9,13},{1... | collective-permute-start | bytes 1572872 | tf_op jit(solution)/shard_map/ppermute | solution.py:131
  34.8 2.0 %collective-permute-start.7 = (bf16[256,1024]{1,0:T(8,128)(2,1)S(1)}, bf16[256,1024]{1,0:T(8,128)(2,1)S(1)}, u32[]{:S(2)}, u32[]{:S(2)}) collective-permute-start(bf16[256,1024]{1,0:T(8,128)(2,1)S(1)} %shard_map.97), channel_id=1, source_target_pairs={{0,12},{1,13},{2,14},{3,15},{4,0},{5,1},{6,2},{7,3},{8,4},{9,5},{1... | collective-permute-start | bytes 1572872 | tf_op jit(solution)/shard_map/ppermute | solution.py:131
  37.3 2.9 %collective-permute-start.9 = (bf16[256,1024]{1,0:T(8,128)(2,1)S(1)}, bf16[256,1024]{1,0:T(8,128)(2,1)S(1)}, u32[]{:S(2)}, u32[]{:S(2)}) collective-permute-start(bf16[256,1024]{1,0:T(8,128)(2,1)S(1)} %shard_map.98), channel_id=1, source_target_pairs={{0,3},{1,0},{2,1},{3,2},{4,7},{5,4},{6,5},{7,6},{8,11},{9,8},{10,9... | collective-permute-start | bytes 1572872 | tf_op jit(solution)/shard_map/ppermute | solution.py:131
  40.2 14.3 %all_to_all.15.got_ref = bf16[16,16,1024]{2,1,0:T(8,128)(2,1)S(1)} all-to-all(bf16[16,16,1024]{2,1,0:T(8,128)(2,1)S(1)} %get-tuple-element.45), channel_id=1, replica_groups=mesh['leaf'=16,'front'=16] {'front'}, dimensions={0} | all-to-all | bytes 1048576 | tf_op jit(solution)/shard_map/all_to_all | solution.py:335
  54.6 2.0 %collective-permute-start.11 = (bf16[128,1024]{1,0:T(8,128)(2,1)S(1)}, bf16[128,1024]{1,0:T(8,128)(2,1)S(1)}, u32[]{:S(2)}, u32[]{:S(2)}) collective-permute-start(bf16[128,1024]{1,0:T(8,128)(2,1)S(1)} %slice.28), channel_id=1, source_target_pairs={{0,12},{1,13},{2,14},{3,15},{4,0},{5,1},{6,2},{7,3},{8,4},{9,5},{1... | collective-permute-start | bytes 786440 | tf_op jit(solution)/shard_map/ppermute | solution.py:131
  56.8 3.1 %shard_map.99 = (f32[16,1024]{1,0:T(8,128)S(1)}, f32[48,1024]{1,0:T(8,128)S(1)}) custom-call(s32[12]{0:T(128)S(1)} %copy-done.5, bf16[16,80,256]{2,1,0:T(8,128)(2,1)S(1)} %all-to-all-done.rhs_ref.first_ref, bf16[16,16,1024]{2,1,0:T(8,128)(2,1)S(1)} %all_to_all.15.got_ref, s32[1,1024]{1,0:T(1,128)S(1)} %copy-done.6), custom_call_target="tpu_custom_call" | custom-call | flops 100000000 | bytes 1000000 | tf_op jit(solution)/shard_map/pallas_call | solution.py:46
  59.9 3.1 %collective-permute-start.13 = (bf16[64,1024]{1,0:T(8,128)(2,1)S(1)}, bf16[64,1024]{1,0:T(8,128)(2,1)S(1)}, u32[]{:S(2)}, u32[]{:S(2)}) collective-permute-start(bf16[64,1024]{1,0:T(8,128)(2,1)S(1)} %slice.30), channel_id=1, source_target_pairs={{0,3},{1,0},{2,1},{3,2},{4,7},{5,4},{6,5},{7,6},{8,11},{9,8},{10,9... | collective-permute-start | bytes 393224 | tf_op jit(solution)/shard_map/ppermute | solution.py:131
  63.0 1.3 collective-permute-done.10.other_ref
  65.8 3.0 %collective-permute-start.18 = (bf16[256,1024]{1,0:T(8,128)(2,1)S(1)}, bf16[256,1024]{1,0:T(8,128)(2,1)S(1)}, u32[]{:S(2)}, u32[]{:S(2)}) collective-permute-start(bf16[256,1024]{1,0:T(8,128)(2,1)S(1)} %shard_map.102), channel_id=1, source_target_pairs={{0,12},{1,13},{2,14},{3,15},{4,0},{5,1},{6,2},{7,3},{8,4},{9,5},{1... | collective-permute-start | bytes 1572872 | tf_op jit(solution)/shard_map/ppermute | solution.py:131
  68.9 3.7 %collective-permute-start.19 = (bf16[128,1024]{1,0:T(8,128)(2,1)S(1)}, bf16[128,1024]{1,0:T(8,128)(2,1)S(1)}, u32[]{:S(2)}, u32[]{:S(2)}) collective-permute-start(bf16[128,1024]{1,0:T(8,128)(2,1)S(1)} %slice.31), channel_id=1, source_target_pairs={{0,3},{1,0},{2,1},{3,2},{4,7},{5,4},{6,5},{7,6},{8,11},{9,8},{10,9... | collective-permute-start | bytes 786440 | tf_op jit(solution)/shard_map/ppermute | solution.py:131
  74.1 2.4 %shard_map.101 = (f32[16,1024]{1,0:T(8,128)S(1)}, f32[32,1024]{1,0:T(8,128)S(1)}) custom-call(s32[12]{0:T(128)S(1)} %copy-done.5, f32[16,1536]{1,0:T(8,128)S(1)} %shard_map.100.own_ref, f32[16,1536]{1,0:T(8,128)S(1)} %collective-permute-done.14.other_ref, f32[48,1024]{1,0:T(8,128)S(1)} %get-tuple-element.63.left_ref, ...), custom_call_target="tpu_custom_call" | custom-call | flops 100000000 | bytes 1000000 | tf_op jit(solution)/shard_map/pallas_call | solution.py:46
  76.7 4.2 %collective-permute-done.16.other_ref = f32[16,1024]{1,0:T(8,128)S(1)} collective-permute-done((f32[16,1024]{1,0:T(8,128)S(1)}, f32[16,1024]{1,0:T(8,128)S(1)}, u32[]{:S(2)}, u32[]{:S(2)}) %collective-permute-start.16) | collective-permute-done | bytes 65568 | tf_op jit(solution)/shard_map/ppermute | solution.py:292
  80.9 2.8 %collective-permute-start.24 = (bf16[128,1024]{1,0:T(8,128)(2,1)S(1)}, bf16[128,1024]{1,0:T(8,128)(2,1)S(1)}, u32[]{:S(2)}, u32[]{:S(2)}) collective-permute-start(bf16[128,1024]{1,0:T(8,128)(2,1)S(1)} %slice.33), channel_id=1, source_target_pairs={{0,12},{1,13},{2,14},{3,15},{4,0},{5,1},{6,2},{7,3},{8,4},{9,5},{1... | collective-permute-start | bytes 786440 | tf_op jit(solution)/shard_map/ppermute | solution.py:131
  85.1 3.7 %collective-permute-done.22.left_other_ref = f32[32,1024]{1,0:T(8,128)S(1)} collective-permute-done((f32[32,1024]{1,0:T(8,128)S(1)}, f32[32,1024]{1,0:T(8,128)S(1)}, u32[]{:S(2)}, u32[]{:S(2)}) %collective-permute-start.22) | collective-permute-done | bytes 131104 | tf_op jit(solution)/shard_map/ppermute | solution.py:292
  88.9 1.8 %shard_map.104 = (f32[16,1024]{1,0:T(8,128)S(1)}, f32[16,1024]{1,0:T(8,128)S(1)}) custom-call(s32[12]{0:T(128)S(1)} %copy-done.5, f32[16,1536]{1,0:T(8,128)S(1)} %shard_map.103.own_ref, f32[16,1536]{1,0:T(8,128)S(1)} %collective-permute-done.21.other_ref, f32[32,1024]{1,0:T(8,128)S(1)} %get-tuple-element.71.left_ref, ...), custom_call_target="tpu_custom_call" | custom-call | flops 100000000 | bytes 1000000 | tf_op jit(solution)/shard_map/pallas_call | solution.py:46
  90.7 3.3 %collective-permute-start.23 = (f32[16,1024]{1,0:T(8,128)S(1)}, f32[16,1024]{1,0:T(8,128)S(1)}, u32[]{:S(2)}, u32[]{:S(2)}) collective-permute-start(f32[16,1024]{1,0:T(8,128)S(1)} %get-tuple-element.72.own_ref), channel_id=1, source_target_pairs={{0,64},{16,80},{32,96},{48,112},{64,0},{80,16},{96,32},{112,48},{1... | collective-permute-start | bytes 196616 | tf_op jit(solution)/shard_map/ppermute | solution.py:292
  94.3 2.4 %collective-permute-done.23.other_ref = f32[16,1024]{1,0:T(8,128)S(1)} collective-permute-done((f32[16,1024]{1,0:T(8,128)S(1)}, f32[16,1024]{1,0:T(8,128)S(1)}, u32[]{:S(2)}, u32[]{:S(2)}) %collective-permute-start.23) | collective-permute-done | bytes 65568 | tf_op jit(solution)/shard_map/ppermute | solution.py:292
  97.8 1.3 %collective-permute-done.26.left_other_ref = f32[16,1024]{1,0:T(8,128)S(1)} collective-permute-done((f32[16,1024]{1,0:T(8,128)S(1)}, f32[16,1024]{1,0:T(8,128)S(1)}, u32[]{:S(2)}, u32[]{:S(2)}) %collective-permute-start.26) | collective-permute-done | bytes 65568 | tf_op jit(solution)/shard_map/ppermute | solution.py:292
  99.2 1.3 collective-permute-done.27.other_ref
  100.5 1.2 shard_map.106.own_ref
  101.7 4.7 %collective-permute-start.28 = (f32[16,1024]{1,0:T(8,128)S(1)}, f32[16,1024]{1,0:T(8,128)S(1)}, u32[]{:S(2)}, u32[]{:S(2)}) collective-permute-start(f32[16,1024]{1,0:T(8,128)S(1)} %shard_map.106.own_ref), channel_id=1, source_target_pairs={{0,192},{16,208},{32,224},{48,240},{64,128},{80,144},{96,160},{112... | collective-permute-start | bytes 196616 | tf_op jit(solution)/shard_map/ppermute | solution.py:292
  110.6 5.4 %all-to-all-start.2 = ((bf16[16,16,1408]{2,1,0:T(8,128)(2,1)}), bf16[16,16,1408]{2,1,0:T(8,128)(2,1)S(1)}, u32[]{:S(2)}, u32[]{:S(2)}) async-start(bf16[16,16,1408]{2,1,0:T(8,128)(2,1)} %shard_map.110), calls=%async_computation.2 | async-start | bytes 1441792 | tf_op jit(solution)/shard_map/all_to_all | solution.py:388
  117.0 12.9 %all-to-all-done.2.got_ref = bf16[16,16,1408]{2,1,0:T(8,128)(2,1)S(1)} async-done(((bf16[16,16,1408]{2,1,0:T(8,128)(2,1)}), bf16[16,16,1408]{2,1,0:T(8,128)(2,1)S(1)}, u32[]{:S(2)}, u32[]{:S(2)}) %all-to-all-start.2) | async-done | bytes 720928 | tf_op jit(solution)/shard_map/all_to_all | solution.py:388
  (72 shorter events, 15.9 us)
Async XLA Ops:
  4.6 32.2 %copy-start.4 = (bf16[64,1024]{1,0:T(8,128)(2,1)S(1)}, bf16[64,1024]{1,0:T(8,128)(2,1)}, u32[]{:S(2)}) copy-start(bf16[64,1024]{1,0:T(8,128)(2,1)} %get-tuple-element.50.refs_0_) | copy-start | bytes 393220
  4.6 24.8 %all-to-all-start = ((bf16[16,80,256]{2,1,0:T(8,128)(2,1)}), bf16[16,80,256]{2,1,0:T(8,128)(2,1)S(1)}, u32[]{:S(2)}, u32[]{:S(2)}) async-start(bf16[16,80,256]{2,1,0:T(8,128)(2,1)} %get-tuple-element.40), calls=%async_computation | async-start | bytes 1310720 | tf_op jit(solution)/shard_map/all_to_all | solution.py:324
  12.7 14.0 %collective-permute-start = (bf16[64,1024]{1,0:T(8,128)(2,1)S(1)}, bf16[64,1024]{1,0:T(8,128)(2,1)S(1)}, u32[]{:S(2)}, u32[]{:S(2)}) collective-permute-start(bf16[64,1024]{1,0:T(8,128)(2,1)S(1)} %slice.27), channel_id=1, source_target_pairs={{0,2},{1,3},{2,0},{3,1},{4,6},{5,7},{6,4},{7,5},{8,10},{9,11},{10,... | collective-permute-start | bytes 393224 | tf_op jit(solution)/shard_map/ppermute | solution.py:131
  16.3 17.2 %collective-permute-start.1 = (bf16[128,1024]{1,0:T(8,128)(2,1)}, bf16[128,1024]{1,0:T(8,128)(2,1)S(1)}, u32[]{:S(2)}, u32[]{:S(2)}) collective-permute-start(bf16[128,1024]{1,0:T(8,128)(2,1)} %get-tuple-element.65.refs_0_), channel_id=1, source_target_pairs={{0,1},{1,2},{2,3},{3,0},{4,5},{5,6},{6,7},{7,4},{8,9},{9,10},{10,1... | collective-permute-start | bytes 786440 | tf_op jit(solution)/shard_map/ppermute | solution.py:131
  16.8 16.6 %collective-permute-start.2 = (bf16[128,1024]{1,0:T(8,128)(2,1)}, bf16[128,1024]{1,0:T(8,128)(2,1)S(1)}, u32[]{:S(2)}, u32[]{:S(2)}) collective-permute-start(bf16[128,1024]{1,0:T(8,128)(2,1)} %get-tuple-element.65.refs_0_), channel_id=1, source_target_pairs={{0,3},{1,0},{2,1},{3,2},{4,7},{5,4},{6,5},{7,6},{8,11},{9,8},{10,9... | collective-permute-start | bytes 786440 | tf_op jit(solution)/shard_map/ppermute | solution.py:131
  19.5 10.8 %collective-permute-start.3 = (bf16[64,1024]{1,0:T(8,128)(2,1)}, bf16[64,1024]{1,0:T(8,128)(2,1)S(1)}, u32[]{:S(2)}, u32[]{:S(2)}) collective-permute-start(bf16[64,1024]{1,0:T(8,128)(2,1)} %get-tuple-element.50.refs_0_), channel_id=1, source_target_pairs={{0,4},{1,5},{2,6},{3,7},{4,8},{5,9},{6,10},{7,11},{8,12},{9,13},{1... | collective-permute-start | bytes 393224 | tf_op jit(solution)/shard_map/ppermute | solution.py:131
  21.0 9.4 %collective-permute-start.4 = (bf16[64,1024]{1,0:T(8,128)(2,1)}, bf16[64,1024]{1,0:T(8,128)(2,1)S(1)}, u32[]{:S(2)}, u32[]{:S(2)}) collective-permute-start(bf16[64,1024]{1,0:T(8,128)(2,1)} %get-tuple-element.50.refs_0_), channel_id=1, source_target_pairs={{0,12},{1,13},{2,14},{3,15},{4,0},{5,1},{6,2},{7,3},{8,4},{9,5},{1... | collective-permute-start | bytes 393224 | tf_op jit(solution)/shard_map/ppermute | solution.py:131
  26.7 6.7 %collective-permute-start.5 = (bf16[64,1024]{1,0:T(8,128)(2,1)}, bf16[64,1024]{1,0:T(8,128)(2,1)S(1)}, u32[]{:S(2)}, u32[]{:S(2)}) collective-permute-start(bf16[64,1024]{1,0:T(8,128)(2,1)} %get-tuple-element.50.refs_0_), channel_id=1, source_target_pairs={{0,8},{1,9},{2,10},{3,11},{4,12},{5,13},{6,14},{7,15},{8,0},{9,1},... | collective-permute-start | bytes 393224 | tf_op jit(solution)/shard_map/ppermute | solution.py:131
  33.5 21.0 %collective-permute-start.6 = (bf16[256,1024]{1,0:T(8,128)(2,1)S(1)}, bf16[256,1024]{1,0:T(8,128)(2,1)S(1)}, u32[]{:S(2)}, u32[]{:S(2)}) collective-permute-start(bf16[256,1024]{1,0:T(8,128)(2,1)S(1)} %shard_map.97), channel_id=1, source_target_pairs={{0,4},{1,5},{2,6},{3,7},{4,8},{5,9},{6,10},{7,11},{8,12},{9,13},{1... | collective-permute-start | bytes 1572872 | tf_op jit(solution)/shard_map/ppermute | solution.py:131
  34.8 19.7 %collective-permute-start.7 = (bf16[256,1024]{1,0:T(8,128)(2,1)S(1)}, bf16[256,1024]{1,0:T(8,128)(2,1)S(1)}, u32[]{:S(2)}, u32[]{:S(2)}) collective-permute-start(bf16[256,1024]{1,0:T(8,128)(2,1)S(1)} %shard_map.97), channel_id=1, source_target_pairs={{0,12},{1,13},{2,14},{3,15},{4,0},{5,1},{6,2},{7,3},{8,4},{9,5},{1... | collective-permute-start | bytes 1572872 | tf_op jit(solution)/shard_map/ppermute | solution.py:131
  36.9 17.7 %collective-permute-start.8 = (bf16[256,1024]{1,0:T(8,128)(2,1)S(1)}, bf16[256,1024]{1,0:T(8,128)(2,1)S(1)}, u32[]{:S(2)}, u32[]{:S(2)}) collective-permute-start(bf16[256,1024]{1,0:T(8,128)(2,1)S(1)} %shard_map.98), channel_id=1, source_target_pairs={{0,1},{1,2},{2,3},{3,0},{4,5},{5,6},{6,7},{7,4},{8,9},{9,10},{10,1... | collective-permute-start | bytes 1572872 | tf_op jit(solution)/shard_map/ppermute | solution.py:131
  37.3 17.3 %collective-permute-start.9 = (bf16[256,1024]{1,0:T(8,128)(2,1)S(1)}, bf16[256,1024]{1,0:T(8,128)(2,1)S(1)}, u32[]{:S(2)}, u32[]{:S(2)}) collective-permute-start(bf16[256,1024]{1,0:T(8,128)(2,1)S(1)} %shard_map.98), channel_id=1, source_target_pairs={{0,3},{1,0},{2,1},{3,2},{4,7},{5,4},{6,5},{7,6},{8,11},{9,8},{10,9... | collective-permute-start | bytes 1572872 | tf_op jit(solution)/shard_map/ppermute | solution.py:131
  54.6 9.7 %collective-permute-start.11 = (bf16[128,1024]{1,0:T(8,128)(2,1)S(1)}, bf16[128,1024]{1,0:T(8,128)(2,1)S(1)}, u32[]{:S(2)}, u32[]{:S(2)}) collective-permute-start(bf16[128,1024]{1,0:T(8,128)(2,1)S(1)} %slice.28), channel_id=1, source_target_pairs={{0,12},{1,13},{2,14},{3,15},{4,0},{5,1},{6,2},{7,3},{8,4},{9,5},{1... | collective-permute-start | bytes 786440 | tf_op jit(solution)/shard_map/ppermute | solution.py:131
  56.6 7.7 %collective-permute-start.12 = (bf16[128,1024]{1,0:T(8,128)(2,1)S(1)}, bf16[128,1024]{1,0:T(8,128)(2,1)S(1)}, u32[]{:S(2)}, u32[]{:S(2)}) collective-permute-start(bf16[128,1024]{1,0:T(8,128)(2,1)S(1)} %slice.29), channel_id=1, source_target_pairs={{0,4},{1,5},{2,6},{3,7},{4,8},{5,9},{6,10},{7,11},{8,12},{9,13},{1... | collective-permute-start | bytes 786440 | tf_op jit(solution)/shard_map/ppermute | solution.py:131
  59.9 5.6 %collective-permute-start.13 = (bf16[64,1024]{1,0:T(8,128)(2,1)S(1)}, bf16[64,1024]{1,0:T(8,128)(2,1)S(1)}, u32[]{:S(2)}, u32[]{:S(2)}) collective-permute-start(bf16[64,1024]{1,0:T(8,128)(2,1)S(1)} %slice.30), channel_id=1, source_target_pairs={{0,3},{1,0},{2,1},{3,2},{4,7},{5,4},{6,5},{7,6},{8,11},{9,8},{10,9... | collective-permute-start | bytes 393224 | tf_op jit(solution)/shard_map/ppermute | solution.py:131
  63.0 1.3 collective-permute-start.10
  65.5 15.3 %collective-permute-start.17 = (bf16[256,1024]{1,0:T(8,128)(2,1)S(1)}, bf16[256,1024]{1,0:T(8,128)(2,1)S(1)}, u32[]{:S(2)}, u32[]{:S(2)}) collective-permute-start(bf16[256,1024]{1,0:T(8,128)(2,1)S(1)} %shard_map.102), channel_id=1, source_target_pairs={{0,4},{1,5},{2,6},{3,7},{4,8},{5,9},{6,10},{7,11},{8,12},{9,13},{1... | collective-permute-start | bytes 1572872 | tf_op jit(solution)/shard_map/ppermute | solution.py:131
  65.8 15.0 %collective-permute-start.18 = (bf16[256,1024]{1,0:T(8,128)(2,1)S(1)}, bf16[256,1024]{1,0:T(8,128)(2,1)S(1)}, u32[]{:S(2)}, u32[]{:S(2)}) collective-permute-start(bf16[256,1024]{1,0:T(8,128)(2,1)S(1)} %shard_map.102), channel_id=1, source_target_pairs={{0,12},{1,13},{2,14},{3,15},{4,0},{5,1},{6,2},{7,3},{8,4},{9,5},{1... | collective-permute-start | bytes 1572872 | tf_op jit(solution)/shard_map/ppermute | solution.py:131
  68.9 3.9 %collective-permute-start.15 = (f32[48,1024]{1,0:T(8,128)S(1)}, f32[48,1024]{1,0:T(8,128)S(1)}, u32[]{:S(2)}, u32[]{:S(2)}) collective-permute-start(f32[48,1024]{1,0:T(8,128)S(1)} %get-tuple-element.63.left_ref), channel_id=1, source_target_pairs={{0,16},{16,0},{32,48},{48,32},{64,80},{80,64},{96,112},{112,96},{1... | collective-permute-start | bytes 589832 | tf_op jit(solution)/shard_map/ppermute | solution.py:292
  68.9 15.1 %collective-permute-start.19 = (bf16[128,1024]{1,0:T(8,128)(2,1)S(1)}, bf16[128,1024]{1,0:T(8,128)(2,1)S(1)}, u32[]{:S(2)}, u32[]{:S(2)}) collective-permute-start(bf16[128,1024]{1,0:T(8,128)(2,1)S(1)} %slice.31), channel_id=1, source_target_pairs={{0,3},{1,0},{2,1},{3,2},{4,7},{5,4},{6,5},{7,6},{8,11},{9,8},{10,9... | collective-permute-start | bytes 786440 | tf_op jit(solution)/shard_map/ppermute | solution.py:131
  72.6 11.4 %collective-permute-start.20 = (bf16[128,1024]{1,0:T(8,128)(2,1)S(1)}, bf16[128,1024]{1,0:T(8,128)(2,1)S(1)}, u32[]{:S(2)}, u32[]{:S(2)}) collective-permute-start(bf16[128,1024]{1,0:T(8,128)(2,1)S(1)} %slice.32), channel_id=1, source_target_pairs={{0,1},{1,2},{2,3},{3,0},{4,5},{5,6},{6,7},{7,4},{8,9},{9,10},{10,1... | collective-permute-start | bytes 786440 | tf_op jit(solution)/shard_map/ppermute | solution.py:131
  72.7 1.4 %collective-permute-start.14 = (f32[16,1536]{1,0:T(8,128)S(1)}, f32[16,1536]{1,0:T(8,128)S(1)}, u32[]{:S(2)}, u32[]{:S(2)}) collective-permute-start(f32[16,1536]{1,0:T(8,128)S(1)} %shard_map.100.own_ref), channel_id=1, source_target_pairs={{0,16},{16,0},{32,48},{48,32},{64,80},{80,64},{96,112},{112,96},{1... | collective-permute-start | bytes 294920 | tf_op jit(solution)/shard_map/ppermute | solution.py:292
  76.6 4.3 %collective-permute-start.16 = (f32[16,1024]{1,0:T(8,128)S(1)}, f32[16,1024]{1,0:T(8,128)S(1)}, u32[]{:S(2)}, u32[]{:S(2)}) collective-permute-start(f32[16,1024]{1,0:T(8,128)S(1)} %get-tuple-element.64.own_ref), channel_id=1, source_target_pairs={{0,32},{16,48},{32,0},{48,16},{64,96},{80,112},{96,64},{112,80},{1... | collective-permute-start | bytes 196616 | tf_op jit(solution)/shard_map/ppermute | solution.py:292
  80.9 15.9 %collective-permute-start.24 = (bf16[128,1024]{1,0:T(8,128)(2,1)S(1)}, bf16[128,1024]{1,0:T(8,128)(2,1)S(1)}, u32[]{:S(2)}, u32[]{:S(2)}) collective-permute-start(bf16[128,1024]{1,0:T(8,128)(2,1)S(1)} %slice.33), channel_id=1, source_target_pairs={{0,12},{1,13},{2,14},{3,15},{4,0},{5,1},{6,2},{7,3},{8,4},{9,5},{1... | collective-permute-start | bytes 786440 | tf_op jit(solution)/shard_map/ppermute | solution.py:131
  83.7 13.0 %collective-permute-start.25 = (bf16[128,1024]{1,0:T(8,128)(2,1)S(1)}, bf16[128,1024]{1,0:T(8,128)(2,1)S(1)}, u32[]{:S(2)}, u32[]{:S(2)}) collective-permute-start(bf16[128,1024]{1,0:T(8,128)(2,1)S(1)} %slice.34), channel_id=1, source_target_pairs={{0,4},{1,5},{2,6},{3,7},{4,8},{5,9},{6,10},{7,11},{8,12},{9,13},{1... | collective-permute-start | bytes 786440 | tf_op jit(solution)/shard_map/ppermute | solution.py:131
  83.8 5.1 %collective-permute-start.22 = (f32[32,1024]{1,0:T(8,128)S(1)}, f32[32,1024]{1,0:T(8,128)S(1)}, u32[]{:S(2)}, u32[]{:S(2)}) collective-permute-start(f32[32,1024]{1,0:T(8,128)S(1)} %get-tuple-element.71.left_ref), channel_id=1, source_target_pairs={{0,32},{16,48},{32,0},{48,16},{64,96},{80,112},{96,64},{112,80},{1... | collective-permute-start | bytes 393224 | tf_op jit(solution)/shard_map/ppermute | solution.py:292
  85.1 3.8 %collective-permute-start.21 = (f32[16,1536]{1,0:T(8,128)S(1)}, f32[16,1536]{1,0:T(8,128)S(1)}, u32[]{:S(2)}, u32[]{:S(2)}) collective-permute-start(f32[16,1536]{1,0:T(8,128)S(1)} %shard_map.103.own_ref), channel_id=1, source_target_pairs={{0,16},{16,0},{32,48},{48,32},{64,80},{80,64},{96,112},{112,96},{1... | collective-permute-start | bytes 294920 | tf_op jit(solution)/shard_map/ppermute | solution.py:292
  90.7 6.0 %collective-permute-start.23 = (f32[16,1024]{1,0:T(8,128)S(1)}, f32[16,1024]{1,0:T(8,128)S(1)}, u32[]{:S(2)}, u32[]{:S(2)}) collective-permute-start(f32[16,1024]{1,0:T(8,128)S(1)} %get-tuple-element.72.own_ref), channel_id=1, source_target_pairs={{0,64},{16,80},{32,96},{48,112},{64,0},{80,16},{96,32},{112,48},{1... | collective-permute-start | bytes 196616 | tf_op jit(solution)/shard_map/ppermute | solution.py:292
  94.0 5.2 %collective-permute-start.26 = (f32[16,1024]{1,0:T(8,128)S(1)}, f32[16,1024]{1,0:T(8,128)S(1)}, u32[]{:S(2)}, u32[]{:S(2)}) collective-permute-start(f32[16,1024]{1,0:T(8,128)S(1)} %get-tuple-element.75.left_ref), channel_id=1, source_target_pairs={{0,64},{16,80},{32,96},{48,112},{64,0},{80,16},{96,32},{112,48},{1... | collective-permute-start | bytes 196616 | tf_op jit(solution)/shard_map/ppermute | solution.py:292
  99.2 1.3 collective-permute-start.27
  101.7 8.0 %collective-permute-start.28 = (f32[16,1024]{1,0:T(8,128)S(1)}, f32[16,1024]{1,0:T(8,128)S(1)}, u32[]{:S(2)}, u32[]{:S(2)}) collective-permute-start(f32[16,1024]{1,0:T(8,128)S(1)} %shard_map.106.own_ref), channel_id=1, source_target_pairs={{0,192},{16,208},{32,224},{48,240},{64,128},{80,144},{96,160},{112... | collective-permute-start | bytes 196616 | tf_op jit(solution)/shard_map/ppermute | solution.py:292
  110.6 19.3 %all-to-all-start.2 = ((bf16[16,16,1408]{2,1,0:T(8,128)(2,1)}), bf16[16,16,1408]{2,1,0:T(8,128)(2,1)S(1)}, u32[]{:S(2)}, u32[]{:S(2)}) async-start(bf16[16,16,1408]{2,1,0:T(8,128)(2,1)} %shard_map.110), calls=%async_computation.2 | async-start | bytes 1441792 | tf_op jit(solution)/shard_map/all_to_all | solution.py:388
  (6 other events, 141.6 us)

commit v11 on v10

--- a/solution.py
+++ b/solution.py
@@ -112,14 +112,14 @@
     )(place, rhs_leaf, rhs_top, inv_top, off_top)
 
 
-def stack_kernel(starts, *refs):
-    for k, (start, ref) in enumerate(zip(starts, refs)):
+def stack_kernel(start, *refs):
+    for k, ref in enumerate(refs[:-1]):
         refs[-1][k * 64 : (k + 1) * 64, :] = ref[start : start + 64, :]
 
 
-def stack(parts, starts):
+def stack(parts, start):
     return call(
-        functools.partial(stack_kernel, starts),
+        functools.partial(stack_kernel, start),
         jax.ShapeDtypeStruct((256, 1024), BF),
         [VMEM] * 4,
         tuple(parts),
@@ -323,7 +323,7 @@
     sent, second, pair = first_payload(place, rhs_leaf, rhs_top, inv_top, off_top)
     first = lax.all_to_all(sent, "front", 0, 0)
     pair = (pair, *near(pair, "y"))
-    third = opposite(pair[0][:64], "y")
+    pair = (*pair, opposite(pair[0], "y"))
     second = (second, *near(second, "x"), opposite(second, "x"))
     leaf_x, sent = call(
         leaf_solve_kernel,
@@ -331,12 +331,14 @@
         [VMEM] * 3,
         (inv_leaf, first, off_leaf),
     )
-    sent, third, pair, second = lax.optimization_barrier((sent, third, pair, second))
+    sent, pair, second = lax.optimization_barrier((sent, pair, second))
     got = lax.all_to_all(sent, "front", 0, 0)
-    third = stack((*pair, third), (0, 0, 0, 0))
-    second = stack(second, (0, 0, 0, 0))
+    third, second = stack(pair, 0), stack(second, 0)
     third_near, second_near = near(third, "x"), near(second, "y")
-    got, third_near, second_near = lax.optimization_barrier((got, third_near, second_near))
+    got, third_near, second_near, pair = lax.optimization_barrier(
+        (got, third_near, second_near, pair)
+    )
+    lowest = stack(pair, 64)
     third_far = far(third_near, "x")
     state, left = call(
         leaf_update_kernel,
@@ -344,9 +346,8 @@
         [SMEM] + [VMEM] * 3,
         (place, first, got, idx_leaf),
     )
-    state, second_near, pair = lax.optimization_barrier((state, second_near, pair))
+    state, second_near = lax.optimization_barrier((state, second_near))
     second_far = far(second_near, "y")
-    lowest = turn(pair[2][64:], 0, -1)
     other, left_other = swap(state, core_pairs()), swap(left, core_pairs())
     ships = []
     for level in range(3):
@@ -359,9 +360,8 @@
         ux = top_solve(state, other, parts)
         if level == 0:
             ux, lowest = lax.optimization_barrier((ux, lowest))
-            lowest = stack((*pair, lowest), (64, 64, 64, 0))
             lowest_near = near(lowest, "x")
-        if level == 2:
+        if level > 0:
             ux, left_other = lax.optimization_barrier((ux, left_other))
         ux_other = swap(ux, core_pairs())
         state, *more = top_update(level, place, ux, ux_other, left, left_other, idx_top)

time: 131 us -> 132 us (level); the launches traced: 131 us -> 130 us
  starting transfers between devices: 56.1 us -> 50.4 us
  waiting for transfers between devices: 36.7 us -> 40.8 us
  blocking collectives: 14.3 us -> 16.1 us
    ppermute x19 -> x18, starting transfers between devices: 34.6 us -> 27.2 us  [turn(): return lax.ppermute(block, 'front', route)]
    ppermute x19 -> x18, waiting for transfers between devices: 7.34 us -> 14.1 us  [turn(): return lax.ppermute(block, 'front', route)]
    ppermute x10, waiting for transfers between devices: 16.4 us -> 14.2 us  [swap(): return lax.ppermute(block, 'leaf', pairs)]
    all_to_all x1, blocking collectives: 14.3 us -> 16.1 us  [local(): got = lax.all_to_all(sent, 'front', 0, 0)]
    ppermute x10, starting transfers between devices: 8.92 us -> 10.3 us  [swap(): return lax.ppermute(block, 'leaf', pairs)]
  transfers between devices with their start and end apart: 31 -> 30, of which waited for: 12 -> 13; matrix products, arithmetic and copies ran while one was open for 1% -> 1% of each run, Pallas kernels for 11% -> 10%
where the time goes in v11:
time: 132 us; the launch traced here: 130 us
  starting transfers between devices  50.4 us (38%)
  waiting for transfers between devices  40.8 us (31%)
  Pallas kernels  20.3 us (15%)
  blocking collectives  16.1 us (12%)
  local copies, waits for them, and re-layouts  1.73 us (1%)
    ppermute x18, starting transfers between devices, turn(): return lax.ppermute(block, 'front', route)  27.2 us
    pallas_call x16, Pallas kernels, call(): pl.pallas_call(kernel, out_shape=outs, in_specs=specs, out_specs=tuple((V...  17 us
    all_to_all x1, blocking collectives, local(): got = lax.all_to_all(sent, 'front', 0, 0)  16.1 us
    ppermute x10, waiting for transfers between devices, swap(): return lax.ppermute(block, 'leaf', pairs)  14.2 us
    ppermute x18, waiting for transfers between devices, turn(): return lax.ppermute(block, 'front', route)  14.1 us
    all_to_all x1, waiting for transfers between devices, local(): got = lax.all_to_all(sent, 'front', 0, 0)  12.5 us
    ppermute x10, starting transfers between devices, swap(): return lax.ppermute(block, 'leaf', pairs)  10.3 us
    all_to_all x1, starting transfers between devices, local(): first = lax.all_to_all(sent, 'front', 0, 0)  7.18 us
  transfers between devices with their start and end apart: 30, of which 13 were waited for; matrix products, arithmetic and copies ran while one was open for 1% of the time, Pallas kernels for 10%

profile of v11, /device:TPU:32, one launch (start us, length us, event | category | flops | bytes accessed | tf_op | source)
XLA Modules:
  0.0 130.2 jit_solution(17824015374670412931)
XLA Ops:
  1.3 3.3 %shard_map.95 = (bf16[16,80,256]{2,1,0:T(8,128)(2,1)}, bf16[64,1024]{1,0:T(8,128)(2,1)}, bf16[128,1024]{1,0:T(8,128)(2,1)}) custom-call(s32[12]{0:T(128)} %stack.48.place, f32[1,64,256]{2,1,0:T(8,128)} %leaf_ref.1, f32[15,64,256]{2,1,0:T(8,128)} %rhs_ref.1, bf16[15,64,1024]{2,1,0:T(8,128)(2,1)} %inv_ref.2, bf16[14,64,1024]{2,1,0:T(8,128)(2,1)} %bitcast.46), custom_call_target="tpu_custom_call" | custom-call | tf_op jit(solution)/shard_map/pallas_call | solution.py:101
  4.7 7.2 %all-to-all-start = ((bf16[16,80,256]{2,1,0:T(8,128)(2,1)}), bf16[16,80,256]{2,1,0:T(8,128)(2,1)S(1)}, u32[]{:S(2)}, u32[]{:S(2)}) async-start(bf16[16,80,256]{2,1,0:T(8,128)(2,1)} %get-tuple-element.43), calls=%async_computation | async-start | bytes 1310720 | tf_op jit(solution)/shard_map/all_to_all | solution.py:324
  11.9 1.9 %collective-permute-start.3 = (bf16[64,1024]{1,0:T(8,128)(2,1)}, bf16[64,1024]{1,0:T(8,128)(2,1)S(1)}, u32[]{:S(2)}, u32[]{:S(2)}) collective-permute-start(bf16[64,1024]{1,0:T(8,128)(2,1)} %get-tuple-element.53.refs_0_), channel_id=1, source_target_pairs={{0,4},{1,5},{2,6},{3,7},{4,8},{5,9},{6,10},{7,11},{8,12},{9,13},{1... | collective-permute-start | bytes 393224 | tf_op jit(solution)/shard_map/ppermute | solution.py:131
  13.8 1.5 %collective-permute-start = (bf16[128,1024]{1,0:T(8,128)(2,1)}, bf16[128,1024]{1,0:T(8,128)(2,1)S(1)}, u32[]{:S(2)}, u32[]{:S(2)}) collective-permute-start(bf16[128,1024]{1,0:T(8,128)(2,1)} %get-tuple-element.64.refs_0_), channel_id=1, source_target_pairs={{0,1},{1,2},{2,3},{3,0},{4,5},{5,6},{6,7},{7,4},{8,9},{9,10},{10,1... | collective-permute-start | bytes 786440 | tf_op jit(solution)/shard_map/ppermute | solution.py:131
  15.2 1.8 %collective-permute-start.1 = (bf16[128,1024]{1,0:T(8,128)(2,1)}, bf16[128,1024]{1,0:T(8,128)(2,1)S(1)}, u32[]{:S(2)}, u32[]{:S(2)}) collective-permute-start(bf16[128,1024]{1,0:T(8,128)(2,1)} %get-tuple-element.64.refs_0_), channel_id=1, source_target_pairs={{0,3},{1,0},{2,1},{3,2},{4,7},{5,4},{6,5},{7,6},{8,11},{9,8},{10,9... | collective-permute-start | bytes 786440 | tf_op jit(solution)/shard_map/ppermute | solution.py:131
  17.0 1.8 %collective-permute-start.2 = (bf16[128,1024]{1,0:T(8,128)(2,1)}, bf16[128,1024]{1,0:T(8,128)(2,1)S(1)}, u32[]{:S(2)}, u32[]{:S(2)}) collective-permute-start(bf16[128,1024]{1,0:T(8,128)(2,1)} %get-tuple-element.64.refs_0_), channel_id=1, source_target_pairs={{0,2},{1,3},{2,0},{3,1},{4,6},{5,7},{6,4},{7,5},{8,10},{9,11},{10,... | collective-permute-start | bytes 786440 | tf_op jit(solution)/shard_map/ppermute | solution.py:131
  18.8 1.8 %collective-permute-start.4 = (bf16[64,1024]{1,0:T(8,128)(2,1)}, bf16[64,1024]{1,0:T(8,128)(2,1)S(1)}, u32[]{:S(2)}, u32[]{:S(2)}) collective-permute-start(bf16[64,1024]{1,0:T(8,128)(2,1)} %get-tuple-element.53.refs_0_), channel_id=1, source_target_pairs={{0,12},{1,13},{2,14},{3,15},{4,0},{5,1},{6,2},{7,3},{8,4},{9,5},{1... | collective-permute-start | bytes 393224 | tf_op jit(solution)/shard_map/ppermute | solution.py:131
  20.5 4.6 %collective-permute-done.3.refs_1_ = bf16[64,1024]{1,0:T(8,128)(2,1)S(1)} collective-permute-done((bf16[64,1024]{1,0:T(8,128)(2,1)}, bf16[64,1024]{1,0:T(8,128)(2,1)S(1)}, u32[]{:S(2)}, u32[]{:S(2)}) %collective-permute-start.3) | collective-permute-done | bytes 131104 | tf_op jit(solution)/shard_map/ppermute | solution.py:131
  26.9 4.9 %collective-permute-done.5.refs_3_ = bf16[64,1024]{1,0:T(8,128)(2,1)S(1)} collective-permute-done((bf16[64,1024]{1,0:T(8,128)(2,1)}, bf16[64,1024]{1,0:T(8,128)(2,1)S(1)}, u32[]{:S(2)}, u32[]{:S(2)}) %collective-permute-start.5) | collective-permute-done | bytes 131104 | tf_op jit(solution)/shard_map/ppermute | solution.py:131
  31.8 2.6 %collective-permute-done.2.refs_3_ = bf16[128,1024]{1,0:T(8,128)(2,1)S(1)} collective-permute-done((bf16[128,1024]{1,0:T(8,128)(2,1)}, bf16[128,1024]{1,0:T(8,128)(2,1)S(1)}, u32[]{:S(2)}, u32[]{:S(2)}) %collective-permute-start.2) | collective-permute-done | bytes 262176 | tf_op jit(solution)/shard_map/ppermute | solution.py:131
  35.6 2.2 %collective-permute-start.7 = (bf16[256,1024]{1,0:T(8,128)(2,1)S(1)}, bf16[256,1024]{1,0:T(8,128)(2,1)S(1)}, u32[]{:S(2)}, u32[]{:S(2)}) collective-permute-start(bf16[256,1024]{1,0:T(8,128)(2,1)S(1)} %shard_map.97), channel_id=1, source_target_pairs={{0,12},{1,13},{2,14},{3,15},{4,0},{5,1},{6,2},{7,3},{8,4},{9,5},{1... | collective-permute-start | bytes 1572872 | tf_op jit(solution)/shard_map/ppermute | solution.py:131
  38.5 2.7 %collective-permute-start.9 = (bf16[256,1024]{1,0:T(8,128)(2,1)S(1)}, bf16[256,1024]{1,0:T(8,128)(2,1)S(1)}, u32[]{:S(2)}, u32[]{:S(2)}) collective-permute-start(bf16[256,1024]{1,0:T(8,128)(2,1)S(1)} %shard_map.98), channel_id=1, source_target_pairs={{0,3},{1,0},{2,1},{3,2},{4,7},{5,4},{6,5},{7,6},{8,11},{9,8},{10,9... | collective-permute-start | bytes 1572872 | tf_op jit(solution)/shard_map/ppermute | solution.py:131
  41.1 16.1 %all_to_all.15.got_ref = bf16[16,16,1024]{2,1,0:T(8,128)(2,1)S(1)} all-to-all(bf16[16,16,1024]{2,1,0:T(8,128)(2,1)S(1)} %get-tuple-element.48), channel_id=1, replica_groups=mesh['leaf'=16,'front'=16] {'front'}, dimensions={0} | all-to-all | bytes 1048576 | tf_op jit(solution)/shard_map/all_to_all | solution.py:335
  57.3 1.2 collective-permute-start.11
  59.5 3.1 %shard_map.99 = (f32[16,1024]{1,0:T(8,128)S(1)}, f32[48,1024]{1,0:T(8,128)S(1)}) custom-call(s32[12]{0:T(128)S(1)} %copy-done.5, bf16[16,80,256]{2,1,0:T(8,128)(2,1)S(1)} %all-to-all-done.rhs_ref.first_ref, bf16[16,16,1024]{2,1,0:T(8,128)(2,1)S(1)} %all_to_all.15.got_ref, s32[1,1024]{1,0:T(1,128)S(1)} %copy-done.6), custom_call_target="tpu_custom_call" | custom-call | flops 100000000 | bytes 1000000 | tf_op jit(solution)/shard_map/pallas_call | solution.py:46
  63.0 1.2 collective-permute-done.10.other_ref
  64.2 2.0 %collective-permute-done.12 = bf16[128,1024]{1,0:T(8,128)(2,1)S(1)} collective-permute-done((bf16[128,1024]{1,0:T(8,128)(2,1)S(1)}, bf16[128,1024]{1,0:T(8,128)(2,1)S(1)}, u32[]{:S(2)}, u32[]{:S(2)}) %collective-permute-start.12) | collective-permute-done | bytes 262176 | tf_op jit(solution)/shard_map/ppermute | solution.py:131
  67.3 3.2 %collective-permute-start.17 = (bf16[256,1024]{1,0:T(8,128)(2,1)S(1)}, bf16[256,1024]{1,0:T(8,128)(2,1)S(1)}, u32[]{:S(2)}, u32[]{:S(2)}) collective-permute-start(bf16[256,1024]{1,0:T(8,128)(2,1)S(1)} %shard_map.101), channel_id=1, source_target_pairs={{0,12},{1,13},{2,14},{3,15},{4,0},{5,1},{6,2},{7,3},{8,4},{9,5},{1... | collective-permute-start | bytes 1572872 | tf_op jit(solution)/shard_map/ppermute | solution.py:131
  71.0 3.0 %collective-permute-start.18 = (bf16[128,1024]{1,0:T(8,128)(2,1)S(1)}, bf16[128,1024]{1,0:T(8,128)(2,1)S(1)}, u32[]{:S(2)}, u32[]{:S(2)}) collective-permute-start(bf16[128,1024]{1,0:T(8,128)(2,1)S(1)} %slice.23), channel_id=1, source_target_pairs={{0,3},{1,0},{2,1},{3,2},{4,7},{5,4},{6,5},{7,6},{8,11},{9,8},{10,9... | collective-permute-start | bytes 786440 | tf_op jit(solution)/shard_map/ppermute | solution.py:131
  74.2 2.4 %shard_map.102 = (f32[16,1024]{1,0:T(8,128)S(1)}, f32[32,1024]{1,0:T(8,128)S(1)}) custom-call(s32[12]{0:T(128)S(1)} %copy-done.5, f32[16,1536]{1,0:T(8,128)S(1)} %shard_map.100.own_ref, f32[16,1536]{1,0:T(8,128)S(1)} %collective-permute-done.13.other_ref, f32[48,1024]{1,0:T(8,128)S(1)} %get-tuple-element.69.left_ref, ...), custom_call_target="tpu_custom_call" | custom-call | flops 100000000 | bytes 1000000 | tf_op jit(solution)/shard_map/pallas_call | solution.py:46
  76.8 4.2 %collective-permute-done.15.other_ref = f32[16,1024]{1,0:T(8,128)S(1)} collective-permute-done((f32[16,1024]{1,0:T(8,128)S(1)}, f32[16,1024]{1,0:T(8,128)S(1)}, u32[]{:S(2)}, u32[]{:S(2)}) %collective-permute-start.15) | collective-permute-done | bytes 65568 | tf_op jit(solution)/shard_map/ppermute | solution.py:292
  81.1 2.4 %collective-permute-start.23 = (bf16[128,1024]{1,0:T(8,128)(2,1)S(1)}, bf16[128,1024]{1,0:T(8,128)(2,1)S(1)}, u32[]{:S(2)}, u32[]{:S(2)}) collective-permute-start(bf16[128,1024]{1,0:T(8,128)(2,1)S(1)} %slice.25), channel_id=1, source_target_pairs={{0,12},{1,13},{2,14},{3,15},{4,0},{5,1},{6,2},{7,3},{8,4},{9,5},{1... | collective-permute-start | bytes 786440 | tf_op jit(solution)/shard_map/ppermute | solution.py:131
  84.7 1.2 collective-permute-done.20.left_other_ref
  85.9 1.3 collective-permute-done.21.other_ref
  87.2 1.8 %shard_map.104 = (f32[16,1024]{1,0:T(8,128)S(1)}, f32[16,1024]{1,0:T(8,128)S(1)}) custom-call(s32[12]{0:T(128)S(1)} %copy-done.5, f32[16,1536]{1,0:T(8,128)S(1)} %shard_map.103.own_ref, f32[16,1536]{1,0:T(8,128)S(1)} %collective-permute-done.21.other_ref, f32[32,1024]{1,0:T(8,128)S(1)} %get-tuple-element.75.left_ref, ...), custom_call_target="tpu_custom_call" | custom-call | flops 100000000 | bytes 1000000 | tf_op jit(solution)/shard_map/pallas_call | solution.py:46
  89.0 3.3 %collective-permute-start.22 = (f32[16,1024]{1,0:T(8,128)S(1)}, f32[16,1024]{1,0:T(8,128)S(1)}, u32[]{:S(2)}, u32[]{:S(2)}) collective-permute-start(f32[16,1024]{1,0:T(8,128)S(1)} %get-tuple-element.78.own_ref), channel_id=1, source_target_pairs={{0,64},{16,80},{32,96},{48,112},{64,0},{80,16},{96,32},{112,48},{1... | collective-permute-start | bytes 196616 | tf_op jit(solution)/shard_map/ppermute | solution.py:292
  92.4 4.4 %collective-permute-done.22.other_ref = f32[16,1024]{1,0:T(8,128)S(1)} collective-permute-done((f32[16,1024]{1,0:T(8,128)S(1)}, f32[16,1024]{1,0:T(8,128)S(1)}, u32[]{:S(2)}, u32[]{:S(2)}) %collective-permute-start.22) | collective-permute-done | bytes 65568 | tf_op jit(solution)/shard_map/ppermute | solution.py:292
  98.2 1.3 collective-permute-done.26.other_ref
  99.4 1.2 shard_map.106.own_ref
  100.7 5.9 %collective-permute-start.27 = (f32[16,1024]{1,0:T(8,128)S(1)}, f32[16,1024]{1,0:T(8,128)S(1)}, u32[]{:S(2)}, u32[]{:S(2)}) collective-permute-start(f32[16,1024]{1,0:T(8,128)S(1)} %shard_map.106.own_ref), channel_id=1, source_target_pairs={{0,192},{16,208},{32,224},{48,240},{64,128},{80,144},{96,160},{112... | collective-permute-start | bytes 196616 | tf_op jit(solution)/shard_map/ppermute | solution.py:292
  110.1 5.7 %all-to-all-start.2 = ((bf16[16,16,1408]{2,1,0:T(8,128)(2,1)}), bf16[16,16,1408]{2,1,0:T(8,128)(2,1)S(1)}, u32[]{:S(2)}, u32[]{:S(2)}) async-start(bf16[16,16,1408]{2,1,0:T(8,128)(2,1)} %shard_map.110), calls=%async_computation.2 | async-start | bytes 1441792 | tf_op jit(solution)/shard_map/all_to_all | solution.py:388
  116.7 12.5 %all-to-all-done.2.got_ref = bf16[16,16,1408]{2,1,0:T(8,128)(2,1)S(1)} async-done(((bf16[16,16,1408]{2,1,0:T(8,128)(2,1)}), bf16[16,16,1408]{2,1,0:T(8,128)(2,1)S(1)}, u32[]{:S(2)}, u32[]{:S(2)}) %all-to-all-start.2) | async-done | bytes 720928 | tf_op jit(solution)/shard_map/all_to_all | solution.py:388
  (68 shorter events, 15.7 us)
Async XLA Ops:
  4.6 29.8 %copy-start = (bf16[128,1024]{1,0:T(8,128)(2,1)S(1)}, bf16[128,1024]{1,0:T(8,128)(2,1)}, u32[]{:S(2)}) copy-start(bf16[128,1024]{1,0:T(8,128)(2,1)} %get-tuple-element.64.refs_0_) | copy-start | bytes 786436
  4.7 33.1 %copy-start.4 = (bf16[64,1024]{1,0:T(8,128)(2,1)S(1)}, bf16[64,1024]{1,0:T(8,128)(2,1)}, u32[]{:S(2)}) copy-start(bf16[64,1024]{1,0:T(8,128)(2,1)} %get-tuple-element.53.refs_0_) | copy-start | bytes 393220
  4.7 21.3 %all-to-all-start = ((bf16[16,80,256]{2,1,0:T(8,128)(2,1)}), bf16[16,80,256]{2,1,0:T(8,128)(2,1)S(1)}, u32[]{:S(2)}, u32[]{:S(2)}) async-start(bf16[16,80,256]{2,1,0:T(8,128)(2,1)} %get-tuple-element.43), calls=%async_computation | async-start | bytes 1310720 | tf_op jit(solution)/shard_map/all_to_all | solution.py:324
  11.9 13.3 %collective-permute-start.3 = (bf16[64,1024]{1,0:T(8,128)(2,1)}, bf16[64,1024]{1,0:T(8,128)(2,1)S(1)}, u32[]{:S(2)}, u32[]{:S(2)}) collective-permute-start(bf16[64,1024]{1,0:T(8,128)(2,1)} %get-tuple-element.53.refs_0_), channel_id=1, source_target_pairs={{0,4},{1,5},{2,6},{3,7},{4,8},{5,9},{6,10},{7,11},{8,12},{9,13},{1... | collective-permute-start | bytes 393224 | tf_op jit(solution)/shard_map/ppermute | solution.py:131
  13.8 18.1 %collective-permute-start = (bf16[128,1024]{1,0:T(8,128)(2,1)}, bf16[128,1024]{1,0:T(8,128)(2,1)S(1)}, u32[]{:S(2)}, u32[]{:S(2)}) collective-permute-start(bf16[128,1024]{1,0:T(8,128)(2,1)} %get-tuple-element.64.refs_0_), channel_id=1, source_target_pairs={{0,1},{1,2},{2,3},{3,0},{4,5},{5,6},{6,7},{7,4},{8,9},{9,10},{10,1... | collective-permute-start | bytes 786440 | tf_op jit(solution)/shard_map/ppermute | solution.py:131
  15.2 16.6 %collective-permute-start.1 = (bf16[128,1024]{1,0:T(8,128)(2,1)}, bf16[128,1024]{1,0:T(8,128)(2,1)S(1)}, u32[]{:S(2)}, u32[]{:S(2)}) collective-permute-start(bf16[128,1024]{1,0:T(8,128)(2,1)} %get-tuple-element.64.refs_0_), channel_id=1, source_target_pairs={{0,3},{1,0},{2,1},{3,2},{4,7},{5,4},{6,5},{7,6},{8,11},{9,8},{10,9... | collective-permute-start | bytes 786440 | tf_op jit(solution)/shard_map/ppermute | solution.py:131
  17.0 17.4 %collective-permute-start.2 = (bf16[128,1024]{1,0:T(8,128)(2,1)}, bf16[128,1024]{1,0:T(8,128)(2,1)S(1)}, u32[]{:S(2)}, u32[]{:S(2)}) collective-permute-start(bf16[128,1024]{1,0:T(8,128)(2,1)} %get-tuple-element.64.refs_0_), channel_id=1, source_target_pairs={{0,2},{1,3},{2,0},{3,1},{4,6},{5,7},{6,4},{7,5},{8,10},{9,11},{10,... | collective-permute-start | bytes 786440 | tf_op jit(solution)/shard_map/ppermute | solution.py:131
  18.8 8.1 %collective-permute-start.4 = (bf16[64,1024]{1,0:T(8,128)(2,1)}, bf16[64,1024]{1,0:T(8,128)(2,1)S(1)}, u32[]{:S(2)}, u32[]{:S(2)}) collective-permute-start(bf16[64,1024]{1,0:T(8,128)(2,1)} %get-tuple-element.53.refs_0_), channel_id=1, source_target_pairs={{0,12},{1,13},{2,14},{3,15},{4,0},{5,1},{6,2},{7,3},{8,4},{9,5},{1... | collective-permute-start | bytes 393224 | tf_op jit(solution)/shard_map/ppermute | solution.py:131
  25.2 6.7 %collective-permute-start.5 = (bf16[64,1024]{1,0:T(8,128)(2,1)}, bf16[64,1024]{1,0:T(8,128)(2,1)S(1)}, u32[]{:S(2)}, u32[]{:S(2)}) collective-permute-start(bf16[64,1024]{1,0:T(8,128)(2,1)} %get-tuple-element.53.refs_0_), channel_id=1, source_target_pairs={{0,8},{1,9},{2,10},{3,11},{4,12},{5,13},{6,14},{7,15},{8,0},{9,1},... | collective-permute-start | bytes 393224 | tf_op jit(solution)/shard_map/ppermute | solution.py:131
  34.5 22.8 %collective-permute-start.6 = (bf16[256,1024]{1,0:T(8,128)(2,1)S(1)}, bf16[256,1024]{1,0:T(8,128)(2,1)S(1)}, u32[]{:S(2)}, u32[]{:S(2)}) collective-permute-start(bf16[256,1024]{1,0:T(8,128)(2,1)S(1)} %shard_map.97), channel_id=1, source_target_pairs={{0,4},{1,5},{2,6},{3,7},{4,8},{5,9},{6,10},{7,11},{8,12},{9,13},{1... | collective-permute-start | bytes 1572872 | tf_op jit(solution)/shard_map/ppermute | solution.py:131
  35.6 21.7 %collective-permute-start.7 = (bf16[256,1024]{1,0:T(8,128)(2,1)S(1)}, bf16[256,1024]{1,0:T(8,128)(2,1)S(1)}, u32[]{:S(2)}, u32[]{:S(2)}) collective-permute-start(bf16[256,1024]{1,0:T(8,128)(2,1)S(1)} %shard_map.97), channel_id=1, source_target_pairs={{0,12},{1,13},{2,14},{3,15},{4,0},{5,1},{6,2},{7,3},{8,4},{9,5},{1... | collective-permute-start | bytes 1572872 | tf_op jit(solution)/shard_map/ppermute | solution.py:131
  37.8 19.4 %collective-permute-start.8 = (bf16[256,1024]{1,0:T(8,128)(2,1)S(1)}, bf16[256,1024]{1,0:T(8,128)(2,1)S(1)}, u32[]{:S(2)}, u32[]{:S(2)}) collective-permute-start(bf16[256,1024]{1,0:T(8,128)(2,1)S(1)} %shard_map.98), channel_id=1, source_target_pairs={{0,1},{1,2},{2,3},{3,0},{4,5},{5,6},{6,7},{7,4},{8,9},{9,10},{10,1... | collective-permute-start | bytes 1572872 | tf_op jit(solution)/shard_map/ppermute | solution.py:131
  38.5 18.8 %collective-permute-start.9 = (bf16[256,1024]{1,0:T(8,128)(2,1)S(1)}, bf16[256,1024]{1,0:T(8,128)(2,1)S(1)}, u32[]{:S(2)}, u32[]{:S(2)}) collective-permute-start(bf16[256,1024]{1,0:T(8,128)(2,1)S(1)} %shard_map.98), channel_id=1, source_target_pairs={{0,3},{1,0},{2,1},{3,2},{4,7},{5,4},{6,5},{7,6},{8,11},{9,8},{10,9... | collective-permute-start | bytes 1572872 | tf_op jit(solution)/shard_map/ppermute | solution.py:131
  57.3 6.8 %collective-permute-start.11 = (bf16[128,1024]{1,0:T(8,128)(2,1)S(1)}, bf16[128,1024]{1,0:T(8,128)(2,1)S(1)}, u32[]{:S(2)}, u32[]{:S(2)}) collective-permute-start(bf16[128,1024]{1,0:T(8,128)(2,1)S(1)} %slice.21), channel_id=1, source_target_pairs={{0,12},{1,13},{2,14},{3,15},{4,0},{5,1},{6,2},{7,3},{8,4},{9,5},{1... | collective-permute-start | bytes 786440 | tf_op jit(solution)/shard_map/ppermute | solution.py:131
  58.5 7.7 %collective-permute-start.12 = (bf16[128,1024]{1,0:T(8,128)(2,1)S(1)}, bf16[128,1024]{1,0:T(8,128)(2,1)S(1)}, u32[]{:S(2)}, u32[]{:S(2)}) collective-permute-start(bf16[128,1024]{1,0:T(8,128)(2,1)S(1)} %slice.22), channel_id=1, source_target_pairs={{0,4},{1,5},{2,6},{3,7},{4,8},{5,9},{6,10},{7,11},{8,12},{9,13},{1... | collective-permute-start | bytes 786440 | tf_op jit(solution)/shard_map/ppermute | solution.py:131
  62.6 1.5 %collective-permute-start.10 = (f32[16,1024]{1,0:T(8,128)S(1)}, f32[16,1024]{1,0:T(8,128)S(1)}, u32[]{:S(2)}, u32[]{:S(2)}) collective-permute-start(f32[16,1024]{1,0:T(8,128)S(1)} %get-tuple-element.61.own_ref), channel_id=1, source_target_pairs={{0,16},{16,0},{32,48},{48,32},{64,80},{80,64},{96,112},{112,96},{1... | collective-permute-start | bytes 196616 | tf_op jit(solution)/shard_map/ppermute | solution.py:292
  67.3 13.8 %collective-permute-start.16 = (bf16[256,1024]{1,0:T(8,128)(2,1)S(1)}, bf16[256,1024]{1,0:T(8,128)(2,1)S(1)}, u32[]{:S(2)}, u32[]{:S(2)}) collective-permute-start(bf16[256,1024]{1,0:T(8,128)(2,1)S(1)} %shard_map.101), channel_id=1, source_target_pairs={{0,4},{1,5},{2,6},{3,7},{4,8},{5,9},{6,10},{7,11},{8,12},{9,13},{1... | collective-permute-start | bytes 1572872 | tf_op jit(solution)/shard_map/ppermute | solution.py:131
  67.3 13.8 %collective-permute-start.17 = (bf16[256,1024]{1,0:T(8,128)(2,1)S(1)}, bf16[256,1024]{1,0:T(8,128)(2,1)S(1)}, u32[]{:S(2)}, u32[]{:S(2)}) collective-permute-start(bf16[256,1024]{1,0:T(8,128)(2,1)S(1)} %shard_map.101), channel_id=1, source_target_pairs={{0,12},{1,13},{2,14},{3,15},{4,0},{5,1},{6,2},{7,3},{8,4},{9,5},{1... | collective-permute-start | bytes 1572872 | tf_op jit(solution)/shard_map/ppermute | solution.py:131
  70.5 3.6 %collective-permute-start.14 = (f32[48,1024]{1,0:T(8,128)S(1)}, f32[48,1024]{1,0:T(8,128)S(1)}, u32[]{:S(2)}, u32[]{:S(2)}) collective-permute-start(f32[48,1024]{1,0:T(8,128)S(1)} %get-tuple-element.69.left_ref), channel_id=1, source_target_pairs={{0,16},{16,0},{32,48},{48,32},{64,80},{80,64},{96,112},{112,96},{1... | collective-permute-start | bytes 589832 | tf_op jit(solution)/shard_map/ppermute | solution.py:292
  70.5 3.7 %collective-permute-start.13 = (f32[16,1536]{1,0:T(8,128)S(1)}, f32[16,1536]{1,0:T(8,128)S(1)}, u32[]{:S(2)}, u32[]{:S(2)}) collective-permute-start(f32[16,1536]{1,0:T(8,128)S(1)} %shard_map.100.own_ref), channel_id=1, source_target_pairs={{0,16},{16,0},{32,48},{48,32},{64,80},{80,64},{96,112},{112,96},{1... | collective-permute-start | bytes 294920 | tf_op jit(solution)/shard_map/ppermute | solution.py:292
  71.0 12.6 %collective-permute-start.18 = (bf16[128,1024]{1,0:T(8,128)(2,1)S(1)}, bf16[128,1024]{1,0:T(8,128)(2,1)S(1)}, u32[]{:S(2)}, u32[]{:S(2)}) collective-permute-start(bf16[128,1024]{1,0:T(8,128)(2,1)S(1)} %slice.23), channel_id=1, source_target_pairs={{0,3},{1,0},{2,1},{3,2},{4,7},{5,4},{6,5},{7,6},{8,11},{9,8},{10,9... | collective-permute-start | bytes 786440 | tf_op jit(solution)/shard_map/ppermute | solution.py:131
  74.1 9.5 %collective-permute-start.19 = (bf16[128,1024]{1,0:T(8,128)(2,1)S(1)}, bf16[128,1024]{1,0:T(8,128)(2,1)S(1)}, u32[]{:S(2)}, u32[]{:S(2)}) collective-permute-start(bf16[128,1024]{1,0:T(8,128)(2,1)S(1)} %slice.24), channel_id=1, source_target_pairs={{0,1},{1,2},{2,3},{3,0},{4,5},{5,6},{6,7},{7,4},{8,9},{9,10},{10,1... | collective-permute-start | bytes 786440 | tf_op jit(solution)/shard_map/ppermute | solution.py:131
  76.7 4.3 %collective-permute-start.15 = (f32[16,1024]{1,0:T(8,128)S(1)}, f32[16,1024]{1,0:T(8,128)S(1)}, u32[]{:S(2)}, u32[]{:S(2)}) collective-permute-start(f32[16,1024]{1,0:T(8,128)S(1)} %get-tuple-element.70.own_ref), channel_id=1, source_target_pairs={{0,32},{16,48},{32,0},{48,16},{64,96},{80,112},{96,64},{112,80},{1... | collective-permute-start | bytes 196616 | tf_op jit(solution)/shard_map/ppermute | solution.py:292
  80.9 5.0 %collective-permute-start.20 = (f32[32,1024]{1,0:T(8,128)S(1)}, f32[32,1024]{1,0:T(8,128)S(1)}, u32[]{:S(2)}, u32[]{:S(2)}) collective-permute-start(f32[32,1024]{1,0:T(8,128)S(1)} %get-tuple-element.75.left_ref), channel_id=1, source_target_pairs={{0,32},{16,48},{32,0},{48,16},{64,96},{80,112},{96,64},{112,80},{1... | collective-permute-start | bytes 393224 | tf_op jit(solution)/shard_map/ppermute | solution.py:292
  81.1 15.7 %collective-permute-start.23 = (bf16[128,1024]{1,0:T(8,128)(2,1)S(1)}, bf16[128,1024]{1,0:T(8,128)(2,1)S(1)}, u32[]{:S(2)}, u32[]{:S(2)}) collective-permute-start(bf16[128,1024]{1,0:T(8,128)(2,1)S(1)} %slice.25), channel_id=1, source_target_pairs={{0,12},{1,13},{2,14},{3,15},{4,0},{5,1},{6,2},{7,3},{8,4},{9,5},{1... | collective-permute-start | bytes 786440 | tf_op jit(solution)/shard_map/ppermute | solution.py:131
  83.5 13.3 %collective-permute-start.24 = (bf16[128,1024]{1,0:T(8,128)(2,1)S(1)}, bf16[128,1024]{1,0:T(8,128)(2,1)S(1)}, u32[]{:S(2)}, u32[]{:S(2)}) collective-permute-start(bf16[128,1024]{1,0:T(8,128)(2,1)S(1)} %slice.26), channel_id=1, source_target_pairs={{0,4},{1,5},{2,6},{3,7},{4,8},{5,9},{6,10},{7,11},{8,12},{9,13},{1... | collective-permute-start | bytes 786440 | tf_op jit(solution)/shard_map/ppermute | solution.py:131
  85.9 1.3 collective-permute-start.21
  89.0 7.7 %collective-permute-start.22 = (f32[16,1024]{1,0:T(8,128)S(1)}, f32[16,1024]{1,0:T(8,128)S(1)}, u32[]{:S(2)}, u32[]{:S(2)}) collective-permute-start(f32[16,1024]{1,0:T(8,128)S(1)} %get-tuple-element.78.own_ref), channel_id=1, source_target_pairs={{0,64},{16,80},{32,96},{48,112},{64,0},{80,16},{96,32},{112,48},{1... | collective-permute-start | bytes 196616 | tf_op jit(solution)/shard_map/ppermute | solution.py:292
  92.3 5.8 %collective-permute-start.25 = (f32[16,1024]{1,0:T(8,128)S(1)}, f32[16,1024]{1,0:T(8,128)S(1)}, u32[]{:S(2)}, u32[]{:S(2)}) collective-permute-start(f32[16,1024]{1,0:T(8,128)S(1)} %get-tuple-element.81.left_ref), channel_id=1, source_target_pairs={{0,64},{16,80},{32,96},{48,112},{64,0},{80,16},{96,32},{112,48},{1... | collective-permute-start | bytes 196616 | tf_op jit(solution)/shard_map/ppermute | solution.py:292
  98.1 1.3 collective-permute-start.26
  100.7 8.5 %collective-permute-start.27 = (f32[16,1024]{1,0:T(8,128)S(1)}, f32[16,1024]{1,0:T(8,128)S(1)}, u32[]{:S(2)}, u32[]{:S(2)}) collective-permute-start(f32[16,1024]{1,0:T(8,128)S(1)} %shard_map.106.own_ref), channel_id=1, source_target_pairs={{0,192},{16,208},{32,224},{48,240},{64,128},{80,144},{96,160},{112... | collective-permute-start | bytes 196616 | tf_op jit(solution)/shard_map/ppermute | solution.py:292
  110.1 19.1 %all-to-all-start.2 = ((bf16[16,16,1408]{2,1,0:T(8,128)(2,1)}), bf16[16,16,1408]{2,1,0:T(8,128)(2,1)S(1)}, u32[]{:S(2)}, u32[]{:S(2)}) async-start(bf16[16,16,1408]{2,1,0:T(8,128)(2,1)} %shard_map.110), calls=%async_computation.2 | async-start | bytes 1441792 | tf_op jit(solution)/shard_map/all_to_all | solution.py:388
  (5 other events, 110.7 us)

commit v12 on v11

--- a/solution.py
+++ b/solution.py
@@ -161,12 +161,12 @@
     out_ref[...] = update.astype(BF).reshape(16, 16, 1024)
 
 
-def push(update, idx, count):
+def push(update, idx, ancestors):
     high, low = halves(update)
     both = jnp.concatenate([high, low], axis=0)
     blocks = []
     step = 512
-    for a in range(count):
+    for a in ancestors:
         parts = []
         for t in range(1024 // step):
             hit = iota((step, 1024), 0) + (a * 1024 + t * step) == idx
@@ -176,11 +176,11 @@
     return blocks
 
 
-def leaf_update_kernel(place, first_ref, got_ref, idx_ref, next_ref, rest_ref):
+def leaf_update_kernel(ancestors, place, first_ref, got_ref, idx_ref, out_ref):
     update = jnp.zeros((16, 1024), F32)
     for s in range(FRONTS):
         update = update + got_ref[s].astype(F32)
-    pending = push(update, idx_ref[...], 4)
+    pending = push(update, idx_ref[...], ancestors)
     high, low = [], []
     for g in range(FRONTS // 2):
         pair = first_ref[2 * g, 64:, :].astype(F32) + first_ref[2 * g + 1, 64:, :].astype(F32)
@@ -190,16 +190,21 @@
     low = jnp.concatenate(low, axis=1).astype(BF)
     row = iota((16, 16), 0)
     slot = iota((16, 16), 1)
-    for a in range(4):
+    for k, a in enumerate(ancestors):
         width, start = WIDTHS[a], STARTS[a]
         put = (slot >= start) & (slot < start + width)
         put = put & (row == place[4 + a] * width + slot - start)
         put = jnp.where(put, 1.0, 0.0).astype(BF)
-        block = nn(put, high) + nn(put, low) - pending[a]
-        if a == 0:
-            next_ref[...] = block
-        else:
-            rest_ref[(a - 1) * 16 : a * 16, :] = block
+        out_ref[k * 16 : (k + 1) * 16, :] = nn(put, high) + nn(put, low) - pending[k]
+
+
+def leaf_update(place, first, got, idx_leaf, ancestors):
+    return call(
+        functools.partial(leaf_update_kernel, ancestors),
+        jax.ShapeDtypeStruct((16 * len(ancestors), 1024), F32),
+        [SMEM] + [VMEM] * 3,
+        (place, first, got, idx_leaf),
+    )
 
 
 def solve_kernel(own_ref, other_ref, *refs):
@@ -226,28 +231,20 @@
     )
 
 
-def update_kernel(level, place, own_ref, other_ref, left_ref, left_other_ref, idx_ref, *outs):
+def update_kernel(level, ancestors, place, own_ref, other_ref, left_ref, left_other_ref, idx_ref, out_ref):
     update = own_ref[:, :1024] + other_ref[:, :1024]
-    count = left_ref.shape[0] // 16
     idx = idx_ref[pl.ds(place[level] - 2, 1), :]
-    for a, block in enumerate(push(update, idx, count)):
+    for k, (a, block) in enumerate(zip(ancestors, push(update, idx, ancestors))):
         at = slice(a * 16, (a + 1) * 16)
-        block = left_ref[at, :] + left_other_ref[at, :] - block
-        if a == 0:
-            outs[0][...] = block
-        else:
-            outs[1][(a - 1) * 16 : a * 16, :] = block
-
-
-def top_update(level, place, ux, ux_other, left, left_other, idx_top):
-    shapes = [jax.ShapeDtypeStruct((16, 1024), F32)]
-    if left.shape[0] > 16:
-        shapes.append(jax.ShapeDtypeStruct((left.shape[0] - 16, 1024), F32))
+        out_ref[k * 16 : (k + 1) * 16, :] = left_ref[at, :] + left_other_ref[at, :] - block
+
+
+def top_update(level, ancestors, args):
     return call(
-        functools.partial(update_kernel, level),
-        tuple(shapes),
+        functools.partial(update_kernel, level, ancestors),
+        jax.ShapeDtypeStruct((16 * len(ancestors), 1024), F32),
         [SMEM] + [VMEM] * 5,
-        (place, ux, ux_other, left, left_other, idx_top),
+        args,
     )
 
 
@@ -340,15 +337,12 @@
     )
     lowest = stack(pair, 64)
     third_far = far(third_near, "x")
-    state, left = call(
-        leaf_update_kernel,
-        (jax.ShapeDtypeStruct((16, 1024), F32), jax.ShapeDtypeStruct((48, 1024), F32)),
-        [SMEM] + [VMEM] * 3,
-        (place, first, got, idx_leaf),
-    )
+    state = leaf_update(place, first, got, idx_leaf, (0,))
+    left = leaf_update(place, first, got, idx_leaf, (1, 2, 3))
     state, second_near = lax.optimization_barrier((state, second_near))
     second_far = far(second_near, "y")
-    other, left_other = swap(state, core_pairs()), swap(left, core_pairs())
+    other, left = lax.optimization_barrier((swap(state, core_pairs()), left))
+    left_other = swap(left, core_pairs())
     ships = []
     for level in range(3):
         if level == 0:
@@ -364,13 +358,15 @@
         if level > 0:
             ux, left_other = lax.optimization_barrier((ux, left_other))
         ux_other = swap(ux, core_pairs())
-        state, *more = top_update(level, place, ux, ux_other, left, left_other, idx_top)
+        args = (place, ux, ux_other, left, left_other, idx_top)
+        state = top_update(level, (0,), args)
         other = swap(state, chip_pairs(level))
         if level == 0:
             other, lowest_near = lax.optimization_barrier((other, lowest_near))
             lowest_far = far(lowest_near, "x")
-        if more:
-            left, left_other = more[0], swap(more[0], chip_pairs(level))
+        if level < 2:
+            left = top_update(level, tuple(range(1, 3 - level)), args)
+            left_other = swap(left, chip_pairs(level))
         ships.append(
             call(
                 functools.partial(ship_kernel, ("yx", "xy", "yx")[level]),

time: 132 us -> 131 us (level); the launches traced: 130 us -> 131 us
  waiting for transfers between devices: 40.8 us -> 38.7 us
  Pallas kernels: 20.3 us -> 22.3 us
    ppermute x10, waiting for transfers between devices: 14.2 us -> 10.7 us  [swap(): return lax.ppermute(block, 'leaf', pairs)]
    pallas_call x16 -> x19, Pallas kernels: 17 us -> 19 us  [call(): pl.pallas_call(kernel, out_shape=outs, in_specs=specs, out_specs=tuple((V...]
  transfers between devices with their start and end apart: 30 -> 30, of which waited for: 13 -> 14; matrix products, arithmetic and copies ran while one was open for 1% -> 1% of each run, Pallas kernels for 10% -> 11%
where the time goes in v12:
time: 131 us
  starting transfers between devices  51.2 us (39%)
  waiting for transfers between devices  38.7 us (30%)
  Pallas kernels  22.3 us (17%)
  blocking collectives  16.1 us (12%)
  local copies, waits for them, and re-layouts  1.73 us (1%)
    ppermute x18, starting transfers between devices, turn(): return lax.ppermute(block, 'front', route)  27.8 us
    pallas_call x19, Pallas kernels, call(): pl.pallas_call(kernel, out_shape=outs, in_specs=specs, out_specs=tuple((V...  19 us
    all_to_all x1, blocking collectives, local(): got = lax.all_to_all(sent, 'front', 0, 0)  16.1 us
    ppermute x18, waiting for transfers between devices, turn(): return lax.ppermute(block, 'front', route)  15.1 us
    all_to_all x1, waiting for transfers between devices, local(): got = lax.all_to_all(sent, 'front', 0, 0)  12.8 us
    ppermute x10, waiting for transfers between devices, swap(): return lax.ppermute(block, 'leaf', pairs)  10.7 us
    ppermute x10, starting transfers between devices, swap(): return lax.ppermute(block, 'leaf', pairs)  9.32 us
    all_to_all x1, starting transfers between devices, local(): first = lax.all_to_all(sent, 'front', 0, 0)  7.18 us
  transfers between devices with their start and end apart: 30, of which 14 were waited for; matrix products, arithmetic and copies ran while one was open for 1% of the time, Pallas kernels for 11%

profile of v12, /device:TPU:32, one launch (start us, length us, event | category | flops | bytes accessed | tf_op | source)
XLA Modules:
  0.0 130.9 jit_solution(8078062137525565293)
XLA Ops:
  1.3 3.3 %shard_map.95 = (bf16[16,80,256]{2,1,0:T(8,128)(2,1)}, bf16[64,1024]{1,0:T(8,128)(2,1)}, bf16[128,1024]{1,0:T(8,128)(2,1)}) custom-call(s32[12]{0:T(128)} %stack.48.place, f32[1,64,256]{2,1,0:T(8,128)} %leaf_ref.1, f32[15,64,256]{2,1,0:T(8,128)} %rhs_ref.1, bf16[15,64,1024]{2,1,0:T(8,128)(2,1)} %inv_ref.2, bf16[14,64,1024]{2,1,0:T(8,128)(2,1)} %bitcast.46), custom_call_target="tpu_custom_call" | custom-call | tf_op jit(solution)/shard_map/pallas_call | solution.py:101
  4.7 7.2 %all-to-all-start = ((bf16[16,80,256]{2,1,0:T(8,128)(2,1)}), bf16[16,80,256]{2,1,0:T(8,128)(2,1)S(1)}, u32[]{:S(2)}, u32[]{:S(2)}) async-start(bf16[16,80,256]{2,1,0:T(8,128)(2,1)} %get-tuple-element.39), calls=%async_computation | async-start | bytes 1310720 | tf_op jit(solution)/shard_map/all_to_all | solution.py:321
  11.9 1.9 %collective-permute-start.3 = (bf16[64,1024]{1,0:T(8,128)(2,1)}, bf16[64,1024]{1,0:T(8,128)(2,1)S(1)}, u32[]{:S(2)}, u32[]{:S(2)}) collective-permute-start(bf16[64,1024]{1,0:T(8,128)(2,1)} %get-tuple-element.49.refs_0_), channel_id=1, source_target_pairs={{0,4},{1,5},{2,6},{3,7},{4,8},{5,9},{6,10},{7,11},{8,12},{9,13},{1... | collective-permute-start | bytes 393224 | tf_op jit(solution)/shard_map/ppermute | solution.py:131
  13.8 1.5 %collective-permute-start = (bf16[128,1024]{1,0:T(8,128)(2,1)}, bf16[128,1024]{1,0:T(8,128)(2,1)S(1)}, u32[]{:S(2)}, u32[]{:S(2)}) collective-permute-start(bf16[128,1024]{1,0:T(8,128)(2,1)} %get-tuple-element.60.refs_0_), channel_id=1, source_target_pairs={{0,1},{1,2},{2,3},{3,0},{4,5},{5,6},{6,7},{7,4},{8,9},{9,10},{10,1... | collective-permute-start | bytes 786440 | tf_op jit(solution)/shard_map/ppermute | solution.py:131
  15.3 1.8 %collective-permute-start.1 = (bf16[128,1024]{1,0:T(8,128)(2,1)}, bf16[128,1024]{1,0:T(8,128)(2,1)S(1)}, u32[]{:S(2)}, u32[]{:S(2)}) collective-permute-start(bf16[128,1024]{1,0:T(8,128)(2,1)} %get-tuple-element.60.refs_0_), channel_id=1, source_target_pairs={{0,3},{1,0},{2,1},{3,2},{4,7},{5,4},{6,5},{7,6},{8,11},{9,8},{10,9... | collective-permute-start | bytes 786440 | tf_op jit(solution)/shard_map/ppermute | solution.py:131
  17.0 1.8 %collective-permute-start.2 = (bf16[128,1024]{1,0:T(8,128)(2,1)}, bf16[128,1024]{1,0:T(8,128)(2,1)S(1)}, u32[]{:S(2)}, u32[]{:S(2)}) collective-permute-start(bf16[128,1024]{1,0:T(8,128)(2,1)} %get-tuple-element.60.refs_0_), channel_id=1, source_target_pairs={{0,2},{1,3},{2,0},{3,1},{4,6},{5,7},{6,4},{7,5},{8,10},{9,11},{10,... | collective-permute-start | bytes 786440 | tf_op jit(solution)/shard_map/ppermute | solution.py:131
  18.8 1.8 %collective-permute-start.4 = (bf16[64,1024]{1,0:T(8,128)(2,1)}, bf16[64,1024]{1,0:T(8,128)(2,1)S(1)}, u32[]{:S(2)}, u32[]{:S(2)}) collective-permute-start(bf16[64,1024]{1,0:T(8,128)(2,1)} %get-tuple-element.49.refs_0_), channel_id=1, source_target_pairs={{0,12},{1,13},{2,14},{3,15},{4,0},{5,1},{6,2},{7,3},{8,4},{9,5},{1... | collective-permute-start | bytes 393224 | tf_op jit(solution)/shard_map/ppermute | solution.py:131
  20.6 4.6 %collective-permute-done.3.refs_1_ = bf16[64,1024]{1,0:T(8,128)(2,1)S(1)} collective-permute-done((bf16[64,1024]{1,0:T(8,128)(2,1)}, bf16[64,1024]{1,0:T(8,128)(2,1)S(1)}, u32[]{:S(2)}, u32[]{:S(2)}) %collective-permute-start.3) | collective-permute-done | bytes 131104 | tf_op jit(solution)/shard_map/ppermute | solution.py:131
  26.9 4.9 %collective-permute-done.5.refs_3_ = bf16[64,1024]{1,0:T(8,128)(2,1)S(1)} collective-permute-done((bf16[64,1024]{1,0:T(8,128)(2,1)}, bf16[64,1024]{1,0:T(8,128)(2,1)S(1)}, u32[]{:S(2)}, u32[]{:S(2)}) %collective-permute-start.5) | collective-permute-done | bytes 131104 | tf_op jit(solution)/shard_map/ppermute | solution.py:131
  31.9 2.6 %collective-permute-done.2.refs_3_ = bf16[128,1024]{1,0:T(8,128)(2,1)S(1)} collective-permute-done((bf16[128,1024]{1,0:T(8,128)(2,1)}, bf16[128,1024]{1,0:T(8,128)(2,1)S(1)}, u32[]{:S(2)}, u32[]{:S(2)}) %collective-permute-start.2) | collective-permute-done | bytes 262176 | tf_op jit(solution)/shard_map/ppermute | solution.py:131
  35.6 2.2 %collective-permute-start.7 = (bf16[256,1024]{1,0:T(8,128)(2,1)S(1)}, bf16[256,1024]{1,0:T(8,128)(2,1)S(1)}, u32[]{:S(2)}, u32[]{:S(2)}) collective-permute-start(bf16[256,1024]{1,0:T(8,128)(2,1)S(1)} %shard_map.97), channel_id=1, source_target_pairs={{0,12},{1,13},{2,14},{3,15},{4,0},{5,1},{6,2},{7,3},{8,4},{9,5},{1... | collective-permute-start | bytes 1572872 | tf_op jit(solution)/shard_map/ppermute | solution.py:131
  38.5 2.7 %collective-permute-start.9 = (bf16[256,1024]{1,0:T(8,128)(2,1)S(1)}, bf16[256,1024]{1,0:T(8,128)(2,1)S(1)}, u32[]{:S(2)}, u32[]{:S(2)}) collective-permute-start(bf16[256,1024]{1,0:T(8,128)(2,1)S(1)} %shard_map.98), channel_id=1, source_target_pairs={{0,3},{1,0},{2,1},{3,2},{4,7},{5,4},{6,5},{7,6},{8,11},{9,8},{10,9... | collective-permute-start | bytes 1572872 | tf_op jit(solution)/shard_map/ppermute | solution.py:131
  41.2 16.1 %all_to_all.15.got_ref = bf16[16,16,1024]{2,1,0:T(8,128)(2,1)S(1)} all-to-all(bf16[16,16,1024]{2,1,0:T(8,128)(2,1)S(1)} %get-tuple-element.44), channel_id=1, replica_groups=mesh['leaf'=16,'front'=16] {'front'}, dimensions={0} | all-to-all | bytes 1048576 | tf_op jit(solution)/shard_map/all_to_all | solution.py:332
  59.5 1.3 shard_map.99.own_ref
  61.1 2.5 %shard_map.100.left_ref = f32[48,1024]{1,0:T(8,128)S(1)} custom-call(s32[12]{0:T(128)S(1)} %copy-done.5, bf16[16,80,256]{2,1,0:T(8,128)(2,1)S(1)} %all-to-all-done.rhs_ref.first_ref, bf16[16,16,1024]{2,1,0:T(8,128)(2,1)S(1)} %all_to_all.15.got_ref, s32[1,1024]{1,0:T(1,128)S(1)} %copy-done.6), custom_call_target="tpu_custom_call" | custom-call | flops 100000000 | bytes 1000000 | tf_op jit(solution)/shard_map/pallas_call | solution.py:46
  63.8 2.4 %collective-permute-done.12 = bf16[128,1024]{1,0:T(8,128)(2,1)S(1)} collective-permute-done((bf16[128,1024]{1,0:T(8,128)(2,1)S(1)}, bf16[128,1024]{1,0:T(8,128)(2,1)S(1)}, u32[]{:S(2)}, u32[]{:S(2)}) %collective-permute-start.12) | collective-permute-done | bytes 262176 | tf_op jit(solution)/shard_map/ppermute | solution.py:131
  67.3 3.2 %collective-permute-start.17 = (bf16[256,1024]{1,0:T(8,128)(2,1)S(1)}, bf16[256,1024]{1,0:T(8,128)(2,1)S(1)}, u32[]{:S(2)}, u32[]{:S(2)}) collective-permute-start(bf16[256,1024]{1,0:T(8,128)(2,1)S(1)} %shard_map.102), channel_id=1, source_target_pairs={{0,12},{1,13},{2,14},{3,15},{4,0},{5,1},{6,2},{7,3},{8,4},{9,5},{1... | collective-permute-start | bytes 1572872 | tf_op jit(solution)/shard_map/ppermute | solution.py:131
  71.1 3.0 %collective-permute-start.18 = (bf16[128,1024]{1,0:T(8,128)(2,1)S(1)}, bf16[128,1024]{1,0:T(8,128)(2,1)S(1)}, u32[]{:S(2)}, u32[]{:S(2)}) collective-permute-start(bf16[128,1024]{1,0:T(8,128)(2,1)S(1)} %slice.23), channel_id=1, source_target_pairs={{0,3},{1,0},{2,1},{3,2},{4,7},{5,4},{6,5},{7,6},{8,11},{9,8},{10,9... | collective-permute-start | bytes 786440 | tf_op jit(solution)/shard_map/ppermute | solution.py:131
  74.2 1.2 shard_map.103.own_ref
  75.6 1.8 %shard_map.105.left_ref = f32[32,1024]{1,0:T(8,128)S(1)} custom-call(s32[12]{0:T(128)S(1)} %copy-done.5, f32[16,1536]{1,0:T(8,128)S(1)} %shard_map.101.own_ref, f32[16,1536]{1,0:T(8,128)S(1)} %collective-permute-done.13.other_ref, f32[48,1024]{1,0:T(8,128)S(1)} %shard_map.100.left_ref, f32[48,1024]{1,0:T(8,128)S(1)} %collective-permute-done.14.left_other_ref, ...), custom_call_target="tpu_custom_call" | custom-call | flops 100000000 | bytes 1000000 | tf_op jit(solution)/shard_map/pallas_call | solution.py:46
  77.5 2.3 %collective-permute-done.15.other_ref = f32[16,1024]{1,0:T(8,128)S(1)} collective-permute-done((f32[16,1024]{1,0:T(8,128)S(1)}, f32[16,1024]{1,0:T(8,128)S(1)}, u32[]{:S(2)}, u32[]{:S(2)}) %collective-permute-start.15) | collective-permute-done | bytes 65568 | tf_op jit(solution)/shard_map/ppermute | solution.py:289
  80.3 3.0 %collective-permute-start.23 = (bf16[128,1024]{1,0:T(8,128)(2,1)S(1)}, bf16[128,1024]{1,0:T(8,128)(2,1)S(1)}, u32[]{:S(2)}, u32[]{:S(2)}) collective-permute-start(bf16[128,1024]{1,0:T(8,128)(2,1)S(1)} %slice.25), channel_id=1, source_target_pairs={{0,12},{1,13},{2,14},{3,15},{4,0},{5,1},{6,2},{7,3},{8,4},{9,5},{1... | collective-permute-start | bytes 786440 | tf_op jit(solution)/shard_map/ppermute | solution.py:131
  84.7 1.3 collective-permute-done.21.other_ref
  86.0 1.2 shard_map.106.own_ref
  87.3 3.3 %collective-permute-start.22 = (f32[16,1024]{1,0:T(8,128)S(1)}, f32[16,1024]{1,0:T(8,128)S(1)}, u32[]{:S(2)}, u32[]{:S(2)}) collective-permute-start(f32[16,1024]{1,0:T(8,128)S(1)} %shard_map.106.own_ref), channel_id=1, source_target_pairs={{0,64},{16,80},{32,96},{48,112},{64,0},{80,16},{96,32},{112,48},{1... | collective-permute-start | bytes 196616 | tf_op jit(solution)/shard_map/ppermute | solution.py:289
  92.0 3.0 %collective-permute-done.22.other_ref = f32[16,1024]{1,0:T(8,128)S(1)} collective-permute-done((f32[16,1024]{1,0:T(8,128)S(1)}, f32[16,1024]{1,0:T(8,128)S(1)}, u32[]{:S(2)}, u32[]{:S(2)}) %collective-permute-start.22) | collective-permute-done | bytes 65568 | tf_op jit(solution)/shard_map/ppermute | solution.py:289
  97.2 1.3 collective-permute-done.26.other_ref
  98.5 1.2 shard_map.109.own_ref
  99.7 4.8 %collective-permute-start.27 = (f32[16,1024]{1,0:T(8,128)S(1)}, f32[16,1024]{1,0:T(8,128)S(1)}, u32[]{:S(2)}, u32[]{:S(2)}) collective-permute-start(f32[16,1024]{1,0:T(8,128)S(1)} %shard_map.109.own_ref), channel_id=1, source_target_pairs={{0,192},{16,208},{32,224},{48,240},{64,128},{80,144},{96,160},{112... | collective-permute-start | bytes 196616 | tf_op jit(solution)/shard_map/ppermute | solution.py:289
  106.7 1.6 %collective-permute-done.27.other_ref = f32[16,1024]{1,0:T(8,128)S(1)} collective-permute-done((f32[16,1024]{1,0:T(8,128)S(1)}, f32[16,1024]{1,0:T(8,128)S(1)}, u32[]{:S(2)}, u32[]{:S(2)}) %collective-permute-start.27) | collective-permute-done | bytes 65568 | tf_op jit(solution)/shard_map/ppermute | solution.py:289
  109.3 6.9 %all-to-all-start.2 = ((bf16[16,16,1408]{2,1,0:T(8,128)(2,1)}), bf16[16,16,1408]{2,1,0:T(8,128)(2,1)S(1)}, u32[]{:S(2)}, u32[]{:S(2)}) async-start(bf16[16,16,1408]{2,1,0:T(8,128)(2,1)} %shard_map.113), calls=%async_computation.2 | async-start | bytes 1441792 | tf_op jit(solution)/shard_map/all_to_all | solution.py:384
  117.1 12.8 %all-to-all-done.2.got_ref = bf16[16,16,1408]{2,1,0:T(8,128)(2,1)S(1)} async-done(((bf16[16,16,1408]{2,1,0:T(8,128)(2,1)}), bf16[16,16,1408]{2,1,0:T(8,128)(2,1)S(1)}, u32[]{:S(2)}, u32[]{:S(2)}) %all-to-all-start.2) | async-done | bytes 720928 | tf_op jit(solution)/shard_map/all_to_all | solution.py:384
  (71 shorter events, 19.3 us)
Async XLA Ops:
  4.7 29.8 %copy-start.1 = (bf16[128,1024]{1,0:T(8,128)(2,1)S(1)}, bf16[128,1024]{1,0:T(8,128)(2,1)}, u32[]{:S(2)}) copy-start(bf16[128,1024]{1,0:T(8,128)(2,1)} %get-tuple-element.60.refs_0_) | copy-start | bytes 786436
  4.7 33.1 %copy-start.4 = (bf16[64,1024]{1,0:T(8,128)(2,1)S(1)}, bf16[64,1024]{1,0:T(8,128)(2,1)}, u32[]{:S(2)}) copy-start(bf16[64,1024]{1,0:T(8,128)(2,1)} %get-tuple-element.49.refs_0_) | copy-start | bytes 393220
  4.7 21.3 %all-to-all-start = ((bf16[16,80,256]{2,1,0:T(8,128)(2,1)}), bf16[16,80,256]{2,1,0:T(8,128)(2,1)S(1)}, u32[]{:S(2)}, u32[]{:S(2)}) async-start(bf16[16,80,256]{2,1,0:T(8,128)(2,1)} %get-tuple-element.39), calls=%async_computation | async-start | bytes 1310720 | tf_op jit(solution)/shard_map/all_to_all | solution.py:321
  11.9 13.3 %collective-permute-start.3 = (bf16[64,1024]{1,0:T(8,128)(2,1)}, bf16[64,1024]{1,0:T(8,128)(2,1)S(1)}, u32[]{:S(2)}, u32[]{:S(2)}) collective-permute-start(bf16[64,1024]{1,0:T(8,128)(2,1)} %get-tuple-element.49.refs_0_), channel_id=1, source_target_pairs={{0,4},{1,5},{2,6},{3,7},{4,8},{5,9},{6,10},{7,11},{8,12},{9,13},{1... | collective-permute-start | bytes 393224 | tf_op jit(solution)/shard_map/ppermute | solution.py:131
  13.8 18.1 %collective-permute-start = (bf16[128,1024]{1,0:T(8,128)(2,1)}, bf16[128,1024]{1,0:T(8,128)(2,1)S(1)}, u32[]{:S(2)}, u32[]{:S(2)}) collective-permute-start(bf16[128,1024]{1,0:T(8,128)(2,1)} %get-tuple-element.60.refs_0_), channel_id=1, source_target_pairs={{0,1},{1,2},{2,3},{3,0},{4,5},{5,6},{6,7},{7,4},{8,9},{9,10},{10,1... | collective-permute-start | bytes 786440 | tf_op jit(solution)/shard_map/ppermute | solution.py:131
  15.3 16.6 %collective-permute-start.1 = (bf16[128,1024]{1,0:T(8,128)(2,1)}, bf16[128,1024]{1,0:T(8,128)(2,1)S(1)}, u32[]{:S(2)}, u32[]{:S(2)}) collective-permute-start(bf16[128,1024]{1,0:T(8,128)(2,1)} %get-tuple-element.60.refs_0_), channel_id=1, source_target_pairs={{0,3},{1,0},{2,1},{3,2},{4,7},{5,4},{6,5},{7,6},{8,11},{9,8},{10,9... | collective-permute-start | bytes 786440 | tf_op jit(solution)/shard_map/ppermute | solution.py:131
  17.0 17.4 %collective-permute-start.2 = (bf16[128,1024]{1,0:T(8,128)(2,1)}, bf16[128,1024]{1,0:T(8,128)(2,1)S(1)}, u32[]{:S(2)}, u32[]{:S(2)}) collective-permute-start(bf16[128,1024]{1,0:T(8,128)(2,1)} %get-tuple-element.60.refs_0_), channel_id=1, source_target_pairs={{0,2},{1,3},{2,0},{3,1},{4,6},{5,7},{6,4},{7,5},{8,10},{9,11},{10,... | collective-permute-start | bytes 786440 | tf_op jit(solution)/shard_map/ppermute | solution.py:131
  18.8 8.1 %collective-permute-start.4 = (bf16[64,1024]{1,0:T(8,128)(2,1)}, bf16[64,1024]{1,0:T(8,128)(2,1)S(1)}, u32[]{:S(2)}, u32[]{:S(2)}) collective-permute-start(bf16[64,1024]{1,0:T(8,128)(2,1)} %get-tuple-element.49.refs_0_), channel_id=1, source_target_pairs={{0,12},{1,13},{2,14},{3,15},{4,0},{5,1},{6,2},{7,3},{8,4},{9,5},{1... | collective-permute-start | bytes 393224 | tf_op jit(solution)/shard_map/ppermute | solution.py:131
  25.2 6.7 %collective-permute-start.5 = (bf16[64,1024]{1,0:T(8,128)(2,1)}, bf16[64,1024]{1,0:T(8,128)(2,1)S(1)}, u32[]{:S(2)}, u32[]{:S(2)}) collective-permute-start(bf16[64,1024]{1,0:T(8,128)(2,1)} %get-tuple-element.49.refs_0_), channel_id=1, source_target_pairs={{0,8},{1,9},{2,10},{3,11},{4,12},{5,13},{6,14},{7,15},{8,0},{9,1},... | collective-permute-start | bytes 393224 | tf_op jit(solution)/shard_map/ppermute | solution.py:131
  34.5 22.8 %collective-permute-start.6 = (bf16[256,1024]{1,0:T(8,128)(2,1)S(1)}, bf16[256,1024]{1,0:T(8,128)(2,1)S(1)}, u32[]{:S(2)}, u32[]{:S(2)}) collective-permute-start(bf16[256,1024]{1,0:T(8,128)(2,1)S(1)} %shard_map.97), channel_id=1, source_target_pairs={{0,4},{1,5},{2,6},{3,7},{4,8},{5,9},{6,10},{7,11},{8,12},{9,13},{1... | collective-permute-start | bytes 1572872 | tf_op jit(solution)/shard_map/ppermute | solution.py:131
  35.6 21.7 %collective-permute-start.7 = (bf16[256,1024]{1,0:T(8,128)(2,1)S(1)}, bf16[256,1024]{1,0:T(8,128)(2,1)S(1)}, u32[]{:S(2)}, u32[]{:S(2)}) collective-permute-start(bf16[256,1024]{1,0:T(8,128)(2,1)S(1)} %shard_map.97), channel_id=1, source_target_pairs={{0,12},{1,13},{2,14},{3,15},{4,0},{5,1},{6,2},{7,3},{8,4},{9,5},{1... | collective-permute-start | bytes 1572872 | tf_op jit(solution)/shard_map/ppermute | solution.py:131
  37.8 19.4 %collective-permute-start.8 = (bf16[256,1024]{1,0:T(8,128)(2,1)S(1)}, bf16[256,1024]{1,0:T(8,128)(2,1)S(1)}, u32[]{:S(2)}, u32[]{:S(2)}) collective-permute-start(bf16[256,1024]{1,0:T(8,128)(2,1)S(1)} %shard_map.98), channel_id=1, source_target_pairs={{0,1},{1,2},{2,3},{3,0},{4,5},{5,6},{6,7},{7,4},{8,9},{9,10},{10,1... | collective-permute-start | bytes 1572872 | tf_op jit(solution)/shard_map/ppermute | solution.py:131
  38.5 18.8 %collective-permute-start.9 = (bf16[256,1024]{1,0:T(8,128)(2,1)S(1)}, bf16[256,1024]{1,0:T(8,128)(2,1)S(1)}, u32[]{:S(2)}, u32[]{:S(2)}) collective-permute-start(bf16[256,1024]{1,0:T(8,128)(2,1)S(1)} %shard_map.98), channel_id=1, source_target_pairs={{0,3},{1,0},{2,1},{3,2},{4,7},{5,4},{6,5},{7,6},{8,11},{9,8},{10,9... | collective-permute-start | bytes 1572872 | tf_op jit(solution)/shard_map/ppermute | solution.py:131
  57.3 6.4 %collective-permute-start.11 = (bf16[128,1024]{1,0:T(8,128)(2,1)S(1)}, bf16[128,1024]{1,0:T(8,128)(2,1)S(1)}, u32[]{:S(2)}, u32[]{:S(2)}) collective-permute-start(bf16[128,1024]{1,0:T(8,128)(2,1)S(1)} %slice.21), channel_id=1, source_target_pairs={{0,12},{1,13},{2,14},{3,15},{4,0},{5,1},{6,2},{7,3},{8,4},{9,5},{1... | collective-permute-start | bytes 786440 | tf_op jit(solution)/shard_map/ppermute | solution.py:131
  58.6 7.7 %collective-permute-start.12 = (bf16[128,1024]{1,0:T(8,128)(2,1)S(1)}, bf16[128,1024]{1,0:T(8,128)(2,1)S(1)}, u32[]{:S(2)}, u32[]{:S(2)}) collective-permute-start(bf16[128,1024]{1,0:T(8,128)(2,1)S(1)} %slice.22), channel_id=1, source_target_pairs={{0,4},{1,5},{2,6},{3,7},{4,8},{5,9},{6,10},{7,11},{8,12},{9,13},{1... | collective-permute-start | bytes 786440 | tf_op jit(solution)/shard_map/ppermute | solution.py:131
  60.8 2.9 %collective-permute-start.10 = (f32[16,1024]{1,0:T(8,128)S(1)}, f32[16,1024]{1,0:T(8,128)S(1)}, u32[]{:S(2)}, u32[]{:S(2)}) collective-permute-start(f32[16,1024]{1,0:T(8,128)S(1)} %shard_map.99.own_ref), channel_id=1, source_target_pairs={{0,16},{16,0},{32,48},{48,32},{64,80},{80,64},{96,112},{112,96},{1... | collective-permute-start | bytes 196616 | tf_op jit(solution)/shard_map/ppermute | solution.py:289
  67.3 13.0 %collective-permute-start.16 = (bf16[256,1024]{1,0:T(8,128)(2,1)S(1)}, bf16[256,1024]{1,0:T(8,128)(2,1)S(1)}, u32[]{:S(2)}, u32[]{:S(2)}) collective-permute-start(bf16[256,1024]{1,0:T(8,128)(2,1)S(1)} %shard_map.102), channel_id=1, source_target_pairs={{0,4},{1,5},{2,6},{3,7},{4,8},{5,9},{6,10},{7,11},{8,12},{9,13},{1... | collective-permute-start | bytes 1572872 | tf_op jit(solution)/shard_map/ppermute | solution.py:131
  67.3 13.0 %collective-permute-start.17 = (bf16[256,1024]{1,0:T(8,128)(2,1)S(1)}, bf16[256,1024]{1,0:T(8,128)(2,1)S(1)}, u32[]{:S(2)}, u32[]{:S(2)}) collective-permute-start(bf16[256,1024]{1,0:T(8,128)(2,1)S(1)} %shard_map.102), channel_id=1, source_target_pairs={{0,12},{1,13},{2,14},{3,15},{4,0},{5,1},{6,2},{7,3},{8,4},{9,5},{1... | collective-permute-start | bytes 1572872 | tf_op jit(solution)/shard_map/ppermute | solution.py:131
  70.5 3.6 %collective-permute-start.14 = (f32[48,1024]{1,0:T(8,128)S(1)}, f32[48,1024]{1,0:T(8,128)S(1)}, u32[]{:S(2)}, u32[]{:S(2)}) collective-permute-start(f32[48,1024]{1,0:T(8,128)S(1)} %shard_map.100.left_ref), channel_id=1, source_target_pairs={{0,16},{16,0},{32,48},{48,32},{64,80},{80,64},{96,112},{112,96},{1... | collective-permute-start | bytes 589832 | tf_op jit(solution)/shard_map/ppermute | solution.py:289
  70.5 3.7 %collective-permute-start.13 = (f32[16,1536]{1,0:T(8,128)S(1)}, f32[16,1536]{1,0:T(8,128)S(1)}, u32[]{:S(2)}, u32[]{:S(2)}) collective-permute-start(f32[16,1536]{1,0:T(8,128)S(1)} %shard_map.101.own_ref), channel_id=1, source_target_pairs={{0,16},{16,0},{32,48},{48,32},{64,80},{80,64},{96,112},{112,96},{1... | collective-permute-start | bytes 294920 | tf_op jit(solution)/shard_map/ppermute | solution.py:289
  71.1 12.4 %collective-permute-start.18 = (bf16[128,1024]{1,0:T(8,128)(2,1)S(1)}, bf16[128,1024]{1,0:T(8,128)(2,1)S(1)}, u32[]{:S(2)}, u32[]{:S(2)}) collective-permute-start(bf16[128,1024]{1,0:T(8,128)(2,1)S(1)} %slice.23), channel_id=1, source_target_pairs={{0,3},{1,0},{2,1},{3,2},{4,7},{5,4},{6,5},{7,6},{8,11},{9,8},{10,9... | collective-permute-start | bytes 786440 | tf_op jit(solution)/shard_map/ppermute | solution.py:131
  74.1 9.4 %collective-permute-start.19 = (bf16[128,1024]{1,0:T(8,128)(2,1)S(1)}, bf16[128,1024]{1,0:T(8,128)(2,1)S(1)}, u32[]{:S(2)}, u32[]{:S(2)}) collective-permute-start(bf16[128,1024]{1,0:T(8,128)(2,1)S(1)} %slice.24), channel_id=1, source_target_pairs={{0,1},{1,2},{2,3},{3,0},{4,5},{5,6},{6,7},{7,4},{8,9},{9,10},{10,1... | collective-permute-start | bytes 786440 | tf_op jit(solution)/shard_map/ppermute | solution.py:131
  75.5 4.3 %collective-permute-start.15 = (f32[16,1024]{1,0:T(8,128)S(1)}, f32[16,1024]{1,0:T(8,128)S(1)}, u32[]{:S(2)}, u32[]{:S(2)}) collective-permute-start(f32[16,1024]{1,0:T(8,128)S(1)} %shard_map.103.own_ref), channel_id=1, source_target_pairs={{0,32},{16,48},{32,0},{48,16},{64,96},{80,112},{96,64},{112,80},{1... | collective-permute-start | bytes 196616 | tf_op jit(solution)/shard_map/ppermute | solution.py:289
  79.8 5.0 %collective-permute-start.20 = (f32[32,1024]{1,0:T(8,128)S(1)}, f32[32,1024]{1,0:T(8,128)S(1)}, u32[]{:S(2)}, u32[]{:S(2)}) collective-permute-start(f32[32,1024]{1,0:T(8,128)S(1)} %shard_map.105.left_ref), channel_id=1, source_target_pairs={{0,32},{16,48},{32,0},{48,16},{64,96},{80,112},{96,64},{112,80},{1... | collective-permute-start | bytes 393224 | tf_op jit(solution)/shard_map/ppermute | solution.py:289
  80.3 14.7 %collective-permute-start.23 = (bf16[128,1024]{1,0:T(8,128)(2,1)S(1)}, bf16[128,1024]{1,0:T(8,128)(2,1)S(1)}, u32[]{:S(2)}, u32[]{:S(2)}) collective-permute-start(bf16[128,1024]{1,0:T(8,128)(2,1)S(1)} %slice.25), channel_id=1, source_target_pairs={{0,12},{1,13},{2,14},{3,15},{4,0},{5,1},{6,2},{7,3},{8,4},{9,5},{1... | collective-permute-start | bytes 786440 | tf_op jit(solution)/shard_map/ppermute | solution.py:131
  83.4 11.7 %collective-permute-start.24 = (bf16[128,1024]{1,0:T(8,128)(2,1)S(1)}, bf16[128,1024]{1,0:T(8,128)(2,1)S(1)}, u32[]{:S(2)}, u32[]{:S(2)}) collective-permute-start(bf16[128,1024]{1,0:T(8,128)(2,1)S(1)} %slice.26), channel_id=1, source_target_pairs={{0,4},{1,5},{2,6},{3,7},{4,8},{5,9},{6,10},{7,11},{8,12},{9,13},{1... | collective-permute-start | bytes 786440 | tf_op jit(solution)/shard_map/ppermute | solution.py:131
  84.7 1.3 collective-permute-start.21
  87.3 7.8 %collective-permute-start.22 = (f32[16,1024]{1,0:T(8,128)S(1)}, f32[16,1024]{1,0:T(8,128)S(1)}, u32[]{:S(2)}, u32[]{:S(2)}) collective-permute-start(f32[16,1024]{1,0:T(8,128)S(1)} %shard_map.106.own_ref), channel_id=1, source_target_pairs={{0,64},{16,80},{32,96},{48,112},{64,0},{80,16},{96,32},{112,48},{1... | collective-permute-start | bytes 196616 | tf_op jit(solution)/shard_map/ppermute | solution.py:289
  91.8 5.4 %collective-permute-start.25 = (f32[16,1024]{1,0:T(8,128)S(1)}, f32[16,1024]{1,0:T(8,128)S(1)}, u32[]{:S(2)}, u32[]{:S(2)}) collective-permute-start(f32[16,1024]{1,0:T(8,128)S(1)} %shard_map.108.left_ref), channel_id=1, source_target_pairs={{0,64},{16,80},{32,96},{48,112},{64,0},{80,16},{96,32},{112,48},{1... | collective-permute-start | bytes 196616 | tf_op jit(solution)/shard_map/ppermute | solution.py:289
  97.2 1.3 collective-permute-start.26
  99.7 8.6 %collective-permute-start.27 = (f32[16,1024]{1,0:T(8,128)S(1)}, f32[16,1024]{1,0:T(8,128)S(1)}, u32[]{:S(2)}, u32[]{:S(2)}) collective-permute-start(f32[16,1024]{1,0:T(8,128)S(1)} %shard_map.109.own_ref), channel_id=1, source_target_pairs={{0,192},{16,208},{32,224},{48,240},{64,128},{80,144},{96,160},{112... | collective-permute-start | bytes 196616 | tf_op jit(solution)/shard_map/ppermute | solution.py:289
  109.3 20.7 %all-to-all-start.2 = ((bf16[16,16,1408]{2,1,0:T(8,128)(2,1)}), bf16[16,16,1408]{2,1,0:T(8,128)(2,1)S(1)}, u32[]{:S(2)}, u32[]{:S(2)}) async-start(bf16[16,16,1408]{2,1,0:T(8,128)(2,1)} %shard_map.113), calls=%async_computation.2 | async-start | bytes 1441792 | tf_op jit(solution)/shard_map/all_to_all | solution.py:384
  (5 other events, 110.1 us)

commit v13 on v11

--- a/solution.py
+++ b/solution.py
@@ -334,10 +334,9 @@
     sent, pair, second = lax.optimization_barrier((sent, pair, second))
     got = lax.all_to_all(sent, "front", 0, 0)
     third, second = stack(pair, 0), stack(second, 0)
-    third_near, second_near = near(third, "x"), near(second, "y")
-    got, third_near, second_near, pair = lax.optimization_barrier(
-        (got, third_near, second_near, pair)
-    )
+    third_near = near(third, "x")
+    got, third_near, second, pair = lax.optimization_barrier((got, third_near, second, pair))
+    second_near = near(second, "y")
     lowest = stack(pair, 64)
     third_far = far(third_near, "x")
     state, left = call(
@@ -346,7 +345,6 @@
         [SMEM] + [VMEM] * 3,
         (place, first, got, idx_leaf),
     )
-    state, second_near = lax.optimization_barrier((state, second_near))
     second_far = far(second_near, "y")
     other, left_other = swap(state, core_pairs()), swap(left, core_pairs())
     ships = []

time: 132 us -> 133 us (level)
  blocking collectives: 16.1 us -> 0 us
  waiting for transfers between devices: 40.8 us -> 49.4 us
  local copies, waits for them, and re-layouts: 1.73 us -> 7.31 us
  starting transfers between devices: 50.4 us -> 53.7 us
    all_to_all x1 -> x0, blocking collectives: 16.1 us -> none  [local(): got = lax.all_to_all(sent, 'front', 0, 0)]
    all_to_all x1 -> x2, waiting for transfers between devices: 12.5 us -> 22.6 us  [local(): got = lax.all_to_all(sent, 'front', 0, 0)]
    unnamed x14 -> x40, local copies, waits for them, and re-layouts: 0.03 us -> 5.67 us
    all_to_all x1 -> x2, starting transfers between devices: 5.65 us -> 9.81 us  [local(): got = lax.all_to_all(sent, 'front', 0, 0)]
  transfers between devices with their start and end apart: 30 -> 31, of which waited for: 13 -> 15; matrix products, arithmetic and copies ran while one was open for 1% -> 1% of each run, Pallas kernels for 10% -> 10%
where the time goes in v13:
time: 133 us; the launch traced here: 132 us
  starting transfers between devices  53.7 us (40%)
  waiting for transfers between devices  49.4 us (37%)
  Pallas kernels  20.3 us (15%)
  local copies, waits for them, and re-layouts  7.31 us (5%)
    ppermute x18, starting transfers between devices, turn(): return lax.ppermute(block, 'front', route)  26.5 us
    all_to_all x2, waiting for transfers between devices, local(): got = lax.all_to_all(sent, 'front', 0, 0)  22.6 us
    pallas_call x16, Pallas kernels, call(): pl.pallas_call(kernel, out_shape=outs, in_specs=specs, out_specs=tuple((V...  17 us
    ppermute x10, waiting for transfers between devices, swap(): return lax.ppermute(block, 'leaf', pairs)  13.9 us
    ppermute x18, waiting for transfers between devices, turn(): return lax.ppermute(block, 'front', route)  12.9 us
    ppermute x10, starting transfers between devices, swap(): return lax.ppermute(block, 'leaf', pairs)  10.2 us
    all_to_all x2, starting transfers between devices, local(): got = lax.all_to_all(sent, 'front', 0, 0)  9.81 us
    all_to_all x1, starting transfers between devices, local(): first = lax.all_to_all(sent, 'front', 0, 0)  7.18 us
  transfers between devices with their start and end apart: 31, of which 15 were waited for; matrix products, arithmetic and copies ran while one was open for 1% of the time, Pallas kernels for 10%

profile of v13, /device:TPU:32, one launch (start us, length us, event | category | flops | bytes accessed | tf_op | source)
XLA Modules:
  0.0 131.7 jit_solution(1152495131766708086)
XLA Ops:
  1.3 3.3 %shard_map.95 = (bf16[16,80,256]{2,1,0:T(8,128)(2,1)}, bf16[64,1024]{1,0:T(8,128)(2,1)}, bf16[128,1024]{1,0:T(8,128)(2,1)}) custom-call(s32[12]{0:T(128)} %stack.48.place, f32[1,64,256]{2,1,0:T(8,128)} %leaf_ref.1, f32[15,64,256]{2,1,0:T(8,128)} %rhs_ref.1, bf16[15,64,1024]{2,1,0:T(8,128)(2,1)} %inv_ref.2, bf16[14,64,1024]{2,1,0:T(8,128)(2,1)} %bitcast.46), custom_call_target="tpu_custom_call" | custom-call | tf_op jit(solution)/shard_map/pallas_call | solution.py:101
  4.6 7.2 %all-to-all-start = ((bf16[16,80,256]{2,1,0:T(8,128)(2,1)}), bf16[16,80,256]{2,1,0:T(8,128)(2,1)S(1)}, u32[]{:S(2)}, u32[]{:S(2)}) async-start(bf16[16,80,256]{2,1,0:T(8,128)(2,1)} %get-tuple-element.39), calls=%async_computation | async-start | bytes 1310720 | tf_op jit(solution)/shard_map/all_to_all | solution.py:324
  11.8 1.9 %collective-permute-start.3 = (bf16[64,1024]{1,0:T(8,128)(2,1)}, bf16[64,1024]{1,0:T(8,128)(2,1)S(1)}, u32[]{:S(2)}, u32[]{:S(2)}) collective-permute-start(bf16[64,1024]{1,0:T(8,128)(2,1)} %get-tuple-element.49.refs_0_), channel_id=1, source_target_pairs={{0,4},{1,5},{2,6},{3,7},{4,8},{5,9},{6,10},{7,11},{8,12},{9,13},{1... | collective-permute-start | bytes 393224 | tf_op jit(solution)/shard_map/ppermute | solution.py:131
  13.7 1.5 %collective-permute-start = (bf16[128,1024]{1,0:T(8,128)(2,1)}, bf16[128,1024]{1,0:T(8,128)(2,1)S(1)}, u32[]{:S(2)}, u32[]{:S(2)}) collective-permute-start(bf16[128,1024]{1,0:T(8,128)(2,1)} %get-tuple-element.57.refs_0_), channel_id=1, source_target_pairs={{0,1},{1,2},{2,3},{3,0},{4,5},{5,6},{6,7},{7,4},{8,9},{9,10},{10,1... | collective-permute-start | bytes 786440 | tf_op jit(solution)/shard_map/ppermute | solution.py:131
  15.2 1.8 %collective-permute-start.1 = (bf16[128,1024]{1,0:T(8,128)(2,1)}, bf16[128,1024]{1,0:T(8,128)(2,1)S(1)}, u32[]{:S(2)}, u32[]{:S(2)}) collective-permute-start(bf16[128,1024]{1,0:T(8,128)(2,1)} %get-tuple-element.57.refs_0_), channel_id=1, source_target_pairs={{0,3},{1,0},{2,1},{3,2},{4,7},{5,4},{6,5},{7,6},{8,11},{9,8},{10,9... | collective-permute-start | bytes 786440 | tf_op jit(solution)/shard_map/ppermute | solution.py:131
  17.0 1.8 %collective-permute-start.2 = (bf16[128,1024]{1,0:T(8,128)(2,1)}, bf16[128,1024]{1,0:T(8,128)(2,1)S(1)}, u32[]{:S(2)}, u32[]{:S(2)}) collective-permute-start(bf16[128,1024]{1,0:T(8,128)(2,1)} %get-tuple-element.57.refs_0_), channel_id=1, source_target_pairs={{0,2},{1,3},{2,0},{3,1},{4,6},{5,7},{6,4},{7,5},{8,10},{9,11},{10,... | collective-permute-start | bytes 786440 | tf_op jit(solution)/shard_map/ppermute | solution.py:131
  18.7 1.8 %collective-permute-start.4 = (bf16[64,1024]{1,0:T(8,128)(2,1)}, bf16[64,1024]{1,0:T(8,128)(2,1)S(1)}, u32[]{:S(2)}, u32[]{:S(2)}) collective-permute-start(bf16[64,1024]{1,0:T(8,128)(2,1)} %get-tuple-element.49.refs_0_), channel_id=1, source_target_pairs={{0,12},{1,13},{2,14},{3,15},{4,0},{5,1},{6,2},{7,3},{8,4},{9,5},{1... | collective-permute-start | bytes 393224 | tf_op jit(solution)/shard_map/ppermute | solution.py:131
  20.5 4.6 %collective-permute-done.3.refs_1_ = bf16[64,1024]{1,0:T(8,128)(2,1)S(1)} collective-permute-done((bf16[64,1024]{1,0:T(8,128)(2,1)}, bf16[64,1024]{1,0:T(8,128)(2,1)S(1)}, u32[]{:S(2)}, u32[]{:S(2)}) %collective-permute-start.3) | collective-permute-done | bytes 131104 | tf_op jit(solution)/shard_map/ppermute | solution.py:131
  28.2 4.2 %collective-permute-done.5.refs_3_ = bf16[64,1024]{1,0:T(8,128)(2,1)S(1)} collective-permute-done((bf16[64,1024]{1,0:T(8,128)(2,1)}, bf16[64,1024]{1,0:T(8,128)(2,1)S(1)}, u32[]{:S(2)}, u32[]{:S(2)}) %collective-permute-start.5) | collective-permute-done | bytes 131104 | tf_op jit(solution)/shard_map/ppermute | solution.py:131
  33.1 1.2 collective-permute-done.2.refs_3_
  35.5 2.2 %collective-permute-start.7 = (bf16[256,1024]{1,0:T(8,128)(2,1)S(1)}, bf16[256,1024]{1,0:T(8,128)(2,1)S(1)}, u32[]{:S(2)}, u32[]{:S(2)}) collective-permute-start(bf16[256,1024]{1,0:T(8,128)(2,1)S(1)} %shard_map.97), channel_id=1, source_target_pairs={{0,12},{1,13},{2,14},{3,15},{4,0},{5,1},{6,2},{7,3},{8,4},{9,5},{1... | collective-permute-start | bytes 1572872 | tf_op jit(solution)/shard_map/ppermute | solution.py:131
  37.8 3.6 %all-to-all-start.1 = ((bf16[16,16,1024]{2,1,0:T(8,128)(2,1)}), bf16[16,16,1024]{2,1,0:T(8,128)(2,1)S(1)}, u32[]{:S(2)}, u32[]{:S(2)}) async-start(bf16[16,16,1024]{2,1,0:T(8,128)(2,1)} %copy-done.8), calls=%async_computation.1 | async-start | bytes 1048576 | tf_op jit(solution)/shard_map/all_to_all | solution.py:335
  45.0 10.0 %all-to-all-done.1.got_ref = bf16[16,16,1024]{2,1,0:T(8,128)(2,1)S(1)} async-done(((bf16[16,16,1024]{2,1,0:T(8,128)(2,1)}), bf16[16,16,1024]{2,1,0:T(8,128)(2,1)S(1)}, u32[]{:S(2)}, u32[]{:S(2)}) %all-to-all-start.1) | async-done | bytes 524320 | tf_op jit(solution)/shard_map/all_to_all | solution.py:335
  55.1 2.8 %collective-permute-start.9 = (bf16[128,1024]{1,0:T(8,128)(2,1)S(1)}, bf16[128,1024]{1,0:T(8,128)(2,1)S(1)}, u32[]{:S(2)}, u32[]{:S(2)}) collective-permute-start(bf16[128,1024]{1,0:T(8,128)(2,1)S(1)} %slice.21), channel_id=1, source_target_pairs={{0,12},{1,13},{2,14},{3,15},{4,0},{5,1},{6,2},{7,3},{8,4},{9,5},{1... | collective-permute-start | bytes 786440 | tf_op jit(solution)/shard_map/ppermute | solution.py:131
  57.9 2.4 %collective-permute-start.17 = (bf16[256,1024]{1,0:T(8,128)(2,1)S(1)}, bf16[256,1024]{1,0:T(8,128)(2,1)S(1)}, u32[]{:S(2)}, u32[]{:S(2)}) collective-permute-start(bf16[256,1024]{1,0:T(8,128)(2,1)S(1)} %shard_map.98), channel_id=1, source_target_pairs={{0,3},{1,0},{2,1},{3,2},{4,7},{5,4},{6,5},{7,6},{8,11},{9,8},{10,9... | collective-permute-start | bytes 1572872 | tf_op jit(solution)/shard_map/ppermute | solution.py:131
  60.4 3.1 %shard_map.99 = (f32[16,1024]{1,0:T(8,128)S(1)}, f32[48,1024]{1,0:T(8,128)S(1)}) custom-call(s32[12]{0:T(128)S(1)} %copy-done.18, bf16[16,80,256]{2,1,0:T(8,128)(2,1)S(1)} %all-to-all-done.rhs_ref.first_ref, bf16[16,16,1024]{2,1,0:T(8,128)(2,1)S(1)} %all-to-all-done.1.got_ref, s32[1,1024]{1,0:T(1,128)S(1)} %copy-done.19), custom_call_target="tpu_custom_call" | custom-call | flops 100000000 | bytes 1000000 | tf_op jit(solution)/shard_map/pallas_call | solution.py:46
  63.9 1.2 collective-permute-done.8.other_ref
  66.6 3.2 %collective-permute-start.15 = (bf16[256,1024]{1,0:T(8,128)(2,1)S(1)}, bf16[256,1024]{1,0:T(8,128)(2,1)S(1)}, u32[]{:S(2)}, u32[]{:S(2)}) collective-permute-start(bf16[256,1024]{1,0:T(8,128)(2,1)S(1)} %shard_map.101), channel_id=1, source_target_pairs={{0,12},{1,13},{2,14},{3,15},{4,0},{5,1},{6,2},{7,3},{8,4},{9,5},{1... | collective-permute-start | bytes 1572872 | tf_op jit(solution)/shard_map/ppermute | solution.py:131
  70.4 2.3 %collective-permute-done.16 = bf16[256,1024]{1,0:T(8,128)(2,1)S(1)} collective-permute-done((bf16[256,1024]{1,0:T(8,128)(2,1)S(1)}, bf16[256,1024]{1,0:T(8,128)(2,1)S(1)}, u32[]{:S(2)}, u32[]{:S(2)}) %collective-permute-start.16) | collective-permute-done | bytes 524320 | tf_op jit(solution)/shard_map/ppermute | solution.py:131
  73.3 1.6 %collective-permute-start.19 = (bf16[128,1024]{1,0:T(8,128)(2,1)S(1)}, bf16[128,1024]{1,0:T(8,128)(2,1)S(1)}, u32[]{:S(2)}, u32[]{:S(2)}) collective-permute-start(bf16[128,1024]{1,0:T(8,128)(2,1)S(1)} %slice.29), channel_id=1, source_target_pairs={{0,1},{1,2},{2,3},{3,0},{4,5},{5,6},{6,7},{7,4},{8,9},{9,10},{10,1... | collective-permute-start | bytes 786440 | tf_op jit(solution)/shard_map/ppermute | solution.py:131
  74.8 2.4 %shard_map.102 = (f32[16,1024]{1,0:T(8,128)S(1)}, f32[32,1024]{1,0:T(8,128)S(1)}) custom-call(s32[12]{0:T(128)S(1)} %copy-done.18, f32[16,1536]{1,0:T(8,128)S(1)} %shard_map.100.own_ref, f32[16,1536]{1,0:T(8,128)S(1)} %collective-permute-done.11.other_ref, f32[48,1024]{1,0:T(8,128)S(1)} %get-tuple-element.62.left_ref, ...), custom_call_target="tpu_custom_call" | custom-call | flops 100000000 | bytes 1000000 | tf_op jit(solution)/shard_map/pallas_call | solution.py:46
  77.4 4.2 %collective-permute-done.13.other_ref = f32[16,1024]{1,0:T(8,128)S(1)} collective-permute-done((f32[16,1024]{1,0:T(8,128)S(1)}, f32[16,1024]{1,0:T(8,128)S(1)}, u32[]{:S(2)}, u32[]{:S(2)}) %collective-permute-start.13) | collective-permute-done | bytes 65568 | tf_op jit(solution)/shard_map/ppermute | solution.py:292
  81.7 3.0 %collective-permute-start.23 = (bf16[128,1024]{1,0:T(8,128)(2,1)S(1)}, bf16[128,1024]{1,0:T(8,128)(2,1)S(1)}, u32[]{:S(2)}, u32[]{:S(2)}) collective-permute-start(bf16[128,1024]{1,0:T(8,128)(2,1)S(1)} %slice.25), channel_id=1, source_target_pairs={{0,12},{1,13},{2,14},{3,15},{4,0},{5,1},{6,2},{7,3},{8,4},{9,5},{1... | collective-permute-start | bytes 786440 | tf_op jit(solution)/shard_map/ppermute | solution.py:131
  86.5 1.3 collective-permute-done.21.other_ref
  87.8 1.8 %shard_map.104 = (f32[16,1024]{1,0:T(8,128)S(1)}, f32[16,1024]{1,0:T(8,128)S(1)}) custom-call(s32[12]{0:T(128)S(1)} %copy-done.18, f32[16,1536]{1,0:T(8,128)S(1)} %shard_map.103.own_ref, f32[16,1536]{1,0:T(8,128)S(1)} %collective-permute-done.21.other_ref, f32[32,1024]{1,0:T(8,128)S(1)} %get-tuple-element.67.left_ref, ...), custom_call_target="tpu_custom_call" | custom-call | flops 100000000 | bytes 1000000 | tf_op jit(solution)/shard_map/pallas_call | solution.py:46
  89.7 3.3 %collective-permute-start.22 = (f32[16,1024]{1,0:T(8,128)S(1)}, f32[16,1024]{1,0:T(8,128)S(1)}, u32[]{:S(2)}, u32[]{:S(2)}) collective-permute-start(f32[16,1024]{1,0:T(8,128)S(1)} %get-tuple-element.70.own_ref), channel_id=1, source_target_pairs={{0,64},{16,80},{32,96},{48,112},{64,0},{80,16},{96,32},{112,48},{1... | collective-permute-start | bytes 196616 | tf_op jit(solution)/shard_map/ppermute | solution.py:292
  93.0 4.6 %collective-permute-done.22.other_ref = f32[16,1024]{1,0:T(8,128)S(1)} collective-permute-done((f32[16,1024]{1,0:T(8,128)S(1)}, f32[16,1024]{1,0:T(8,128)S(1)}, u32[]{:S(2)}, u32[]{:S(2)}) %collective-permute-start.22) | collective-permute-done | bytes 65568 | tf_op jit(solution)/shard_map/ppermute | solution.py:292
  98.8 1.3 collective-permute-done.26.other_ref
  100.1 1.2 shard_map.106.own_ref
  101.4 5.8 %collective-permute-start.27 = (f32[16,1024]{1,0:T(8,128)S(1)}, f32[16,1024]{1,0:T(8,128)S(1)}, u32[]{:S(2)}, u32[]{:S(2)}) collective-permute-start(f32[16,1024]{1,0:T(8,128)S(1)} %shard_map.106.own_ref), channel_id=1, source_target_pairs={{0,192},{16,208},{32,224},{48,240},{64,128},{80,144},{96,160},{112... | collective-permute-start | bytes 196616 | tf_op jit(solution)/shard_map/ppermute | solution.py:292
  111.0 6.2 %all-to-all-start.2 = ((bf16[16,16,1408]{2,1,0:T(8,128)(2,1)}), bf16[16,16,1408]{2,1,0:T(8,128)(2,1)S(1)}, u32[]{:S(2)}, u32[]{:S(2)}) async-start(bf16[16,16,1408]{2,1,0:T(8,128)(2,1)} %shard_map.110), calls=%async_computation.2 | async-start | bytes 1441792 | tf_op jit(solution)/shard_map/all_to_all | solution.py:386
  118.1 12.5 %all-to-all-done.2.got_ref = bf16[16,16,1408]{2,1,0:T(8,128)(2,1)S(1)} async-done(((bf16[16,16,1408]{2,1,0:T(8,128)(2,1)}), bf16[16,16,1408]{2,1,0:T(8,128)(2,1)S(1)}, u32[]{:S(2)}, u32[]{:S(2)}) %all-to-all-start.2) | async-done | bytes 720928 | tf_op jit(solution)/shard_map/all_to_all | solution.py:386
  (95 shorter events, 21.4 us)
Async XLA Ops:
  4.6 29.8 %copy-start = (bf16[128,1024]{1,0:T(8,128)(2,1)S(1)}, bf16[128,1024]{1,0:T(8,128)(2,1)}, u32[]{:S(2)}) copy-start(bf16[128,1024]{1,0:T(8,128)(2,1)} %get-tuple-element.57.refs_0_) | copy-start | bytes 786436
  4.6 22.0 %all-to-all-start = ((bf16[16,80,256]{2,1,0:T(8,128)(2,1)}), bf16[16,80,256]{2,1,0:T(8,128)(2,1)S(1)}, u32[]{:S(2)}, u32[]{:S(2)}) async-start(bf16[16,80,256]{2,1,0:T(8,128)(2,1)} %get-tuple-element.39), calls=%async_computation | async-start | bytes 1310720 | tf_op jit(solution)/shard_map/all_to_all | solution.py:324
  11.8 13.3 %collective-permute-start.3 = (bf16[64,1024]{1,0:T(8,128)(2,1)}, bf16[64,1024]{1,0:T(8,128)(2,1)S(1)}, u32[]{:S(2)}, u32[]{:S(2)}) collective-permute-start(bf16[64,1024]{1,0:T(8,128)(2,1)} %get-tuple-element.49.refs_0_), channel_id=1, source_target_pairs={{0,4},{1,5},{2,6},{3,7},{4,8},{5,9},{6,10},{7,11},{8,12},{9,13},{1... | collective-permute-start | bytes 393224 | tf_op jit(solution)/shard_map/ppermute | solution.py:131
  13.7 19.4 %collective-permute-start = (bf16[128,1024]{1,0:T(8,128)(2,1)}, bf16[128,1024]{1,0:T(8,128)(2,1)S(1)}, u32[]{:S(2)}, u32[]{:S(2)}) collective-permute-start(bf16[128,1024]{1,0:T(8,128)(2,1)} %get-tuple-element.57.refs_0_), channel_id=1, source_target_pairs={{0,1},{1,2},{2,3},{3,0},{4,5},{5,6},{6,7},{7,4},{8,9},{9,10},{10,1... | collective-permute-start | bytes 786440 | tf_op jit(solution)/shard_map/ppermute | solution.py:131
  15.2 17.9 %collective-permute-start.1 = (bf16[128,1024]{1,0:T(8,128)(2,1)}, bf16[128,1024]{1,0:T(8,128)(2,1)S(1)}, u32[]{:S(2)}, u32[]{:S(2)}) collective-permute-start(bf16[128,1024]{1,0:T(8,128)(2,1)} %get-tuple-element.57.refs_0_), channel_id=1, source_target_pairs={{0,3},{1,0},{2,1},{3,2},{4,7},{5,4},{6,5},{7,6},{8,11},{9,8},{10,9... | collective-permute-start | bytes 786440 | tf_op jit(solution)/shard_map/ppermute | solution.py:131
  17.0 17.4 %collective-permute-start.2 = (bf16[128,1024]{1,0:T(8,128)(2,1)}, bf16[128,1024]{1,0:T(8,128)(2,1)S(1)}, u32[]{:S(2)}, u32[]{:S(2)}) collective-permute-start(bf16[128,1024]{1,0:T(8,128)(2,1)} %get-tuple-element.57.refs_0_), channel_id=1, source_target_pairs={{0,2},{1,3},{2,0},{3,1},{4,6},{5,7},{6,4},{7,5},{8,10},{9,11},{10,... | collective-permute-start | bytes 786440 | tf_op jit(solution)/shard_map/ppermute | solution.py:131
  18.7 8.8 %collective-permute-start.4 = (bf16[64,1024]{1,0:T(8,128)(2,1)}, bf16[64,1024]{1,0:T(8,128)(2,1)S(1)}, u32[]{:S(2)}, u32[]{:S(2)}) collective-permute-start(bf16[64,1024]{1,0:T(8,128)(2,1)} %get-tuple-element.49.refs_0_), channel_id=1, source_target_pairs={{0,12},{1,13},{2,14},{3,15},{4,0},{5,1},{6,2},{7,3},{8,4},{9,5},{1... | collective-permute-start | bytes 393224 | tf_op jit(solution)/shard_map/ppermute | solution.py:131
  25.8 6.7 %collective-permute-start.5 = (bf16[64,1024]{1,0:T(8,128)(2,1)}, bf16[64,1024]{1,0:T(8,128)(2,1)S(1)}, u32[]{:S(2)}, u32[]{:S(2)}) collective-permute-start(bf16[64,1024]{1,0:T(8,128)(2,1)} %get-tuple-element.49.refs_0_), channel_id=1, source_target_pairs={{0,8},{1,9},{2,10},{3,11},{4,12},{5,13},{6,14},{7,15},{8,0},{9,1},... | collective-permute-start | bytes 393224 | tf_op jit(solution)/shard_map/ppermute | solution.py:131
  34.4 20.6 %collective-permute-start.6 = (bf16[256,1024]{1,0:T(8,128)(2,1)S(1)}, bf16[256,1024]{1,0:T(8,128)(2,1)S(1)}, u32[]{:S(2)}, u32[]{:S(2)}) collective-permute-start(bf16[256,1024]{1,0:T(8,128)(2,1)S(1)} %shard_map.97), channel_id=1, source_target_pairs={{0,4},{1,5},{2,6},{3,7},{4,8},{5,9},{6,10},{7,11},{8,12},{9,13},{1... | collective-permute-start | bytes 1572872 | tf_op jit(solution)/shard_map/ppermute | solution.py:131
  35.5 19.5 %collective-permute-start.7 = (bf16[256,1024]{1,0:T(8,128)(2,1)S(1)}, bf16[256,1024]{1,0:T(8,128)(2,1)S(1)}, u32[]{:S(2)}, u32[]{:S(2)}) collective-permute-start(bf16[256,1024]{1,0:T(8,128)(2,1)S(1)} %shard_map.97), channel_id=1, source_target_pairs={{0,12},{1,13},{2,14},{3,15},{4,0},{5,1},{6,2},{7,3},{8,4},{9,5},{1... | collective-permute-start | bytes 1572872 | tf_op jit(solution)/shard_map/ppermute | solution.py:131
  37.8 17.3 %all-to-all-start.1 = ((bf16[16,16,1024]{2,1,0:T(8,128)(2,1)}), bf16[16,16,1024]{2,1,0:T(8,128)(2,1)S(1)}, u32[]{:S(2)}, u32[]{:S(2)}) async-start(bf16[16,16,1024]{2,1,0:T(8,128)(2,1)} %copy-done.8), calls=%async_computation.1 | async-start | bytes 1048576 | tf_op jit(solution)/shard_map/all_to_all | solution.py:335
  55.1 10.0 %collective-permute-start.9 = (bf16[128,1024]{1,0:T(8,128)(2,1)S(1)}, bf16[128,1024]{1,0:T(8,128)(2,1)S(1)}, u32[]{:S(2)}, u32[]{:S(2)}) collective-permute-start(bf16[128,1024]{1,0:T(8,128)(2,1)S(1)} %slice.21), channel_id=1, source_target_pairs={{0,12},{1,13},{2,14},{3,15},{4,0},{5,1},{6,2},{7,3},{8,4},{9,5},{1... | collective-permute-start | bytes 786440 | tf_op jit(solution)/shard_map/ppermute | solution.py:131
  57.8 7.7 %collective-permute-start.10 = (bf16[128,1024]{1,0:T(8,128)(2,1)S(1)}, bf16[128,1024]{1,0:T(8,128)(2,1)S(1)}, u32[]{:S(2)}, u32[]{:S(2)}) collective-permute-start(bf16[128,1024]{1,0:T(8,128)(2,1)S(1)} %slice.22), channel_id=1, source_target_pairs={{0,4},{1,5},{2,6},{3,7},{4,8},{5,9},{6,10},{7,11},{8,12},{9,13},{1... | collective-permute-start | bytes 786440 | tf_op jit(solution)/shard_map/ppermute | solution.py:131
  57.9 11.9 %collective-permute-start.17 = (bf16[256,1024]{1,0:T(8,128)(2,1)S(1)}, bf16[256,1024]{1,0:T(8,128)(2,1)S(1)}, u32[]{:S(2)}, u32[]{:S(2)}) collective-permute-start(bf16[256,1024]{1,0:T(8,128)(2,1)S(1)} %shard_map.98), channel_id=1, source_target_pairs={{0,3},{1,0},{2,1},{3,2},{4,7},{5,4},{6,5},{7,6},{8,11},{9,8},{10,9... | collective-permute-start | bytes 1572872 | tf_op jit(solution)/shard_map/ppermute | solution.py:131
  60.4 12.3 %collective-permute-start.16 = (bf16[256,1024]{1,0:T(8,128)(2,1)S(1)}, bf16[256,1024]{1,0:T(8,128)(2,1)S(1)}, u32[]{:S(2)}, u32[]{:S(2)}) collective-permute-start(bf16[256,1024]{1,0:T(8,128)(2,1)S(1)} %shard_map.98), channel_id=1, source_target_pairs={{0,1},{1,2},{2,3},{3,0},{4,5},{5,6},{6,7},{7,4},{8,9},{9,10},{10,1... | collective-permute-start | bytes 1572872 | tf_op jit(solution)/shard_map/ppermute | solution.py:131
  63.5 1.5 %collective-permute-start.8 = (f32[16,1024]{1,0:T(8,128)S(1)}, f32[16,1024]{1,0:T(8,128)S(1)}, u32[]{:S(2)}, u32[]{:S(2)}) collective-permute-start(f32[16,1024]{1,0:T(8,128)S(1)} %get-tuple-element.54.own_ref), channel_id=1, source_target_pairs={{0,16},{16,0},{32,48},{48,32},{64,80},{80,64},{96,112},{112,96},{1... | collective-permute-start | bytes 196616 | tf_op jit(solution)/shard_map/ppermute | solution.py:292
  66.6 15.1 %collective-permute-start.14 = (bf16[256,1024]{1,0:T(8,128)(2,1)S(1)}, bf16[256,1024]{1,0:T(8,128)(2,1)S(1)}, u32[]{:S(2)}, u32[]{:S(2)}) collective-permute-start(bf16[256,1024]{1,0:T(8,128)(2,1)S(1)} %shard_map.101), channel_id=1, source_target_pairs={{0,4},{1,5},{2,6},{3,7},{4,8},{5,9},{6,10},{7,11},{8,12},{9,13},{1... | collective-permute-start | bytes 1572872 | tf_op jit(solution)/shard_map/ppermute | solution.py:131
  66.6 15.1 %collective-permute-start.15 = (bf16[256,1024]{1,0:T(8,128)(2,1)S(1)}, bf16[256,1024]{1,0:T(8,128)(2,1)S(1)}, u32[]{:S(2)}, u32[]{:S(2)}) collective-permute-start(bf16[256,1024]{1,0:T(8,128)(2,1)S(1)} %shard_map.101), channel_id=1, source_target_pairs={{0,12},{1,13},{2,14},{3,15},{4,0},{5,1},{6,2},{7,3},{8,4},{9,5},{1... | collective-permute-start | bytes 1572872 | tf_op jit(solution)/shard_map/ppermute | solution.py:131
  69.8 3.4 %collective-permute-start.12 = (f32[48,1024]{1,0:T(8,128)S(1)}, f32[48,1024]{1,0:T(8,128)S(1)}, u32[]{:S(2)}, u32[]{:S(2)}) collective-permute-start(f32[48,1024]{1,0:T(8,128)S(1)} %get-tuple-element.62.left_ref), channel_id=1, source_target_pairs={{0,16},{16,0},{32,48},{48,32},{64,80},{80,64},{96,112},{112,96},{1... | collective-permute-start | bytes 589832 | tf_op jit(solution)/shard_map/ppermute | solution.py:292
  69.8 5.0 %collective-permute-start.11 = (f32[16,1536]{1,0:T(8,128)S(1)}, f32[16,1536]{1,0:T(8,128)S(1)}, u32[]{:S(2)}, u32[]{:S(2)}) collective-permute-start(f32[16,1536]{1,0:T(8,128)S(1)} %shard_map.100.own_ref), channel_id=1, source_target_pairs={{0,16},{16,0},{32,48},{48,32},{64,80},{80,64},{96,112},{112,96},{1... | collective-permute-start | bytes 294920 | tf_op jit(solution)/shard_map/ppermute | solution.py:292
  72.7 12.1 %collective-permute-start.18 = (bf16[128,1024]{1,0:T(8,128)(2,1)S(1)}, bf16[128,1024]{1,0:T(8,128)(2,1)S(1)}, u32[]{:S(2)}, u32[]{:S(2)}) collective-permute-start(bf16[128,1024]{1,0:T(8,128)(2,1)S(1)} %slice.28), channel_id=1, source_target_pairs={{0,3},{1,0},{2,1},{3,2},{4,7},{5,4},{6,5},{7,6},{8,11},{9,8},{10,9... | collective-permute-start | bytes 786440 | tf_op jit(solution)/shard_map/ppermute | solution.py:131
  73.3 11.5 %collective-permute-start.19 = (bf16[128,1024]{1,0:T(8,128)(2,1)S(1)}, bf16[128,1024]{1,0:T(8,128)(2,1)S(1)}, u32[]{:S(2)}, u32[]{:S(2)}) collective-permute-start(bf16[128,1024]{1,0:T(8,128)(2,1)S(1)} %slice.29), channel_id=1, source_target_pairs={{0,1},{1,2},{2,3},{3,0},{4,5},{5,6},{6,7},{7,4},{8,9},{9,10},{10,1... | collective-permute-start | bytes 786440 | tf_op jit(solution)/shard_map/ppermute | solution.py:131
  77.3 4.3 %collective-permute-start.13 = (f32[16,1024]{1,0:T(8,128)S(1)}, f32[16,1024]{1,0:T(8,128)S(1)}, u32[]{:S(2)}, u32[]{:S(2)}) collective-permute-start(f32[16,1024]{1,0:T(8,128)S(1)} %get-tuple-element.63.own_ref), channel_id=1, source_target_pairs={{0,32},{16,48},{32,0},{48,16},{64,96},{80,112},{96,64},{112,80},{1... | collective-permute-start | bytes 196616 | tf_op jit(solution)/shard_map/ppermute | solution.py:292
  81.5 5.0 %collective-permute-start.20 = (f32[32,1024]{1,0:T(8,128)S(1)}, f32[32,1024]{1,0:T(8,128)S(1)}, u32[]{:S(2)}, u32[]{:S(2)}) collective-permute-start(f32[32,1024]{1,0:T(8,128)S(1)} %get-tuple-element.67.left_ref), channel_id=1, source_target_pairs={{0,32},{16,48},{32,0},{48,16},{64,96},{80,112},{96,64},{112,80},{1... | collective-permute-start | bytes 393224 | tf_op jit(solution)/shard_map/ppermute | solution.py:292
  81.7 16.0 %collective-permute-start.23 = (bf16[128,1024]{1,0:T(8,128)(2,1)S(1)}, bf16[128,1024]{1,0:T(8,128)(2,1)S(1)}, u32[]{:S(2)}, u32[]{:S(2)}) collective-permute-start(bf16[128,1024]{1,0:T(8,128)(2,1)S(1)} %slice.25), channel_id=1, source_target_pairs={{0,12},{1,13},{2,14},{3,15},{4,0},{5,1},{6,2},{7,3},{8,4},{9,5},{1... | collective-permute-start | bytes 786440 | tf_op jit(solution)/shard_map/ppermute | solution.py:131
  84.7 13.0 %collective-permute-start.24 = (bf16[128,1024]{1,0:T(8,128)(2,1)S(1)}, bf16[128,1024]{1,0:T(8,128)(2,1)S(1)}, u32[]{:S(2)}, u32[]{:S(2)}) collective-permute-start(bf16[128,1024]{1,0:T(8,128)(2,1)S(1)} %slice.26), channel_id=1, source_target_pairs={{0,4},{1,5},{2,6},{3,7},{4,8},{5,9},{6,10},{7,11},{8,12},{9,13},{1... | collective-permute-start | bytes 786440 | tf_op jit(solution)/shard_map/ppermute | solution.py:131
  86.5 1.3 collective-permute-start.21
  89.7 8.0 %collective-permute-start.22 = (f32[16,1024]{1,0:T(8,128)S(1)}, f32[16,1024]{1,0:T(8,128)S(1)}, u32[]{:S(2)}, u32[]{:S(2)}) collective-permute-start(f32[16,1024]{1,0:T(8,128)S(1)} %get-tuple-element.70.own_ref), channel_id=1, source_target_pairs={{0,64},{16,80},{32,96},{48,112},{64,0},{80,16},{96,32},{112,48},{1... | collective-permute-start | bytes 196616 | tf_op jit(solution)/shard_map/ppermute | solution.py:292
  92.9 5.9 %collective-permute-start.25 = (f32[16,1024]{1,0:T(8,128)S(1)}, f32[16,1024]{1,0:T(8,128)S(1)}, u32[]{:S(2)}, u32[]{:S(2)}) collective-permute-start(f32[16,1024]{1,0:T(8,128)S(1)} %get-tuple-element.73.left_ref), channel_id=1, source_target_pairs={{0,64},{16,80},{32,96},{48,112},{64,0},{80,16},{96,32},{112,48},{1... | collective-permute-start | bytes 196616 | tf_op jit(solution)/shard_map/ppermute | solution.py:292
  98.8 1.3 collective-permute-start.26
  101.4 8.7 %collective-permute-start.27 = (f32[16,1024]{1,0:T(8,128)S(1)}, f32[16,1024]{1,0:T(8,128)S(1)}, u32[]{:S(2)}, u32[]{:S(2)}) collective-permute-start(f32[16,1024]{1,0:T(8,128)S(1)} %shard_map.106.own_ref), channel_id=1, source_target_pairs={{0,192},{16,208},{32,224},{48,240},{64,128},{80,144},{96,160},{112... | collective-permute-start | bytes 196616 | tf_op jit(solution)/shard_map/ppermute | solution.py:292
  111.0 19.7 %all-to-all-start.2 = ((bf16[16,16,1408]{2,1,0:T(8,128)(2,1)}), bf16[16,16,1408]{2,1,0:T(8,128)(2,1)S(1)}, u32[]{:S(2)}, u32[]{:S(2)}) async-start(bf16[16,16,1408]{2,1,0:T(8,128)(2,1)} %shard_map.110), calls=%async_computation.2 | async-start | bytes 1441792 | tf_op jit(solution)/shard_map/all_to_all | solution.py:386
  (19 other events, 165.0 us)
